TPU v7x, 128 devices: a whole 4x4x4 slice. The times are simulated.
128 devices in a mesh: drop: 8 (over x, core), blk: 16 (over z, y).
Axes of the slice: x: 4, y: 4, z: 4, core: 2. Of those that a mesh axis runs over, the one named last changes fastest.
Arguments:
- right_side: float32 [65536, 128], P(('drop', 'blk')), may hold values from -6 to 6
- near_blocks: bfloat16 [512, 40, 128, 128], P(('drop', 'blk')), may hold values from -0.15625 to 0.15625
- neighbours: int32 [512, 40], P(('drop', 'blk')), may hold values from 0 to 191
- counts: int32 [512], P(('drop', 'blk')), may hold values from 1 to 40
- leaf_inverse: bfloat16 [512, 128, 128], P(('drop', 'blk'))
- couple_left: bfloat16 [3, 64, 65536], P(None, None, ('drop', 'blk')), may hold values from -0.75 to 0.75
- couple_right: bfloat16 [3, 64, 65536], P(None, None, ('drop', 'blk')), may hold values from -0.0625 to 0.0625
- prec_left: bfloat16 [3, 64, 65536], P(None, None, ('drop', 'blk')), may hold values from -1 to 1
- prec_right: bfloat16 [3, 64, 65536], P(None, None, ('drop', 'blk')), may hold values from -0.0625 to 0.0625
Outputs:
- solution: float32 [65536, 128], P(('drop', 'blk'))
- residual: float32 [65536, 128], P(('drop', 'blk'))
Inputs may be any that keep to these rules, and one draw needn't show every extreme that they name: `neighbours`: the three groups' blocks are numbered group g - 1 first, each group's blocks in row order. Slots k >= counts of a row are ignored.
All inputs are finite; a program needn't handle non-finite values.
Results may differ from a plain program's by a relative error of at most 0.035.
Values may be sent and summed in bfloat16 or wider, within the bound.
No kernel may reach another device: no remote copies, remote signals or barrier semaphores. Data moves between devices by JAX's collectives and lax.ppermute only.
A program may use at most 64 MiB of HBM per device.

v0:
```python
import jax
import jax.numpy as jnp
from jax import lax
from jax.sharding import PartitionSpec as P

ITERS = 3


def with_halo(array, sides, width):
    for axis, dim in sides:
        size, length = (lax.axis_size(axis), array.shape[dim])
        up = [(i, (i + 1) % size) for i in range(size - 1)]
        down = [(j, i) for i, j in up]
        last = lax.slice_in_dim(array, length - width, length, axis=dim)
        leading = lax.slice_in_dim(array, 0, width, axis=dim)
        before = lax.ppermute(last, axis, up)
        after = lax.ppermute(leading, axis, down)
        array = jnp.concatenate([before, array, after], axis=dim)
    return array


def from_partner(array, axis, bit):
    return lax.ppermute(array, axis, [(i, i ^ 1 << bit) for i in range(lax.axis_size(axis))])


def near_field(flat_b, near_blocks, neighbours, counts):
    rows, width = flat_b.shape
    nblocks, slots, size, _ = near_blocks.shape
    grouped = lax.all_gather(flat_b, "blk", axis=0, tiled=True)
    window = with_halo(grouped, (("drop", 0),), grouped.shape[0])
    tiles = window.reshape(-1, size, width)
    picked = tiles[neighbours]
    live = lax.broadcasted_iota(jnp.int32, (nblocks, slots), 1) < counts[:, None]
    picked = jnp.where(live[:, :, None, None], picked, jnp.zeros((), picked.dtype))
    product = jnp.einsum("bkij,bkjn->bin", near_blocks, picked, preferred_element_type=jnp.float32)
    return product.reshape(rows, width)


def subtree(term, level):
    partial_value = lax.psum(term, "blk")
    for bit in range(level):
        partial_value = partial_value + from_partner(partial_value, "drop", bit)
    return from_partner(partial_value.astype(jnp.bfloat16), "drop", level).astype(
        partial_value.dtype
    )


def coupling(flat_b, left, right, level):
    term = jnp.dot(right, flat_b, preferred_element_type=jnp.float32)
    other = subtree(term, level)
    other_b = other.astype(jnp.bfloat16)
    return lax.dot_general(
        left, other_b, (((0,), (0,)), ((), ())), preferred_element_type=jnp.float32
    )


def operate(solution, near_blocks, neighbours, counts, couple_left, couple_right):
    flat_b = solution.astype(jnp.bfloat16)
    image = solution + near_field(flat_b, near_blocks, neighbours, counts)
    for level in range(couple_left.shape[0]):
        image = image + coupling(flat_b, couple_left[level], couple_right[level], level)
    return image


def precondition(resid, leaf_inverse, prec_left, prec_right):
    nblocks, size, _ = leaf_inverse.shape
    tiles = resid.astype(jnp.bfloat16).reshape(nblocks, size, resid.shape[1])
    fixed = jnp.einsum(
        "bij,bjn->bin", leaf_inverse, tiles, preferred_element_type=jnp.float32
    ).reshape(resid.shape)
    for level in range(prec_left.shape[0]):
        fixed = fixed - coupling(
            fixed.astype(jnp.bfloat16), prec_left[level], prec_right[level], level
        )
    return fixed


def on_device(
    right_side,
    near_blocks,
    neighbours,
    counts,
    leaf_inverse,
    couple_left,
    couple_right,
    prec_left,
    prec_right,
):
    solution = precondition(right_side, leaf_inverse, prec_left, prec_right)
    resid = right_side
    for step in range(ITERS):
        resid = right_side - operate(
            solution, near_blocks, neighbours, counts, couple_left, couple_right
        )
        solution = solution + precondition(resid, leaf_inverse, prec_left, prec_right)
    return (solution, resid)


def solution(mesh):
    in_specs = (
        P(("drop", "blk"), None),
        P(("drop", "blk"), None, None, None),
        P(("drop", "blk"), None),
        P(("drop", "blk")),
        P(("drop", "blk"), None, None),
        P(None, None, ("drop", "blk")),
        P(None, None, ("drop", "blk")),
        P(None, None, ("drop", "blk")),
        P(None, None, ("drop", "blk")),
    )
    out_specs = (P(("drop", "blk"), None), P(("drop", "blk"), None))
    return jax.shard_map(
        on_device, mesh=mesh, in_specs=in_specs, out_specs=out_specs, check_vma=False
    )
```

profile of v0, /device:TPU:0, one launch (start us, length us, event | category | flops | bytes accessed | tf_op | source)
XLA Modules:
  0.0 1441.3 jit_solution(13425123487029382715)
XLA Ops:
  9.6 76.1 %psum.147 = bf16[64,128]{0,1:T(8,128)(2,1)S(1)} all-reduce(f32[64,128]{0,1:T(8,128)S(1)} %convolution_bitcast_fusion.27), channel_id=1, replica_groups=mesh['drop'=8,'blk'=16] {'blk'}, use_global_device_ids=true, to_apply=%region_0.0 | all-reduce | flops 8192 | bytes 49152 | tf_op jit(solution)/shard_map/psum | solution.py:40
  88.9 69.5 %psum.148 = f32[64,128]{1,0:T(8,128)S(1)} all-reduce(f32[64,128]{1,0:T(8,128)S(1)} %convolution_bitcast_fusion.41), channel_id=1, replica_groups=mesh['drop'=8,'blk'=16] {'blk'}, use_global_device_ids=true, to_apply=%region_1.0 | all-reduce | flops 8192 | bytes 65536 | tf_op jit(solution)/shard_map/psum | solution.py:40
  159.6 1.6 collective-permute-start.2
  161.2 2.2 collective-permute-done.2
  165.5 69.5 %psum.149 = f32[64,128]{1,0:T(8,128)S(1)} all-reduce(f32[64,128]{1,0:T(8,128)S(1)} %convolution_bitcast_fusion.40), channel_id=1, replica_groups=mesh['drop'=8,'blk'=16] {'blk'}, use_global_device_ids=true, to_apply=%region_2.0 | all-reduce | flops 8192 | bytes 65536 | tf_op jit(solution)/shard_map/psum | solution.py:40
  236.3 1.5 collective-permute-start.4
  237.8 2.4 collective-permute-done.4
  240.2 3.1 collective-permute-start.5
  243.3 2.2 collective-permute-done.5
  245.5 1.7 fusion.134
  247.3 44.2 %all-gather.4.cloned.1.call-done = bf16[8192,128]{0,1:T(8,128)(2,1)} async-done(((bf16[512,128]{0,1:T(8,128)(2,1)}), bf16[8192,128]{0,1:T(8,128)(2,1)}) %all-gather.4.cloned.1.call-update) | async-done | bytes 2097168 | tf_op jit(solution)/shard_map/all_gather | solution.py:29
  291.5 1.4 collective-permute-start.6
  298.9 73.1 %all-reduce.6 = (f32[64,128]{1,0:T(8,128)S(1)}, bf16[64,128]{0,1:T(8,128)(2,1)S(1)}, f32[64,128]{1,0:T(8,128)S(1)}) all-reduce(f32[64,128]{1,0:T(8,128)S(1)} %convolution_bitcast_fusion.39, f32[64,128]{0,1:T(8,128)S(1)} %convolution_bitcast_fusion.26, ...), channel_id=1, replica_groups=mesh['drop'=8,'blk'=16] {'blk'}, use_global_device_ids=true, to_apply=%region_4.5 | all-reduce | flops 24576 | bytes 180224 | tf_op jit(solution)/shard_map/psum | solution.py:40
  373.9 4.3 collective-permute-start.10
  381.1 2.0 collective-permute-done.12
  383.1 2.8 collective-permute-start.13
  385.9 5.4 pad_maximum_fusion
  391.3 8.7 copy.50
  399.9 10.5 gather_fusion
  410.5 5.7 fusion.4
  417.1 69.6 %psum.153 = bf16[64,128]{0,1:T(8,128)(2,1)S(1)} all-reduce(f32[64,128]{0,1:T(8,128)S(1)} %convolution_bitcast_fusion.25), channel_id=1, replica_groups=mesh['drop'=8,'blk'=16] {'blk'}, use_global_device_ids=true, to_apply=%region_6.7 | all-reduce | flops 8192 | bytes 49152 | tf_op jit(solution)/shard_map/psum | solution.py:40
  488.3 69.7 %psum.154 = f32[64,128]{1,0:T(8,128)S(1)} all-reduce(f32[64,128]{1,0:T(8,128)S(1)} %convolution_bitcast_fusion.37), channel_id=1, replica_groups=mesh['drop'=8,'blk'=16] {'blk'}, use_global_device_ids=true, to_apply=%region_7.8 | all-reduce | flops 8192 | bytes 65536 | tf_op jit(solution)/shard_map/psum | solution.py:40
  559.7 3.3 collective-permute-done.16
  563.4 69.5 %psum.155 = f32[64,128]{1,0:T(8,128)S(1)} all-reduce(f32[64,128]{1,0:T(8,128)S(1)} %convolution_bitcast_fusion.36), channel_id=1, replica_groups=mesh['drop'=8,'blk'=16] {'blk'}, use_global_device_ids=true, to_apply=%region_8.9 | all-reduce | flops 8192 | bytes 65536 | tf_op jit(solution)/shard_map/psum | solution.py:40
  634.6 3.5 collective-permute-done.18
  639.0 4.4 collective-permute-done.19
  644.3 42.1 %all-gather.6.cloned.1.call-done = bf16[8192,128]{0,1:T(8,128)(2,1)} async-done(((bf16[512,128]{0,1:T(8,128)(2,1)}), bf16[8192,128]{0,1:T(8,128)(2,1)}) %all-gather.6.cloned.1.call-update) | async-done | bytes 2097168 | tf_op jit(solution)/shard_map/all_gather | solution.py:29
  686.5 2.6 collective-permute-start.20
  693.7 73.0 %all-reduce.7 = (f32[64,128]{1,0:T(8,128)S(1)}, f32[64,128]{1,0:T(8,128)S(1)}, bf16[64,128]{0,1:T(8,128)(2,1)S(1)}) all-reduce(f32[64,128]{1,0:T(8,128)S(1)} %convolution_bitcast_fusion.34, f32[64,128]{1,0:T(8,128)S(1)} %convolution_bitcast_fusion.35, ...), channel_id=1, replica_groups=mesh['drop'=8,'blk'=16] {'blk'}, use_global_device_ids=true, to_apply=%region_11.12 | all-reduce | flops 24576 | bytes 180224 | tf_op jit(solution)/shard_map/psum | solution.py:40
  768.0 3.1 collective-permute-start.26
  771.3 1.7 collective-permute-done.26
  773.0 3.7 collective-permute-start.27
  776.9 1.5 collective-permute-done.27
  778.7 5.9 pad_maximum_fusion.1
  784.5 8.7 copy.54
  793.2 10.5 gather_fusion.1
  803.7 5.6 fusion.2
  810.2 69.6 %psum.159 = bf16[64,128]{0,1:T(8,128)(2,1)S(1)} all-reduce(f32[64,128]{0,1:T(8,128)S(1)} %convolution_bitcast_fusion.23), channel_id=1, replica_groups=mesh['drop'=8,'blk'=16] {'blk'}, use_global_device_ids=true, to_apply=%region_12.13 | all-reduce | flops 8192 | bytes 49152 | tf_op jit(solution)/shard_map/psum | solution.py:40
  881.4 69.5 %psum.160 = f32[64,128]{1,0:T(8,128)S(1)} all-reduce(f32[64,128]{1,0:T(8,128)S(1)} %convolution_bitcast_fusion.33), channel_id=1, replica_groups=mesh['drop'=8,'blk'=16] {'blk'}, use_global_device_ids=true, to_apply=%region_13.14 | all-reduce | flops 8192 | bytes 65536 | tf_op jit(solution)/shard_map/psum | solution.py:40
  952.1 1.9 collective-permute-start.30
  954.1 1.9 collective-permute-done.30
  956.3 69.5 %psum.161 = f32[64,128]{1,0:T(8,128)S(1)} all-reduce(f32[64,128]{1,0:T(8,128)S(1)} %convolution_bitcast_fusion.32), channel_id=1, replica_groups=mesh['drop'=8,'blk'=16] {'blk'}, use_global_device_ids=true, to_apply=%region_14.15 | all-reduce | flops 8192 | bytes 65536 | tf_op jit(solution)/shard_map/psum | solution.py:40
  1027.1 1.9 collective-permute-start.32
  1028.9 2.1 collective-permute-done.32
  1031.0 3.6 collective-permute-start.33
  1034.6 1.7 collective-permute-done.33
  1037.2 44.7 %all-gather.8.cloned.1.call-done = bf16[8192,128]{0,1:T(8,128)(2,1)} async-done(((bf16[512,128]{0,1:T(8,128)(2,1)}), bf16[8192,128]{0,1:T(8,128)(2,1)}) %all-gather.8.cloned.1.call-update) | async-done | bytes 2097168 | tf_op jit(solution)/shard_map/all_gather | solution.py:29
  1087.9 73.1 %all-reduce.8 = (f32[64,128]{1,0:T(8,128)S(1)}, f32[64,128]{1,0:T(8,128)S(1)}, bf16[64,128]{0,1:T(8,128)(2,1)S(1)}) all-reduce(f32[64,128]{1,0:T(8,128)S(1)} %convolution_bitcast_fusion.30, f32[64,128]{1,0:T(8,128)S(1)} %convolution_bitcast_fusion.31, ...), channel_id=1, replica_groups=mesh['drop'=8,'blk'=16] {'blk'}, use_global_device_ids=true, to_apply=%region_17.18 | all-reduce | flops 24576 | bytes 180224 | tf_op jit(solution)/shard_map/psum | solution.py:40
  1162.3 4.2 collective-permute-start.40
  1166.8 1.7 collective-permute-done.40
  1168.4 3.7 collective-permute-start.41
  1173.9 1.8 convolution_bitcast_fusion.3
  1175.7 5.4 pad_maximum_fusion.2
  1181.0 8.7 copy.58
  1189.7 10.5 gather_fusion.2
  1200.2 5.7 fusion
  1207.6 69.6 %psum.165 = bf16[64,128]{0,1:T(8,128)(2,1)S(1)} all-reduce(f32[64,128]{0,1:T(8,128)S(1)} %convolution_bitcast_fusion.21), channel_id=1, replica_groups=mesh['drop'=8,'blk'=16] {'blk'}, use_global_device_ids=true, to_apply=%region_18.19 | all-reduce | flops 8192 | bytes 49152 | tf_op jit(solution)/shard_map/psum | solution.py:40
  1278.7 69.5 %psum.166 = f32[64,128]{1,0:T(8,128)S(1)} all-reduce(f32[64,128]{1,0:T(8,128)S(1)} %convolution_bitcast_fusion.29), channel_id=1, replica_groups=mesh['drop'=8,'blk'=16] {'blk'}, use_global_device_ids=true, to_apply=%region_19.20 | all-reduce | flops 8192 | bytes 65536 | tf_op jit(solution)/shard_map/psum | solution.py:40
  1349.5 2.0 collective-permute-start.44
  1351.4 1.9 collective-permute-done.44
  1353.7 69.5 %psum.167 = f32[64,128]{1,0:T(8,128)S(1)} all-reduce(f32[64,128]{1,0:T(8,128)S(1)} %convolution_bitcast_fusion.28), channel_id=1, replica_groups=mesh['drop'=8,'blk'=16] {'blk'}, use_global_device_ids=true, to_apply=%region_20.21 | all-reduce | flops 8192 | bytes 65536 | tf_op jit(solution)/shard_map/psum | solution.py:40
  1424.4 1.9 collective-permute-start.46
  1426.3 2.0 collective-permute-done.46
  1428.4 3.6 collective-permute-start.47
  (173 shorter events, 59.2 us)
Async XLA Ops:
  7.2 1.2 copy-start
  7.2 289.6 %copy-start.3 = (bf16[3,64,512]{2,1,0:T(8,128)(2,1)S(1)}, bf16[3,64,512]{2,1,0:T(8,128)(2,1)}, u32[]{:S(2)}) copy-start(bf16[3,64,512]{2,1,0:T(8,128)(2,1)} %param.15) | copy-start | bytes 589828
  7.2 371.0 %copy-start.5 = (bf16[3,64,512]{2,1,0:T(8,128)(2,1)S(1)}, bf16[3,64,512]{2,1,0:T(8,128)(2,1)}, u32[]{:S(2)}) copy-start(bf16[3,64,512]{2,1,0:T(8,128)(2,1)} %param.14) | copy-start | bytes 589828
  7.2 284.3 %all-gather.4.cloned.1.call-start = ((), (), s32[]{:S(2)}) async-start(), calls=%async_computation | async-start | bytes 2228224 | tf_op jit(solution)/shard_map/all_gather | solution.py:29
  85.6 1.2 collective-permute-start
  158.4 1.2 collective-permute-start.1
  159.6 3.8 collective-permute-start.2
  235.0 1.2 collective-permute-start.3
  236.3 3.9 collective-permute-start.4
  240.2 5.3 collective-permute-start.5
  247.2 439.3 %all-gather.6.cloned.1.call-start = ((), (), s32[]{:S(2)}) async-start(), calls=%async_computation.1 | async-start | bytes 2228224 | tf_op jit(solution)/shard_map/all_gather | solution.py:29
  291.5 94.4 %collective-permute-start.6 = (bf16[8192,128]{0,1:T(8,128)(2,1)}, bf16[8192,128]{0,1:T(8,128)(2,1)S(1)}, u32[]{:S(2)}, u32[]{:S(2)}) collective-permute-start(bf16[8192,128]{0,1:T(8,128)(2,1)} %all-gather.4.cloned.1.call-done), channel_id=1, source_target_pairs={{0,16},{16,32},{32,48},{48,64},{64,80},{80,96},{96,112},{1,17},{17... | collective-permute-start | bytes 6291464 | tf_op jit(solution)/shard_map/ppermute | solution.py:16
  292.9 93.0 %collective-permute-start.7 = (bf16[8192,128]{0,1:T(8,128)(2,1)}, bf16[8192,128]{0,1:T(8,128)(2,1)}, u32[]{:S(2)}, u32[]{:S(2)}) collective-permute-start(bf16[8192,128]{0,1:T(8,128)(2,1)} %all-gather.4.cloned.1.call-done), channel_id=1, source_target_pairs={{16,0},{32,16},{48,32},{64,48},{80,64},{96,80},{112,96},{17,1},{33... | collective-permute-start | bytes 6291464 | tf_op jit(solution)/shard_map/ppermute | solution.py:17
  372.0 1.9 collective-permute-start.9
  373.2 5.9 collective-permute-start.11
  373.8 4.4 collective-permute-start.8
  373.9 6.3 collective-permute-start.10
  379.1 4.0 collective-permute-start.12
  383.1 33.2 %collective-permute-start.13 = (bf16[64,128]{1,0:T(8,128)(2,1)S(1)}, bf16[64,128]{1,0:T(8,128)(2,1)S(1)}, u32[]{:S(2)}, u32[]{:S(2)}) collective-permute-start(bf16[64,128]{1,0:T(8,128)(2,1)S(1)} %add_convert_fusion.10), channel_id=1, source_target_pairs={{0,64},{16,80},{32,96},{48,112},{64,0},{80,16},{96,32},{112,48},{1... | collective-permute-start | bytes 49160 | tf_op jit(solution)/shard_map/ppermute | solution.py:23
  410.4 5.9 copy-start.8
  410.4 5.9 copy-start.9
  410.4 6.4 copy-start.2
  410.4 77.5 %copy-start.1 = (bf16[3,64,512]{2,1,0:T(8,128)(2,1)S(1)}, bf16[3,64,512]{2,1,0:T(8,128)(2,1)}, u32[]{:S(2)}) copy-start(bf16[3,64,512]{2,1,0:T(8,128)(2,1)} %param.16) | copy-start | bytes 589828
  416.2 274.3 %copy-start.4 = (bf16[3,64,512]{2,1,0:T(8,128)(2,1)S(1)}, bf16[3,64,512]{2,1,0:T(8,128)(2,1)}, u32[]{:S(2)}) copy-start(bf16[3,64,512]{2,1,0:T(8,128)(2,1)} %param.15) | copy-start | bytes 589828
  416.2 360.6 %copy-start.6 = (bf16[3,64,512]{2,1,0:T(8,128)(2,1)S(1)}, bf16[3,64,512]{2,1,0:T(8,128)(2,1)}, u32[]{:S(2)}) copy-start(bf16[3,64,512]{2,1,0:T(8,128)(2,1)} %param.14) | copy-start | bytes 589828
  486.7 1.2 collective-permute-start.14
  558.0 1.2 collective-permute-start.15
  559.2 3.8 collective-permute-start.16
  632.9 1.2 collective-permute-start.17
  634.2 3.9 collective-permute-start.18
  638.1 5.3 collective-permute-start.19
  644.3 437.7 %all-gather.8.cloned.1.call-start = ((), (), s32[]{:S(2)}) async-start(), calls=%async_computation.2 | async-start | bytes 2228224 | tf_op jit(solution)/shard_map/all_gather | solution.py:29
  686.5 92.2 %collective-permute-start.20 = (bf16[8192,128]{0,1:T(8,128)(2,1)}, bf16[8192,128]{0,1:T(8,128)(2,1)}, u32[]{:S(2)}, u32[]{:S(2)}) collective-permute-start(bf16[8192,128]{0,1:T(8,128)(2,1)} %all-gather.6.cloned.1.call-done), channel_id=1, source_target_pairs={{0,16},{16,32},{32,48},{48,64},{64,80},{80,96},{96,112},{1,17},{17... | collective-permute-start | bytes 6291464 | tf_op jit(solution)/shard_map/ppermute | solution.py:16
  689.1 89.5 %collective-permute-start.21 = (bf16[8192,128]{0,1:T(8,128)(2,1)}, bf16[8192,128]{0,1:T(8,128)(2,1)}, u32[]{:S(2)}, u32[]{:S(2)}) collective-permute-start(bf16[8192,128]{0,1:T(8,128)(2,1)} %all-gather.6.cloned.1.call-done), channel_id=1, source_target_pairs={{16,0},{32,16},{48,32},{64,48},{80,64},{96,80},{112,96},{17,1},{33... | collective-permute-start | bytes 6291464 | tf_op jit(solution)/shard_map/ppermute | solution.py:17
  766.7 1.3 collective-permute-start.25
  766.8 4.3 collective-permute-start.23
  767.3 42.2 %collective-permute-start.22 = (bf16[64,128]{0,1:T(8,128)(2,1)S(1)}, bf16[64,128]{0,1:T(8,128)(2,1)S(1)}, u32[]{:S(2)}, u32[]{:S(2)}) collective-permute-start(bf16[64,128]{0,1:T(8,128)(2,1)S(1)} %get-tuple-element.11), channel_id=1, source_target_pairs={{0,16},{16,0},{32,48},{48,32},{64,80},{80,64},{96,112},{112,96},{1... | collective-permute-start | bytes 49160 | tf_op jit(solution)/shard_map/ppermute | solution.py:23
  768.0 5.0 collective-permute-start.26
  771.1 5.6 collective-permute-start.24
  773.0 5.5 collective-permute-start.27
  879.8 1.2 collective-permute-start.28
  950.9 1.2 collective-permute-start.29
  952.1 3.8 collective-permute-start.30
  1025.9 1.2 collective-permute-start.31
  1027.1 3.9 collective-permute-start.32
  1031.0 5.3 collective-permute-start.33
  1082.0 93.7 %collective-permute-start.34 = (bf16[8192,128]{0,1:T(8,128)(2,1)}, bf16[8192,128]{0,1:T(8,128)(2,1)S(1)}, u32[]{:S(2)}, u32[]{:S(2)}) collective-permute-start(bf16[8192,128]{0,1:T(8,128)(2,1)} %all-gather.8.cloned.1.call-done), channel_id=1, source_target_pairs={{0,16},{16,32},{32,48},{48,64},{64,80},{80,96},{96,112},{1,17},{17... | collective-permute-start | bytes 6291464 | tf_op jit(solution)/shard_map/ppermute | solution.py:16
  1083.4 92.3 %collective-permute-start.35 = (bf16[8192,128]{0,1:T(8,128)(2,1)}, bf16[8192,128]{0,1:T(8,128)(2,1)}, u32[]{:S(2)}, u32[]{:S(2)}) collective-permute-start(bf16[8192,128]{0,1:T(8,128)(2,1)} %all-gather.8.cloned.1.call-done), channel_id=1, source_target_pairs={{16,0},{32,16},{48,32},{64,48},{80,64},{96,80},{112,96},{17,1},{33... | collective-permute-start | bytes 6291464 | tf_op jit(solution)/shard_map/ppermute | solution.py:17
  1161.0 1.3 collective-permute-start.39
  1161.1 5.4 collective-permute-start.37
  1161.6 44.4 %collective-permute-start.36 = (bf16[64,128]{0,1:T(8,128)(2,1)S(1)}, bf16[64,128]{0,1:T(8,128)(2,1)S(1)}, u32[]{:S(2)}, u32[]{:S(2)}) collective-permute-start(bf16[64,128]{0,1:T(8,128)(2,1)S(1)} %get-tuple-element.8), channel_id=1, source_target_pairs={{0,16},{16,0},{32,48},{48,32},{64,80},{80,64},{96,112},{112,96},{1... | collective-permute-start | bytes 49160 | tf_op jit(solution)/shard_map/ppermute | solution.py:23
  1162.3 6.1 collective-permute-start.40
  1166.6 5.6 collective-permute-start.38
  1168.4 5.5 collective-permute-start.41
  1200.2 5.8 copy-start.7
  1277.2 1.2 collective-permute-start.42
  1348.3 1.2 collective-permute-start.43
  1349.5 3.8 collective-permute-start.44
  1423.2 1.2 collective-permute-start.45
  1424.4 3.9 collective-permute-start.46
  1428.4 5.3 collective-permute-start.47
Sparse Core Ops, SparseCore 0:
  247.4 44.0 all-gather.3
  644.4 42.0 all-gather.5
  1037.3 44.5 all-gather.7
where the time goes:
time: 1440 us
  blocking collectives  1060 us (74%)
  waiting for transfers between devices  182 us (13%)
  local copies, waits for them, and re-layouts  61.6 us (4%)
  starting transfers between devices  57.8 us (4%)
  matrix products  45.3 us (3%)
  other arithmetic  19.2 us (1%)
  between operations  14.4 us (1%)
    psum x15, blocking collectives, subtree(): partial_value = lax.psum(term, 'blk')  1060 us
    all_gather x3, waiting for transfers between devices, near_field(): grouped = lax.all_gather(flat_b, 'blk', axis=0, tiled=True)  131 us
    ppermute x42, waiting for transfers between devices, from_partner(): lax.ppermute(array, axis, [(i, i ^ 1 << bit) for i in range(lax.axis_size...  51.2 us
    ppermute x42, starting transfers between devices, from_partner(): lax.ppermute(array, axis, [(i, i ^ 1 << bit) for i in range(lax.axis_size...  48.4 us
    gather x3, local copies, waits for them, and re-layouts, near_field(): picked = tiles[neighbours]  31.5 us
  transfers between devices with their start and end apart: 51, of which 34 were waited for; matrix products, arithmetic and copies ran while one was open for 8% of the time, Pallas kernels for 0%

commit v1 on v0

v1 whole, which is shorter than its diff:
```python
import jax
import jax.numpy as jnp
from jax import lax
from jax.experimental import pallas as pl
from jax.experimental.pallas import tpu as pltpu
from jax.sharding import PartitionSpec as P

ITERS = 3
AXES = ("drop", "blk")
BS = 128
NBD = 4
SLOTS = 40
R = 64
ROWS = NBD * BS
RING = 4 * ROWS
TERMS = 3 * R
PIECE = RING + TERMS
BF = jnp.bfloat16
F32 = jnp.float32


def coords(i):
    return i // 32, i // 16 % 2, i % 4, i // 4 % 4


def index(x, core, y, z):
    return (x % 4) * 32 + core * 16 + (z % 4) * 4 + y % 4


def pull(source):
    return [(source(i), i) for i in range(128)]


def along(axis, other):
    def source(i):
        x, core, y, z = coords(i)
        even = (x + core) % 2 == 1
        if even == (axis == 1):
            return index(x, core, other(y), z)
        return index(x, core, y, other(z))

    return pull(source)


UP, DOWN = along(1, lambda d: d + 1), along(1, lambda d: d - 1)
FIRST_NEAR, FIRST_FAR = along(1, lambda d: d ^ 1), along(1, lambda d: 3 - d)
SECOND_NEAR, SECOND_FAR = along(2, lambda d: d ^ 1), along(2, lambda d: 3 - d)
CORE = pull(lambda i: i ^ 16)
CHIP_NEAR = pull(lambda i: i ^ 32)
CHIP_FAR = pull(lambda i: i ^ 96)


def groups_of_eight():
    out = []
    for p in range(4):
        for k in range(4):
            members = []
            for x, core in ((p, 1), (p + 1, 0)):
                for j in range(4):
                    members.append(index(x, core, k, j) if p % 2 == 0 else index(x, core, j, k))
            out.append(members)
    return out


EIGHTS = groups_of_eight()


def move(array, pairs):
    return lax.ppermute(array, AXES, pairs)


def ring(array):
    half = array.shape[0] // 2
    up, down = move(array, UP), move(array, DOWN)
    far_a, far_b = move(up[:half], UP), move(down[half:], DOWN)
    return [up, down, far_a, far_b]


def add_pairwise(term, steps):
    for pairs in steps:
        term = term + move(term.astype(BF), pairs).astype(F32)
    return term


def siblings(term):
    other = move(term.astype(BF), CORE)
    chip = term[R:] + other[R:].astype(F32)
    near = move(chip.astype(BF), CHIP_NEAR)
    half = chip[R:] + near[R:].astype(F32)
    far = move(half.astype(BF), CHIP_FAR)
    return jnp.concatenate([other[:R], near[:R], far], axis=0)


def dot(a, b):
    return jnp.dot(a.astype(BF), b.astype(BF), preferred_element_type=F32)


def dot_t(a, b):
    return lax.dot_general(
        a.astype(BF), b.astype(BF), (((0,), (0,)), ((), ())), preferred_element_type=F32
    )


def dot_bt(a, b):
    return lax.dot_general(
        a.astype(BF), b.astype(BF), (((1,), (1,)), ((), ())), preferred_element_type=F32
    )


def slot_tables(neighbours, counts):
    drop, blk = lax.axis_index("drop"), lax.axis_index("blk")
    core, mine = drop % 2, (blk % 4, blk // 4)
    kind = neighbours // 64
    group = drop - 1 + kind
    block = neighbours % 64
    owner, part = block // 4, block % 4
    place = lax.rem(kind - core + 3, 3)
    even = (drop // 2 + core) % 2 == 1
    y_first = even == (place < 2)
    y, z = owner % 4, owner // 4
    first = jnp.where(y_first, y, z)
    second = jnp.where(y_first, z, y)
    mine_first = jnp.where(y_first, mine[0], mine[1])
    apart = (first - mine_first + 4) % 4
    at = jnp.where(apart < 2, apart, 5 - apart)
    member = jnp.where(place == 1, 4, 0) + second
    row = member * PIECE + at * ROWS + part * BS
    slot = lax.broadcasted_iota(jnp.int32, neighbours.shape, 1)
    live = (slot < counts[:, None]) & (group >= 0) & (group <= 7)
    key = jnp.where(live, jnp.where(place < 2, 0, 1), 2)
    rank_key = key * SLOTS + slot
    rank = jnp.sum((rank_key[:, None, :] < rank_key[:, :, None]).astype(jnp.int32), axis=2)
    put = rank[:, :, None] == lax.broadcasted_iota(jnp.int32, (1, 1, SLOTS), 2)
    order = jnp.sum(jnp.where(put, slot[:, :, None], 0), axis=1)
    start = jnp.sum(jnp.where(put, row[:, :, None], 0), axis=1)
    n_pair = jnp.sum((key == 0).astype(jnp.int32), axis=1)
    n_live = jnp.sum((key < 2).astype(jnp.int32), axis=1)
    return order.reshape(-1), start.reshape(-1), n_pair, n_live


def near_kernel(order, start, n_pair, n_live, blocks, pair, other, out):
    q = pl.program_id(0)
    base = q * SLOTS

    def span(field, lo, hi, acc):
        def two(i, acc):
            j = lo + 2 * i
            k = jnp.minimum(j + 1, hi - 1)
            left = blocks[0, order[base + j]]
            right = blocks[0, order[base + k]]
            right = jnp.where(j + 1 < hi, right, jnp.zeros_like(right))
            upper = field[pl.ds(pl.multiple_of(start[base + j], 64), BS), :]
            lower = field[pl.ds(pl.multiple_of(start[base + k], 64), BS), :]
            return acc + jnp.dot(
                jnp.concatenate([left, right], axis=1),
                jnp.concatenate([upper, lower], axis=0),
                preferred_element_type=F32,
            )

        return lax.fori_loop(0, (hi - lo + 1) // 2, two, acc)

    acc = jnp.zeros((BS, BS), F32)
    acc = span(pair, 0, n_pair[q], acc)
    acc = span(other, n_pair[q], n_live[q], acc)
    out[...] = acc


def near(tables, near_blocks, pair, other):
    return pl.pallas_call(
        near_kernel,
        grid_spec=pltpu.PrefetchScalarGridSpec(
            num_scalar_prefetch=4,
            grid=(NBD,),
            in_specs=[
                pl.BlockSpec((1, SLOTS, BS, BS), lambda q, *_: (q, 0, 0, 0)),
                pl.BlockSpec((8 * PIECE, BS), lambda q, *_: (0, 0)),
                pl.BlockSpec((4 * PIECE, BS), lambda q, *_: (0, 0)),
            ],
            out_specs=pl.BlockSpec((BS, BS), lambda q, *_: (q, 0)),
        ),
        out_shape=jax.ShapeDtypeStruct((ROWS, BS), F32),
        compiler_params=pltpu.CompilerParams(vmem_limit_bytes=40 * 2**20),
        cost_estimate=pl.CostEstimate(flops=2 * 80 * BS**3, bytes_accessed=12 * 2**20, transcendentals=0),
    )(*tables, near_blocks, pair, other)


def leaf(resid, leaf_inverse):
    tiles = resid.astype(BF).reshape(NBD, BS, BS)
    return jnp.einsum("bij,bjn->bin", leaf_inverse, tiles, preferred_element_type=F32).reshape(ROWS, BS)


def first_siblings(z_ring, right, left):
    r0, r1, r2 = right[:, :R], right[:, R : 2 * R], right[:, 2 * R :]
    terms = dot_t(right, z_ring)
    cross = dot_t(right, left)
    low = jnp.concatenate([cross[R : 2 * R, :R], cross[2 * R :, :R]], axis=1)
    high = jnp.concatenate([cross[2 * R :, R : 2 * R]] * 2, axis=1)
    mine = add_pairwise(jnp.concatenate([terms, low, high], axis=0), (SECOND_NEAR, SECOND_FAR))
    other = move(mine.astype(BF), CORE).astype(F32)

    def parts(a):
        return a[:R], a[R : 2 * R], a[2 * R : 3 * R], a[3 * R : 4 * R, :R], a[3 * R : 4 * R, R:], a[4 * R :, :R]

    a0, a1, a2, m10, m20, m21 = parts(mine)
    b0, b1, b2, k10, k20, k21 = parts(other)
    t1 = a1 - dot(m10, b0) + b1 - dot(k10, a0)
    t2 = a2 - dot(m20, b0) + b2 - dot(k20, a0)
    m21 = m21 + k21
    chip = jnp.concatenate([t1, t2, jnp.concatenate([m21, m21], axis=1)], axis=0)
    near_chip = move(chip.astype(BF), CHIP_NEAR).astype(F32)
    s1, u2, k21 = near_chip[:R], near_chip[R : 2 * R], near_chip[2 * R :, :R]
    half = t2 - dot(m21, s1) + u2 - dot(k21, t1)
    s2 = move(half.astype(BF), CHIP_FAR)
    sums = jnp.concatenate([b0.astype(BF), s1.astype(BF), s2], axis=0)
    f1 = r1.astype(F32) - dot_bt(r0, k10)
    f2 = r2.astype(F32) - dot_bt(r0, k20) - dot_bt(f1, k21)
    folded = jnp.concatenate([r0, f1.astype(BF), f2.astype(BF)], axis=1)
    return sums, folded


def on_device(
    right_side, near_blocks, neighbours, counts, leaf_inverse, couple_left, couple_right, prec_left, prec_right
):
    upper = lax.axis_index("drop") % 2 == 0
    tables = slot_tables(neighbours, counts)

    def by_row(factors):
        return factors.reshape(TERMS, ROWS).T

    z = leaf(right_side, leaf_inverse)
    mine = jnp.concatenate([z.astype(BF), by_row(prec_right), by_row(prec_left), by_row(couple_right)], axis=1)
    whole = jnp.concatenate([mine] + ring(mine), axis=0)
    right, left, c_right = (whole[:, BS + i * TERMS : BS + (i + 1) * TERMS] for i in range(3))
    z_ring = whole[:, :BS]
    sums, folded = first_siblings(z_ring, right, left)
    c_left = couple_left.reshape(TERMS, ROWS)
    field = jnp.concatenate([z, z_ring[ROWS:].astype(F32)], axis=0) - dot(left, sums)

    for step in range(ITERS):
        field_b = field.astype(BF)
        c_terms = dot_t(c_right, field_b)
        piece = jnp.concatenate([field_b, c_terms.astype(BF)], axis=0)
        pieces = lax.all_to_all(
            jnp.broadcast_to(piece[None], (8, PIECE, BS)), AXES, 0, 0, tiled=True, axis_index_groups=EIGHTS
        )
        own = lax.dynamic_slice_in_dim(pieces, jnp.where(upper, 4, 0), 4, axis=0)
        other = move(own, CORE)
        c_sums = siblings(jnp.sum(own[:, RING:].astype(F32), axis=0))
        product = near(tables, near_blocks, pieces.reshape(8 * PIECE, BS), other.reshape(4 * PIECE, BS))
        x = field[:ROWS]
        resid = right_side - (x + product + dot_t(c_left, c_sums))
        z = leaf(resid, leaf_inverse)
        if step < ITERS - 1:
            rest = jnp.concatenate(ring(z.astype(BF)), axis=0)
            z_ring = jnp.concatenate([z, rest.astype(F32)], axis=0)
            terms = add_pairwise(dot_t(folded, z_ring), (SECOND_NEAR, SECOND_FAR))
            field = field + z_ring - dot(left, siblings(terms))
        else:
            terms = dot_t(folded[:ROWS], z)
            terms = add_pairwise(terms, (FIRST_NEAR, FIRST_FAR, SECOND_NEAR, SECOND_FAR))
            x = x + z - dot(left[:ROWS], siblings(terms))
    return x, resid


def solution(mesh):
    in_specs = (
        P(("drop", "blk"), None),
        P(("drop", "blk"), None, None, None),
        P(("drop", "blk"), None),
        P(("drop", "blk")),
        P(("drop", "blk"), None, None),
        P(None, None, ("drop", "blk")),
        P(None, None, ("drop", "blk")),
        P(None, None, ("drop", "blk")),
        P(None, None, ("drop", "blk")),
    )
    out_specs = (P(("drop", "blk"), None), P(("drop", "blk"), None))
    return jax.shard_map(on_device, mesh=mesh, in_specs=in_specs, out_specs=out_specs, check_vma=False)
```

time: 1440 us -> 344 us (0.24)
  blocking collectives: 1060 us -> 72.3 us
  waiting for transfers between devices: 182 us -> 122 us
  matrix products: 45.3 us -> 12.3 us
  local copies, waits for them, and re-layouts: 61.6 us -> 29.9 us
  starting transfers between devices: 57.8 us -> 77 us
  Pallas kernels: 0 us -> 14.5 us
    psum x15 -> x0, blocking collectives: 1060 us -> none  [subtree(): partial_value = lax.psum(term, 'blk')]
    all_gather x3 -> x0, waiting for transfers between devices: 131 us -> none  [near_field(): grouped = lax.all_gather(flat_b, 'blk', axis=0, tiled=True)]
    all_to_all x0 -> x2, blocking collectives: none -> 72.3 us  [on_device(): lax.all_to_all(jnp.broadcast_to(piece[None], (8, PIECE, BS)), AXES, 0, 0,...]
    ppermute x48 -> x46, waiting for transfers between devices: 51.2 us -> 93.2 us  [move(): return lax.ppermute(array, AXES, pairs)]
    dot_general x49 -> x28, matrix products: 45.3 us -> 12.3 us  [the longest x11 4.29 us: dot_t(): lax.dot_general(a.astype(BF), b.astype(BF), (((0,), (0,)), ((), ())), pre...]
    gather x3 -> x0, local copies, waits for them, and re-layouts: 31.5 us -> none  [near_field(): picked = tiles[neighbours]]
    all_to_all x0 -> x1, waiting for transfers between devices: none -> 29.1 us  [on_device(): lax.all_to_all(jnp.broadcast_to(piece[None], (8, PIECE, BS)), AXES, 0, 0,...]
    reshape x13 -> x2, local copies, waits for them, and re-layouts: 27.2 us -> 1.51 us  [slot_tables(): return (order.reshape(-1), start.reshape(-1), n_pair, n_live)]
  transfers between devices with their start and end apart: 51 -> 47, of which waited for: 34 -> 34; matrix products, arithmetic and copies ran while one was open for 8% -> 7% of each run, Pallas kernels for 0% -> 4%
where the time goes in v1:
time: 344 us; the launch traced here: 339 us
  waiting for transfers between devices  122 us (35%)
  starting transfers between devices  77 us (22%)
  blocking collectives  72.3 us (21%)
  local copies, waits for them, and re-layouts  29.9 us (9%)
  Pallas kernels  14.5 us (4%)
  matrix products  12.3 us (4%)
  other arithmetic  8.86 us (3%)
    ppermute x46, waiting for transfers between devices, move(): return lax.ppermute(array, AXES, pairs)  93.2 us
    all_to_all x2, blocking collectives, on_device(): lax.all_to_all(jnp.broadcast_to(piece[None], (8, PIECE, BS)), AXES, 0, 0,...  72.3 us
    ppermute x46, starting transfers between devices, move(): return lax.ppermute(array, AXES, pairs)  70.3 us
    all_to_all x1, waiting for transfers between devices, on_device(): lax.all_to_all(jnp.broadcast_to(piece[None], (8, PIECE, BS)), AXES, 0, 0,...  29.1 us
    pallas_call x3, Pallas kernels, near(): pl.pallas_call(near_kernel, grid_spec=pltpu.PrefetchScalarGridSpec(num_sc...  14.5 us
    ppermute x4, local copies, waits for them, and re-layouts, move(): return lax.ppermute(array, AXES, pairs)  8.45 us
  transfers between devices with their start and end apart: 47, of which 34 were waited for; matrix products, arithmetic and copies ran while one was open for 7% of the time, Pallas kernels for 4%

profile of v1, /device:TPU:0, one launch (start us, length us, event | category | flops | bytes accessed | tf_op | source)
XLA Modules:
  0.0 338.6 jit_solution(18066234625978108428)
XLA Ops:
  2.9 2.1 constant_dynamic-update-slice_fusion.4
  5.0 4.1 %collective-permute-start = (bf16[512,704]{0,1:T(8,128)(2,1)}, bf16[512,704]{0,1:T(8,128)(2,1)}, u32[]{:S(2)}, u32[]{:S(2)}) collective-permute-start(bf16[512,704]{0,1:T(8,128)(2,1)} %get-tuple-element.29), channel_id=1, source_target_pairs={{4,0},{5,1},{6,2},{7,3},{8,4},{9,5},{10,6},{11,7},{12,8},{13,9},{1... | collective-permute-start | bytes 2162696 | tf_op jit(solution)/shard_map/ppermute | solution.py:69
  9.2 9.1 %collective-permute-done = bf16[512,704]{0,1:T(8,128)(2,1)} collective-permute-done((bf16[512,704]{0,1:T(8,128)(2,1)}, bf16[512,704]{0,1:T(8,128)(2,1)}, u32[]{:S(2)}, u32[]{:S(2)}) %collective-permute-start) | collective-permute-done | bytes 720928 | tf_op jit(solution)/shard_map/ppermute | solution.py:69
  18.3 2.3 copy.45
  20.6 1.8 slice.320
  22.4 3.7 %collective-permute-start.2 = (bf16[256,704]{1,0:T(8,128)(2,1)}, bf16[256,704]{1,0:T(8,128)(2,1)}, u32[]{:S(2)}, u32[]{:S(2)}) collective-permute-start(bf16[256,704]{1,0:T(8,128)(2,1)} %slice.320), channel_id=1, source_target_pairs={{4,0},{5,1},{6,2},{7,3},{8,4},{9,5},{10,6},{11,7},{12,8},{13,9},{1... | collective-permute-start | bytes 1081352 | tf_op jit(solution)/shard_map/ppermute | solution.py:69
  26.1 2.3 copy.46
  28.3 1.8 slice.321
  32.6 1.9 copy.47
  35.6 3.9 %collective-permute-done.3 = bf16[256,704]{1,0:T(8,128)(2,1)} collective-permute-done((bf16[256,704]{1,0:T(8,128)(2,1)}, bf16[256,704]{1,0:T(8,128)(2,1)}, u32[]{:S(2)}, u32[]{:S(2)}) %collective-permute-start.3) | collective-permute-done | bytes 360480 | tf_op jit(solution)/shard_map/ppermute | solution.py:69
  39.4 1.9 copy.48
  43.3 1.7 collective-permute-start.4
  45.0 2.9 collective-permute-done.4
  48.0 3.1 collective-permute-start.5
  51.1 2.6 collective-permute-done.5
  57.2 2.8 collective-permute-done.7
  60.3 2.5 collective-permute-start.8
  66.2 2.7 broadcast_in_dim.66
  68.9 6.7 %all-to-all-start = ((bf16[8,2240,128]{2,1,0:T(8,128)(2,1)}), bf16[8,2240,128]{2,1,0:T(8,128)(2,1)}, u32[]{:S(2)}, u32[]{:S(2)}) async-start(bf16[8,2240,128]{2,1,0:T(8,128)(2,1)} %broadcast_in_dim.66), calls=%async_computation | async-start | bytes 9175040 | tf_op jit(solution)/shard_map/all_to_all | solution.py:243
  75.6 29.1 %all-to-all-done = bf16[8,2240,128]{2,1,0:T(8,128)(2,1)} async-done(((bf16[8,2240,128]{2,1,0:T(8,128)(2,1)}), bf16[8,2240,128]{2,1,0:T(8,128)(2,1)}, u32[]{:S(2)}, u32[]{:S(2)}) %all-to-all-start) | async-done | bytes 4587552 | tf_op jit(solution)/shard_map/all_to_all | solution.py:243
  104.7 3.2 constant_dynamic-slice_fusion.2
  116.7 1.9 collective-permute-done.11
  118.6 1.6 collective-permute-start.12
  120.2 2.5 copy-done.1
  122.7 6.6 %shard_map.104 = f32[512,128]{1,0:T(8,128)S(1)} custom-call(s32[160]{0:T(256)S(1)} %reshape.77.order, s32[160]{0:T(256)S(1)} %reshape.78.start, s32[4]{0:T(128)S(1)} %get-tuple-element.5.n_pair, s32[4]{0:T(128)S(1)} %get-tuple-element.4.n_live, bf16[4,40,128,128]{3,2,1,0:T(8,128)(2,1)S(1)} %copy-done.1, bf16[17920,128]{1,0:T(8,128)(2,1)} %bitcast.8.pair, ...), custom_call_target="tpu_custom_call" | custom-call | flops 335544320 | bytes 12582912 | tf_op jit(solution)/shard_map/pallas_call | solution.py:169
  131.3 2.2 collective-permute-start.13
  134.4 1.9 collective-permute-done.14
  136.4 3.3 collective-permute-start.15
  142.3 4.1 %collective-permute-done.17 = bf16[192,128]{1,0:T(8,128)(2,1)S(1)} collective-permute-done((bf16[192,128]{1,0:T(8,128)(2,1)S(1)}, bf16[192,128]{1,0:T(8,128)(2,1)S(1)}, u32[]{:S(2)}, u32[]{:S(2)}) %collective-permute-start.17) | collective-permute-done | bytes 49184 | tf_op jit(solution)/shard_map/ppermute | solution.py:69
  146.4 2.8 collective-permute-start.18
  149.3 2.7 collective-permute-done.18
  153.3 3.2 collective-permute-start.20
  156.6 1.9 collective-permute-done.20
  158.5 4.5 %collective-permute-start.21 = (bf16[64,128]{1,0:T(8,128)(2,1)S(1)}, bf16[64,128]{1,0:T(8,128)(2,1)S(1)}, u32[]{:S(2)}, u32[]{:S(2)}) collective-permute-start(bf16[64,128]{1,0:T(8,128)(2,1)S(1)} %fusion.94), channel_id=1, source_target_pairs={{96,0},{97,1},{98,2},{99,3},{100,4},{101,5},{102,6},{103,7},{104,8... | collective-permute-start | bytes 49160 | tf_op jit(solution)/shard_map/ppermute | solution.py:69
  163.0 1.7 collective-permute-done.21
  166.2 36.1 %all_to_all.15 = bf16[8,2240,128]{2,1,0:T(8,128)(2,1)S(1)} all-to-all(bf16[8,2240,128]{2,1,0:T(8,128)(2,1)S(1)} %broadcast_in_dim.67), channel_id=1, replica_groups={{16,20,24,28,32,36,40,44},{17,21,25,29,33,37,41,45},{18,22,26,30,34,38,..., dimensions={0} | all-to-all | bytes 9175040 | tf_op jit(solution)/shard_map/all_to_all | solution.py:243
  203.2 3.9 %collective-permute-done.23 = bf16[192,128]{1,0:T(8,128)(2,1)S(1)} collective-permute-done((bf16[192,128]{1,0:T(8,128)(2,1)S(1)}, bf16[192,128]{1,0:T(8,128)(2,1)S(1)}, u32[]{:S(2)}, u32[]{:S(2)}) %collective-permute-start.23) | collective-permute-done | bytes 49184 | tf_op jit(solution)/shard_map/ppermute | solution.py:69
  207.2 3.9 %collective-permute-done.24 = bf16[128,128]{1,0:T(8,128)(2,1)S(1)} collective-permute-done((bf16[128,128]{1,0:T(8,128)(2,1)S(1)}, bf16[128,128]{1,0:T(8,128)(2,1)S(1)}, u32[]{:S(2)}, u32[]{:S(2)}) %collective-permute-start.24) | collective-permute-done | bytes 32800 | tf_op jit(solution)/shard_map/ppermute | solution.py:69
  211.1 2.2 collective-permute-start.25
  213.3 4.0 %shard_map.105 = f32[512,128]{1,0:T(8,128)S(1)} custom-call(s32[160]{0:T(256)S(1)} %reshape.77.order, s32[160]{0:T(256)S(1)} %reshape.78.start, s32[4]{0:T(128)S(1)} %get-tuple-element.5.n_pair, s32[4]{0:T(128)S(1)} %get-tuple-element.4.n_live, bf16[4,40,128,128]{3,2,1,0:T(8,128)(2,1)S(1)} %copy-done.1, bf16[17920,128]{1,0:T(8,128)(2,1)S(1)} %bitcast.74, ...), custom_call_target="tpu_custom_call" | custom-call | flops 335544320 | bytes 12582912 | tf_op jit(solution)/shard_map/pallas_call | solution.py:169
  217.9 4.3 %collective-permute-start.26 = (bf16[512,128]{1,0:T(8,128)(2,1)S(1)}, bf16[512,128]{1,0:T(8,128)(2,1)S(1)}, u32[]{:S(2)}, u32[]{:S(2)}) collective-permute-start(bf16[512,128]{1,0:T(8,128)(2,1)S(1)} %bitcast_convert_fusion.1), channel_id=1, source_target_pairs={{4,0},{5,1},{6,2},{7,3},{8,4},{9,5},{10,6},{11,7},{12,8},{13,9},{1... | collective-permute-start | bytes 393224 | tf_op jit(solution)/shard_map/ppermute | solution.py:69
  222.2 2.9 collective-permute-done.27
  225.1 3.3 collective-permute-start.28
  228.4 2.1 collective-permute-done.29
  231.1 4.1 %collective-permute-done.30 = bf16[192,128]{1,0:T(8,128)(2,1)S(1)} collective-permute-done((bf16[192,128]{1,0:T(8,128)(2,1)S(1)}, bf16[192,128]{1,0:T(8,128)(2,1)S(1)}, u32[]{:S(2)}, u32[]{:S(2)}) %collective-permute-start.30) | collective-permute-done | bytes 49184 | tf_op jit(solution)/shard_map/ppermute | solution.py:69
  236.6 4.0 %collective-permute-done.31 = bf16[192,128]{1,0:T(8,128)(2,1)S(1)} collective-permute-done((bf16[192,128]{1,0:T(8,128)(2,1)S(1)}, bf16[192,128]{1,0:T(8,128)(2,1)S(1)}, u32[]{:S(2)}, u32[]{:S(2)}) %collective-permute-start.31) | collective-permute-done | bytes 49184 | tf_op jit(solution)/shard_map/ppermute | solution.py:69
  241.9 2.4 collective-permute-start.33
  244.3 1.9 collective-permute-done.33
  246.2 4.0 %collective-permute-start.34 = (bf16[64,128]{1,0:T(8,128)(2,1)S(1)}, bf16[64,128]{1,0:T(8,128)(2,1)S(1)}, u32[]{:S(2)}, u32[]{:S(2)}) collective-permute-start(bf16[64,128]{1,0:T(8,128)(2,1)S(1)} %fusion.92), channel_id=1, source_target_pairs={{96,0},{97,1},{98,2},{99,3},{100,4},{101,5},{102,6},{103,7},{104,8... | collective-permute-start | bytes 49160 | tf_op jit(solution)/shard_map/ppermute | solution.py:69
  250.2 1.7 collective-permute-done.34
  253.5 36.2 %all_to_all.16 = bf16[8,2240,128]{2,1,0:T(8,128)(2,1)S(1)} all-to-all(bf16[8,2240,128]{2,1,0:T(8,128)(2,1)S(1)} %broadcast_in_dim.68), channel_id=1, replica_groups={{16,20,24,28,32,36,40,44},{17,21,25,29,33,37,41,45},{18,22,26,30,34,38,..., dimensions={0} | all-to-all | bytes 9175040 | tf_op jit(solution)/shard_map/all_to_all | solution.py:243
  290.5 3.9 %collective-permute-done.36 = bf16[192,128]{1,0:T(8,128)(2,1)S(1)} collective-permute-done((bf16[192,128]{1,0:T(8,128)(2,1)S(1)}, bf16[192,128]{1,0:T(8,128)(2,1)S(1)}, u32[]{:S(2)}, u32[]{:S(2)}) %collective-permute-start.36) | collective-permute-done | bytes 49184 | tf_op jit(solution)/shard_map/ppermute | solution.py:69
  294.5 3.9 %collective-permute-done.37 = bf16[128,128]{1,0:T(8,128)(2,1)S(1)} collective-permute-done((bf16[128,128]{1,0:T(8,128)(2,1)S(1)}, bf16[128,128]{1,0:T(8,128)(2,1)S(1)}, u32[]{:S(2)}, u32[]{:S(2)}) %collective-permute-start.37) | collective-permute-done | bytes 32800 | tf_op jit(solution)/shard_map/ppermute | solution.py:69
  298.4 2.2 collective-permute-start.38
  300.6 4.0 %shard_map.106 = f32[512,128]{1,0:T(8,128)S(1)} custom-call(s32[160]{0:T(256)S(1)} %reshape.77.order, s32[160]{0:T(256)S(1)} %reshape.78.start, s32[4]{0:T(128)S(1)} %get-tuple-element.5.n_pair, s32[4]{0:T(128)S(1)} %get-tuple-element.4.n_live, bf16[4,40,128,128]{3,2,1,0:T(8,128)(2,1)S(1)} %copy-done.1, bf16[17920,128]{1,0:T(8,128)(2,1)S(1)} %bitcast.73, ...), custom_call_target="tpu_custom_call" | custom-call | flops 335544320 | bytes 12582912 | tf_op jit(solution)/shard_map/pallas_call | solution.py:169
  306.1 4.1 %collective-permute-done.39 = bf16[192,128]{1,0:T(8,128)(2,1)S(1)} collective-permute-done((bf16[192,128]{1,0:T(8,128)(2,1)S(1)}, bf16[192,128]{1,0:T(8,128)(2,1)S(1)}, u32[]{:S(2)}, u32[]{:S(2)}) %collective-permute-start.39) | collective-permute-done | bytes 49184 | tf_op jit(solution)/shard_map/ppermute | solution.py:69
  310.2 4.8 %collective-permute-start.40 = (bf16[192,128]{1,0:T(8,128)(2,1)S(1)}, bf16[192,128]{1,0:T(8,128)(2,1)S(1)}, u32[]{:S(2)}, u32[]{:S(2)}) collective-permute-start(bf16[192,128]{1,0:T(8,128)(2,1)S(1)} %fusion.47), channel_id=1, source_target_pairs={{12,0},{13,1},{14,2},{15,3},{8,4},{9,5},{10,6},{11,7},{4,8},{5,9},... | collective-permute-start | bytes 147464 | tf_op jit(solution)/shard_map/ppermute | solution.py:69
  315.0 2.1 collective-permute-done.40
  317.2 4.1 %collective-permute-done.41 = bf16[192,128]{1,0:T(8,128)(2,1)S(1)} collective-permute-done((bf16[192,128]{1,0:T(8,128)(2,1)S(1)}, bf16[192,128]{1,0:T(8,128)(2,1)S(1)}, u32[]{:S(2)}, u32[]{:S(2)}) %collective-permute-start.41) | collective-permute-done | bytes 49184 | tf_op jit(solution)/shard_map/ppermute | solution.py:69
  322.6 4.0 %collective-permute-done.42 = bf16[192,128]{1,0:T(8,128)(2,1)S(1)} collective-permute-done((bf16[192,128]{1,0:T(8,128)(2,1)S(1)}, bf16[192,128]{1,0:T(8,128)(2,1)S(1)}, u32[]{:S(2)}, u32[]{:S(2)}) %collective-permute-start.42) | collective-permute-done | bytes 49184 | tf_op jit(solution)/shard_map/ppermute | solution.py:69
  328.0 2.4 collective-permute-start.44
  330.4 1.9 collective-permute-done.44
  332.3 3.5 %collective-permute-start.45 = (bf16[64,128]{1,0:T(8,128)(2,1)S(1)}, bf16[64,128]{1,0:T(8,128)(2,1)S(1)}, u32[]{:S(2)}, u32[]{:S(2)}) collective-permute-start(bf16[64,128]{1,0:T(8,128)(2,1)S(1)} %fusion.90), channel_id=1, source_target_pairs={{96,0},{97,1},{98,2},{99,3},{100,4},{101,5},{102,6},{103,7},{104,8... | collective-permute-start | bytes 49160 | tf_op jit(solution)/shard_map/ppermute | solution.py:69
  335.9 1.7 collective-permute-done.45
  (185 shorter events, 44.5 us)
Async XLA Ops:
  0.6 128.7 %copy-start = (bf16[3,64,512]{2,1,0:T(8,128)(2,1)S(1)}, bf16[3,64,512]{2,1,0:T(8,128)(2,1)}, u32[]{:S(2)}) copy-start(bf16[3,64,512]{2,1,0:T(8,128)(2,1)} %param.14) | copy-start | bytes 589828
  5.0 13.2 %collective-permute-start = (bf16[512,704]{0,1:T(8,128)(2,1)}, bf16[512,704]{0,1:T(8,128)(2,1)}, u32[]{:S(2)}, u32[]{:S(2)}) collective-permute-start(bf16[512,704]{0,1:T(8,128)(2,1)} %get-tuple-element.29), channel_id=1, source_target_pairs={{4,0},{5,1},{6,2},{7,3},{8,4},{9,5},{10,6},{11,7},{12,8},{13,9},{1... | collective-permute-start | bytes 2162696 | tf_op jit(solution)/shard_map/ppermute | solution.py:69
  9.1 16.9 %collective-permute-start.1 = (bf16[512,704]{0,1:T(8,128)(2,1)}, bf16[512,704]{0,1:T(8,128)(2,1)}, u32[]{:S(2)}, u32[]{:S(2)}) collective-permute-start(bf16[512,704]{0,1:T(8,128)(2,1)} %get-tuple-element.29), channel_id=1, source_target_pairs={{12,0},{13,1},{14,2},{15,3},{0,4},{1,5},{2,6},{3,7},{4,8},{5,9},{6... | collective-permute-start | bytes 2162696 | tf_op jit(solution)/shard_map/ppermute | solution.py:69
  22.4 10.2 %collective-permute-start.2 = (bf16[256,704]{1,0:T(8,128)(2,1)}, bf16[256,704]{1,0:T(8,128)(2,1)}, u32[]{:S(2)}, u32[]{:S(2)}) collective-permute-start(bf16[256,704]{1,0:T(8,128)(2,1)} %slice.320), channel_id=1, source_target_pairs={{4,0},{5,1},{6,2},{7,3},{8,4},{9,5},{10,6},{11,7},{12,8},{13,9},{1... | collective-permute-start | bytes 1081352 | tf_op jit(solution)/shard_map/ppermute | solution.py:69
  30.1 9.3 %collective-permute-start.3 = (bf16[256,704]{1,0:T(8,128)(2,1)}, bf16[256,704]{1,0:T(8,128)(2,1)}, u32[]{:S(2)}, u32[]{:S(2)}) collective-permute-start(bf16[256,704]{1,0:T(8,128)(2,1)} %slice.321), channel_id=1, source_target_pairs={{12,0},{13,1},{14,2},{15,3},{0,4},{1,5},{2,6},{3,7},{4,8},{5,9},{6... | collective-permute-start | bytes 1081352 | tf_op jit(solution)/shard_map/ppermute | solution.py:69
  42.4 12.8 %copy-start.2 = (bf16[2048,704]{0,1:T(8,128)(2,1)}, bf16[2048,704]{0,1:T(8,128)(2,1)S(1)}, u32[]{:S(2)}) copy-start(bf16[2048,704]{0,1:T(8,128)(2,1)S(1)} %constant_dynamic-update-slice_fusion) | copy-start | bytes 8650756
  42.4 20.4 %copy-start.5 = (bf16[512,704]{1,0:T(8,128)(2,1)S(1)}, bf16[512,704]{1,0:T(8,128)(2,1)}, u32[]{:S(2)}) copy-start(bf16[512,704]{1,0:T(8,128)(2,1)} %copy.45) | copy-start | bytes 2162692
  42.4 20.4 %copy-start.6 = (bf16[512,704]{1,0:T(8,128)(2,1)S(1)}, bf16[512,704]{1,0:T(8,128)(2,1)}, u32[]{:S(2)}) copy-start(bf16[512,704]{1,0:T(8,128)(2,1)} %copy.46) | copy-start | bytes 2162692
  43.3 4.5 %collective-permute-start.4 = (bf16[320,128]{1,0:T(8,128)(2,1)S(1)}, bf16[320,128]{1,0:T(8,128)(2,1)S(1)}, u32[]{:S(2)}, u32[]{:S(2)}) collective-permute-start(bf16[320,128]{1,0:T(8,128)(2,1)S(1)} %fusion.156), channel_id=1, source_target_pairs={{1,0},{0,1},{3,2},{2,3},{5,4},{4,5},{7,6},{6,7},{9,8},{8,9},{11,10... | collective-permute-start | bytes 245768 | tf_op jit(solution)/shard_map/ppermute | solution.py:69
  48.0 5.7 %collective-permute-start.5 = (bf16[320,128]{1,0:T(8,128)(2,1)S(1)}, bf16[320,128]{1,0:T(8,128)(2,1)S(1)}, u32[]{:S(2)}, u32[]{:S(2)}) collective-permute-start(bf16[320,128]{1,0:T(8,128)(2,1)S(1)} %fusion.44), channel_id=1, source_target_pairs={{3,0},{2,1},{1,2},{0,3},{7,4},{6,5},{5,6},{4,7},{11,8},{10,9},{9,1... | collective-permute-start | bytes 245768 | tf_op jit(solution)/shard_map/ppermute | solution.py:69
  53.8 1.4 collective-permute-start.6
  55.1 10.6 %copy-start.13 = (bf16[320,128]{1,0:T(8,128)(2,1)}, bf16[320,128]{1,0:T(8,128)(2,1)S(1)}, u32[]{:S(2)}) copy-start(bf16[320,128]{1,0:T(8,128)(2,1)S(1)} %collective-permute-done.6) | copy-start | bytes 245764
  55.2 10.1 %copy-start.3 = (bf16[2048,704]{0,1:T(8,128)(2,1)S(1)}, bf16[2048,704]{0,1:T(8,128)(2,1)}, u32[]{:S(2)}) copy-start(bf16[2048,704]{0,1:T(8,128)(2,1)} %copy-done.2) | copy-start | bytes 8650756
  55.9 4.1 %collective-permute-start.7 = (bf16[192,128]{1,0:T(8,128)(2,1)S(1)}, bf16[192,128]{1,0:T(8,128)(2,1)S(1)}, u32[]{:S(2)}, u32[]{:S(2)}) collective-permute-start(bf16[192,128]{1,0:T(8,128)(2,1)S(1)} %maximum_maximum_fusion.1), channel_id=1, source_target_pairs={{32,0},{33,1},{34,2},{35,3},{36,4},{37,5},{38,6},{39,7},{40,8},{41... | collective-permute-start | bytes 147464 | tf_op jit(solution)/shard_map/ppermute | solution.py:69
  60.0 5.7 %copy-start.14 = (bf16[192,128]{1,0:T(8,128)(2,1)}, bf16[192,128]{1,0:T(8,128)(2,1)S(1)}, u32[]{:S(2)}) copy-start(bf16[192,128]{1,0:T(8,128)(2,1)S(1)} %collective-permute-done.7) | copy-start | bytes 147460
  60.3 5.0 %collective-permute-start.8 = (bf16[64,128]{1,0:T(8,128)(2,1)S(1)}, bf16[64,128]{1,0:T(8,128)(2,1)S(1)}, u32[]{:S(2)}, u32[]{:S(2)}) collective-permute-start(bf16[64,128]{1,0:T(8,128)(2,1)S(1)} %fusion.3), channel_id=1, source_target_pairs={{96,0},{97,1},{98,2},{99,3},{100,4},{101,5},{102,6},{103,7},{104,8... | collective-permute-start | bytes 49160 | tf_op jit(solution)/shard_map/ppermute | solution.py:69
  68.9 35.8 %all-to-all-start = ((bf16[8,2240,128]{2,1,0:T(8,128)(2,1)}), bf16[8,2240,128]{2,1,0:T(8,128)(2,1)}, u32[]{:S(2)}, u32[]{:S(2)}) async-start(bf16[8,2240,128]{2,1,0:T(8,128)(2,1)} %broadcast_in_dim.66), calls=%async_computation | async-start | bytes 9175040 | tf_op jit(solution)/shard_map/all_to_all | solution.py:243
  75.6 32.3 %copy-start.15 = (s32[4,40]{1,0:T(4,128)S(1)}, s32[4,40]{1,0:T(4,128)}, u32[]{:S(2)}) copy-start(s32[4,40]{1,0:T(4,128)} %param.11) | copy-start | bytes 1924
  75.6 32.3 %copy-start.16 = (s32[4]{0:T(128)S(1)}, s32[4]{0:T(128)}, u32[]{:S(2)}) copy-start(s32[4]{0:T(128)} %param.12) | copy-start | bytes 52
  107.8 12.4 %collective-permute-start.9 = (bf16[4,2240,128]{2,1,0:T(8,128)(2,1)}, bf16[4,2240,128]{2,1,0:T(8,128)(2,1)S(1)}, u32[]{:S(2)}, u32[]{:S(2)}) collective-permute-start(bf16[4,2240,128]{2,1,0:T(8,128)(2,1)} %constant_dynamic-slice_fusion.2), channel_id=1, source_target_pairs={{16,0},{17,1},{18,2},{19,3},{20,4},{21,5},{22,6},{23,7},{24,8},{25... | collective-permute-start | bytes 6881288 | tf_op jit(solution)/shard_map/ppermute | solution.py:69
  109.3 1.9 copy-start.12
  109.9 3.7 %collective-permute-start.10 = (bf16[192,128]{1,0:T(8,128)(2,1)}, bf16[192,128]{1,0:T(8,128)(2,1)}, u32[]{:S(2)}, u32[]{:S(2)}) collective-permute-start(bf16[192,128]{1,0:T(8,128)(2,1)} %convert_element_type.282), channel_id=1, source_target_pairs={{16,0},{17,1},{18,2},{19,3},{20,4},{21,5},{22,6},{23,7},{24,8},{25... | collective-permute-start | bytes 147464 | tf_op jit(solution)/shard_map/ppermute | solution.py:69
  113.6 117.0 %copy-start.9 = (bf16[2048,64]{0,1:T(8,128)(2,1)}, bf16[2048,64]{0,1:T(8,128)(2,1)S(1)}, u32[]{:S(2)}) copy-start(bf16[2048,64]{0,1:T(8,128)(2,1)S(1)} %slice.353) | copy-start | bytes 786436
  114.6 4.0 %collective-permute-start.11 = (bf16[128,128]{1,0:T(8,128)(2,1)S(1)}, bf16[128,128]{1,0:T(8,128)(2,1)S(1)}, u32[]{:S(2)}, u32[]{:S(2)}) collective-permute-start(bf16[128,128]{1,0:T(8,128)(2,1)S(1)} %get-tuple-element.22), channel_id=1, source_target_pairs={{32,0},{33,1},{34,2},{35,3},{36,4},{37,5},{38,6},{39,7},{40,8},{41... | collective-permute-start | bytes 98312 | tf_op jit(solution)/shard_map/ppermute | solution.py:69
  118.6 10.7 %collective-permute-start.12 = (bf16[64,128]{1,0:T(8,128)(2,1)S(1)}, bf16[64,128]{1,0:T(8,128)(2,1)S(1)}, u32[]{:S(2)}, u32[]{:S(2)}) collective-permute-start(bf16[64,128]{1,0:T(8,128)(2,1)S(1)} %fusion.95), channel_id=1, source_target_pairs={{96,0},{97,1},{98,2},{99,3},{100,4},{101,5},{102,6},{103,7},{104,8... | collective-permute-start | bytes 49160 | tf_op jit(solution)/shard_map/ppermute | solution.py:69
  120.2 2.5 copy-start.1
  122.7 6.6 %copy-start.7 = (f32[512,128]{1,0:T(8,128)S(1)}, f32[512,128]{1,0:T(8,128)}, u32[]{:S(2)}) copy-start(f32[512,128]{1,0:T(8,128)} %param.9) | copy-start | bytes 786436
  122.7 6.9 %copy-start.8 = (bf16[4,128,128]{2,1,0:T(8,128)(2,1)S(1)}, bf16[4,128,128]{2,1,0:T(8,128)(2,1)}, u32[]{:S(2)}) copy-start(bf16[4,128,128]{2,1,0:T(8,128)(2,1)} %param.13) | copy-start | bytes 393220
  122.7 10.7 %copy-start.4 = (bf16[2048,704]{0,1:T(8,128)(2,1)S(1)}, bf16[2048,704]{0,1:T(8,128)(2,1)}, u32[]{:S(2)}) copy-start(bf16[2048,704]{0,1:T(8,128)(2,1)} %copy-done.2) | copy-start | bytes 8650756
  129.8 6.5 %collective-permute-start.14 = (bf16[512,128]{1,0:T(8,128)(2,1)S(1)}, bf16[512,128]{1,0:T(8,128)(2,1)S(1)}, u32[]{:S(2)}, u32[]{:S(2)}) collective-permute-start(bf16[512,128]{1,0:T(8,128)(2,1)S(1)} %bitcast_convert_fusion.2), channel_id=1, source_target_pairs={{12,0},{13,1},{14,2},{15,3},{0,4},{1,5},{2,6},{3,7},{4,8},{5,9},{6... | collective-permute-start | bytes 393224 | tf_op jit(solution)/shard_map/ppermute | solution.py:69
  131.3 5.1 %collective-permute-start.13 = (bf16[512,128]{1,0:T(8,128)(2,1)S(1)}, bf16[512,128]{1,0:T(8,128)(2,1)S(1)}, u32[]{:S(2)}, u32[]{:S(2)}) collective-permute-start(bf16[512,128]{1,0:T(8,128)(2,1)S(1)} %bitcast_convert_fusion.2), channel_id=1, source_target_pairs={{4,0},{5,1},{6,2},{7,3},{8,4},{9,5},{10,6},{11,7},{12,8},{13,9},{1... | collective-permute-start | bytes 393224 | tf_op jit(solution)/shard_map/ppermute | solution.py:69
  136.3 5.5 %collective-permute-start.16 = (bf16[256,128]{1,0:T(8,128)(2,1)S(1)}, bf16[256,128]{1,0:T(8,128)(2,1)S(1)}, u32[]{:S(2)}, u32[]{:S(2)}) collective-permute-start(bf16[256,128]{1,0:T(8,128)(2,1)S(1)} %slice.352), channel_id=1, source_target_pairs={{12,0},{13,1},{14,2},{15,3},{0,4},{1,5},{2,6},{3,7},{4,8},{5,9},{6... | collective-permute-start | bytes 196616 | tf_op jit(solution)/shard_map/ppermute | solution.py:69
  136.4 5.4 %collective-permute-start.15 = (bf16[256,128]{1,0:T(8,128)(2,1)S(1)}, bf16[256,128]{1,0:T(8,128)(2,1)S(1)}, u32[]{:S(2)}, u32[]{:S(2)}) collective-permute-start(bf16[256,128]{1,0:T(8,128)(2,1)S(1)} %slice.351), channel_id=1, source_target_pairs={{4,0},{5,1},{6,2},{7,3},{8,4},{9,5},{10,6},{11,7},{12,8},{13,9},{1... | collective-permute-start | bytes 196616 | tf_op jit(solution)/shard_map/ppermute | solution.py:69
  142.2 4.2 %collective-permute-start.17 = (bf16[192,128]{1,0:T(8,128)(2,1)S(1)}, bf16[192,128]{1,0:T(8,128)(2,1)S(1)}, u32[]{:S(2)}, u32[]{:S(2)}) collective-permute-start(bf16[192,128]{1,0:T(8,128)(2,1)S(1)} %get-tuple-element.39), channel_id=1, source_target_pairs={{1,0},{0,1},{3,2},{2,3},{5,4},{4,5},{7,6},{6,7},{9,8},{8,9},{11,10... | collective-permute-start | bytes 147464 | tf_op jit(solution)/shard_map/ppermute | solution.py:69
  146.4 5.6 %collective-permute-start.18 = (bf16[192,128]{1,0:T(8,128)(2,1)S(1)}, bf16[192,128]{1,0:T(8,128)(2,1)S(1)}, u32[]{:S(2)}, u32[]{:S(2)}) collective-permute-start(bf16[192,128]{1,0:T(8,128)(2,1)S(1)} %fusion.45), channel_id=1, source_target_pairs={{3,0},{2,1},{1,2},{0,3},{7,4},{6,5},{5,6},{4,7},{11,8},{10,9},{9,1... | collective-permute-start | bytes 147464 | tf_op jit(solution)/shard_map/ppermute | solution.py:69
  152.0 1.3 collective-permute-start.19
  153.3 5.1 %collective-permute-start.20 = (bf16[128,128]{1,0:T(8,128)(2,1)S(1)}, bf16[128,128]{1,0:T(8,128)(2,1)S(1)}, u32[]{:S(2)}, u32[]{:S(2)}) collective-permute-start(bf16[128,128]{1,0:T(8,128)(2,1)S(1)} %get-tuple-element.18), channel_id=1, source_target_pairs={{32,0},{33,1},{34,2},{35,3},{36,4},{37,5},{38,6},{39,7},{40,8},{41... | collective-permute-start | bytes 98312 | tf_op jit(solution)/shard_map/ppermute | solution.py:69
  158.5 6.2 %collective-permute-start.21 = (bf16[64,128]{1,0:T(8,128)(2,1)S(1)}, bf16[64,128]{1,0:T(8,128)(2,1)S(1)}, u32[]{:S(2)}, u32[]{:S(2)}) collective-permute-start(bf16[64,128]{1,0:T(8,128)(2,1)S(1)} %fusion.94), channel_id=1, source_target_pairs={{96,0},{97,1},{98,2},{99,3},{100,4},{101,5},{102,6},{103,7},{104,8... | collective-permute-start | bytes 49160 | tf_op jit(solution)/shard_map/ppermute | solution.py:69
  202.5 10.8 %collective-permute-start.22 = (bf16[4,2240,128]{2,1,0:T(8,128)(2,1)S(1)}, bf16[4,2240,128]{2,1,0:T(8,128)(2,1)S(1)}, u32[]{:S(2)}, u32[]{:S(2)}) collective-permute-start(bf16[4,2240,128]{2,1,0:T(8,128)(2,1)S(1)} %constant_dynamic-slice_fusion.1), channel_id=1, source_target_pairs={{16,0},{17,1},{18,2},{19,3},{20,4},{21,5},{22,6},{23,7},{24,8},{25... | collective-permute-start | bytes 6881288 | tf_op jit(solution)/shard_map/ppermute | solution.py:69
  202.6 4.4 %collective-permute-start.23 = (bf16[192,128]{1,0:T(8,128)(2,1)S(1)}, bf16[192,128]{1,0:T(8,128)(2,1)S(1)}, u32[]{:S(2)}, u32[]{:S(2)}) collective-permute-start(bf16[192,128]{1,0:T(8,128)(2,1)S(1)} %convert_element_type.307), channel_id=1, source_target_pairs={{16,0},{17,1},{18,2},{19,3},{20,4},{21,5},{22,6},{23,7},{24,8},{25... | collective-permute-start | bytes 147464 | tf_op jit(solution)/shard_map/ppermute | solution.py:69
  207.1 4.0 %collective-permute-start.24 = (bf16[128,128]{1,0:T(8,128)(2,1)S(1)}, bf16[128,128]{1,0:T(8,128)(2,1)S(1)}, u32[]{:S(2)}, u32[]{:S(2)}) collective-permute-start(bf16[128,128]{1,0:T(8,128)(2,1)S(1)} %get-tuple-element.16), channel_id=1, source_target_pairs={{32,0},{33,1},{34,2},{35,3},{36,4},{37,5},{38,6},{39,7},{40,8},{41... | collective-permute-start | bytes 98312 | tf_op jit(solution)/shard_map/ppermute | solution.py:69
  211.1 6.2 %collective-permute-start.25 = (bf16[64,128]{1,0:T(8,128)(2,1)S(1)}, bf16[64,128]{1,0:T(8,128)(2,1)S(1)}, u32[]{:S(2)}, u32[]{:S(2)}) collective-permute-start(bf16[64,128]{1,0:T(8,128)(2,1)S(1)} %fusion.93), channel_id=1, source_target_pairs={{96,0},{97,1},{98,2},{99,3},{100,4},{101,5},{102,6},{103,7},{104,8... | collective-permute-start | bytes 49160 | tf_op jit(solution)/shard_map/ppermute | solution.py:69
  217.8 7.3 %collective-permute-start.27 = (bf16[512,128]{1,0:T(8,128)(2,1)S(1)}, bf16[512,128]{1,0:T(8,128)(2,1)S(1)}, u32[]{:S(2)}, u32[]{:S(2)}) collective-permute-start(bf16[512,128]{1,0:T(8,128)(2,1)S(1)} %bitcast_convert_fusion.1), channel_id=1, source_target_pairs={{12,0},{13,1},{14,2},{15,3},{0,4},{1,5},{2,6},{3,7},{4,8},{5,9},{6... | collective-permute-start | bytes 393224 | tf_op jit(solution)/shard_map/ppermute | solution.py:69
  217.9 7.2 %collective-permute-start.26 = (bf16[512,128]{1,0:T(8,128)(2,1)S(1)}, bf16[512,128]{1,0:T(8,128)(2,1)S(1)}, u32[]{:S(2)}, u32[]{:S(2)}) collective-permute-start(bf16[512,128]{1,0:T(8,128)(2,1)S(1)} %bitcast_convert_fusion.1), channel_id=1, source_target_pairs={{4,0},{5,1},{6,2},{7,3},{8,4},{9,5},{10,6},{11,7},{12,8},{13,9},{1... | collective-permute-start | bytes 393224 | tf_op jit(solution)/shard_map/ppermute | solution.py:69
  225.1 5.5 %collective-permute-start.29 = (bf16[256,128]{1,0:T(8,128)(2,1)S(1)}, bf16[256,128]{1,0:T(8,128)(2,1)S(1)}, u32[]{:S(2)}, u32[]{:S(2)}) collective-permute-start(bf16[256,128]{1,0:T(8,128)(2,1)S(1)} %slice.370), channel_id=1, source_target_pairs={{12,0},{13,1},{14,2},{15,3},{0,4},{1,5},{2,6},{3,7},{4,8},{5,9},{6... | collective-permute-start | bytes 196616 | tf_op jit(solution)/shard_map/ppermute | solution.py:69
  225.1 5.4 %collective-permute-start.28 = (bf16[256,128]{1,0:T(8,128)(2,1)S(1)}, bf16[256,128]{1,0:T(8,128)(2,1)S(1)}, u32[]{:S(2)}, u32[]{:S(2)}) collective-permute-start(bf16[256,128]{1,0:T(8,128)(2,1)S(1)} %slice.369), channel_id=1, source_target_pairs={{4,0},{5,1},{6,2},{7,3},{8,4},{9,5},{10,6},{11,7},{12,8},{13,9},{1... | collective-permute-start | bytes 196616 | tf_op jit(solution)/shard_map/ppermute | solution.py:69
  231.0 4.2 %collective-permute-start.30 = (bf16[192,128]{1,0:T(8,128)(2,1)S(1)}, bf16[192,128]{1,0:T(8,128)(2,1)S(1)}, u32[]{:S(2)}, u32[]{:S(2)}) collective-permute-start(bf16[192,128]{1,0:T(8,128)(2,1)S(1)} %get-tuple-element.43), channel_id=1, source_target_pairs={{1,0},{0,1},{3,2},{2,3},{5,4},{4,5},{7,6},{6,7},{9,8},{8,9},{11,10... | collective-permute-start | bytes 147464 | tf_op jit(solution)/shard_map/ppermute | solution.py:69
  235.2 5.4 %collective-permute-start.31 = (bf16[192,128]{1,0:T(8,128)(2,1)S(1)}, bf16[192,128]{1,0:T(8,128)(2,1)S(1)}, u32[]{:S(2)}, u32[]{:S(2)}) collective-permute-start(bf16[192,128]{1,0:T(8,128)(2,1)S(1)} %fusion.46), channel_id=1, source_target_pairs={{3,0},{2,1},{1,2},{0,3},{7,4},{6,5},{5,6},{4,7},{11,8},{10,9},{9,1... | collective-permute-start | bytes 147464 | tf_op jit(solution)/shard_map/ppermute | solution.py:69
  240.6 1.3 collective-permute-start.32
  241.9 4.3 %collective-permute-start.33 = (bf16[128,128]{1,0:T(8,128)(2,1)S(1)}, bf16[128,128]{1,0:T(8,128)(2,1)S(1)}, u32[]{:S(2)}, u32[]{:S(2)}) collective-permute-start(bf16[128,128]{1,0:T(8,128)(2,1)S(1)} %get-tuple-element.12), channel_id=1, source_target_pairs={{32,0},{33,1},{34,2},{35,3},{36,4},{37,5},{38,6},{39,7},{40,8},{41... | collective-permute-start | bytes 98312 | tf_op jit(solution)/shard_map/ppermute | solution.py:69
  246.2 5.7 %collective-permute-start.34 = (bf16[64,128]{1,0:T(8,128)(2,1)S(1)}, bf16[64,128]{1,0:T(8,128)(2,1)S(1)}, u32[]{:S(2)}, u32[]{:S(2)}) collective-permute-start(bf16[64,128]{1,0:T(8,128)(2,1)S(1)} %fusion.92), channel_id=1, source_target_pairs={{96,0},{97,1},{98,2},{99,3},{100,4},{101,5},{102,6},{103,7},{104,8... | collective-permute-start | bytes 49160 | tf_op jit(solution)/shard_map/ppermute | solution.py:69
  289.8 10.8 %collective-permute-start.35 = (bf16[4,2240,128]{2,1,0:T(8,128)(2,1)S(1)}, bf16[4,2240,128]{2,1,0:T(8,128)(2,1)S(1)}, u32[]{:S(2)}, u32[]{:S(2)}) collective-permute-start(bf16[4,2240,128]{2,1,0:T(8,128)(2,1)S(1)} %constant_dynamic-slice_fusion), channel_id=1, source_target_pairs={{16,0},{17,1},{18,2},{19,3},{20,4},{21,5},{22,6},{23,7},{24,8},{25... | collective-permute-start | bytes 6881288 | tf_op jit(solution)/shard_map/ppermute | solution.py:69
  289.9 4.4 %collective-permute-start.36 = (bf16[192,128]{1,0:T(8,128)(2,1)S(1)}, bf16[192,128]{1,0:T(8,128)(2,1)S(1)}, u32[]{:S(2)}, u32[]{:S(2)}) collective-permute-start(bf16[192,128]{1,0:T(8,128)(2,1)S(1)} %convert_element_type.328), channel_id=1, source_target_pairs={{16,0},{17,1},{18,2},{19,3},{20,4},{21,5},{22,6},{23,7},{24,8},{25... | collective-permute-start | bytes 147464 | tf_op jit(solution)/shard_map/ppermute | solution.py:69
  294.4 4.0 %collective-permute-start.37 = (bf16[128,128]{1,0:T(8,128)(2,1)S(1)}, bf16[128,128]{1,0:T(8,128)(2,1)S(1)}, u32[]{:S(2)}, u32[]{:S(2)}) collective-permute-start(bf16[128,128]{1,0:T(8,128)(2,1)S(1)} %get-tuple-element.10), channel_id=1, source_target_pairs={{32,0},{33,1},{34,2},{35,3},{36,4},{37,5},{38,6},{39,7},{40,8},{41... | collective-permute-start | bytes 98312 | tf_op jit(solution)/shard_map/ppermute | solution.py:69
  298.4 6.2 %collective-permute-start.38 = (bf16[64,128]{1,0:T(8,128)(2,1)S(1)}, bf16[64,128]{1,0:T(8,128)(2,1)S(1)}, u32[]{:S(2)}, u32[]{:S(2)}) collective-permute-start(bf16[64,128]{1,0:T(8,128)(2,1)S(1)} %fusion.91), channel_id=1, source_target_pairs={{96,0},{97,1},{98,2},{99,3},{100,4},{101,5},{102,6},{103,7},{104,8... | collective-permute-start | bytes 49160 | tf_op jit(solution)/shard_map/ppermute | solution.py:69
  300.6 5.2 %copy-start.10 = (bf16[2048,64]{0,1:T(8,128)(2,1)S(1)}, bf16[2048,64]{0,1:T(8,128)(2,1)}, u32[]{:S(2)}) copy-start(bf16[2048,64]{0,1:T(8,128)(2,1)} %copy-done.9) | copy-start | bytes 786436
  304.6 33.0 %copy-start.11 = (bf16[3,64,512]{2,1,0:T(8,128)(2,1)S(1)}, bf16[3,64,512]{2,1,0:T(8,128)(2,1)}, u32[]{:S(2)}) copy-start(bf16[3,64,512]{2,1,0:T(8,128)(2,1)} %param.16) | copy-start | bytes 589828
  306.0 4.2 %collective-permute-start.39 = (bf16[192,128]{1,0:T(8,128)(2,1)S(1)}, bf16[192,128]{1,0:T(8,128)(2,1)S(1)}, u32[]{:S(2)}, u32[]{:S(2)}) collective-permute-start(bf16[192,128]{1,0:T(8,128)(2,1)S(1)} %get-tuple-element.49), channel_id=1, source_target_pairs={{4,0},{5,1},{6,2},{7,3},{0,4},{1,5},{2,6},{3,7},{12,8},{13,9},{14,... | collective-permute-start | bytes 147464 | tf_op jit(solution)/shard_map/ppermute | solution.py:69
  310.2 6.9 %collective-permute-start.40 = (bf16[192,128]{1,0:T(8,128)(2,1)S(1)}, bf16[192,128]{1,0:T(8,128)(2,1)S(1)}, u32[]{:S(2)}, u32[]{:S(2)}) collective-permute-start(bf16[192,128]{1,0:T(8,128)(2,1)S(1)} %fusion.47), channel_id=1, source_target_pairs={{12,0},{13,1},{14,2},{15,3},{8,4},{9,5},{10,6},{11,7},{4,8},{5,9},... | collective-permute-start | bytes 147464 | tf_op jit(solution)/shard_map/ppermute | solution.py:69
  317.1 4.2 %collective-permute-start.41 = (bf16[192,128]{1,0:T(8,128)(2,1)S(1)}, bf16[192,128]{1,0:T(8,128)(2,1)S(1)}, u32[]{:S(2)}, u32[]{:S(2)}) collective-permute-start(bf16[192,128]{1,0:T(8,128)(2,1)S(1)} %fusion.155), channel_id=1, source_target_pairs={{1,0},{0,1},{3,2},{2,3},{5,4},{4,5},{7,6},{6,7},{9,8},{8,9},{11,10... | collective-permute-start | bytes 147464 | tf_op jit(solution)/shard_map/ppermute | solution.py:69
  321.3 5.4 %collective-permute-start.42 = (bf16[192,128]{1,0:T(8,128)(2,1)S(1)}, bf16[192,128]{1,0:T(8,128)(2,1)S(1)}, u32[]{:S(2)}, u32[]{:S(2)}) collective-permute-start(bf16[192,128]{1,0:T(8,128)(2,1)S(1)} %fusion.48), channel_id=1, source_target_pairs={{3,0},{2,1},{1,2},{0,3},{7,4},{6,5},{5,6},{4,7},{11,8},{10,9},{9,1... | collective-permute-start | bytes 147464 | tf_op jit(solution)/shard_map/ppermute | solution.py:69
  326.7 1.3 collective-permute-start.43
  328.0 4.3 %collective-permute-start.44 = (bf16[128,128]{1,0:T(8,128)(2,1)S(1)}, bf16[128,128]{1,0:T(8,128)(2,1)S(1)}, u32[]{:S(2)}, u32[]{:S(2)}) collective-permute-start(bf16[128,128]{1,0:T(8,128)(2,1)S(1)} %get-tuple-element.6), channel_id=1, source_target_pairs={{32,0},{33,1},{34,2},{35,3},{36,4},{37,5},{38,6},{39,7},{40,8},{41... | collective-permute-start | bytes 98312 | tf_op jit(solution)/shard_map/ppermute | solution.py:69
  332.3 5.2 %collective-permute-start.45 = (bf16[64,128]{1,0:T(8,128)(2,1)S(1)}, bf16[64,128]{1,0:T(8,128)(2,1)S(1)}, u32[]{:S(2)}, u32[]{:S(2)}) collective-permute-start(bf16[64,128]{1,0:T(8,128)(2,1)S(1)} %fusion.90), channel_id=1, source_target_pairs={{96,0},{97,1},{98,2},{99,3},{100,4},{101,5},{102,6},{103,7},{104,8... | collective-permute-start | bytes 49160 | tf_op jit(solution)/shard_map/ppermute | solution.py:69

commit v2 on v1

v2 whole, which is shorter than its diff:
```python
import jax
import jax.numpy as jnp
from jax import lax
from jax.experimental import pallas as pl
from jax.experimental.pallas import tpu as pltpu
from jax.sharding import PartitionSpec as P

ITERS = 3
AXES = ("drop", "blk")
BS = 128
NBD = 4
SLOTS = 40
R = 64
ROWS = NBD * BS
RING = 4 * ROWS
TERMS = 3 * R
PIECE = RING + TERMS
BF = jnp.bfloat16
F32 = jnp.float32


def coords(i):
    return i // 32, i // 16 % 2, i % 4, i // 4 % 4


def index(x, core, y, z):
    return (x % 4) * 32 + core * 16 + (z % 4) * 4 + y % 4


def pull(source):
    return [(source(i), i) for i in range(128)]


def along(axis, other):
    def source(i):
        x, core, y, z = coords(i)
        even = (x + core) % 2 == 1
        if even == (axis == 1):
            return index(x, core, other(y), z)
        return index(x, core, y, other(z))

    return pull(source)


FIRST = [along(1, lambda d, k=k: d + k) for k in (1, 3, 2)]
SECOND = [along(2, lambda d, k=k: d + k) for k in (1, 3, 2)]
CORE = pull(lambda i: i ^ 16)
CHIP = [pull(lambda i, k=k: i ^ (32 * k)) for k in (1, 2, 3)]


def groups_of_eight():
    out = []
    for p in range(4):
        for k in range(4):
            members = []
            for x, core in ((p, 1), (p + 1, 0)):
                for j in range(4):
                    members.append(index(x, core, k, j) if p % 2 == 0 else index(x, core, j, k))
            out.append(members)
    return out


EIGHTS = groups_of_eight()


def move(array, pairs):
    return lax.ppermute(array, AXES, pairs)


def ring(array):
    return [move(array, pairs) for pairs in FIRST]


def long_ring(array):
    half = array.shape[0] // 2
    up, down = move(array, FIRST[0]), move(array, FIRST[1])
    return [up, down, jnp.concatenate([move(up[:half], FIRST[0]), move(down[half:], FIRST[1])], axis=0)]


def add_over(term, steps):
    sent = term.astype(BF)
    return term + sum(move(sent, pairs).astype(F32) for pairs in steps)


def siblings(term):
    other = move(term.astype(BF), CORE)
    return siblings_of(other, term)


def siblings_of(other, term):
    chip = (term[R:] + other[R:].astype(F32)).astype(BF)
    near, far_a, far_b = move(chip[:R], CHIP[0]), move(chip[R:], CHIP[1]), move(chip[R:], CHIP[2])
    return jnp.concatenate([other[:R], near, (far_a.astype(F32) + far_b.astype(F32)).astype(BF)], axis=0)


def dot(a, b):
    return jnp.dot(a.astype(BF), b.astype(BF), preferred_element_type=F32)


def dot_t(a, b):
    return lax.dot_general(
        a.astype(BF), b.astype(BF), (((0,), (0,)), ((), ())), preferred_element_type=F32
    )


def dot_bt(a, b):
    return lax.dot_general(
        a.astype(BF), b.astype(BF), (((1,), (1,)), ((), ())), preferred_element_type=F32
    )


def slot_tables(neighbours, counts):
    drop, blk = lax.axis_index("drop"), lax.axis_index("blk")
    core, mine = drop % 2, (blk % 4, blk // 4)
    kind = neighbours // 64
    group = drop - 1 + kind
    block = neighbours % 64
    owner, part = block // 4, block % 4
    place = lax.rem(kind - core + 3, 3)
    even = (drop // 2 + core) % 2 == 1
    y_first = even == (place < 2)
    y, z = owner % 4, owner // 4
    first = jnp.where(y_first, y, z)
    second = jnp.where(y_first, z, y)
    mine_first = jnp.where(y_first, mine[0], mine[1])
    apart = (first - mine_first + 4) % 4
    at = jnp.where(apart < 2, apart, 5 - apart)
    member = jnp.where(place == 1, 4, 0) + second
    row = member * jnp.where(place < 2, PIECE, RING) + at * ROWS + part * BS
    slot = lax.broadcasted_iota(jnp.int32, neighbours.shape, 1)
    live = (slot < counts[:, None]) & (group >= 0) & (group <= 7)
    key = jnp.where(live, jnp.where(place < 2, 0, 1), 2)
    rank_key = key * SLOTS + slot
    rank = jnp.sum((rank_key[:, None, :] < rank_key[:, :, None]).astype(jnp.int32), axis=2)
    put = rank[:, :, None] == lax.broadcasted_iota(jnp.int32, (1, 1, SLOTS), 2)
    order = jnp.sum(jnp.where(put, slot[:, :, None], 0), axis=1)
    start = jnp.sum(jnp.where(put, row[:, :, None], 0), axis=1)
    n_pair = jnp.sum((key == 0).astype(jnp.int32), axis=1)
    n_live = jnp.sum((key < 2).astype(jnp.int32), axis=1)
    return order.reshape(-1), start.reshape(-1), n_pair, n_live


def near_kernel(order, start, lo, hi, blocks, field, before, out):
    for q in range(NBD):
        first, last = lo[q], hi[q]

        def two(i, acc, q=q, first=first, last=last):
            j = first + 2 * i
            k = jnp.minimum(j + 1, last - 1)
            left = blocks[q, order[q * SLOTS + j]]
            right = blocks[q, order[q * SLOTS + k]]
            right = jnp.where(j + 1 < last, right, jnp.zeros_like(right))
            upper = field[pl.ds(pl.multiple_of(start[q * SLOTS + j], 64), BS), :]
            lower = field[pl.ds(pl.multiple_of(start[q * SLOTS + k], 64), BS), :]
            return acc + jnp.dot(
                jnp.concatenate([left, right], axis=1),
                jnp.concatenate([upper, lower], axis=0),
                preferred_element_type=F32,
            )

        rows = pl.ds(q * BS, BS)
        out[rows, :] = lax.fori_loop(0, (last - first + 1) // 2, two, before[rows, :])


def near(order, start, lo, hi, near_blocks, field, before):
    small, whole = pl.BlockSpec(memory_space=pltpu.SMEM), pl.BlockSpec(memory_space=pltpu.VMEM)
    return pl.pallas_call(
        near_kernel,
        in_specs=[small] * 4 + [whole] * 3,
        out_specs=whole,
        out_shape=jax.ShapeDtypeStruct((ROWS, BS), F32),
        compiler_params=pltpu.CompilerParams(vmem_limit_bytes=32 * 2**20),
        cost_estimate=pl.CostEstimate(flops=2 * 80 * BS**3, bytes_accessed=10 * 2**20, transcendentals=0),
    )(order, start, lo, hi, near_blocks, field, before)


def leaf(resid, leaf_inverse):
    tiles = resid.astype(BF).reshape(NBD, BS, BS)
    return jnp.einsum("bij,bjn->bin", leaf_inverse, tiles, preferred_element_type=F32).reshape(ROWS, BS)


def first_terms(z, right, left):
    terms = dot(right, z)
    cross = dot_bt(right, left)
    low = jnp.concatenate([cross[R : 2 * R, :R], cross[2 * R :, :R]], axis=1)
    high = jnp.concatenate([cross[2 * R :, R : 2 * R]] * 2, axis=1)
    return jnp.concatenate([terms, low, high], axis=0)


def first_siblings(mine):
    other = move(mine.astype(BF), CORE).astype(F32)

    def parts(a):
        return a[:R], a[R : 2 * R], a[2 * R : 3 * R], a[3 * R : 4 * R, :R], a[3 * R : 4 * R, R:], a[4 * R :, :R]

    a0, a1, a2, m10, m20, m21 = parts(mine)
    b0, b1, b2, k10, k20, k21 = parts(other)
    t1 = a1 - dot(m10, b0) + b1 - dot(k10, a0)
    t2 = a2 - dot(m20, b0) + b2 - dot(k20, a0)
    m21 = m21 + k21
    chip = jnp.concatenate([t1, t2, jnp.concatenate([m21, m21], axis=1)], axis=0)
    near_chip = move(chip.astype(BF), CHIP[0]).astype(F32)
    s1, u2, k21 = near_chip[:R], near_chip[R : 2 * R], near_chip[2 * R :, :R]
    half = t2 - dot(m21, s1) + u2 - dot(k21, t1)
    s2 = move(half.astype(BF), CHIP[2])
    return jnp.concatenate([b0.astype(BF), s1.astype(BF), s2], axis=0), (k10, k20, k21)


def fold(right, mixes):
    k10, k20, k21 = mixes
    r0, r1, r2 = right[:R], right[R : 2 * R], right[2 * R :]
    f1 = r1.astype(F32) - dot(k10, r0)
    f2 = r2.astype(F32) - dot(k20, r0) - dot(k21, f1)
    return jnp.concatenate([r0, f1.astype(BF), f2.astype(BF)], axis=0)


def by_block(factors):
    return jnp.concatenate([factors[:, i * BS : (i + 1) * BS] for i in range(NBD)], axis=0)


def on_device(
    right_side, near_blocks, neighbours, counts, leaf_inverse, couple_left, couple_right, prec_left, prec_right
):
    upper = lax.axis_index("drop") % 2 == 0
    order, start, n_pair, n_live = slot_tables(neighbours, counts)
    none = jnp.zeros_like(n_pair)
    c_left, c_right, left, right = (
        f.reshape(TERMS, ROWS) for f in (couple_left, couple_right, prec_left, prec_right)
    )

    z = leaf(right_side, leaf_inverse)
    terms = first_terms(z, right, left)
    count = terms.shape[0]
    sent = jnp.concatenate([z.astype(BF), terms.astype(BF), by_block(left), by_block(c_right)], axis=0)
    rest = long_ring(sent)
    terms = terms + sum(a[ROWS : ROWS + count].astype(F32) for a in rest)
    sums, mixes = first_siblings(add_over(terms, SECOND))
    sums, order, start, n_pair, n_live = lax.optimization_barrier((sums, order, start, n_pair, n_live))
    at = ROWS + count
    ring_left = jnp.concatenate([a[at : at + NBD * TERMS] for a in [sent] + rest], axis=0).reshape(-1, TERMS, BS)
    at += NBD * TERMS
    ring_c = jnp.concatenate([a[at : at + NBD * TERMS] for a in [sent] + rest], axis=0).reshape(-1, TERMS, BS)
    ring_c = ring_c.transpose(1, 0, 2).reshape(TERMS, RING)

    def corrected(field, sums):
        fix = jnp.einsum("bkr,kn->brn", ring_left, sums, preferred_element_type=F32)
        return field - fix.reshape(RING, BS)

    field = corrected(jnp.concatenate([z] + [a[:ROWS].astype(F32) for a in rest], axis=0), sums)
    folded = fold(right, mixes)

    for step in range(ITERS):
        field_b = field.astype(BF)
        piece = jnp.concatenate([field_b, dot(ring_c, field_b).astype(BF)], axis=0)
        pieces = lax.all_to_all(
            jnp.broadcast_to(piece[None], (8, PIECE, BS)), AXES, 0, 0, tiled=True, axis_index_groups=EIGHTS
        )
        c_parts = lax.dynamic_slice(pieces, (jnp.where(upper, 4, 0), RING, 0), (4, TERMS, BS))
        c_terms = jnp.sum(c_parts.astype(F32), axis=0)
        c_other = move(c_terms.astype(BF), CORE)
        pieces, c_other = lax.optimization_barrier((pieces, c_other))
        own = lax.dynamic_slice(pieces, (jnp.where(upper, 4, 0), 0, 0), (4, RING, BS))
        other = move(own, CORE)
        c_sums = siblings_of(c_other, c_terms)
        x = field[:ROWS]
        image = near(order, start, none, n_pair, near_blocks, pieces.reshape(8 * PIECE, BS), x)
        image = near(order, start, n_pair, n_live, near_blocks, other.reshape(4 * RING, BS), image)
        resid = right_side - (image + dot_t(c_left, c_sums))
        z = leaf(resid, leaf_inverse)
        terms = dot(folded, z)
        if step < ITERS - 1:
            rest = ring(jnp.concatenate([z.astype(BF), terms.astype(BF)], axis=0))
            terms = terms + sum(a[ROWS:].astype(F32) for a in rest)
            sums = siblings(add_over(terms, SECOND))
            z_ring = jnp.concatenate([z] + [a[:ROWS].astype(F32) for a in rest], axis=0)
            field = corrected(field + z_ring, sums)
        else:
            sums = siblings(add_over(add_over(terms, FIRST), SECOND))
            x = x + z - dot_t(left, sums)
    return x, resid


def solution(mesh):
    in_specs = (
        P(("drop", "blk"), None),
        P(("drop", "blk"), None, None, None),
        P(("drop", "blk"), None),
        P(("drop", "blk")),
        P(("drop", "blk"), None, None),
        P(None, None, ("drop", "blk")),
        P(None, None, ("drop", "blk")),
        P(None, None, ("drop", "blk")),
        P(None, None, ("drop", "blk")),
    )
    out_specs = (P(("drop", "blk"), None), P(("drop", "blk"), None))
    return jax.shard_map(on_device, mesh=mesh, in_specs=in_specs, out_specs=out_specs, check_vma=False)
```

time: 344 us -> 302 us (0.88); the launches traced: 339 us -> 302 us
  waiting for transfers between devices: 122 us -> 96.1 us
  local copies, waits for them, and re-layouts: 29.9 us -> 16.4 us
  Pallas kernels: 14.5 us -> 27 us
  blocking collectives: 72.3 us -> 67.5 us
  other arithmetic: 8.86 us -> 4.62 us
    ppermute x46 -> x55, waiting for transfers between devices: 93.2 us -> 67 us  [move(): return lax.ppermute(array, AXES, pairs)]
    pallas_call x3 -> x6, Pallas kernels: 14.5 us -> 27 us  [near(): pl.pallas_call(near_kernel, in_specs=[small] * 4 + [whole] * 3, out_specs...]
    ppermute x4 -> x0, local copies, waits for them, and re-layouts: 8.45 us -> none  [move(): return lax.ppermute(array, AXES, pairs)]
    slice x20 -> x22, local copies, waits for them, and re-layouts: 5.4 us -> 0.22 us  [the longest x1 0.08 us: first_terms(): low = jnp.concatenate([cross[R:2 * R, :R], cross[2 * R:, :R]], axis=1)]
    all_to_all x2, blocking collectives: 72.3 us -> 67.5 us  [on_device(): lax.all_to_all(jnp.broadcast_to(piece[None], (8, PIECE, BS)), AXES, 0, 0,...]
    unnamed x37 -> x42, local copies, waits for them, and re-layouts: 5.99 us -> 9.04 us
    ppermute x46 -> x55, starting transfers between devices: 70.3 us -> 70.9 us  [move(): return lax.ppermute(array, AXES, pairs)]
  transfers between devices with their start and end apart: 47 -> 56, of which waited for: 34 -> 37; matrix products, arithmetic and copies ran while one was open for 7% -> 2% of each run, Pallas kernels for 4% -> 5%
where the time goes in v2:
time: 302 us
  waiting for transfers between devices  96.1 us (32%)
  starting transfers between devices  77.8 us (26%)
  blocking collectives  67.5 us (22%)
  Pallas kernels  27 us (9%)
  local copies, waits for them, and re-layouts  16.4 us (5%)
  matrix products  10.5 us (3%)
  other arithmetic  4.62 us (2%)
    ppermute x55, starting transfers between devices, move(): return lax.ppermute(array, AXES, pairs)  70.9 us
    all_to_all x2, blocking collectives, on_device(): lax.all_to_all(jnp.broadcast_to(piece[None], (8, PIECE, BS)), AXES, 0, 0,...  67.5 us
    ppermute x55, waiting for transfers between devices, move(): return lax.ppermute(array, AXES, pairs)  67 us
    all_to_all x1, waiting for transfers between devices, on_device(): lax.all_to_all(jnp.broadcast_to(piece[None], (8, PIECE, BS)), AXES, 0, 0,...  29.1 us
    pallas_call x6, Pallas kernels, near(): pl.pallas_call(near_kernel, in_specs=[small] * 4 + [whole] * 3, out_specs...  27 us
    unnamed x42, local copies, waits for them, and re-layouts  9.04 us
    all_to_all x1, starting transfers between devices, on_device(): lax.all_to_all(jnp.broadcast_to(piece[None], (8, PIECE, BS)), AXES, 0, 0,...  6.88 us
  transfers between devices with their start and end apart: 56, of which 37 were waited for; matrix products, arithmetic and copies ran while one was open for 2% of the time, Pallas kernels for 5%

profile of v2, /device:TPU:0, one launch (start us, length us, event | category | flops | bytes accessed | tf_op | source)
XLA Modules:
  0.0 301.6 jit_solution(14385193985310864618)
XLA Ops:
  0.7 1.3 fusion.143
  8.0 4.1 %collective-permute-start = (bf16[2368,128]{1,0:T(8,128)(2,1)S(1)}, bf16[2368,128]{1,0:T(8,128)(2,1)S(1)}, u32[]{:S(2)}, u32[]{:S(2)}) collective-permute-start(bf16[2368,128]{1,0:T(8,128)(2,1)S(1)} %get-tuple-element.47), channel_id=1, source_target_pairs={{4,0},{5,1},{6,2},{7,3},{8,4},{9,5},{10,6},{11,7},{12,8},{13,9},{1... | collective-permute-start | bytes 1818632 | tf_op jit(solution)/shard_map/ppermute | solution.py:67
  12.9 6.8 %collective-permute-done = bf16[2368,128]{1,0:T(8,128)(2,1)S(1)} collective-permute-done((bf16[2368,128]{1,0:T(8,128)(2,1)S(1)}, bf16[2368,128]{1,0:T(8,128)(2,1)S(1)}, u32[]{:S(2)}, u32[]{:S(2)}) %collective-permute-start) | collective-permute-done | bytes 606240 | tf_op jit(solution)/shard_map/ppermute | solution.py:67
  19.7 3.8 %collective-permute-start.2 = (bf16[1184,128]{1,0:T(8,128)(2,1)S(1)}, bf16[1184,128]{1,0:T(8,128)(2,1)S(1)}, u32[]{:S(2)}, u32[]{:S(2)}) collective-permute-start(bf16[1184,128]{1,0:T(8,128)(2,1)S(1)} %slice.389), channel_id=1, source_target_pairs={{4,0},{5,1},{6,2},{7,3},{8,4},{9,5},{10,6},{11,7},{12,8},{13,9},{1... | collective-permute-start | bytes 909320 | tf_op jit(solution)/shard_map/ppermute | solution.py:67
  25.0 2.8 collective-permute-done.2
  27.9 3.1 %collective-permute-start.4 = (bf16[320,128]{1,0:T(8,128)(2,1)S(1)}, bf16[320,128]{1,0:T(8,128)(2,1)S(1)}, u32[]{:S(2)}, u32[]{:S(2)}) collective-permute-start(bf16[320,128]{1,0:T(8,128)(2,1)S(1)} %fusion.120), channel_id=1, source_target_pairs={{1,0},{2,1},{3,2},{0,3},{5,4},{6,5},{7,6},{4,7},{9,8},{10,9},{11,1... | collective-permute-start | bytes 245768 | tf_op jit(solution)/shard_map/ppermute | solution.py:67
  31.0 2.2 collective-permute-start.6
  33.2 4.3 %collective-permute-done.5 = bf16[320,128]{1,0:T(8,128)(2,1)S(1)} collective-permute-done((bf16[320,128]{1,0:T(8,128)(2,1)S(1)}, bf16[320,128]{1,0:T(8,128)(2,1)S(1)}, u32[]{:S(2)}, u32[]{:S(2)}) %collective-permute-start.5) | collective-permute-done | bytes 81952 | tf_op jit(solution)/shard_map/ppermute | solution.py:67
  39.7 1.5 collective-permute-start.8
  41.3 2.5 collective-permute-done.8
  44.1 2.8 collective-permute-start.9
  50.0 2.7 broadcast_in_dim.74
  52.7 6.9 %all-to-all-start = ((bf16[8,2240,128]{2,1,0:T(8,128)(2,1)}), bf16[8,2240,128]{2,1,0:T(8,128)(2,1)}, u32[]{:S(2)}, u32[]{:S(2)}) async-start(bf16[8,2240,128]{2,1,0:T(8,128)(2,1)} %broadcast_in_dim.74), calls=%async_computation | async-start | bytes 9175040 | tf_op jit(solution)/shard_map/all_to_all | solution.py:255
  59.6 29.1 %all-to-all-done = bf16[8,2240,128]{2,1,0:T(8,128)(2,1)} async-done(((bf16[8,2240,128]{2,1,0:T(8,128)(2,1)}), bf16[8,2240,128]{2,1,0:T(8,128)(2,1)}, u32[]{:S(2)}, u32[]{:S(2)}) %all-to-all-start) | async-done | bytes 4587552 | tf_op jit(solution)/shard_map/all_to_all | solution.py:255
  91.0 1.7 constant_dynamic-slice_fusion.1
  93.9 1.4 collective-permute-start.14
  95.4 1.8 collective-permute-start.12
  97.2 2.5 copy-done.1
  99.7 5.9 %shard_map.104.before = f32[512,128]{1,0:T(8,128)S(1)} custom-call(s32[160]{0:T(256)S(1)} %reshape.101.order, s32[160]{0:T(256)S(1)} %reshape.102.start, s32[4]{0:T(128)S(1)} %broadcast_6_lo.2.lo, s32[4]{0:T(128)S(1)} %get-tuple-element.16.hi.lo, bf16[4,40,128,128]{3,2,1,0:T(8,128)(2,1)S(1)} %copy-done.1, bf16[17920,128]{1,0:T(8,128)(2,1)} %bitcast.12.field, ...), custom_call_target="tpu_custom_call" | custom-call | flops 335544320 | bytes 10485760 | tf_op jit(solution)/shard_map/pallas_call | solution.py:167
  105.9 2.5 copy-done.2
  108.4 4.3 %shard_map.105 = f32[512,128]{1,0:T(8,128)S(1)} custom-call(s32[160]{0:T(256)S(1)} %reshape.101.order, s32[160]{0:T(256)S(1)} %reshape.102.start, s32[4]{0:T(128)S(1)} %get-tuple-element.16.hi.lo, s32[4]{0:T(128)S(1)} %get-tuple-element.17.hi, bf16[4,40,128,128]{3,2,1,0:T(8,128)(2,1)S(1)} %copy-done.2, bf16[8192,128]{1,0:T(8,128)(2,1)S(1)} %bitcast.118, ...), custom_call_target="tpu_custom_call" | custom-call | flops 335544320 | bytes 10485760 | tf_op jit(solution)/shard_map/pallas_call | solution.py:167
  113.3 2.0 collective-permute-start.16
  115.3 3.5 %collective-permute-done.15 = bf16[704,128]{1,0:T(8,128)(2,1)S(1)} collective-permute-done((bf16[704,128]{1,0:T(8,128)(2,1)S(1)}, bf16[704,128]{1,0:T(8,128)(2,1)S(1)}, u32[]{:S(2)}, u32[]{:S(2)}) %collective-permute-start.15) | collective-permute-done | bytes 180256 | tf_op jit(solution)/shard_map/ppermute | solution.py:67
  118.8 1.3 collective-permute-done.16
  120.1 2.2 collective-permute-done.17
  122.9 1.7 collective-permute-start.19
  124.6 1.9 collective-permute-start.20
  126.7 1.5 collective-permute-done.19
  128.2 2.0 collective-permute-done.20
  131.8 4.2 %collective-permute-start.23 = (bf16[64,128]{1,0:T(8,128)(2,1)S(1)}, bf16[64,128]{1,0:T(8,128)(2,1)S(1)}, u32[]{:S(2)}, u32[]{:S(2)}) collective-permute-start(bf16[64,128]{1,0:T(8,128)(2,1)S(1)} %get-tuple-element.74), channel_id=1, source_target_pairs={{64,0},{65,1},{66,2},{67,3},{68,4},{69,5},{70,6},{71,7},{72,8},{73... | collective-permute-start | bytes 49160 | tf_op jit(solution)/shard_map/ppermute | solution.py:67
  135.9 2.8 collective-permute-start.24
  140.9 1.7 collective-permute-done.22
  144.2 33.9 %all_to_all.15 = bf16[8,2240,128]{2,1,0:T(8,128)(2,1)S(1)} all-to-all(bf16[8,2240,128]{2,1,0:T(8,128)(2,1)S(1)} %broadcast_in_dim.75), channel_id=1, replica_groups={{16,20,24,28,32,36,40,44},{17,21,25,29,33,37,41,45},{18,22,26,30,34,38,..., dimensions={0} | all-to-all | bytes 9175040 | tf_op jit(solution)/shard_map/all_to_all | solution.py:255
  179.8 1.7 collective-permute-start.28
  181.6 1.7 collective-permute-start.29
  183.4 4.1 %shard_map.106.before = f32[512,128]{1,0:T(8,128)S(1)} custom-call(s32[160]{0:T(256)S(1)} %reshape.101.order, s32[160]{0:T(256)S(1)} %reshape.102.start, s32[4]{0:T(128)S(1)} %broadcast_6_lo.2.lo, s32[4]{0:T(128)S(1)} %get-tuple-element.16.hi.lo, bf16[4,40,128,128]{3,2,1,0:T(8,128)(2,1)S(1)} %bitcast.115, bf16[17920,128]{1,0:T(8,128)(2,1)S(1)} %bitcast.117, ...), custom_call_target="tpu_custom_call" | custom-call | flops 335544320 | bytes 10485760 | tf_op jit(solution)/shard_map/pallas_call | solution.py:167
  187.9 4.3 %shard_map.107 = f32[512,128]{1,0:T(8,128)S(1)} custom-call(s32[160]{0:T(256)S(1)} %reshape.101.order, s32[160]{0:T(256)S(1)} %reshape.102.start, s32[4]{0:T(128)S(1)} %get-tuple-element.16.hi.lo, s32[4]{0:T(128)S(1)} %get-tuple-element.17.hi, bf16[4,40,128,128]{3,2,1,0:T(8,128)(2,1)S(1)} %bitcast.115, bf16[8192,128]{1,0:T(8,128)(2,1)S(1)} %bitcast.120, ...), custom_call_target="tpu_custom_call" | custom-call | flops 335544320 | bytes 10485760 | tf_op jit(solution)/shard_map/pallas_call | solution.py:167
  192.8 2.0 collective-permute-start.31
  195.4 2.8 collective-permute-done.30
  198.3 1.3 collective-permute-done.31
  199.5 2.2 collective-permute-done.32
  202.2 1.7 collective-permute-start.34
  203.9 1.3 collective-permute-start.35
  206.0 1.5 collective-permute-done.34
  207.5 2.0 collective-permute-done.35
  210.9 4.3 %collective-permute-start.38 = (bf16[64,128]{1,0:T(8,128)(2,1)S(1)}, bf16[64,128]{1,0:T(8,128)(2,1)S(1)}, u32[]{:S(2)}, u32[]{:S(2)}) collective-permute-start(bf16[64,128]{1,0:T(8,128)(2,1)S(1)} %get-tuple-element.70), channel_id=1, source_target_pairs={{64,0},{65,1},{66,2},{67,3},{68,4},{69,5},{70,6},{71,7},{72,8},{73... | collective-permute-start | bytes 49160 | tf_op jit(solution)/shard_map/ppermute | solution.py:67
  215.2 3.4 %collective-permute-start.39 = (bf16[64,128]{1,0:T(8,128)(2,1)S(1)}, bf16[64,128]{1,0:T(8,128)(2,1)S(1)}, u32[]{:S(2)}, u32[]{:S(2)}) collective-permute-start(bf16[64,128]{1,0:T(8,128)(2,1)S(1)} %get-tuple-element.70), channel_id=1, source_target_pairs={{96,0},{97,1},{98,2},{99,3},{100,4},{101,5},{102,6},{103,7},{104,8... | collective-permute-start | bytes 49160 | tf_op jit(solution)/shard_map/ppermute | solution.py:67
  220.3 2.1 collective-permute-done.37
  224.0 33.7 %all_to_all.16 = bf16[8,2240,128]{2,1,0:T(8,128)(2,1)S(1)} all-to-all(bf16[8,2240,128]{2,1,0:T(8,128)(2,1)S(1)} %broadcast_in_dim.76), channel_id=1, replica_groups={{16,20,24,28,32,36,40,44},{17,21,25,29,33,37,41,45},{18,22,26,30,34,38,..., dimensions={0} | all-to-all | bytes 9175040 | tf_op jit(solution)/shard_map/all_to_all | solution.py:255
  259.5 1.8 collective-permute-start.43
  261.3 1.7 collective-permute-start.44
  263.3 4.1 %shard_map.108.before = f32[512,128]{1,0:T(8,128)S(1)} custom-call(s32[160]{0:T(256)S(1)} %reshape.101.order, s32[160]{0:T(256)S(1)} %reshape.102.start, s32[4]{0:T(128)S(1)} %broadcast_6_lo.2.lo, s32[4]{0:T(128)S(1)} %get-tuple-element.16.hi.lo, bf16[4,40,128,128]{3,2,1,0:T(8,128)(2,1)S(1)} %bitcast.115, bf16[17920,128]{1,0:T(8,128)(2,1)S(1)} %bitcast.116, ...), custom_call_target="tpu_custom_call" | custom-call | flops 335544320 | bytes 10485760 | tf_op jit(solution)/shard_map/pallas_call | solution.py:167
  267.7 4.3 %shard_map.109 = f32[512,128]{1,0:T(8,128)S(1)} custom-call(s32[160]{0:T(256)S(1)} %reshape.101.order, s32[160]{0:T(256)S(1)} %reshape.102.start, s32[4]{0:T(128)S(1)} %get-tuple-element.16.hi.lo, s32[4]{0:T(128)S(1)} %get-tuple-element.17.hi, bf16[4,40,128,128]{3,2,1,0:T(8,128)(2,1)S(1)} %bitcast.115, bf16[8192,128]{1,0:T(8,128)(2,1)S(1)} %bitcast.119, ...), custom_call_target="tpu_custom_call" | custom-call | flops 335544320 | bytes 10485760 | tf_op jit(solution)/shard_map/pallas_call | solution.py:167
  273.3 2.0 collective-permute-start.46
  275.9 1.4 collective-permute-done.45
  277.4 1.3 collective-permute-done.46
  278.6 2.2 collective-permute-done.47
  281.0 2.0 collective-permute-start.49
  283.0 2.1 collective-permute-done.48
  286.4 2.2 collective-permute-done.50
  290.0 4.2 %collective-permute-start.53 = (bf16[64,128]{1,0:T(8,128)(2,1)S(1)}, bf16[64,128]{1,0:T(8,128)(2,1)S(1)}, u32[]{:S(2)}, u32[]{:S(2)}) collective-permute-start(bf16[64,128]{1,0:T(8,128)(2,1)S(1)} %get-tuple-element.66), channel_id=1, source_target_pairs={{64,0},{65,1},{66,2},{67,3},{68,4},{69,5},{70,6},{71,7},{72,8},{73... | collective-permute-start | bytes 49160 | tf_op jit(solution)/shard_map/ppermute | solution.py:67
  294.2 2.6 collective-permute-start.54
  296.9 2.2 collective-permute-done.54
  299.1 1.5 collective-permute-done.52
  (221 shorter events, 41.2 us)
Async XLA Ops:
  0.6 105.0 %copy-start = (bf16[3,64,512]{2,1,0:T(8,128)(2,1)S(1)}, bf16[3,64,512]{2,1,0:T(8,128)(2,1)}, u32[]{:S(2)}) copy-start(bf16[3,64,512]{2,1,0:T(8,128)(2,1)} %param.14) | copy-start | bytes 589828
  0.7 4.8 %copy-start.8 = (bf16[3,64,512]{2,1,0:T(8,128)(2,1)S(1)}, bf16[3,64,512]{2,1,0:T(8,128)(2,1)}, u32[]{:S(2)}) copy-start(bf16[3,64,512]{2,1,0:T(8,128)(2,1)} %param.15) | copy-start | bytes 589828
  0.7 11.5 %copy-start.12 = (s32[4,40]{1,0:T(4,128)S(1)}, s32[4,40]{1,0:T(4,128)}, u32[]{:S(2)}) copy-start(s32[4,40]{1,0:T(4,128)} %param.11) | copy-start | bytes 1924
  0.7 11.5 %copy-start.13 = (s32[4]{0:T(128)S(1)}, s32[4]{0:T(128)}, u32[]{:S(2)}) copy-start(s32[4]{0:T(128)} %param.12) | copy-start | bytes 52
  8.0 11.7 %collective-permute-start = (bf16[2368,128]{1,0:T(8,128)(2,1)S(1)}, bf16[2368,128]{1,0:T(8,128)(2,1)S(1)}, u32[]{:S(2)}, u32[]{:S(2)}) collective-permute-start(bf16[2368,128]{1,0:T(8,128)(2,1)S(1)} %get-tuple-element.47), channel_id=1, source_target_pairs={{4,0},{5,1},{6,2},{7,3},{8,4},{9,5},{10,6},{11,7},{12,8},{13,9},{1... | collective-permute-start | bytes 1818632 | tf_op jit(solution)/shard_map/ppermute | solution.py:67
  12.1 11.4 %collective-permute-start.1 = (bf16[2368,128]{1,0:T(8,128)(2,1)S(1)}, bf16[2368,128]{1,0:T(8,128)(2,1)S(1)}, u32[]{:S(2)}, u32[]{:S(2)}) collective-permute-start(bf16[2368,128]{1,0:T(8,128)(2,1)S(1)} %get-tuple-element.47), channel_id=1, source_target_pairs={{12,0},{13,1},{14,2},{15,3},{0,4},{1,5},{2,6},{3,7},{4,8},{5,9},{6... | collective-permute-start | bytes 1818632 | tf_op jit(solution)/shard_map/ppermute | solution.py:67
  19.7 8.1 %collective-permute-start.2 = (bf16[1184,128]{1,0:T(8,128)(2,1)S(1)}, bf16[1184,128]{1,0:T(8,128)(2,1)S(1)}, u32[]{:S(2)}, u32[]{:S(2)}) collective-permute-start(bf16[1184,128]{1,0:T(8,128)(2,1)S(1)} %slice.389), channel_id=1, source_target_pairs={{4,0},{5,1},{6,2},{7,3},{8,4},{9,5},{10,6},{11,7},{12,8},{13,9},{1... | collective-permute-start | bytes 909320 | tf_op jit(solution)/shard_map/ppermute | solution.py:67
  23.5 17.7 %collective-permute-start.3 = (bf16[1184,128]{1,0:T(8,128)(2,1)S(1)}, bf16[1184,128]{1,0:T(8,128)(2,1)S(1)}, u32[]{:S(2)}, u32[]{:S(2)}) collective-permute-start(bf16[1184,128]{1,0:T(8,128)(2,1)S(1)} %slice.393), channel_id=1, source_target_pairs={{12,0},{13,1},{14,2},{15,3},{0,4},{1,5},{2,6},{3,7},{4,8},{5,9},{6... | collective-permute-start | bytes 909320 | tf_op jit(solution)/shard_map/ppermute | solution.py:67
  25.0 16.2 %copy-start.7 = (bf16[3072,128]{1,0:T(8,128)(2,1)S(1)}, bf16[3072,128]{1,0:T(8,128)(2,1)}, u32[]{:S(2)}) copy-start(bf16[3072,128]{1,0:T(8,128)(2,1)} %get-tuple-element.40) | copy-start | bytes 2359300
  27.9 5.3 %collective-permute-start.4 = (bf16[320,128]{1,0:T(8,128)(2,1)S(1)}, bf16[320,128]{1,0:T(8,128)(2,1)S(1)}, u32[]{:S(2)}, u32[]{:S(2)}) collective-permute-start(bf16[320,128]{1,0:T(8,128)(2,1)S(1)} %fusion.120), channel_id=1, source_target_pairs={{1,0},{2,1},{3,2},{0,3},{5,4},{6,5},{7,6},{4,7},{9,8},{10,9},{11,1... | collective-permute-start | bytes 245768 | tf_op jit(solution)/shard_map/ppermute | solution.py:67
  31.0 6.5 %collective-permute-start.5 = (bf16[320,128]{1,0:T(8,128)(2,1)S(1)}, bf16[320,128]{1,0:T(8,128)(2,1)S(1)}, u32[]{:S(2)}, u32[]{:S(2)}) collective-permute-start(bf16[320,128]{1,0:T(8,128)(2,1)S(1)} %fusion.120), channel_id=1, source_target_pairs={{3,0},{0,1},{1,2},{2,3},{7,4},{4,5},{5,6},{6,7},{11,8},{8,9},{9,10... | collective-permute-start | bytes 245768 | tf_op jit(solution)/shard_map/ppermute | solution.py:67
  31.0 6.5 %collective-permute-start.6 = (bf16[320,128]{1,0:T(8,128)(2,1)S(1)}, bf16[320,128]{1,0:T(8,128)(2,1)S(1)}, u32[]{:S(2)}, u32[]{:S(2)}) collective-permute-start(bf16[320,128]{1,0:T(8,128)(2,1)S(1)} %fusion.120), channel_id=1, source_target_pairs={{2,0},{3,1},{0,2},{1,3},{6,4},{7,5},{4,6},{5,7},{10,8},{11,9},{8,1... | collective-permute-start | bytes 245768 | tf_op jit(solution)/shard_map/ppermute | solution.py:67
  37.6 1.4 collective-permute-start.7
  39.7 4.1 %collective-permute-start.8 = (bf16[192,128]{1,0:T(8,128)(2,1)S(1)}, bf16[192,128]{1,0:T(8,128)(2,1)S(1)}, u32[]{:S(2)}, u32[]{:S(2)}) collective-permute-start(bf16[192,128]{1,0:T(8,128)(2,1)S(1)} %maximum_maximum_fusion.1), channel_id=1, source_target_pairs={{32,0},{33,1},{34,2},{35,3},{36,4},{37,5},{38,6},{39,7},{40,8},{41... | collective-permute-start | bytes 147464 | tf_op jit(solution)/shard_map/ppermute | solution.py:67
  44.1 5.0 %collective-permute-start.9 = (bf16[64,128]{1,0:T(8,128)(2,1)S(1)}, bf16[64,128]{1,0:T(8,128)(2,1)S(1)}, u32[]{:S(2)}, u32[]{:S(2)}) collective-permute-start(bf16[64,128]{1,0:T(8,128)(2,1)S(1)} %fusion.6), channel_id=1, source_target_pairs={{96,0},{97,1},{98,2},{99,3},{100,4},{101,5},{102,6},{103,7},{104,8... | collective-permute-start | bytes 49160 | tf_op jit(solution)/shard_map/ppermute | solution.py:67
  52.7 36.0 %all-to-all-start = ((bf16[8,2240,128]{2,1,0:T(8,128)(2,1)}), bf16[8,2240,128]{2,1,0:T(8,128)(2,1)}, u32[]{:S(2)}, u32[]{:S(2)}) async-start(bf16[8,2240,128]{2,1,0:T(8,128)(2,1)} %broadcast_in_dim.74), calls=%async_computation | async-start | bytes 9175040 | tf_op jit(solution)/shard_map/all_to_all | solution.py:255
  89.7 1.3 collective-permute-start.10
  92.8 13.1 %collective-permute-start.11 = (bf16[4,2048,128]{2,1,0:T(8,128)(2,1)S(1)}, bf16[4,2048,128]{2,1,0:T(8,128)(2,1)S(1)}, u32[]{:S(2)}, u32[]{:S(2)}) collective-permute-start(bf16[4,2048,128]{2,1,0:T(8,128)(2,1)S(1)} %constant_dynamic-slice_fusion.1), channel_id=1, source_target_pairs={{16,0},{17,1},{18,2},{19,3},{20,4},{21,5},{22,6},{23,7},{24,8},{25... | collective-permute-start | bytes 6291464 | tf_op jit(solution)/shard_map/ppermute | solution.py:67
  93.6 12.0 %collective-permute-start.13 = (bf16[64,128]{1,0:T(8,128)(2,1)S(1)}, bf16[64,128]{1,0:T(8,128)(2,1)S(1)}, u32[]{:S(2)}, u32[]{:S(2)}) collective-permute-start(bf16[64,128]{1,0:T(8,128)(2,1)S(1)} %get-tuple-element.76), channel_id=1, source_target_pairs={{64,0},{65,1},{66,2},{67,3},{68,4},{69,5},{70,6},{71,7},{72,8},{73... | collective-permute-start | bytes 49160 | tf_op jit(solution)/shard_map/ppermute | solution.py:67
  93.9 11.6 %collective-permute-start.14 = (bf16[64,128]{1,0:T(8,128)(2,1)S(1)}, bf16[64,128]{1,0:T(8,128)(2,1)S(1)}, u32[]{:S(2)}, u32[]{:S(2)}) collective-permute-start(bf16[64,128]{1,0:T(8,128)(2,1)S(1)} %get-tuple-element.76), channel_id=1, source_target_pairs={{96,0},{97,1},{98,2},{99,3},{100,4},{101,5},{102,6},{103,7},{104,8... | collective-permute-start | bytes 49160 | tf_op jit(solution)/shard_map/ppermute | solution.py:67
  95.4 10.2 %collective-permute-start.12 = (bf16[64,128]{1,0:T(8,128)(2,1)S(1)}, bf16[64,128]{1,0:T(8,128)(2,1)S(1)}, u32[]{:S(2)}, u32[]{:S(2)}) collective-permute-start(bf16[64,128]{1,0:T(8,128)(2,1)S(1)} %get-tuple-element.75), channel_id=1, source_target_pairs={{32,0},{33,1},{34,2},{35,3},{36,4},{37,5},{38,6},{39,7},{40,8},{41... | collective-permute-start | bytes 49160 | tf_op jit(solution)/shard_map/ppermute | solution.py:67
  99.7 6.0 %slice-start.2 = ((bf16[192,128]{1,0:T(8,128)(2,1)}), bf16[64,128]{1,0:T(8,128)(2,1)S(1)}, s32[]{:S(2)}) async-start(bf16[192,128]{1,0:T(8,128)(2,1)} %copy-done.9), calls=%async_computation.5 | async-start | bytes 32768 | tf_op jit(solution)/shard_map/slice | solution.py:93
  113.2 5.6 %collective-permute-start.15 = (bf16[704,128]{1,0:T(8,128)(2,1)S(1)}, bf16[704,128]{1,0:T(8,128)(2,1)S(1)}, u32[]{:S(2)}, u32[]{:S(2)}) collective-permute-start(bf16[704,128]{1,0:T(8,128)(2,1)S(1)} %pad_maximum_fusion.5), channel_id=1, source_target_pairs={{4,0},{5,1},{6,2},{7,3},{8,4},{9,5},{10,6},{11,7},{12,8},{13,9},{1... | collective-permute-start | bytes 540680 | tf_op jit(solution)/shard_map/ppermute | solution.py:67
  113.3 6.8 %collective-permute-start.16 = (bf16[704,128]{1,0:T(8,128)(2,1)S(1)}, bf16[704,128]{1,0:T(8,128)(2,1)S(1)}, u32[]{:S(2)}, u32[]{:S(2)}) collective-permute-start(bf16[704,128]{1,0:T(8,128)(2,1)S(1)} %pad_maximum_fusion.5), channel_id=1, source_target_pairs={{12,0},{13,1},{14,2},{15,3},{0,4},{1,5},{2,6},{3,7},{4,8},{5,9},{6... | collective-permute-start | bytes 540680 | tf_op jit(solution)/shard_map/ppermute | solution.py:67
  115.3 7.0 %collective-permute-start.17 = (bf16[704,128]{1,0:T(8,128)(2,1)S(1)}, bf16[704,128]{1,0:T(8,128)(2,1)S(1)}, u32[]{:S(2)}, u32[]{:S(2)}) collective-permute-start(bf16[704,128]{1,0:T(8,128)(2,1)S(1)} %pad_maximum_fusion.5), channel_id=1, source_target_pairs={{8,0},{9,1},{10,2},{11,3},{12,4},{13,5},{14,6},{15,7},{0,8},{1,9},... | collective-permute-start | bytes 540680 | tf_op jit(solution)/shard_map/ppermute | solution.py:67
  122.3 4.3 %collective-permute-start.18 = (bf16[192,128]{1,0:T(8,128)(2,1)S(1)}, bf16[192,128]{1,0:T(8,128)(2,1)S(1)}, u32[]{:S(2)}, u32[]{:S(2)}) collective-permute-start(bf16[192,128]{1,0:T(8,128)(2,1)S(1)} %fusion.115), channel_id=1, source_target_pairs={{1,0},{2,1},{3,2},{0,3},{5,4},{6,5},{7,6},{4,7},{9,8},{10,9},{11,1... | collective-permute-start | bytes 147464 | tf_op jit(solution)/shard_map/ppermute | solution.py:67
  122.9 5.3 %collective-permute-start.19 = (bf16[192,128]{1,0:T(8,128)(2,1)S(1)}, bf16[192,128]{1,0:T(8,128)(2,1)S(1)}, u32[]{:S(2)}, u32[]{:S(2)}) collective-permute-start(bf16[192,128]{1,0:T(8,128)(2,1)S(1)} %fusion.115), channel_id=1, source_target_pairs={{3,0},{0,1},{1,2},{2,3},{7,4},{4,5},{5,6},{6,7},{11,8},{8,9},{9,10... | collective-permute-start | bytes 147464 | tf_op jit(solution)/shard_map/ppermute | solution.py:67
  124.6 5.6 %collective-permute-start.20 = (bf16[192,128]{1,0:T(8,128)(2,1)S(1)}, bf16[192,128]{1,0:T(8,128)(2,1)S(1)}, u32[]{:S(2)}, u32[]{:S(2)}) collective-permute-start(bf16[192,128]{1,0:T(8,128)(2,1)S(1)} %fusion.115), channel_id=1, source_target_pairs={{2,0},{3,1},{0,2},{1,3},{6,4},{7,5},{4,6},{5,7},{10,8},{11,9},{8,1... | collective-permute-start | bytes 147464 | tf_op jit(solution)/shard_map/ppermute | solution.py:67
  130.2 1.5 collective-permute-start.21
  131.8 7.9 %collective-permute-start.23 = (bf16[64,128]{1,0:T(8,128)(2,1)S(1)}, bf16[64,128]{1,0:T(8,128)(2,1)S(1)}, u32[]{:S(2)}, u32[]{:S(2)}) collective-permute-start(bf16[64,128]{1,0:T(8,128)(2,1)S(1)} %get-tuple-element.74), channel_id=1, source_target_pairs={{64,0},{65,1},{66,2},{67,3},{68,4},{69,5},{70,6},{71,7},{72,8},{73... | collective-permute-start | bytes 49160 | tf_op jit(solution)/shard_map/ppermute | solution.py:67
  135.9 4.9 %collective-permute-start.24 = (bf16[64,128]{1,0:T(8,128)(2,1)S(1)}, bf16[64,128]{1,0:T(8,128)(2,1)S(1)}, u32[]{:S(2)}, u32[]{:S(2)}) collective-permute-start(bf16[64,128]{1,0:T(8,128)(2,1)S(1)} %get-tuple-element.74), channel_id=1, source_target_pairs={{96,0},{97,1},{98,2},{99,3},{100,4},{101,5},{102,6},{103,7},{104,8... | collective-permute-start | bytes 49160 | tf_op jit(solution)/shard_map/ppermute | solution.py:67
  138.8 3.8 %collective-permute-start.22 = (bf16[64,128]{1,0:T(8,128)(2,1)S(1)}, bf16[64,128]{1,0:T(8,128)(2,1)S(1)}, u32[]{:S(2)}, u32[]{:S(2)}) collective-permute-start(bf16[64,128]{1,0:T(8,128)(2,1)S(1)} %get-tuple-element.73), channel_id=1, source_target_pairs={{32,0},{33,1},{34,2},{35,3},{36,4},{37,5},{38,6},{39,7},{40,8},{41... | collective-permute-start | bytes 49160 | tf_op jit(solution)/shard_map/ppermute | solution.py:67
  143.6 39.9 %slice-start = ((s8[5242880]{0:T(1024)(128)(4,1)}), s8[4194304]{0:T(1024)(128)(4,1)S(1)}, s32[]{:S(2)}) async-start(s8[5242880]{0:T(1024)(128)(4,1)} %bitcast.114), calls=%async_computation.3 | async-start | bytes 8388608
  144.2 39.3 %slice-start.1 = ((s8[5242880]{0:T(1024)(128)(4,1)}), s8[1048576]{0:T(1024)(128)(4,1)S(1)}, s32[]{:S(2)}) async-start(s8[5242880]{0:T(1024)(128)(4,1)} %bitcast.114), calls=%async_computation.4 | async-start | bytes 2097152
  178.1 1.3 collective-permute-start.25
  179.6 8.3 %collective-permute-start.26 = (bf16[4,2048,128]{2,1,0:T(8,128)(2,1)S(1)}, bf16[4,2048,128]{2,1,0:T(8,128)(2,1)S(1)}, u32[]{:S(2)}, u32[]{:S(2)}) collective-permute-start(bf16[4,2048,128]{2,1,0:T(8,128)(2,1)S(1)} %constant_dynamic-slice_fusion), channel_id=1, source_target_pairs={{16,0},{17,1},{18,2},{19,3},{20,4},{21,5},{22,6},{23,7},{24,8},{25... | collective-permute-start | bytes 6291464 | tf_op jit(solution)/shard_map/ppermute | solution.py:67
  179.8 7.7 %collective-permute-start.28 = (bf16[64,128]{1,0:T(8,128)(2,1)S(1)}, bf16[64,128]{1,0:T(8,128)(2,1)S(1)}, u32[]{:S(2)}, u32[]{:S(2)}) collective-permute-start(bf16[64,128]{1,0:T(8,128)(2,1)S(1)} %get-tuple-element.72), channel_id=1, source_target_pairs={{64,0},{65,1},{66,2},{67,3},{68,4},{69,5},{70,6},{71,7},{72,8},{73... | collective-permute-start | bytes 49160 | tf_op jit(solution)/shard_map/ppermute | solution.py:67
  181.6 6.0 %collective-permute-start.29 = (bf16[64,128]{1,0:T(8,128)(2,1)S(1)}, bf16[64,128]{1,0:T(8,128)(2,1)S(1)}, u32[]{:S(2)}, u32[]{:S(2)}) collective-permute-start(bf16[64,128]{1,0:T(8,128)(2,1)S(1)} %get-tuple-element.72), channel_id=1, source_target_pairs={{96,0},{97,1},{98,2},{99,3},{100,4},{101,5},{102,6},{103,7},{104,8... | collective-permute-start | bytes 49160 | tf_op jit(solution)/shard_map/ppermute | solution.py:67
  183.3 4.3 %collective-permute-start.27 = (bf16[64,128]{1,0:T(8,128)(2,1)S(1)}, bf16[64,128]{1,0:T(8,128)(2,1)S(1)}, u32[]{:S(2)}, u32[]{:S(2)}) collective-permute-start(bf16[64,128]{1,0:T(8,128)(2,1)S(1)} %get-tuple-element.71), channel_id=1, source_target_pairs={{32,0},{33,1},{34,2},{35,3},{36,4},{37,5},{38,6},{39,7},{40,8},{41... | collective-permute-start | bytes 49160 | tf_op jit(solution)/shard_map/ppermute | solution.py:67
  192.7 5.6 %collective-permute-start.30 = (bf16[704,128]{1,0:T(8,128)(2,1)S(1)}, bf16[704,128]{1,0:T(8,128)(2,1)S(1)}, u32[]{:S(2)}, u32[]{:S(2)}) collective-permute-start(bf16[704,128]{1,0:T(8,128)(2,1)S(1)} %pad_maximum_fusion.6), channel_id=1, source_target_pairs={{4,0},{5,1},{6,2},{7,3},{8,4},{9,5},{10,6},{11,7},{12,8},{13,9},{1... | collective-permute-start | bytes 540680 | tf_op jit(solution)/shard_map/ppermute | solution.py:67
  192.8 6.8 %collective-permute-start.31 = (bf16[704,128]{1,0:T(8,128)(2,1)S(1)}, bf16[704,128]{1,0:T(8,128)(2,1)S(1)}, u32[]{:S(2)}, u32[]{:S(2)}) collective-permute-start(bf16[704,128]{1,0:T(8,128)(2,1)S(1)} %pad_maximum_fusion.6), channel_id=1, source_target_pairs={{12,0},{13,1},{14,2},{15,3},{0,4},{1,5},{2,6},{3,7},{4,8},{5,9},{6... | collective-permute-start | bytes 540680 | tf_op jit(solution)/shard_map/ppermute | solution.py:67
  194.8 7.0 %collective-permute-start.32 = (bf16[704,128]{1,0:T(8,128)(2,1)S(1)}, bf16[704,128]{1,0:T(8,128)(2,1)S(1)}, u32[]{:S(2)}, u32[]{:S(2)}) collective-permute-start(bf16[704,128]{1,0:T(8,128)(2,1)S(1)} %pad_maximum_fusion.6), channel_id=1, source_target_pairs={{8,0},{9,1},{10,2},{11,3},{12,4},{13,5},{14,6},{15,7},{0,8},{1,9},... | collective-permute-start | bytes 540680 | tf_op jit(solution)/shard_map/ppermute | solution.py:67
  201.8 4.2 %collective-permute-start.33 = (bf16[192,128]{1,0:T(8,128)(2,1)S(1)}, bf16[192,128]{1,0:T(8,128)(2,1)S(1)}, u32[]{:S(2)}, u32[]{:S(2)}) collective-permute-start(bf16[192,128]{1,0:T(8,128)(2,1)S(1)} %fusion.116), channel_id=1, source_target_pairs={{1,0},{2,1},{3,2},{0,3},{5,4},{6,5},{7,6},{4,7},{9,8},{10,9},{11,1... | collective-permute-start | bytes 147464 | tf_op jit(solution)/shard_map/ppermute | solution.py:67
  202.2 5.3 %collective-permute-start.34 = (bf16[192,128]{1,0:T(8,128)(2,1)S(1)}, bf16[192,128]{1,0:T(8,128)(2,1)S(1)}, u32[]{:S(2)}, u32[]{:S(2)}) collective-permute-start(bf16[192,128]{1,0:T(8,128)(2,1)S(1)} %fusion.116), channel_id=1, source_target_pairs={{3,0},{0,1},{1,2},{2,3},{7,4},{4,5},{5,6},{6,7},{11,8},{8,9},{9,10... | collective-permute-start | bytes 147464 | tf_op jit(solution)/shard_map/ppermute | solution.py:67
  203.9 5.6 %collective-permute-start.35 = (bf16[192,128]{1,0:T(8,128)(2,1)S(1)}, bf16[192,128]{1,0:T(8,128)(2,1)S(1)}, u32[]{:S(2)}, u32[]{:S(2)}) collective-permute-start(bf16[192,128]{1,0:T(8,128)(2,1)S(1)} %fusion.116), channel_id=1, source_target_pairs={{2,0},{3,1},{0,2},{1,3},{6,4},{7,5},{4,6},{5,7},{10,8},{11,9},{8,1... | collective-permute-start | bytes 147464 | tf_op jit(solution)/shard_map/ppermute | solution.py:67
  209.6 1.3 collective-permute-start.36
  210.9 8.6 %collective-permute-start.38 = (bf16[64,128]{1,0:T(8,128)(2,1)S(1)}, bf16[64,128]{1,0:T(8,128)(2,1)S(1)}, u32[]{:S(2)}, u32[]{:S(2)}) collective-permute-start(bf16[64,128]{1,0:T(8,128)(2,1)S(1)} %get-tuple-element.70), channel_id=1, source_target_pairs={{64,0},{65,1},{66,2},{67,3},{68,4},{69,5},{70,6},{71,7},{72,8},{73... | collective-permute-start | bytes 49160 | tf_op jit(solution)/shard_map/ppermute | solution.py:67
  215.2 5.1 %collective-permute-start.39 = (bf16[64,128]{1,0:T(8,128)(2,1)S(1)}, bf16[64,128]{1,0:T(8,128)(2,1)S(1)}, u32[]{:S(2)}, u32[]{:S(2)}) collective-permute-start(bf16[64,128]{1,0:T(8,128)(2,1)S(1)} %get-tuple-element.70), channel_id=1, source_target_pairs={{96,0},{97,1},{98,2},{99,3},{100,4},{101,5},{102,6},{103,7},{104,8... | collective-permute-start | bytes 49160 | tf_op jit(solution)/shard_map/ppermute | solution.py:67
  218.6 3.8 %collective-permute-start.37 = (bf16[64,128]{1,0:T(8,128)(2,1)S(1)}, bf16[64,128]{1,0:T(8,128)(2,1)S(1)}, u32[]{:S(2)}, u32[]{:S(2)}) collective-permute-start(bf16[64,128]{1,0:T(8,128)(2,1)S(1)} %get-tuple-element.69), channel_id=1, source_target_pairs={{32,0},{33,1},{34,2},{35,3},{36,4},{37,5},{38,6},{39,7},{40,8},{41... | collective-permute-start | bytes 49160 | tf_op jit(solution)/shard_map/ppermute | solution.py:67
  257.7 1.3 collective-permute-start.40
  259.2 8.6 %collective-permute-start.41 = (bf16[4,2048,128]{2,1,0:T(8,128)(2,1)S(1)}, bf16[4,2048,128]{2,1,0:T(8,128)(2,1)S(1)}, u32[]{:S(2)}, u32[]{:S(2)}) collective-permute-start(bf16[4,2048,128]{2,1,0:T(8,128)(2,1)S(1)} %constant_dynamic-slice_fusion.2), channel_id=1, source_target_pairs={{16,0},{17,1},{18,2},{19,3},{20,4},{21,5},{22,6},{23,7},{24,8},{25... | collective-permute-start | bytes 6291464 | tf_op jit(solution)/shard_map/ppermute | solution.py:67
  259.5 7.9 %collective-permute-start.43 = (bf16[64,128]{1,0:T(8,128)(2,1)S(1)}, bf16[64,128]{1,0:T(8,128)(2,1)S(1)}, u32[]{:S(2)}, u32[]{:S(2)}) collective-permute-start(bf16[64,128]{1,0:T(8,128)(2,1)S(1)} %get-tuple-element.68), channel_id=1, source_target_pairs={{64,0},{65,1},{66,2},{67,3},{68,4},{69,5},{70,6},{71,7},{72,8},{73... | collective-permute-start | bytes 49160 | tf_op jit(solution)/shard_map/ppermute | solution.py:67
  261.3 6.1 %collective-permute-start.44 = (bf16[64,128]{1,0:T(8,128)(2,1)S(1)}, bf16[64,128]{1,0:T(8,128)(2,1)S(1)}, u32[]{:S(2)}, u32[]{:S(2)}) collective-permute-start(bf16[64,128]{1,0:T(8,128)(2,1)S(1)} %get-tuple-element.68), channel_id=1, source_target_pairs={{96,0},{97,1},{98,2},{99,3},{100,4},{101,5},{102,6},{103,7},{104,8... | collective-permute-start | bytes 49160 | tf_op jit(solution)/shard_map/ppermute | solution.py:67
  263.0 4.5 %collective-permute-start.42 = (bf16[64,128]{1,0:T(8,128)(2,1)S(1)}, bf16[64,128]{1,0:T(8,128)(2,1)S(1)}, u32[]{:S(2)}, u32[]{:S(2)}) collective-permute-start(bf16[64,128]{1,0:T(8,128)(2,1)S(1)} %get-tuple-element.67), channel_id=1, source_target_pairs={{32,0},{33,1},{34,2},{35,3},{36,4},{37,5},{38,6},{39,7},{40,8},{41... | collective-permute-start | bytes 49160 | tf_op jit(solution)/shard_map/ppermute | solution.py:67
  273.2 4.2 %collective-permute-start.45 = (bf16[192,128]{1,0:T(8,128)(2,1)S(1)}, bf16[192,128]{1,0:T(8,128)(2,1)S(1)}, u32[]{:S(2)}, u32[]{:S(2)}) collective-permute-start(bf16[192,128]{1,0:T(8,128)(2,1)S(1)} %get-tuple-element.93), channel_id=1, source_target_pairs={{4,0},{5,1},{6,2},{7,3},{8,4},{9,5},{10,6},{11,7},{12,8},{13,9},{1... | collective-permute-start | bytes 147464 | tf_op jit(solution)/shard_map/ppermute | solution.py:67
  273.3 5.4 %collective-permute-start.46 = (bf16[192,128]{1,0:T(8,128)(2,1)S(1)}, bf16[192,128]{1,0:T(8,128)(2,1)S(1)}, u32[]{:S(2)}, u32[]{:S(2)}) collective-permute-start(bf16[192,128]{1,0:T(8,128)(2,1)S(1)} %get-tuple-element.93), channel_id=1, source_target_pairs={{12,0},{13,1},{14,2},{15,3},{0,4},{1,5},{2,6},{3,7},{4,8},{5,9},{6... | collective-permute-start | bytes 147464 | tf_op jit(solution)/shard_map/ppermute | solution.py:67
  275.3 5.6 %collective-permute-start.47 = (bf16[192,128]{1,0:T(8,128)(2,1)S(1)}, bf16[192,128]{1,0:T(8,128)(2,1)S(1)}, u32[]{:S(2)}, u32[]{:S(2)}) collective-permute-start(bf16[192,128]{1,0:T(8,128)(2,1)S(1)} %get-tuple-element.93), channel_id=1, source_target_pairs={{8,0},{9,1},{10,2},{11,3},{12,4},{13,5},{14,6},{15,7},{0,8},{1,9},... | collective-permute-start | bytes 147464 | tf_op jit(solution)/shard_map/ppermute | solution.py:67
  280.9 4.2 %collective-permute-start.48 = (bf16[192,128]{1,0:T(8,128)(2,1)S(1)}, bf16[192,128]{1,0:T(8,128)(2,1)S(1)}, u32[]{:S(2)}, u32[]{:S(2)}) collective-permute-start(bf16[192,128]{1,0:T(8,128)(2,1)S(1)} %fusion.91), channel_id=1, source_target_pairs={{1,0},{2,1},{3,2},{0,3},{5,4},{6,5},{7,6},{4,7},{9,8},{10,9},{11,1... | collective-permute-start | bytes 147464 | tf_op jit(solution)/shard_map/ppermute | solution.py:67
  281.0 5.4 %collective-permute-start.49 = (bf16[192,128]{1,0:T(8,128)(2,1)S(1)}, bf16[192,128]{1,0:T(8,128)(2,1)S(1)}, u32[]{:S(2)}, u32[]{:S(2)}) collective-permute-start(bf16[192,128]{1,0:T(8,128)(2,1)S(1)} %fusion.91), channel_id=1, source_target_pairs={{3,0},{0,1},{1,2},{2,3},{7,4},{4,5},{5,6},{6,7},{11,8},{8,9},{9,10... | collective-permute-start | bytes 147464 | tf_op jit(solution)/shard_map/ppermute | solution.py:67
  283.0 5.6 %collective-permute-start.50 = (bf16[192,128]{1,0:T(8,128)(2,1)S(1)}, bf16[192,128]{1,0:T(8,128)(2,1)S(1)}, u32[]{:S(2)}, u32[]{:S(2)}) collective-permute-start(bf16[192,128]{1,0:T(8,128)(2,1)S(1)} %fusion.91), channel_id=1, source_target_pairs={{2,0},{3,1},{0,2},{1,3},{6,4},{7,5},{4,6},{5,7},{10,8},{11,9},{8,1... | collective-permute-start | bytes 147464 | tf_op jit(solution)/shard_map/ppermute | solution.py:67
  288.7 1.3 collective-permute-start.51
  290.0 6.9 %collective-permute-start.53 = (bf16[64,128]{1,0:T(8,128)(2,1)S(1)}, bf16[64,128]{1,0:T(8,128)(2,1)S(1)}, u32[]{:S(2)}, u32[]{:S(2)}) collective-permute-start(bf16[64,128]{1,0:T(8,128)(2,1)S(1)} %get-tuple-element.66), channel_id=1, source_target_pairs={{64,0},{65,1},{66,2},{67,3},{68,4},{69,5},{70,6},{71,7},{72,8},{73... | collective-permute-start | bytes 49160 | tf_op jit(solution)/shard_map/ppermute | solution.py:67
  294.2 4.9 %collective-permute-start.54 = (bf16[64,128]{1,0:T(8,128)(2,1)S(1)}, bf16[64,128]{1,0:T(8,128)(2,1)S(1)}, u32[]{:S(2)}, u32[]{:S(2)}) collective-permute-start(bf16[64,128]{1,0:T(8,128)(2,1)S(1)} %get-tuple-element.66), channel_id=1, source_target_pairs={{96,0},{97,1},{98,2},{99,3},{100,4},{101,5},{102,6},{103,7},{104,8... | collective-permute-start | bytes 49160 | tf_op jit(solution)/shard_map/ppermute | solution.py:67
  296.8 3.8 %collective-permute-start.52 = (bf16[64,128]{1,0:T(8,128)(2,1)S(1)}, bf16[64,128]{1,0:T(8,128)(2,1)S(1)}, u32[]{:S(2)}, u32[]{:S(2)}) collective-permute-start(bf16[64,128]{1,0:T(8,128)(2,1)S(1)} %get-tuple-element.65), channel_id=1, source_target_pairs={{32,0},{33,1},{34,2},{35,3},{36,4},{37,5},{38,6},{39,7},{40,8},{41... | collective-permute-start | bytes 49160 | tf_op jit(solution)/shard_map/ppermute | solution.py:67
  (11 other events, 42.2 us)

commit v3 on v2

--- a/solution.py
+++ b/solution.py
@@ -1,3 +1,5 @@
+import functools
+
 import jax
 import jax.numpy as jnp
 from jax import lax
@@ -84,10 +86,14 @@
 
 def siblings(term):
     other = move(term.astype(BF), CORE)
-    return siblings_of(other, term)
-
-
-def siblings_of(other, term):
+    chip = term[R:] + other[R:].astype(F32)
+    near = move(chip.astype(BF), CHIP[0])
+    half = chip[R:] + near[R:].astype(F32)
+    far = move(half.astype(BF), CHIP[2])
+    return jnp.concatenate([other[:R], near[:R], far], axis=0)
+
+
+def siblings_beside(other, term):
     chip = (term[R:] + other[R:].astype(F32)).astype(BF)
     near, far_a, far_b = move(chip[:R], CHIP[0]), move(chip[R:], CHIP[1]), move(chip[R:], CHIP[2])
     return jnp.concatenate([other[:R], near, (far_a.astype(F32) + far_b.astype(F32)).astype(BF)], axis=0)
@@ -109,14 +115,14 @@
     )
 
 
-def slot_tables(neighbours, counts):
+def slot_tables(neighbours, counts, half):
     drop, blk = lax.axis_index("drop"), lax.axis_index("blk")
     core, mine = drop % 2, (blk % 4, blk // 4)
     kind = neighbours // 64
     group = drop - 1 + kind
     block = neighbours % 64
     owner, part = block // 4, block % 4
-    place = lax.rem(kind - core + 3, 3)
+    place = lax.rem(4 * kind + half + 8, 12) // 4
     even = (drop // 2 + core) % 2 == 1
     y_first = even == (place < 2)
     y, z = owner % 4, owner // 4
@@ -134,42 +140,51 @@
     rank = jnp.sum((rank_key[:, None, :] < rank_key[:, :, None]).astype(jnp.int32), axis=2)
     put = rank[:, :, None] == lax.broadcasted_iota(jnp.int32, (1, 1, SLOTS), 2)
     order = jnp.sum(jnp.where(put, slot[:, :, None], 0), axis=1)
-    start = jnp.sum(jnp.where(put, row[:, :, None], 0), axis=1)
+    start = jnp.sum(jnp.where(put, jnp.where(live, row, 0)[:, :, None], 0), axis=1)
     n_pair = jnp.sum((key == 0).astype(jnp.int32), axis=1)
     n_live = jnp.sum((key < 2).astype(jnp.int32), axis=1)
     return order.reshape(-1), start.reshape(-1), n_pair, n_live
 
 
-def near_kernel(order, start, lo, hi, blocks, field, before, out):
-    for q in range(NBD):
-        first, last = lo[q], hi[q]
-
-        def two(i, acc, q=q, first=first, last=last):
-            j = first + 2 * i
-            k = jnp.minimum(j + 1, last - 1)
-            left = blocks[q, order[q * SLOTS + j]]
-            right = blocks[q, order[q * SLOTS + k]]
-            right = jnp.where(j + 1 < last, right, jnp.zeros_like(right))
-            upper = field[pl.ds(pl.multiple_of(start[q * SLOTS + j], 64), BS), :]
-            lower = field[pl.ds(pl.multiple_of(start[q * SLOTS + k], 64), BS), :]
-            return acc + jnp.dot(
-                jnp.concatenate([left, right], axis=1),
-                jnp.concatenate([upper, lower], axis=0),
-                preferred_element_type=F32,
+def near_kernel(width, order, start, lo, hi, blocks, field, before, out):
+    rows = range(NBD)
+    longest = hi[0] - lo[0]
+    for q in rows[1:]:
+        longest = jnp.maximum(longest, hi[q] - lo[q])
+
+    def some(i, sums):
+        new = []
+        for q in rows:
+            left, right = [], []
+            for u in range(width):
+                j = lo[q] + width * i + u
+                at = q * SLOTS + jnp.minimum(j, SLOTS - 1)
+                block = blocks[q, order[at]]
+                left.append(jnp.where(j < hi[q], block, jnp.zeros_like(block)))
+                row = jnp.minimum(start[at], field.shape[0] - BS)
+                right.append(field[pl.ds(pl.multiple_of(row, 64), BS), :])
+            new.append(
+                sums[q]
+                + jnp.dot(
+                    jnp.concatenate(left, axis=1), jnp.concatenate(right, axis=0), preferred_element_type=F32
+                )
             )
-
-        rows = pl.ds(q * BS, BS)
-        out[rows, :] = lax.fori_loop(0, (last - first + 1) // 2, two, before[rows, :])
-
-
-def near(order, start, lo, hi, near_blocks, field, before):
+        return tuple(new)
+
+    sums = tuple(before[q * BS : (q + 1) * BS, :] for q in rows)
+    sums = lax.fori_loop(0, (longest + width - 1) // width, some, sums)
+    for q in rows:
+        out[q * BS : (q + 1) * BS, :] = sums[q]
+
+
+def near(width, order, start, lo, hi, near_blocks, field, before):
     small, whole = pl.BlockSpec(memory_space=pltpu.SMEM), pl.BlockSpec(memory_space=pltpu.VMEM)
     return pl.pallas_call(
-        near_kernel,
+        functools.partial(near_kernel, width),
         in_specs=[small] * 4 + [whole] * 3,
         out_specs=whole,
         out_shape=jax.ShapeDtypeStruct((ROWS, BS), F32),
-        compiler_params=pltpu.CompilerParams(vmem_limit_bytes=32 * 2**20),
+        compiler_params=pltpu.CompilerParams(vmem_limit_bytes=12 * 2**20),
         cost_estimate=pl.CostEstimate(flops=2 * 80 * BS**3, bytes_accessed=10 * 2**20, transcendentals=0),
     )(order, start, lo, hi, near_blocks, field, before)
 
@@ -206,73 +221,65 @@
     return jnp.concatenate([b0.astype(BF), s1.astype(BF), s2], axis=0), (k10, k20, k21)
 
 
-def fold(right, mixes):
+def fold(terms, mixes):
     k10, k20, k21 = mixes
-    r0, r1, r2 = right[:R], right[R : 2 * R], right[2 * R :]
-    f1 = r1.astype(F32) - dot(k10, r0)
-    f2 = r2.astype(F32) - dot(k20, r0) - dot(k21, f1)
-    return jnp.concatenate([r0, f1.astype(BF), f2.astype(BF)], axis=0)
-
-
-def by_block(factors):
-    return jnp.concatenate([factors[:, i * BS : (i + 1) * BS] for i in range(NBD)], axis=0)
+    t0, t1, t2 = terms[:R], terms[R : 2 * R], terms[2 * R :]
+    t1 = t1 - dot(k10, t0)
+    t2 = t2 - dot(k20, t0) - dot(k21, t1)
+    return jnp.concatenate([t0, t1, t2], axis=0)
 
 
 def on_device(
     right_side, near_blocks, neighbours, counts, leaf_inverse, couple_left, couple_right, prec_left, prec_right
 ):
-    upper = lax.axis_index("drop") % 2 == 0
-    order, start, n_pair, n_live = slot_tables(neighbours, counts)
+    half = 4 - 4 * (lax.axis_index("drop") % 2)
+    order, start, n_pair, n_live = slot_tables(neighbours, counts, half)
     none = jnp.zeros_like(n_pair)
     c_left, c_right, left, right = (
         f.reshape(TERMS, ROWS) for f in (couple_left, couple_right, prec_left, prec_right)
     )
 
+    facts = jnp.concatenate([left, c_right], axis=0)
+    facts = [facts] + long_ring(facts)
     z = leaf(right_side, leaf_inverse)
     terms = first_terms(z, right, left)
-    count = terms.shape[0]
-    sent = jnp.concatenate([z.astype(BF), terms.astype(BF), by_block(left), by_block(c_right)], axis=0)
-    rest = long_ring(sent)
-    terms = terms + sum(a[ROWS : ROWS + count].astype(F32) for a in rest)
+    rest = ring(jnp.concatenate([z, terms], axis=0).astype(BF))
+    terms = terms + sum(a[ROWS:].astype(F32) for a in rest)
     sums, mixes = first_siblings(add_over(terms, SECOND))
     sums, order, start, n_pair, n_live = lax.optimization_barrier((sums, order, start, n_pair, n_live))
-    at = ROWS + count
-    ring_left = jnp.concatenate([a[at : at + NBD * TERMS] for a in [sent] + rest], axis=0).reshape(-1, TERMS, BS)
-    at += NBD * TERMS
-    ring_c = jnp.concatenate([a[at : at + NBD * TERMS] for a in [sent] + rest], axis=0).reshape(-1, TERMS, BS)
-    ring_c = ring_c.transpose(1, 0, 2).reshape(TERMS, RING)
+    ring_left, ring_c = [a[:TERMS] for a in facts], [a[TERMS:] for a in facts]
 
     def corrected(field, sums):
-        fix = jnp.einsum("bkr,kn->brn", ring_left, sums, preferred_element_type=F32)
-        return field - fix.reshape(RING, BS)
+        return field - jnp.concatenate([dot_t(a, sums) for a in ring_left], axis=0)
 
     field = corrected(jnp.concatenate([z] + [a[:ROWS].astype(F32) for a in rest], axis=0), sums)
-    folded = fold(right, mixes)
 
     for step in range(ITERS):
         field_b = field.astype(BF)
-        piece = jnp.concatenate([field_b, dot(ring_c, field_b).astype(BF)], axis=0)
+        c_terms = sum(dot(a, field_b[i * ROWS : (i + 1) * ROWS]) for i, a in enumerate(ring_c))
+        piece = jnp.concatenate([field_b, c_terms.astype(BF)], axis=0)
         pieces = lax.all_to_all(
             jnp.broadcast_to(piece[None], (8, PIECE, BS)), AXES, 0, 0, tiled=True, axis_index_groups=EIGHTS
         )
-        c_parts = lax.dynamic_slice(pieces, (jnp.where(upper, 4, 0), RING, 0), (4, TERMS, BS))
+        c_parts = lax.dynamic_slice(pieces, (half, RING, 0), (4, TERMS, BS), allow_negative_indices=False)
         c_terms = jnp.sum(c_parts.astype(F32), axis=0)
         c_other = move(c_terms.astype(BF), CORE)
         pieces, c_other = lax.optimization_barrier((pieces, c_other))
-        own = lax.dynamic_slice(pieces, (jnp.where(upper, 4, 0), 0, 0), (4, RING, BS))
+        own = lax.dynamic_slice(pieces, (half, 0, 0), (4, RING, BS), allow_negative_indices=False)
         other = move(own, CORE)
-        c_sums = siblings_of(c_other, c_terms)
+        c_sums = siblings_beside(c_other, c_terms)
         x = field[:ROWS]
-        image = near(order, start, none, n_pair, near_blocks, pieces.reshape(8 * PIECE, BS), x)
-        image = near(order, start, n_pair, n_live, near_blocks, other.reshape(4 * RING, BS), image)
+        image = near(8, order, start, none, n_pair, near_blocks, pieces.reshape(8 * PIECE, BS), x)
+        image = near(4, order, start, n_pair, n_live, near_blocks, other.reshape(4 * RING, BS), image)
+        image, c_sums = lax.optimization_barrier((image, c_sums))
         resid = right_side - (image + dot_t(c_left, c_sums))
         z = leaf(resid, leaf_inverse)
-        terms = dot(folded, z)
+        terms = fold(dot(right, z), mixes)
         if step < ITERS - 1:
-            rest = ring(jnp.concatenate([z.astype(BF), terms.astype(BF)], axis=0))
-            terms = terms + sum(a[ROWS:].astype(F32) for a in rest)
+            terms = add_over(terms, FIRST)
+            rest = ring(z.astype(BF))
             sums = siblings(add_over(terms, SECOND))
-            z_ring = jnp.concatenate([z] + [a[:ROWS].astype(F32) for a in rest], axis=0)
+            z_ring = jnp.concatenate([z] + [a.astype(F32) for a in rest], axis=0)
             field = corrected(field + z_ring, sums)
         else:
             sums = siblings(add_over(add_over(terms, FIRST), SECOND))

time: 302 us -> 276 us (0.914)
  blocking collectives: 67.5 us -> 103 us
  waiting for transfers between devices: 96.1 us -> 71.7 us
  Pallas kernels: 27 us -> 10.8 us
  local copies, waits for them, and re-layouts: 16.4 us -> 2.64 us
  starting transfers between devices: 77.8 us -> 68.5 us
    all_to_all x2 -> x3, blocking collectives: 67.5 us -> 103 us  [on_device(): lax.all_to_all(jnp.broadcast_to(piece[None], (8, PIECE, BS)), AXES, 0, 0,...]
    all_to_all x1 -> x0, waiting for transfers between devices: 29.1 us -> none  [on_device(): lax.all_to_all(jnp.broadcast_to(piece[None], (8, PIECE, BS)), AXES, 0, 0,...]
    pallas_call x6, Pallas kernels: 27 us -> 10.8 us  [near(): pl.pallas_call(functools.partial(near_kernel, width), in_specs=[small] *...]
    unnamed x42 -> x26, local copies, waits for them, and re-layouts: 9.04 us -> 0.07 us
    all_to_all x1 -> x0, starting transfers between devices: 6.88 us -> none  [on_device(): lax.all_to_all(jnp.broadcast_to(piece[None], (8, PIECE, BS)), AXES, 0, 0,...]
    ppermute x55 -> x61, waiting for transfers between devices: 67 us -> 71.7 us  [move(): return lax.ppermute(array, AXES, pairs)]
    dot_general x4 -> x16, matrix products: 1.79 us -> 5 us  [dot_t(): lax.dot_general(a.astype(BF), b.astype(BF), (((0,), (0,)), ((), ())), pre...]
    ppermute x55 -> x61, starting transfers between devices: 70.9 us -> 68.5 us  [move(): return lax.ppermute(array, AXES, pairs)]
  transfers between devices with their start and end apart: 56 -> 61, of which waited for: 37 -> 41; matrix products, arithmetic and copies ran while one was open for 2% -> 1% of each run, Pallas kernels for 5% -> 2%
where the time goes in v3:
time: 276 us
  blocking collectives  103 us (37%)
  waiting for transfers between devices  71.7 us (26%)
  starting transfers between devices  68.5 us (25%)
  matrix products  13.3 us (5%)
  Pallas kernels  10.8 us (4%)
  other arithmetic  4.37 us (2%)
    all_to_all x3, blocking collectives, on_device(): lax.all_to_all(jnp.broadcast_to(piece[None], (8, PIECE, BS)), AXES, 0, 0,...  103 us
    ppermute x61, waiting for transfers between devices, move(): return lax.ppermute(array, AXES, pairs)  71.7 us
    ppermute x61, starting transfers between devices, move(): return lax.ppermute(array, AXES, pairs)  68.5 us
    pallas_call x6, Pallas kernels, near(): pl.pallas_call(functools.partial(near_kernel, width), in_specs=[small] *...  10.8 us
  transfers between devices with their start and end apart: 61, of which 41 were waited for; matrix products, arithmetic and copies ran while one was open for 1% of the time, Pallas kernels for 2%

profile of v3, /device:TPU:0, one launch (start us, length us, event | category | flops | bytes accessed | tf_op | source)
XLA Modules:
  0.0 276.3 jit_solution(4561753475010989433)
XLA Ops:
  0.7 1.4 fusion.162
  4.6 4.2 %collective-permute-start = (bf16[832,128]{1,0:T(8,128)(2,1)S(1)}, bf16[832,128]{1,0:T(8,128)(2,1)S(1)}, u32[]{:S(2)}, u32[]{:S(2)}) collective-permute-start(bf16[832,128]{1,0:T(8,128)(2,1)S(1)} %pad_maximum_fusion.4), channel_id=1, source_target_pairs={{4,0},{5,1},{6,2},{7,3},{8,4},{9,5},{10,6},{11,7},{12,8},{13,9},{1... | collective-permute-start | bytes 638984 | tf_op jit(solution)/shard_map/ppermute | solution.py:69
  8.8 1.9 collective-permute-start.2
  10.6 1.5 collective-permute-start.9
  13.5 4.6 %collective-permute-done.1 = bf16[832,128]{1,0:T(8,128)(2,1)S(1)} collective-permute-done((bf16[832,128]{1,0:T(8,128)(2,1)S(1)}, bf16[832,128]{1,0:T(8,128)(2,1)S(1)}, u32[]{:S(2)}, u32[]{:S(2)}) %collective-permute-start.1) | collective-permute-done | bytes 213024 | tf_op jit(solution)/shard_map/ppermute | solution.py:69
  18.2 3.1 %collective-permute-start.3 = (bf16[320,128]{1,0:T(8,128)(2,1)S(1)}, bf16[320,128]{1,0:T(8,128)(2,1)S(1)}, u32[]{:S(2)}, u32[]{:S(2)}) collective-permute-start(bf16[320,128]{1,0:T(8,128)(2,1)S(1)} %fusion.140), channel_id=1, source_target_pairs={{1,0},{2,1},{3,2},{0,3},{5,4},{6,5},{7,6},{4,7},{9,8},{10,9},{11,1... | collective-permute-start | bytes 245768 | tf_op jit(solution)/shard_map/ppermute | solution.py:69
  21.3 2.2 collective-permute-start.5
  23.8 4.0 %collective-permute-done.4 = bf16[320,128]{1,0:T(8,128)(2,1)S(1)} collective-permute-done((bf16[320,128]{1,0:T(8,128)(2,1)S(1)}, bf16[320,128]{1,0:T(8,128)(2,1)S(1)}, u32[]{:S(2)}, u32[]{:S(2)}) %collective-permute-start.4) | collective-permute-done | bytes 81952 | tf_op jit(solution)/shard_map/ppermute | solution.py:69
  28.0 1.2 collective-permute-done.6
  30.0 1.5 collective-permute-start.7
  31.6 2.6 collective-permute-done.7
  34.4 2.8 collective-permute-start.8
  37.2 2.7 collective-permute-start.11
  40.9 2.2 collective-permute-done.11
  43.9 3.0 %collective-permute-done.12 = bf16[192,512]{1,0:T(8,128)(2,1)S(1)} collective-permute-done((bf16[192,512]{1,0:T(8,128)(2,1)S(1)}, bf16[192,512]{1,0:T(8,128)(2,1)S(1)}, u32[]{:S(2)}, u32[]{:S(2)}) %collective-permute-start.12) | collective-permute-done | bytes 196640 | tf_op jit(solution)/shard_map/ppermute | solution.py:69
  48.0 34.1 %all_to_all.15 = bf16[8,2240,128]{2,1,0:T(8,128)(2,1)S(1)} all-to-all(bf16[8,2240,128]{2,1,0:T(8,128)(2,1)S(1)} %broadcast_in_dim.73), channel_id=1, replica_groups={{16,20,24,28,32,36,40,44},{17,21,25,29,33,37,41,45},{18,22,26,30,34,38,..., dimensions={0} | all-to-all | bytes 9175040 | tf_op jit(solution)/shard_map/all_to_all | solution.py:261
  82.2 1.2 collective-permute-done.13
  83.9 2.4 collective-permute-start.17
  87.4 1.7 shard_map.104.before
  90.1 1.9 shard_map.105
  93.8 1.6 collective-permute-start.22
  95.4 2.1 collective-permute-done.21
  97.5 1.6 collective-permute-done.22
  99.1 1.9 collective-permute-done.23
  101.0 1.4 collective-permute-start.24
  104.0 1.4 collective-permute-done.24
  105.4 2.3 collective-permute-done.25
  107.7 1.2 collective-permute-done.26
  109.1 1.2 collective-permute-done.27
  111.1 1.6 collective-permute-start.18
  114.3 3.7 %collective-permute-start.29 = (bf16[64,128]{1,0:T(8,128)(2,1)S(1)}, bf16[64,128]{1,0:T(8,128)(2,1)S(1)}, u32[]{:S(2)}, u32[]{:S(2)}) collective-permute-start(bf16[64,128]{1,0:T(8,128)(2,1)S(1)} %fusion.58), channel_id=1, source_target_pairs={{96,0},{97,1},{98,2},{99,3},{100,4},{101,5},{102,6},{103,7},{104,8... | collective-permute-start | bytes 49160 | tf_op jit(solution)/shard_map/ppermute | solution.py:69
  118.0 2.3 collective-permute-done.19
  123.2 34.5 %all_to_all.16 = bf16[8,2240,128]{2,1,0:T(8,128)(2,1)S(1)} all-to-all(bf16[8,2240,128]{2,1,0:T(8,128)(2,1)S(1)} %broadcast_in_dim.74), channel_id=1, replica_groups={{16,20,24,28,32,36,40,44},{17,21,25,29,33,37,41,45},{18,22,26,30,34,38,..., dimensions={0} | all-to-all | bytes 9175040 | tf_op jit(solution)/shard_map/all_to_all | solution.py:261
  157.9 1.2 collective-permute-done.30
  159.6 2.6 collective-permute-start.33
  162.1 1.7 collective-permute-start.34
  163.9 1.7 shard_map.106.before
  165.5 1.5 collective-permute-done.34
  167.6 2.0 shard_map.107
  170.8 1.8 collective-permute-start.38
  172.9 1.3 collective-permute-start.40
  175.0 3.0 %collective-permute-done.39 = bf16[192,128]{1,0:T(8,128)(2,1)S(1)} collective-permute-done((bf16[192,128]{1,0:T(8,128)(2,1)S(1)}, bf16[192,128]{1,0:T(8,128)(2,1)S(1)}, u32[]{:S(2)}, u32[]{:S(2)}) %collective-permute-start.39) | collective-permute-done | bytes 49184 | tf_op jit(solution)/shard_map/ppermute | solution.py:69
  178.5 1.5 collective-permute-start.41
  182.7 2.6 collective-permute-done.42
  186.4 1.2 collective-permute-done.44
  187.9 3.3 %collective-permute-start.35 = (bf16[512,128]{1,0:T(8,128)(2,1)S(1)}, bf16[512,128]{1,0:T(8,128)(2,1)S(1)}, u32[]{:S(2)}, u32[]{:S(2)}) collective-permute-start(bf16[512,128]{1,0:T(8,128)(2,1)S(1)} %get-tuple-element.64), channel_id=1, source_target_pairs={{4,0},{5,1},{6,2},{7,3},{8,4},{9,5},{10,6},{11,7},{12,8},{13,9},{1... | collective-permute-start | bytes 393224 | tf_op jit(solution)/shard_map/ppermute | solution.py:69
  191.2 1.5 collective-permute-start.37
  192.7 2.2 collective-permute-start.46
  194.9 3.8 %collective-permute-done.36 = bf16[512,128]{1,0:T(8,128)(2,1)S(1)} collective-permute-done((bf16[512,128]{1,0:T(8,128)(2,1)S(1)}, bf16[512,128]{1,0:T(8,128)(2,1)S(1)}, u32[]{:S(2)}, u32[]{:S(2)}) %collective-permute-start.36) | collective-permute-done | bytes 131104 | tf_op jit(solution)/shard_map/ppermute | solution.py:69
  201.6 34.7 %all_to_all.17 = bf16[8,2240,128]{2,1,0:T(8,128)(2,1)S(1)} all-to-all(bf16[8,2240,128]{2,1,0:T(8,128)(2,1)S(1)} %broadcast_in_dim.75), channel_id=1, replica_groups={{16,20,24,28,32,36,40,44},{17,21,25,29,33,37,41,45},{18,22,26,30,34,38,..., dimensions={0} | all-to-all | bytes 9175040 | tf_op jit(solution)/shard_map/all_to_all | solution.py:261
  236.5 1.2 collective-permute-done.47
  238.1 1.5 collective-permute-start.50
  239.6 2.0 collective-permute-start.51
  241.7 1.7 shard_map.108.before
  245.4 1.9 shard_map.109
  249.2 1.6 collective-permute-start.52
  253.3 2.8 %collective-permute-done.53 = bf16[192,128]{1,0:T(8,128)(2,1)S(1)} collective-permute-done((bf16[192,128]{1,0:T(8,128)(2,1)S(1)}, bf16[192,128]{1,0:T(8,128)(2,1)S(1)}, u32[]{:S(2)}, u32[]{:S(2)}) %collective-permute-start.53) | collective-permute-done | bytes 49184 | tf_op jit(solution)/shard_map/ppermute | solution.py:69
  256.9 2.2 collective-permute-start.55
  259.1 1.5 collective-permute-start.57
  261.1 3.8 %collective-permute-done.56 = bf16[192,128]{1,0:T(8,128)(2,1)S(1)} collective-permute-done((bf16[192,128]{1,0:T(8,128)(2,1)S(1)}, bf16[192,128]{1,0:T(8,128)(2,1)S(1)}, u32[]{:S(2)}, u32[]{:S(2)}) %collective-permute-start.56) | collective-permute-done | bytes 49184 | tf_op jit(solution)/shard_map/ppermute | solution.py:69
  265.0 1.2 collective-permute-done.58
  266.9 3.4 %collective-permute-done.59 = bf16[128,128]{1,0:T(8,128)(2,1)S(1)} collective-permute-done((bf16[128,128]{1,0:T(8,128)(2,1)S(1)}, bf16[128,128]{1,0:T(8,128)(2,1)S(1)}, u32[]{:S(2)}, u32[]{:S(2)}) %collective-permute-start.59) | collective-permute-done | bytes 32800 | tf_op jit(solution)/shard_map/ppermute | solution.py:69
  270.3 1.2 collective-permute-start.60
  271.5 3.8 %collective-permute-done.60 = bf16[64,128]{1,0:T(8,128)(2,1)S(1)} collective-permute-done((bf16[64,128]{1,0:T(8,128)(2,1)S(1)}, bf16[64,128]{1,0:T(8,128)(2,1)S(1)}, u32[]{:S(2)}, u32[]{:S(2)}) %collective-permute-start.60) | collective-permute-done | bytes 16416 | tf_op jit(solution)/shard_map/ppermute | solution.py:69
  (247 shorter events, 40.3 us)
Async XLA Ops:
  0.6 91.4 %copy-start = (bf16[3,64,512]{2,1,0:T(8,128)(2,1)S(1)}, bf16[3,64,512]{2,1,0:T(8,128)(2,1)}, u32[]{:S(2)}) copy-start(bf16[3,64,512]{2,1,0:T(8,128)(2,1)} %param.14) | copy-start | bytes 589828
  4.6 8.9 %collective-permute-start = (bf16[832,128]{1,0:T(8,128)(2,1)S(1)}, bf16[832,128]{1,0:T(8,128)(2,1)S(1)}, u32[]{:S(2)}, u32[]{:S(2)}) collective-permute-start(bf16[832,128]{1,0:T(8,128)(2,1)S(1)} %pad_maximum_fusion.4), channel_id=1, source_target_pairs={{4,0},{5,1},{6,2},{7,3},{8,4},{9,5},{10,6},{11,7},{12,8},{13,9},{1... | collective-permute-start | bytes 638984 | tf_op jit(solution)/shard_map/ppermute | solution.py:69
  8.8 9.3 %collective-permute-start.1 = (bf16[832,128]{1,0:T(8,128)(2,1)S(1)}, bf16[832,128]{1,0:T(8,128)(2,1)S(1)}, u32[]{:S(2)}, u32[]{:S(2)}) collective-permute-start(bf16[832,128]{1,0:T(8,128)(2,1)S(1)} %pad_maximum_fusion.4), channel_id=1, source_target_pairs={{12,0},{13,1},{14,2},{15,3},{0,4},{1,5},{2,6},{3,7},{4,8},{5,9},{6... | collective-permute-start | bytes 638984 | tf_op jit(solution)/shard_map/ppermute | solution.py:69
  8.8 9.3 %collective-permute-start.2 = (bf16[832,128]{1,0:T(8,128)(2,1)S(1)}, bf16[832,128]{1,0:T(8,128)(2,1)S(1)}, u32[]{:S(2)}, u32[]{:S(2)}) collective-permute-start(bf16[832,128]{1,0:T(8,128)(2,1)S(1)} %pad_maximum_fusion.4), channel_id=1, source_target_pairs={{8,0},{9,1},{10,2},{11,3},{12,4},{13,5},{14,6},{15,7},{0,8},{1,9},... | collective-permute-start | bytes 638984 | tf_op jit(solution)/shard_map/ppermute | solution.py:69
  10.6 26.5 %collective-permute-start.9 = (bf16[384,512]{1,0:T(8,128)(2,1)S(1)}, bf16[384,512]{1,0:T(8,128)(2,1)S(1)}, u32[]{:S(2)}, u32[]{:S(2)}) collective-permute-start(bf16[384,512]{1,0:T(8,128)(2,1)S(1)} %pad_maximum_fusion.3), channel_id=1, source_target_pairs={{4,0},{5,1},{6,2},{7,3},{8,4},{9,5},{10,6},{11,7},{12,8},{13,9},{1... | collective-permute-start | bytes 1179656 | tf_op jit(solution)/shard_map/ppermute | solution.py:69
  12.1 27.8 %collective-permute-start.10 = (bf16[384,512]{1,0:T(8,128)(2,1)S(1)}, bf16[384,512]{1,0:T(8,128)(2,1)S(1)}, u32[]{:S(2)}, u32[]{:S(2)}) collective-permute-start(bf16[384,512]{1,0:T(8,128)(2,1)S(1)} %pad_maximum_fusion.3), channel_id=1, source_target_pairs={{12,0},{13,1},{14,2},{15,3},{0,4},{1,5},{2,6},{3,7},{4,8},{5,9},{6... | collective-permute-start | bytes 1179656 | tf_op jit(solution)/shard_map/ppermute | solution.py:69
  18.2 5.6 %collective-permute-start.3 = (bf16[320,128]{1,0:T(8,128)(2,1)S(1)}, bf16[320,128]{1,0:T(8,128)(2,1)S(1)}, u32[]{:S(2)}, u32[]{:S(2)}) collective-permute-start(bf16[320,128]{1,0:T(8,128)(2,1)S(1)} %fusion.140), channel_id=1, source_target_pairs={{1,0},{2,1},{3,2},{0,3},{5,4},{6,5},{7,6},{4,7},{9,8},{10,9},{11,1... | collective-permute-start | bytes 245768 | tf_op jit(solution)/shard_map/ppermute | solution.py:69
  21.3 6.5 %collective-permute-start.4 = (bf16[320,128]{1,0:T(8,128)(2,1)S(1)}, bf16[320,128]{1,0:T(8,128)(2,1)S(1)}, u32[]{:S(2)}, u32[]{:S(2)}) collective-permute-start(bf16[320,128]{1,0:T(8,128)(2,1)S(1)} %fusion.140), channel_id=1, source_target_pairs={{3,0},{0,1},{1,2},{2,3},{7,4},{4,5},{5,6},{6,7},{11,8},{8,9},{9,10... | collective-permute-start | bytes 245768 | tf_op jit(solution)/shard_map/ppermute | solution.py:69
  21.3 6.5 %collective-permute-start.5 = (bf16[320,128]{1,0:T(8,128)(2,1)S(1)}, bf16[320,128]{1,0:T(8,128)(2,1)S(1)}, u32[]{:S(2)}, u32[]{:S(2)}) collective-permute-start(bf16[320,128]{1,0:T(8,128)(2,1)S(1)} %fusion.140), channel_id=1, source_target_pairs={{2,0},{3,1},{0,2},{1,3},{6,4},{7,5},{4,6},{5,7},{10,8},{11,9},{8,1... | collective-permute-start | bytes 245768 | tf_op jit(solution)/shard_map/ppermute | solution.py:69
  27.9 1.4 collective-permute-start.6
  30.0 4.1 %collective-permute-start.7 = (bf16[192,128]{1,0:T(8,128)(2,1)S(1)}, bf16[192,128]{1,0:T(8,128)(2,1)S(1)}, u32[]{:S(2)}, u32[]{:S(2)}) collective-permute-start(bf16[192,128]{1,0:T(8,128)(2,1)S(1)} %maximum_maximum_fusion), channel_id=1, source_target_pairs={{32,0},{33,1},{34,2},{35,3},{36,4},{37,5},{38,6},{39,7},{40,8},{41... | collective-permute-start | bytes 147464 | tf_op jit(solution)/shard_map/ppermute | solution.py:69
  34.4 5.7 %collective-permute-start.8 = (bf16[64,128]{1,0:T(8,128)(2,1)S(1)}, bf16[64,128]{1,0:T(8,128)(2,1)S(1)}, u32[]{:S(2)}, u32[]{:S(2)}) collective-permute-start(bf16[64,128]{1,0:T(8,128)(2,1)S(1)} %fusion.15), channel_id=1, source_target_pairs={{96,0},{97,1},{98,2},{99,3},{100,4},{101,5},{102,6},{103,7},{104,8... | collective-permute-start | bytes 49160 | tf_op jit(solution)/shard_map/ppermute | solution.py:69
  37.2 5.9 %collective-permute-start.11 = (bf16[192,512]{1,0:T(8,128)(2,1)S(1)}, bf16[192,512]{1,0:T(8,128)(2,1)S(1)}, u32[]{:S(2)}, u32[]{:S(2)}) collective-permute-start(bf16[192,512]{1,0:T(8,128)(2,1)S(1)} %slice.381), channel_id=1, source_target_pairs={{4,0},{5,1},{6,2},{7,3},{8,4},{9,5},{10,6},{11,7},{12,8},{13,9},{1... | collective-permute-start | bytes 589832 | tf_op jit(solution)/shard_map/ppermute | solution.py:69
  39.9 7.0 %collective-permute-start.12 = (bf16[192,512]{1,0:T(8,128)(2,1)S(1)}, bf16[192,512]{1,0:T(8,128)(2,1)S(1)}, u32[]{:S(2)}, u32[]{:S(2)}) collective-permute-start(bf16[192,512]{1,0:T(8,128)(2,1)S(1)} %slice.386), channel_id=1, source_target_pairs={{12,0},{13,1},{14,2},{15,3},{0,4},{1,5},{2,6},{3,7},{4,8},{5,9},{6... | collective-permute-start | bytes 589832 | tf_op jit(solution)/shard_map/ppermute | solution.py:69
  47.3 40.1 %slice-start = ((s8[5242880]{0:T(1024)(128)(4,1)}), s8[4194304]{0:T(1024)(128)(4,1)S(1)}, s32[]{:S(2)}) async-start(s8[5242880]{0:T(1024)(128)(4,1)} %bitcast.111), calls=%async_computation.3 | async-start | bytes 8388608
  48.0 39.5 %slice-start.1 = ((s8[5242880]{0:T(1024)(128)(4,1)}), s8[1048576]{0:T(1024)(128)(4,1)S(1)}, s32[]{:S(2)}) async-start(s8[5242880]{0:T(1024)(128)(4,1)} %bitcast.111), calls=%async_computation.4 | async-start | bytes 2097152
  82.1 1.3 collective-permute-start.13
  83.5 6.6 %collective-permute-start.14 = (bf16[4,2048,128]{2,1,0:T(8,128)(2,1)S(1)}, bf16[4,2048,128]{2,1,0:T(8,128)(2,1)S(1)}, u32[]{:S(2)}, u32[]{:S(2)}) collective-permute-start(bf16[4,2048,128]{2,1,0:T(8,128)(2,1)S(1)} %constant_dynamic-slice_fusion.1), channel_id=1, source_target_pairs={{16,0},{17,1},{18,2},{19,3},{20,4},{21,5},{22,6},{23,7},{24,8},{25... | collective-permute-start | bytes 6291464 | tf_op jit(solution)/shard_map/ppermute | solution.py:69
  83.8 5.3 %collective-permute-start.16 = (bf16[64,128]{1,0:T(8,128)(2,1)S(1)}, bf16[64,128]{1,0:T(8,128)(2,1)S(1)}, u32[]{:S(2)}, u32[]{:S(2)}) collective-permute-start(bf16[64,128]{1,0:T(8,128)(2,1)S(1)} %get-tuple-element.78), channel_id=1, source_target_pairs={{64,0},{65,1},{66,2},{67,3},{68,4},{69,5},{70,6},{71,7},{72,8},{73... | collective-permute-start | bytes 49160 | tf_op jit(solution)/shard_map/ppermute | solution.py:69
  83.9 5.2 %collective-permute-start.17 = (bf16[64,128]{1,0:T(8,128)(2,1)S(1)}, bf16[64,128]{1,0:T(8,128)(2,1)S(1)}, u32[]{:S(2)}, u32[]{:S(2)}) collective-permute-start(bf16[64,128]{1,0:T(8,128)(2,1)S(1)} %get-tuple-element.78), channel_id=1, source_target_pairs={{96,0},{97,1},{98,2},{99,3},{100,4},{101,5},{102,6},{103,7},{104,8... | collective-permute-start | bytes 49160 | tf_op jit(solution)/shard_map/ppermute | solution.py:69
  86.3 3.7 %collective-permute-start.15 = (bf16[64,128]{1,0:T(8,128)(2,1)S(1)}, bf16[64,128]{1,0:T(8,128)(2,1)S(1)}, u32[]{:S(2)}, u32[]{:S(2)}) collective-permute-start(bf16[64,128]{1,0:T(8,128)(2,1)S(1)} %get-tuple-element.77), channel_id=1, source_target_pairs={{32,0},{33,1},{34,2},{35,3},{36,4},{37,5},{38,6},{39,7},{40,8},{41... | collective-permute-start | bytes 49160 | tf_op jit(solution)/shard_map/ppermute | solution.py:69
  93.3 4.2 %collective-permute-start.21 = (bf16[192,128]{1,0:T(8,128)(2,1)S(1)}, bf16[192,128]{1,0:T(8,128)(2,1)S(1)}, u32[]{:S(2)}, u32[]{:S(2)}) collective-permute-start(bf16[192,128]{1,0:T(8,128)(2,1)S(1)} %fusion.47), channel_id=1, source_target_pairs={{4,0},{5,1},{6,2},{7,3},{8,4},{9,5},{10,6},{11,7},{12,8},{13,9},{1... | collective-permute-start | bytes 147464 | tf_op jit(solution)/shard_map/ppermute | solution.py:69
  93.8 5.3 %collective-permute-start.22 = (bf16[192,128]{1,0:T(8,128)(2,1)S(1)}, bf16[192,128]{1,0:T(8,128)(2,1)S(1)}, u32[]{:S(2)}, u32[]{:S(2)}) collective-permute-start(bf16[192,128]{1,0:T(8,128)(2,1)S(1)} %fusion.47), channel_id=1, source_target_pairs={{12,0},{13,1},{14,2},{15,3},{0,4},{1,5},{2,6},{3,7},{4,8},{5,9},{6... | collective-permute-start | bytes 147464 | tf_op jit(solution)/shard_map/ppermute | solution.py:69
  95.4 5.6 %collective-permute-start.23 = (bf16[192,128]{1,0:T(8,128)(2,1)S(1)}, bf16[192,128]{1,0:T(8,128)(2,1)S(1)}, u32[]{:S(2)}, u32[]{:S(2)}) collective-permute-start(bf16[192,128]{1,0:T(8,128)(2,1)S(1)} %fusion.47), channel_id=1, source_target_pairs={{8,0},{9,1},{10,2},{11,3},{12,4},{13,5},{14,6},{15,7},{0,8},{1,9},... | collective-permute-start | bytes 147464 | tf_op jit(solution)/shard_map/ppermute | solution.py:69
  101.0 4.3 %collective-permute-start.24 = (bf16[192,128]{1,0:T(8,128)(2,1)S(1)}, bf16[192,128]{1,0:T(8,128)(2,1)S(1)}, u32[]{:S(2)}, u32[]{:S(2)}) collective-permute-start(bf16[192,128]{1,0:T(8,128)(2,1)S(1)} %fusion.126), channel_id=1, source_target_pairs={{1,0},{2,1},{3,2},{0,3},{5,4},{6,5},{7,6},{4,7},{9,8},{10,9},{11,1... | collective-permute-start | bytes 147464 | tf_op jit(solution)/shard_map/ppermute | solution.py:69
  102.4 5.3 %collective-permute-start.25 = (bf16[192,128]{1,0:T(8,128)(2,1)S(1)}, bf16[192,128]{1,0:T(8,128)(2,1)S(1)}, u32[]{:S(2)}, u32[]{:S(2)}) collective-permute-start(bf16[192,128]{1,0:T(8,128)(2,1)S(1)} %fusion.126), channel_id=1, source_target_pairs={{3,0},{0,1},{1,2},{2,3},{7,4},{4,5},{5,6},{6,7},{11,8},{8,9},{9,10... | collective-permute-start | bytes 147464 | tf_op jit(solution)/shard_map/ppermute | solution.py:69
  103.3 5.6 %collective-permute-start.26 = (bf16[192,128]{1,0:T(8,128)(2,1)S(1)}, bf16[192,128]{1,0:T(8,128)(2,1)S(1)}, u32[]{:S(2)}, u32[]{:S(2)}) collective-permute-start(bf16[192,128]{1,0:T(8,128)(2,1)S(1)} %fusion.126), channel_id=1, source_target_pairs={{2,0},{3,1},{0,2},{1,3},{6,4},{7,5},{4,6},{5,7},{10,8},{11,9},{8,1... | collective-permute-start | bytes 147464 | tf_op jit(solution)/shard_map/ppermute | solution.py:69
  109.0 1.3 collective-permute-start.27
  110.3 4.0 %collective-permute-start.28 = (bf16[128,128]{1,0:T(8,128)(2,1)S(1)}, bf16[128,128]{1,0:T(8,128)(2,1)S(1)}, u32[]{:S(2)}, u32[]{:S(2)}) collective-permute-start(bf16[128,128]{1,0:T(8,128)(2,1)S(1)} %get-tuple-element.54), channel_id=1, source_target_pairs={{32,0},{33,1},{34,2},{35,3},{36,4},{37,5},{38,6},{39,7},{40,8},{41... | collective-permute-start | bytes 98312 | tf_op jit(solution)/shard_map/ppermute | solution.py:69
  111.1 6.9 %collective-permute-start.18 = (bf16[512,128]{1,0:T(8,128)(2,1)S(1)}, bf16[512,128]{1,0:T(8,128)(2,1)S(1)}, u32[]{:S(2)}, u32[]{:S(2)}) collective-permute-start(bf16[512,128]{1,0:T(8,128)(2,1)S(1)} %get-tuple-element.66), channel_id=1, source_target_pairs={{4,0},{5,1},{6,2},{7,3},{8,4},{9,5},{10,6},{11,7},{12,8},{13,9},{1... | collective-permute-start | bytes 393224 | tf_op jit(solution)/shard_map/ppermute | solution.py:69
  112.7 7.6 %collective-permute-start.19 = (bf16[512,128]{1,0:T(8,128)(2,1)S(1)}, bf16[512,128]{1,0:T(8,128)(2,1)S(1)}, u32[]{:S(2)}, u32[]{:S(2)}) collective-permute-start(bf16[512,128]{1,0:T(8,128)(2,1)S(1)} %get-tuple-element.66), channel_id=1, source_target_pairs={{12,0},{13,1},{14,2},{15,3},{0,4},{1,5},{2,6},{3,7},{4,8},{5,9},{6... | collective-permute-start | bytes 393224 | tf_op jit(solution)/shard_map/ppermute | solution.py:69
  113.1 7.2 %collective-permute-start.20 = (bf16[512,128]{1,0:T(8,128)(2,1)S(1)}, bf16[512,128]{1,0:T(8,128)(2,1)S(1)}, u32[]{:S(2)}, u32[]{:S(2)}) collective-permute-start(bf16[512,128]{1,0:T(8,128)(2,1)S(1)} %get-tuple-element.66), channel_id=1, source_target_pairs={{8,0},{9,1},{10,2},{11,3},{12,4},{13,5},{14,6},{15,7},{0,8},{1,9},... | collective-permute-start | bytes 393224 | tf_op jit(solution)/shard_map/ppermute | solution.py:69
  114.3 6.1 %collective-permute-start.29 = (bf16[64,128]{1,0:T(8,128)(2,1)S(1)}, bf16[64,128]{1,0:T(8,128)(2,1)S(1)}, u32[]{:S(2)}, u32[]{:S(2)}) collective-permute-start(bf16[64,128]{1,0:T(8,128)(2,1)S(1)} %fusion.58), channel_id=1, source_target_pairs={{96,0},{97,1},{98,2},{99,3},{100,4},{101,5},{102,6},{103,7},{104,8... | collective-permute-start | bytes 49160 | tf_op jit(solution)/shard_map/ppermute | solution.py:69
  157.8 1.3 collective-permute-start.30
  159.3 8.3 %collective-permute-start.31 = (bf16[4,2048,128]{2,1,0:T(8,128)(2,1)S(1)}, bf16[4,2048,128]{2,1,0:T(8,128)(2,1)S(1)}, u32[]{:S(2)}, u32[]{:S(2)}) collective-permute-start(bf16[4,2048,128]{2,1,0:T(8,128)(2,1)S(1)} %constant_dynamic-slice_fusion), channel_id=1, source_target_pairs={{16,0},{17,1},{18,2},{19,3},{20,4},{21,5},{22,6},{23,7},{24,8},{25... | collective-permute-start | bytes 6291464 | tf_op jit(solution)/shard_map/ppermute | solution.py:69
  159.6 6.0 %collective-permute-start.33 = (bf16[64,128]{1,0:T(8,128)(2,1)S(1)}, bf16[64,128]{1,0:T(8,128)(2,1)S(1)}, u32[]{:S(2)}, u32[]{:S(2)}) collective-permute-start(bf16[64,128]{1,0:T(8,128)(2,1)S(1)} %get-tuple-element.76), channel_id=1, source_target_pairs={{64,0},{65,1},{66,2},{67,3},{68,4},{69,5},{70,6},{71,7},{72,8},{73... | collective-permute-start | bytes 49160 | tf_op jit(solution)/shard_map/ppermute | solution.py:69
  162.1 4.9 %collective-permute-start.34 = (bf16[64,128]{1,0:T(8,128)(2,1)S(1)}, bf16[64,128]{1,0:T(8,128)(2,1)S(1)}, u32[]{:S(2)}, u32[]{:S(2)}) collective-permute-start(bf16[64,128]{1,0:T(8,128)(2,1)S(1)} %get-tuple-element.76), channel_id=1, source_target_pairs={{96,0},{97,1},{98,2},{99,3},{100,4},{101,5},{102,6},{103,7},{104,8... | collective-permute-start | bytes 49160 | tf_op jit(solution)/shard_map/ppermute | solution.py:69
  163.9 3.7 %collective-permute-start.32 = (bf16[64,128]{1,0:T(8,128)(2,1)S(1)}, bf16[64,128]{1,0:T(8,128)(2,1)S(1)}, u32[]{:S(2)}, u32[]{:S(2)}) collective-permute-start(bf16[64,128]{1,0:T(8,128)(2,1)S(1)} %get-tuple-element.75), channel_id=1, source_target_pairs={{32,0},{33,1},{34,2},{35,3},{36,4},{37,5},{38,6},{39,7},{40,8},{41... | collective-permute-start | bytes 49160 | tf_op jit(solution)/shard_map/ppermute | solution.py:69
  170.8 4.2 %collective-permute-start.38 = (bf16[192,128]{1,0:T(8,128)(2,1)S(1)}, bf16[192,128]{1,0:T(8,128)(2,1)S(1)}, u32[]{:S(2)}, u32[]{:S(2)}) collective-permute-start(bf16[192,128]{1,0:T(8,128)(2,1)S(1)} %fusion.46), channel_id=1, source_target_pairs={{4,0},{5,1},{6,2},{7,3},{8,4},{9,5},{10,6},{11,7},{12,8},{13,9},{1... | collective-permute-start | bytes 147464 | tf_op jit(solution)/shard_map/ppermute | solution.py:69
  172.6 5.3 %collective-permute-start.39 = (bf16[192,128]{1,0:T(8,128)(2,1)S(1)}, bf16[192,128]{1,0:T(8,128)(2,1)S(1)}, u32[]{:S(2)}, u32[]{:S(2)}) collective-permute-start(bf16[192,128]{1,0:T(8,128)(2,1)S(1)} %fusion.46), channel_id=1, source_target_pairs={{12,0},{13,1},{14,2},{15,3},{0,4},{1,5},{2,6},{3,7},{4,8},{5,9},{6... | collective-permute-start | bytes 147464 | tf_op jit(solution)/shard_map/ppermute | solution.py:69
  172.9 5.6 %collective-permute-start.40 = (bf16[192,128]{1,0:T(8,128)(2,1)S(1)}, bf16[192,128]{1,0:T(8,128)(2,1)S(1)}, u32[]{:S(2)}, u32[]{:S(2)}) collective-permute-start(bf16[192,128]{1,0:T(8,128)(2,1)S(1)} %fusion.46), channel_id=1, source_target_pairs={{8,0},{9,1},{10,2},{11,3},{12,4},{13,5},{14,6},{15,7},{0,8},{1,9},... | collective-permute-start | bytes 147464 | tf_op jit(solution)/shard_map/ppermute | solution.py:69
  178.5 4.2 %collective-permute-start.41 = (bf16[192,128]{1,0:T(8,128)(2,1)S(1)}, bf16[192,128]{1,0:T(8,128)(2,1)S(1)}, u32[]{:S(2)}, u32[]{:S(2)}) collective-permute-start(bf16[192,128]{1,0:T(8,128)(2,1)S(1)} %fusion.127), channel_id=1, source_target_pairs={{1,0},{2,1},{3,2},{0,3},{5,4},{6,5},{7,6},{4,7},{9,8},{10,9},{11,1... | collective-permute-start | bytes 147464 | tf_op jit(solution)/shard_map/ppermute | solution.py:69
  180.0 5.3 %collective-permute-start.42 = (bf16[192,128]{1,0:T(8,128)(2,1)S(1)}, bf16[192,128]{1,0:T(8,128)(2,1)S(1)}, u32[]{:S(2)}, u32[]{:S(2)}) collective-permute-start(bf16[192,128]{1,0:T(8,128)(2,1)S(1)} %fusion.127), channel_id=1, source_target_pairs={{3,0},{0,1},{1,2},{2,3},{7,4},{4,5},{5,6},{6,7},{11,8},{8,9},{9,10... | collective-permute-start | bytes 147464 | tf_op jit(solution)/shard_map/ppermute | solution.py:69
  180.6 5.6 %collective-permute-start.43 = (bf16[192,128]{1,0:T(8,128)(2,1)S(1)}, bf16[192,128]{1,0:T(8,128)(2,1)S(1)}, u32[]{:S(2)}, u32[]{:S(2)}) collective-permute-start(bf16[192,128]{1,0:T(8,128)(2,1)S(1)} %fusion.127), channel_id=1, source_target_pairs={{2,0},{3,1},{0,2},{1,3},{6,4},{7,5},{4,6},{5,7},{10,8},{11,9},{8,1... | collective-permute-start | bytes 147464 | tf_op jit(solution)/shard_map/ppermute | solution.py:69
  186.3 1.3 collective-permute-start.44
  187.6 5.1 %collective-permute-start.45 = (bf16[128,128]{1,0:T(8,128)(2,1)S(1)}, bf16[128,128]{1,0:T(8,128)(2,1)S(1)}, u32[]{:S(2)}, u32[]{:S(2)}) collective-permute-start(bf16[128,128]{1,0:T(8,128)(2,1)S(1)} %get-tuple-element.48), channel_id=1, source_target_pairs={{32,0},{33,1},{34,2},{35,3},{36,4},{37,5},{38,6},{39,7},{40,8},{41... | collective-permute-start | bytes 98312 | tf_op jit(solution)/shard_map/ppermute | solution.py:69
  187.9 7.0 %collective-permute-start.35 = (bf16[512,128]{1,0:T(8,128)(2,1)S(1)}, bf16[512,128]{1,0:T(8,128)(2,1)S(1)}, u32[]{:S(2)}, u32[]{:S(2)}) collective-permute-start(bf16[512,128]{1,0:T(8,128)(2,1)S(1)} %get-tuple-element.64), channel_id=1, source_target_pairs={{4,0},{5,1},{6,2},{7,3},{8,4},{9,5},{10,6},{11,7},{12,8},{13,9},{1... | collective-permute-start | bytes 393224 | tf_op jit(solution)/shard_map/ppermute | solution.py:69
  191.2 7.6 %collective-permute-start.36 = (bf16[512,128]{1,0:T(8,128)(2,1)S(1)}, bf16[512,128]{1,0:T(8,128)(2,1)S(1)}, u32[]{:S(2)}, u32[]{:S(2)}) collective-permute-start(bf16[512,128]{1,0:T(8,128)(2,1)S(1)} %get-tuple-element.64), channel_id=1, source_target_pairs={{12,0},{13,1},{14,2},{15,3},{0,4},{1,5},{2,6},{3,7},{4,8},{5,9},{6... | collective-permute-start | bytes 393224 | tf_op jit(solution)/shard_map/ppermute | solution.py:69
  191.2 7.6 %collective-permute-start.37 = (bf16[512,128]{1,0:T(8,128)(2,1)S(1)}, bf16[512,128]{1,0:T(8,128)(2,1)S(1)}, u32[]{:S(2)}, u32[]{:S(2)}) collective-permute-start(bf16[512,128]{1,0:T(8,128)(2,1)S(1)} %get-tuple-element.64), channel_id=1, source_target_pairs={{8,0},{9,1},{10,2},{11,3},{12,4},{13,5},{14,6},{15,7},{0,8},{1,9},... | collective-permute-start | bytes 393224 | tf_op jit(solution)/shard_map/ppermute | solution.py:69
  192.7 6.1 %collective-permute-start.46 = (bf16[64,128]{1,0:T(8,128)(2,1)S(1)}, bf16[64,128]{1,0:T(8,128)(2,1)S(1)}, u32[]{:S(2)}, u32[]{:S(2)}) collective-permute-start(bf16[64,128]{1,0:T(8,128)(2,1)S(1)} %fusion.57), channel_id=1, source_target_pairs={{96,0},{97,1},{98,2},{99,3},{100,4},{101,5},{102,6},{103,7},{104,8... | collective-permute-start | bytes 49160 | tf_op jit(solution)/shard_map/ppermute | solution.py:69
  236.4 1.3 collective-permute-start.47
  237.8 7.5 %collective-permute-start.48 = (bf16[4,2048,128]{2,1,0:T(8,128)(2,1)S(1)}, bf16[4,2048,128]{2,1,0:T(8,128)(2,1)S(1)}, u32[]{:S(2)}, u32[]{:S(2)}) collective-permute-start(bf16[4,2048,128]{2,1,0:T(8,128)(2,1)S(1)} %constant_dynamic-slice_fusion.2), channel_id=1, source_target_pairs={{16,0},{17,1},{18,2},{19,3},{20,4},{21,5},{22,6},{23,7},{24,8},{25... | collective-permute-start | bytes 6291464 | tf_op jit(solution)/shard_map/ppermute | solution.py:69
  238.1 5.3 %collective-permute-start.50 = (bf16[64,128]{1,0:T(8,128)(2,1)S(1)}, bf16[64,128]{1,0:T(8,128)(2,1)S(1)}, u32[]{:S(2)}, u32[]{:S(2)}) collective-permute-start(bf16[64,128]{1,0:T(8,128)(2,1)S(1)} %get-tuple-element.74), channel_id=1, source_target_pairs={{64,0},{65,1},{66,2},{67,3},{68,4},{69,5},{70,6},{71,7},{72,8},{73... | collective-permute-start | bytes 49160 | tf_op jit(solution)/shard_map/ppermute | solution.py:69
  239.6 4.9 %collective-permute-start.51 = (bf16[64,128]{1,0:T(8,128)(2,1)S(1)}, bf16[64,128]{1,0:T(8,128)(2,1)S(1)}, u32[]{:S(2)}, u32[]{:S(2)}) collective-permute-start(bf16[64,128]{1,0:T(8,128)(2,1)S(1)} %get-tuple-element.74), channel_id=1, source_target_pairs={{96,0},{97,1},{98,2},{99,3},{100,4},{101,5},{102,6},{103,7},{104,8... | collective-permute-start | bytes 49160 | tf_op jit(solution)/shard_map/ppermute | solution.py:69
  241.6 3.7 %collective-permute-start.49 = (bf16[64,128]{1,0:T(8,128)(2,1)S(1)}, bf16[64,128]{1,0:T(8,128)(2,1)S(1)}, u32[]{:S(2)}, u32[]{:S(2)}) collective-permute-start(bf16[64,128]{1,0:T(8,128)(2,1)S(1)} %get-tuple-element.73), channel_id=1, source_target_pairs={{32,0},{33,1},{34,2},{35,3},{36,4},{37,5},{38,6},{39,7},{40,8},{41... | collective-permute-start | bytes 49160 | tf_op jit(solution)/shard_map/ppermute | solution.py:69
  249.2 4.2 %collective-permute-start.52 = (bf16[192,128]{1,0:T(8,128)(2,1)S(1)}, bf16[192,128]{1,0:T(8,128)(2,1)S(1)}, u32[]{:S(2)}, u32[]{:S(2)}) collective-permute-start(bf16[192,128]{1,0:T(8,128)(2,1)S(1)} %fusion.45), channel_id=1, source_target_pairs={{4,0},{5,1},{6,2},{7,3},{8,4},{9,5},{10,6},{11,7},{12,8},{13,9},{1... | collective-permute-start | bytes 147464 | tf_op jit(solution)/shard_map/ppermute | solution.py:69
  250.8 5.3 %collective-permute-start.53 = (bf16[192,128]{1,0:T(8,128)(2,1)S(1)}, bf16[192,128]{1,0:T(8,128)(2,1)S(1)}, u32[]{:S(2)}, u32[]{:S(2)}) collective-permute-start(bf16[192,128]{1,0:T(8,128)(2,1)S(1)} %fusion.45), channel_id=1, source_target_pairs={{12,0},{13,1},{14,2},{15,3},{0,4},{1,5},{2,6},{3,7},{4,8},{5,9},{6... | collective-permute-start | bytes 147464 | tf_op jit(solution)/shard_map/ppermute | solution.py:69
  251.3 5.6 %collective-permute-start.54 = (bf16[192,128]{1,0:T(8,128)(2,1)S(1)}, bf16[192,128]{1,0:T(8,128)(2,1)S(1)}, u32[]{:S(2)}, u32[]{:S(2)}) collective-permute-start(bf16[192,128]{1,0:T(8,128)(2,1)S(1)} %fusion.45), channel_id=1, source_target_pairs={{8,0},{9,1},{10,2},{11,3},{12,4},{13,5},{14,6},{15,7},{0,8},{1,9},... | collective-permute-start | bytes 147464 | tf_op jit(solution)/shard_map/ppermute | solution.py:69
  256.9 4.2 %collective-permute-start.55 = (bf16[192,128]{1,0:T(8,128)(2,1)S(1)}, bf16[192,128]{1,0:T(8,128)(2,1)S(1)}, u32[]{:S(2)}, u32[]{:S(2)}) collective-permute-start(bf16[192,128]{1,0:T(8,128)(2,1)S(1)} %fusion.128), channel_id=1, source_target_pairs={{1,0},{2,1},{3,2},{0,3},{5,4},{6,5},{7,6},{4,7},{9,8},{10,9},{11,1... | collective-permute-start | bytes 147464 | tf_op jit(solution)/shard_map/ppermute | solution.py:69
  259.1 5.8 %collective-permute-start.56 = (bf16[192,128]{1,0:T(8,128)(2,1)S(1)}, bf16[192,128]{1,0:T(8,128)(2,1)S(1)}, u32[]{:S(2)}, u32[]{:S(2)}) collective-permute-start(bf16[192,128]{1,0:T(8,128)(2,1)S(1)} %fusion.128), channel_id=1, source_target_pairs={{3,0},{0,1},{1,2},{2,3},{7,4},{4,5},{5,6},{6,7},{11,8},{8,9},{9,10... | collective-permute-start | bytes 147464 | tf_op jit(solution)/shard_map/ppermute | solution.py:69
  259.1 5.8 %collective-permute-start.57 = (bf16[192,128]{1,0:T(8,128)(2,1)S(1)}, bf16[192,128]{1,0:T(8,128)(2,1)S(1)}, u32[]{:S(2)}, u32[]{:S(2)}) collective-permute-start(bf16[192,128]{1,0:T(8,128)(2,1)S(1)} %fusion.128), channel_id=1, source_target_pairs={{2,0},{3,1},{0,2},{1,3},{6,4},{7,5},{4,6},{5,7},{10,8},{11,9},{8,1... | collective-permute-start | bytes 147464 | tf_op jit(solution)/shard_map/ppermute | solution.py:69
  264.9 1.3 collective-permute-start.58
  266.3 4.0 %collective-permute-start.59 = (bf16[128,128]{1,0:T(8,128)(2,1)S(1)}, bf16[128,128]{1,0:T(8,128)(2,1)S(1)}, u32[]{:S(2)}, u32[]{:S(2)}) collective-permute-start(bf16[128,128]{1,0:T(8,128)(2,1)S(1)} %get-tuple-element.40), channel_id=1, source_target_pairs={{32,0},{33,1},{34,2},{35,3},{36,4},{37,5},{38,6},{39,7},{40,8},{41... | collective-permute-start | bytes 98312 | tf_op jit(solution)/shard_map/ppermute | solution.py:69
  270.3 5.0 %collective-permute-start.60 = (bf16[64,128]{1,0:T(8,128)(2,1)S(1)}, bf16[64,128]{1,0:T(8,128)(2,1)S(1)}, u32[]{:S(2)}, u32[]{:S(2)}) collective-permute-start(bf16[64,128]{1,0:T(8,128)(2,1)S(1)} %fusion.56), channel_id=1, source_target_pairs={{96,0},{97,1},{98,2},{99,3},{100,4},{101,5},{102,6},{103,7},{104,8... | collective-permute-start | bytes 49160 | tf_op jit(solution)/shard_map/ppermute | solution.py:69
  (13 other events, 74.4 us)

commit v4 on v3

--- a/solution.py
+++ b/solution.py
@@ -89,14 +89,19 @@
     chip = term[R:] + other[R:].astype(F32)
     near = move(chip.astype(BF), CHIP[0])
     half = chip[R:] + near[R:].astype(F32)
-    far = move(half.astype(BF), CHIP[2])
-    return jnp.concatenate([other[:R], near[:R], far], axis=0)
+    return other, near, move(half.astype(BF), CHIP[2])
 
 
 def siblings_beside(other, term):
     chip = (term[R:] + other[R:].astype(F32)).astype(BF)
-    near, far_a, far_b = move(chip[:R], CHIP[0]), move(chip[R:], CHIP[1]), move(chip[R:], CHIP[2])
-    return jnp.concatenate([other[:R], near, (far_a.astype(F32) + far_b.astype(F32)).astype(BF)], axis=0)
+    return other, move(chip[:R], CHIP[0]), move(chip[R:], CHIP[1]), move(chip[R:], CHIP[2])
+
+
+def sibling_sums(other, near, *far):
+    last = far[0][...].astype(F32)
+    for part in far[1:]:
+        last = last + part[...].astype(F32)
+    return jnp.concatenate([other[:R], near[:R], last.astype(BF)], axis=0)
 
 
 def dot(a, b):
@@ -189,6 +194,51 @@
     )(order, start, lo, hi, near_blocks, field, before)
 
 
+def kernel_call(body, shapes, cost, *given):
+    whole = pl.BlockSpec(memory_space=pltpu.VMEM)
+    return pl.pallas_call(
+        body,
+        in_specs=[whole] * len(given),
+        out_specs=[whole] * len(shapes),
+        out_shape=[jax.ShapeDtypeStruct(*shape) for shape in shapes],
+        compiler_params=pltpu.CompilerParams(vmem_limit_bytes=16 * 2**20),
+        cost_estimate=pl.CostEstimate(flops=cost * 10**6, bytes_accessed=2**20, transcendentals=0),
+    )(*given)
+
+
+def start_kernel(has_field, *refs):
+    *given, field, pieces = refs
+    before, given = (given[0], given[1:]) if has_field else (None, given)
+    z, up, down, far, other, near, last, *facts = given
+    facts = facts[:4]
+    sums = sibling_sums(other, near, last)
+    c_terms = jnp.zeros((TERMS, BS), F32)
+    for i, (part, fact) in enumerate(zip((z, up, down, far), facts)):
+        rows = slice(i * ROWS, (i + 1) * ROWS)
+        new = part[...].astype(F32) - dot_t(fact[:TERMS, :], sums)
+        if has_field:
+            new = before[rows, :] + new
+        field[rows, :] = new
+        new = new.astype(BF)
+        for m in range(8):
+            pieces[m, rows, :] = new
+        c_terms = c_terms + dot(fact[TERMS:, :], new)
+    c_terms = c_terms.astype(BF)
+    for m in range(8):
+        pieces[m, RING:, :] = c_terms
+
+
+def finish_kernel(image, right_side, other, near, far_a, far_b, c_left, leaf_inverse, right, k10, k20, k21, resid, z, terms):
+    sums = sibling_sums(other, near, far_a, far_b)
+    left_over = right_side[...] - (image[...] + dot_t(c_left[...], sums))
+    resid[...] = left_over
+    left_over = left_over.astype(BF)
+    for q in range(NBD):
+        rows = slice(q * BS, (q + 1) * BS)
+        z[rows, :] = dot(leaf_inverse[q], left_over[rows, :])
+    terms[...] = fold(dot(right[...], z[...]), (k10[...], k20[...], k21[...]))
+
+
 def leaf(resid, leaf_inverse):
     tiles = resid.astype(BF).reshape(NBD, BS, BS)
     return jnp.einsum("bij,bjn->bin", leaf_inverse, tiles, preferred_element_type=F32).reshape(ROWS, BS)
@@ -218,7 +268,7 @@
     s1, u2, k21 = near_chip[:R], near_chip[R : 2 * R], near_chip[2 * R :, :R]
     half = t2 - dot(m21, s1) + u2 - dot(k21, t1)
     s2 = move(half.astype(BF), CHIP[2])
-    return jnp.concatenate([b0.astype(BF), s1.astype(BF), s2], axis=0), (k10, k20, k21)
+    return (b0.astype(BF), s1.astype(BF), s2), (k10.astype(BF), k20.astype(BF), k21.astype(BF))
 
 
 def fold(terms, mixes):
@@ -246,21 +296,17 @@
     rest = ring(jnp.concatenate([z, terms], axis=0).astype(BF))
     terms = terms + sum(a[ROWS:].astype(F32) for a in rest)
     sums, mixes = first_siblings(add_over(terms, SECOND))
-    sums, order, start, n_pair, n_live = lax.optimization_barrier((sums, order, start, n_pair, n_live))
-    ring_left, ring_c = [a[:TERMS] for a in facts], [a[TERMS:] for a in facts]
-
-    def corrected(field, sums):
-        return field - jnp.concatenate([dot_t(a, sums) for a in ring_left], axis=0)
-
-    field = corrected(jnp.concatenate([z] + [a[:ROWS].astype(F32) for a in rest], axis=0), sums)
+    field = None
+    z_ring = [z] + [a[:ROWS] for a in rest]
+    field_shape, piece_shape = ((RING, BS), F32), ((8, PIECE, BS), BF)
 
     for step in range(ITERS):
-        field_b = field.astype(BF)
-        c_terms = sum(dot(a, field_b[i * ROWS : (i + 1) * ROWS]) for i, a in enumerate(ring_c))
-        piece = jnp.concatenate([field_b, c_terms.astype(BF)], axis=0)
-        pieces = lax.all_to_all(
-            jnp.broadcast_to(piece[None], (8, PIECE, BS)), AXES, 0, 0, tiled=True, axis_index_groups=EIGHTS
+        given = [*z_ring, *sums, *facts]
+        given = given + [order, start, n_pair, n_live] if step == 0 else [field] + given
+        field, pieces = kernel_call(
+            functools.partial(start_kernel, step > 0), (field_shape, piece_shape), 500, *given
         )
+        pieces = lax.all_to_all(pieces, AXES, 0, 0, tiled=True, axis_index_groups=EIGHTS)
         c_parts = lax.dynamic_slice(pieces, (half, RING, 0), (4, TERMS, BS), allow_negative_indices=False)
         c_terms = jnp.sum(c_parts.astype(F32), axis=0)
         c_other = move(c_terms.astype(BF), CORE)
@@ -271,18 +317,18 @@
         x = field[:ROWS]
         image = near(8, order, start, none, n_pair, near_blocks, pieces.reshape(8 * PIECE, BS), x)
         image = near(4, order, start, n_pair, n_live, near_blocks, other.reshape(4 * RING, BS), image)
-        image, c_sums = lax.optimization_barrier((image, c_sums))
-        resid = right_side - (image + dot_t(c_left, c_sums))
-        z = leaf(resid, leaf_inverse)
-        terms = fold(dot(right, z), mixes)
+        resid, z, terms = kernel_call(
+            finish_kernel,
+            (((ROWS, BS), F32), ((ROWS, BS), F32), ((TERMS, BS), F32)),
+            500,
+            image, right_side, *c_sums, c_left, leaf_inverse, right, *mixes,
+        )
         if step < ITERS - 1:
             terms = add_over(terms, FIRST)
-            rest = ring(z.astype(BF))
+            z_ring = [z] + ring(z.astype(BF))
             sums = siblings(add_over(terms, SECOND))
-            z_ring = jnp.concatenate([z] + [a.astype(F32) for a in rest], axis=0)
-            field = corrected(field + z_ring, sums)
         else:
-            sums = siblings(add_over(add_over(terms, FIRST), SECOND))
+            sums = sibling_sums(*siblings(add_over(add_over(terms, FIRST), SECOND)))
             x = x + z - dot_t(left, sums)
     return x, resid
 

time: 276 us -> 258 us (0.935)
  waiting for transfers between devices: 71.7 us -> 37.4 us
  starting transfers between devices: 68.5 us -> 87.4 us
  matrix products: 13.3 us -> 5.33 us
  Pallas kernels: 10.8 us -> 17 us
    ppermute x61, waiting for transfers between devices: 71.7 us -> 37.4 us  [move(): return lax.ppermute(array, AXES, pairs)]
    ppermute x61, starting transfers between devices: 68.5 us -> 87.4 us  [move(): return lax.ppermute(array, AXES, pairs)]
    pallas_call x0 -> x6, Pallas kernels: none -> 6.62 us  [kernel_call(): pl.pallas_call(body, in_specs=[whole] * len(given), out_specs=[whole] * l...]
    dot_general x16 -> x1, matrix products: 5 us -> 0.98 us  [dot_t(): lax.dot_general(a.astype(BF), b.astype(BF), (((0,), (0,)), ((), ())), pre...]
    dot_general x31 -> x7, matrix products: 5.36 us -> 2.01 us  [dot(): return jnp.dot(a.astype(BF), b.astype(BF), preferred_element_type=F32)]
  transfers between devices with their start and end apart: 61 -> 61, of which waited for: 41 -> 31; matrix products, arithmetic and copies ran while one was open for 1% -> 2% of each run, Pallas kernels for 2% -> 4%
where the time goes in v4:
time: 258 us
  blocking collectives  105 us (41%)
  starting transfers between devices  87.4 us (34%)
  waiting for transfers between devices  37.4 us (14%)
  Pallas kernels  17 us (7%)
  matrix products  5.33 us (2%)
  other arithmetic  4.21 us (2%)
    all_to_all x3, blocking collectives, on_device(): lax.all_to_all(pieces, AXES, 0, 0, tiled=True, axis_index_groups=EIGHTS)  105 us
    ppermute x61, starting transfers between devices, move(): return lax.ppermute(array, AXES, pairs)  87.4 us
    ppermute x61, waiting for transfers between devices, move(): return lax.ppermute(array, AXES, pairs)  37.4 us
    pallas_call x6, Pallas kernels, near(): pl.pallas_call(functools.partial(near_kernel, width), in_specs=[small] *...  10.4 us
    pallas_call x6, Pallas kernels, kernel_call(): pl.pallas_call(body, in_specs=[whole] * len(given), out_specs=[whole] * l...  6.62 us
  transfers between devices with their start and end apart: 61, of which 31 were waited for; matrix products, arithmetic and copies ran while one was open for 2% of the time, Pallas kernels for 4%

profile of v4, /device:TPU:0, one launch (start us, length us, event | category | flops | bytes accessed | tf_op | source)
XLA Modules:
  0.0 258.4 jit_solution(17768701175285115323)
XLA Ops:
  1.6 1.2 fusion.76
  5.3 4.0 %collective-permute-start.2 = (bf16[832,128]{1,0:T(8,128)(2,1)S(1)}, bf16[832,128]{1,0:T(8,128)(2,1)S(1)}, u32[]{:S(2)}, u32[]{:S(2)}) collective-permute-start(bf16[832,128]{1,0:T(8,128)(2,1)S(1)} %pad_maximum_fusion.1), channel_id=1, source_target_pairs={{8,0},{9,1},{10,2},{11,3},{12,4},{13,5},{14,6},{15,7},{0,8},{1,9},... | collective-permute-start | bytes 638984 | tf_op jit(solution)/shard_map/ppermute | solution.py:69
  10.4 2.2 collective-permute-start
  13.7 3.2 %collective-permute-start.9 = (bf16[384,512]{1,0:T(8,128)(2,1)S(1)}, bf16[384,512]{1,0:T(8,128)(2,1)S(1)}, u32[]{:S(2)}, u32[]{:S(2)}) collective-permute-start(bf16[384,512]{1,0:T(8,128)(2,1)S(1)} %pad_maximum_fusion.refs_7_.refs_8_), channel_id=1, source_target_pairs={{4,0},{5,1},{6,2},{7,3},{8,4},{9,5},{10,6},{11,7},{12,8},{13,9},{1... | collective-permute-start | bytes 1179656 | tf_op jit(solution)/shard_map/ppermute | solution.py:69
  18.0 3.3 %collective-permute-start.5 = (bf16[320,128]{1,0:T(8,128)(2,1)S(1)}, bf16[320,128]{1,0:T(8,128)(2,1)S(1)}, u32[]{:S(2)}, u32[]{:S(2)}) collective-permute-start(bf16[320,128]{1,0:T(8,128)(2,1)S(1)} %fusion.59), channel_id=1, source_target_pairs={{2,0},{3,1},{0,2},{1,3},{6,4},{7,5},{4,6},{5,7},{10,8},{11,9},{8,1... | collective-permute-start | bytes 245768 | tf_op jit(solution)/shard_map/ppermute | solution.py:69
  21.9 2.6 collective-permute-start.3
  24.5 2.4 collective-permute-done.4
  29.1 1.5 collective-permute-start.7
  31.2 3.3 %collective-permute-start.11 = (bf16[192,512]{1,0:T(8,128)(2,1)S(1)}, bf16[192,512]{1,0:T(8,128)(2,1)S(1)}, u32[]{:S(2)}, u32[]{:S(2)}) collective-permute-start(bf16[192,512]{1,0:T(8,128)(2,1)S(1)} %slice.259), channel_id=1, source_target_pairs={{4,0},{5,1},{6,2},{7,3},{8,4},{9,5},{10,6},{11,7},{12,8},{13,9},{1... | collective-permute-start | bytes 589832 | tf_op jit(solution)/shard_map/ppermute | solution.py:69
  34.7 2.1 collective-permute-start.8
  38.0 1.7 collective-permute-done.8.refs_6_
  39.7 1.2 shard_map.104
  40.9 34.7 %all_to_all.15 = bf16[8,2240,128]{2,1,0:T(8,128)(2,1)S(1)} all-to-all(bf16[8,2240,128]{2,1,0:T(8,128)(2,1)S(1)} %get-tuple-element.22), channel_id=1, replica_groups={{16,20,24,28,32,36,40,44},{17,21,25,29,33,37,41,45},{18,22,26,30,34,38,..., dimensions={0} | all-to-all | bytes 9175040 | tf_op jit(solution)/shard_map/all_to_all | solution.py:309
  75.7 1.2 collective-permute-done.13.other
  77.5 2.4 collective-permute-start.17
  79.9 1.8 collective-permute-start.15
  81.7 1.6 shard_map.105.before
  83.3 1.9 shard_map.106.image
  86.3 1.6 collective-permute-start.23
  89.0 2.2 collective-permute-start.21
  91.9 1.3 collective-permute-done.22
  93.3 1.2 collective-permute-start.26
  95.3 2.4 collective-permute-start.24
  97.7 1.2 collective-permute-done.26
  99.9 1.2 collective-permute-done.27.refs_5_
  102.2 2.3 collective-permute-start.20
  104.5 1.9 collective-permute-start.19
  106.4 1.4 collective-permute-start.18
  107.8 2.6 %collective-permute-start.29 = (bf16[64,128]{1,0:T(8,128)(2,1)S(1)}, bf16[64,128]{1,0:T(8,128)(2,1)S(1)}, u32[]{:S(2)}, u32[]{:S(2)}) collective-permute-start(bf16[64,128]{1,0:T(8,128)(2,1)S(1)} %fusion.15), channel_id=1, source_target_pairs={{96,0},{97,1},{98,2},{99,3},{100,4},{101,5},{102,6},{103,7},{104,8... | collective-permute-start | bytes 49160 | tf_op jit(solution)/shard_map/ppermute | solution.py:69
  111.4 1.4 collective-permute-done.29.refs_7_
  112.8 1.2 shard_map.108
  114.0 34.9 %all_to_all.16 = bf16[8,2240,128]{2,1,0:T(8,128)(2,1)S(1)} all-to-all(bf16[8,2240,128]{2,1,0:T(8,128)(2,1)S(1)} %get-tuple-element.28), channel_id=1, replica_groups={{16,20,24,28,32,36,40,44},{17,21,25,29,33,37,41,45},{18,22,26,30,34,38,..., dimensions={0} | all-to-all | bytes 9175040 | tf_op jit(solution)/shard_map/all_to_all | solution.py:309
  149.1 1.2 collective-permute-done.30.other
  150.7 2.4 collective-permute-start.34
  153.5 1.4 collective-permute-start.32
  154.9 1.6 shard_map.109.before
  156.5 1.9 shard_map.110.image
  159.5 1.5 collective-permute-start.40
  161.7 2.4 collective-permute-start.38
  165.1 1.1 collective-permute-done.39
  166.2 1.1 collective-permute-start.43
  168.3 2.3 collective-permute-start.41
  170.6 1.3 collective-permute-done.43
  172.8 1.2 collective-permute-done.44.refs_5_
  174.1 1.4 collective-permute-start.45
  175.5 2.6 %collective-permute-start.37 = (bf16[512,128]{1,0:T(8,128)(2,1)S(1)}, bf16[512,128]{1,0:T(8,128)(2,1)S(1)}, u32[]{:S(2)}, u32[]{:S(2)}) collective-permute-start(bf16[512,128]{1,0:T(8,128)(2,1)S(1)} %convert_element_type.267), channel_id=1, source_target_pairs={{8,0},{9,1},{10,2},{11,3},{12,4},{13,5},{14,6},{15,7},{0,8},{1,9},... | collective-permute-start | bytes 393224 | tf_op jit(solution)/shard_map/ppermute | solution.py:69
  179.0 2.3 collective-permute-start.35
  181.3 2.0 collective-permute-start.46
  184.2 2.1 collective-permute-done.46.refs_7_
  186.3 1.2 shard_map.112
  187.5 35.1 %all_to_all.17 = bf16[8,2240,128]{2,1,0:T(8,128)(2,1)S(1)} all-to-all(bf16[8,2240,128]{2,1,0:T(8,128)(2,1)S(1)} %get-tuple-element.34), channel_id=1, replica_groups={{16,20,24,28,32,36,40,44},{17,21,25,29,33,37,41,45},{18,22,26,30,34,38,..., dimensions={0} | all-to-all | bytes 9175040 | tf_op jit(solution)/shard_map/all_to_all | solution.py:309
  222.8 1.2 collective-permute-done.47.other
  224.4 2.6 %collective-permute-start.51 = (bf16[64,128]{1,0:T(8,128)(2,1)S(1)}, bf16[64,128]{1,0:T(8,128)(2,1)S(1)}, u32[]{:S(2)}, u32[]{:S(2)}) collective-permute-start(bf16[64,128]{1,0:T(8,128)(2,1)S(1)} %get-tuple-element.67), channel_id=1, source_target_pairs={{96,0},{97,1},{98,2},{99,3},{100,4},{101,5},{102,6},{103,7},{104,8... | collective-permute-start | bytes 49160 | tf_op jit(solution)/shard_map/ppermute | solution.py:69
  228.8 1.6 shard_map.113.before
  230.4 1.9 shard_map.114.image
  233.8 2.2 collective-permute-start.53
  237.0 2.0 collective-permute-done.54
  242.1 2.2 collective-permute-start.55
  244.3 1.4 collective-permute-done.57
  246.5 1.2 collective-permute-done.58
  247.8 2.7 %collective-permute-start.59 = (bf16[128,128]{1,0:T(8,128)(2,1)S(1)}, bf16[128,128]{1,0:T(8,128)(2,1)S(1)}, u32[]{:S(2)}, u32[]{:S(2)}) collective-permute-start(bf16[128,128]{1,0:T(8,128)(2,1)S(1)} %get-tuple-element.44), channel_id=1, source_target_pairs={{32,0},{33,1},{34,2},{35,3},{36,4},{37,5},{38,6},{39,7},{40,8},{41... | collective-permute-start | bytes 98312 | tf_op jit(solution)/shard_map/ppermute | solution.py:69
  250.4 1.9 collective-permute-done.59
  252.3 2.0 collective-permute-start.60
  254.3 3.1 %collective-permute-done.60 = bf16[64,128]{1,0:T(8,128)(2,1)S(1)} collective-permute-done((bf16[64,128]{1,0:T(8,128)(2,1)S(1)}, bf16[64,128]{1,0:T(8,128)(2,1)S(1)}, u32[]{:S(2)}, u32[]{:S(2)}) %collective-permute-start.60) | collective-permute-done | bytes 16416 | tf_op jit(solution)/shard_map/ppermute | solution.py:69
  (166 shorter events, 35.8 us)
Async XLA Ops:
  5.3 12.5 %collective-permute-start.2 = (bf16[832,128]{1,0:T(8,128)(2,1)S(1)}, bf16[832,128]{1,0:T(8,128)(2,1)S(1)}, u32[]{:S(2)}, u32[]{:S(2)}) collective-permute-start(bf16[832,128]{1,0:T(8,128)(2,1)S(1)} %pad_maximum_fusion.1), channel_id=1, source_target_pairs={{8,0},{9,1},{10,2},{11,3},{12,4},{13,5},{14,6},{15,7},{0,8},{1,9},... | collective-permute-start | bytes 638984 | tf_op jit(solution)/shard_map/ppermute | solution.py:69
  9.4 8.5 %collective-permute-start.1 = (bf16[832,128]{1,0:T(8,128)(2,1)S(1)}, bf16[832,128]{1,0:T(8,128)(2,1)S(1)}, u32[]{:S(2)}, u32[]{:S(2)}) collective-permute-start(bf16[832,128]{1,0:T(8,128)(2,1)S(1)} %pad_maximum_fusion.1), channel_id=1, source_target_pairs={{12,0},{13,1},{14,2},{15,3},{0,4},{1,5},{2,6},{3,7},{4,8},{5,9},{6... | collective-permute-start | bytes 638984 | tf_op jit(solution)/shard_map/ppermute | solution.py:69
  10.4 7.5 %collective-permute-start = (bf16[832,128]{1,0:T(8,128)(2,1)S(1)}, bf16[832,128]{1,0:T(8,128)(2,1)S(1)}, u32[]{:S(2)}, u32[]{:S(2)}) collective-permute-start(bf16[832,128]{1,0:T(8,128)(2,1)S(1)} %pad_maximum_fusion.1), channel_id=1, source_target_pairs={{4,0},{5,1},{6,2},{7,3},{8,4},{9,5},{10,6},{11,7},{12,8},{13,9},{1... | collective-permute-start | bytes 638984 | tf_op jit(solution)/shard_map/ppermute | solution.py:69
  13.7 17.3 %collective-permute-start.10 = (bf16[384,512]{1,0:T(8,128)(2,1)S(1)}, bf16[384,512]{1,0:T(8,128)(2,1)S(1)}, u32[]{:S(2)}, u32[]{:S(2)}) collective-permute-start(bf16[384,512]{1,0:T(8,128)(2,1)S(1)} %pad_maximum_fusion.refs_7_.refs_8_), channel_id=1, source_target_pairs={{12,0},{13,1},{14,2},{15,3},{0,4},{1,5},{2,6},{3,7},{4,8},{5,9},{6... | collective-permute-start | bytes 1179656 | tf_op jit(solution)/shard_map/ppermute | solution.py:69
  13.7 17.4 %collective-permute-start.9 = (bf16[384,512]{1,0:T(8,128)(2,1)S(1)}, bf16[384,512]{1,0:T(8,128)(2,1)S(1)}, u32[]{:S(2)}, u32[]{:S(2)}) collective-permute-start(bf16[384,512]{1,0:T(8,128)(2,1)S(1)} %pad_maximum_fusion.refs_7_.refs_8_), channel_id=1, source_target_pairs={{4,0},{5,1},{6,2},{7,3},{8,4},{9,5},{10,6},{11,7},{12,8},{13,9},{1... | collective-permute-start | bytes 1179656 | tf_op jit(solution)/shard_map/ppermute | solution.py:69
  18.0 6.6 %collective-permute-start.5 = (bf16[320,128]{1,0:T(8,128)(2,1)S(1)}, bf16[320,128]{1,0:T(8,128)(2,1)S(1)}, u32[]{:S(2)}, u32[]{:S(2)}) collective-permute-start(bf16[320,128]{1,0:T(8,128)(2,1)S(1)} %fusion.59), channel_id=1, source_target_pairs={{2,0},{3,1},{0,2},{1,3},{6,4},{7,5},{4,6},{5,7},{10,8},{11,9},{8,1... | collective-permute-start | bytes 245768 | tf_op jit(solution)/shard_map/ppermute | solution.py:69
  21.3 5.7 %collective-permute-start.4 = (bf16[320,128]{1,0:T(8,128)(2,1)S(1)}, bf16[320,128]{1,0:T(8,128)(2,1)S(1)}, u32[]{:S(2)}, u32[]{:S(2)}) collective-permute-start(bf16[320,128]{1,0:T(8,128)(2,1)S(1)} %fusion.59), channel_id=1, source_target_pairs={{3,0},{0,1},{1,2},{2,3},{7,4},{4,5},{5,6},{6,7},{11,8},{8,9},{9,10... | collective-permute-start | bytes 245768 | tf_op jit(solution)/shard_map/ppermute | solution.py:69
  21.9 5.0 %collective-permute-start.3 = (bf16[320,128]{1,0:T(8,128)(2,1)S(1)}, bf16[320,128]{1,0:T(8,128)(2,1)S(1)}, u32[]{:S(2)}, u32[]{:S(2)}) collective-permute-start(bf16[320,128]{1,0:T(8,128)(2,1)S(1)} %fusion.59), channel_id=1, source_target_pairs={{1,0},{2,1},{3,2},{0,3},{5,4},{6,5},{7,6},{4,7},{9,8},{10,9},{11,1... | collective-permute-start | bytes 245768 | tf_op jit(solution)/shard_map/ppermute | solution.py:69
  27.0 1.4 collective-permute-start.6
  29.1 5.3 %collective-permute-start.7 = (bf16[192,128]{1,0:T(8,128)(2,1)S(1)}, bf16[192,128]{1,0:T(8,128)(2,1)S(1)}, u32[]{:S(2)}, u32[]{:S(2)}) collective-permute-start(bf16[192,128]{1,0:T(8,128)(2,1)S(1)} %maximum_maximum_fusion), channel_id=1, source_target_pairs={{32,0},{33,1},{34,2},{35,3},{36,4},{37,5},{38,6},{39,7},{40,8},{41... | collective-permute-start | bytes 147464 | tf_op jit(solution)/shard_map/ppermute | solution.py:69
  31.0 7.0 %collective-permute-start.12 = (bf16[192,512]{1,0:T(8,128)(2,1)S(1)}, bf16[192,512]{1,0:T(8,128)(2,1)S(1)}, u32[]{:S(2)}, u32[]{:S(2)}) collective-permute-start(bf16[192,512]{1,0:T(8,128)(2,1)S(1)} %slice.260), channel_id=1, source_target_pairs={{12,0},{13,1},{14,2},{15,3},{0,4},{1,5},{2,6},{3,7},{4,8},{5,9},{6... | collective-permute-start | bytes 589832 | tf_op jit(solution)/shard_map/ppermute | solution.py:69
  31.2 6.5 %collective-permute-start.11 = (bf16[192,512]{1,0:T(8,128)(2,1)S(1)}, bf16[192,512]{1,0:T(8,128)(2,1)S(1)}, u32[]{:S(2)}, u32[]{:S(2)}) collective-permute-start(bf16[192,512]{1,0:T(8,128)(2,1)S(1)} %slice.259), channel_id=1, source_target_pairs={{4,0},{5,1},{6,2},{7,3},{8,4},{9,5},{10,6},{11,7},{12,8},{13,9},{1... | collective-permute-start | bytes 589832 | tf_op jit(solution)/shard_map/ppermute | solution.py:69
  34.7 5.0 %collective-permute-start.8 = (bf16[64,128]{1,0:T(8,128)(2,1)S(1)}, bf16[64,128]{1,0:T(8,128)(2,1)S(1)}, u32[]{:S(2)}, u32[]{:S(2)}) collective-permute-start(bf16[64,128]{1,0:T(8,128)(2,1)S(1)} %fusion.2), channel_id=1, source_target_pairs={{96,0},{97,1},{98,2},{99,3},{100,4},{101,5},{102,6},{103,7},{104,8... | collective-permute-start | bytes 49160 | tf_op jit(solution)/shard_map/ppermute | solution.py:69
  40.8 40.8 %slice-start = ((s8[5242880]{0:T(1024)(128)(4,1)}), s8[4194304]{0:T(1024)(128)(4,1)S(1)}, s32[]{:S(2)}) async-start(s8[5242880]{0:T(1024)(128)(4,1)} %bitcast.29), calls=%async_computation.3 | async-start | bytes 8388608
  40.9 40.8 %slice-start.1 = ((s8[5242880]{0:T(1024)(128)(4,1)}), s8[1048576]{0:T(1024)(128)(4,1)S(1)}, s32[]{:S(2)}) async-start(s8[5242880]{0:T(1024)(128)(4,1)} %bitcast.29), calls=%async_computation.4 | async-start | bytes 2097152
  75.6 1.3 collective-permute-start.13
  77.1 6.2 %collective-permute-start.14 = (bf16[4,2048,128]{2,1,0:T(8,128)(2,1)S(1)}, bf16[4,2048,128]{2,1,0:T(8,128)(2,1)S(1)}, u32[]{:S(2)}, u32[]{:S(2)}) collective-permute-start(bf16[4,2048,128]{2,1,0:T(8,128)(2,1)S(1)} %constant_dynamic-slice_fusion.1), channel_id=1, source_target_pairs={{16,0},{17,1},{18,2},{19,3},{20,4},{21,5},{22,6},{23,7},{24,8},{25... | collective-permute-start | bytes 6291464 | tf_op jit(solution)/shard_map/ppermute | solution.py:69
  77.5 7.7 %collective-permute-start.17 = (bf16[64,128]{1,0:T(8,128)(2,1)S(1)}, bf16[64,128]{1,0:T(8,128)(2,1)S(1)}, u32[]{:S(2)}, u32[]{:S(2)}) collective-permute-start(bf16[64,128]{1,0:T(8,128)(2,1)S(1)} %get-tuple-element.71), channel_id=1, source_target_pairs={{96,0},{97,1},{98,2},{99,3},{100,4},{101,5},{102,6},{103,7},{104,8... | collective-permute-start | bytes 49160 | tf_op jit(solution)/shard_map/ppermute | solution.py:69
  79.9 5.3 %collective-permute-start.16 = (bf16[64,128]{1,0:T(8,128)(2,1)S(1)}, bf16[64,128]{1,0:T(8,128)(2,1)S(1)}, u32[]{:S(2)}, u32[]{:S(2)}) collective-permute-start(bf16[64,128]{1,0:T(8,128)(2,1)S(1)} %get-tuple-element.71), channel_id=1, source_target_pairs={{64,0},{65,1},{66,2},{67,3},{68,4},{69,5},{70,6},{71,7},{72,8},{73... | collective-permute-start | bytes 49160 | tf_op jit(solution)/shard_map/ppermute | solution.py:69
  79.9 5.3 %collective-permute-start.15 = (bf16[64,128]{1,0:T(8,128)(2,1)S(1)}, bf16[64,128]{1,0:T(8,128)(2,1)S(1)}, u32[]{:S(2)}, u32[]{:S(2)}) collective-permute-start(bf16[64,128]{1,0:T(8,128)(2,1)S(1)} %get-tuple-element.72), channel_id=1, source_target_pairs={{32,0},{33,1},{34,2},{35,3},{36,4},{37,5},{38,6},{39,7},{40,8},{41... | collective-permute-start | bytes 49160 | tf_op jit(solution)/shard_map/ppermute | solution.py:69
  86.3 5.6 %collective-permute-start.23 = (bf16[192,128]{1,0:T(8,128)(2,1)S(1)}, bf16[192,128]{1,0:T(8,128)(2,1)S(1)}, u32[]{:S(2)}, u32[]{:S(2)}) collective-permute-start(bf16[192,128]{1,0:T(8,128)(2,1)S(1)} %convert_element_type.250), channel_id=1, source_target_pairs={{8,0},{9,1},{10,2},{11,3},{12,4},{13,5},{14,6},{15,7},{0,8},{1,9},... | collective-permute-start | bytes 147464 | tf_op jit(solution)/shard_map/ppermute | solution.py:69
  87.9 5.3 %collective-permute-start.22 = (bf16[192,128]{1,0:T(8,128)(2,1)S(1)}, bf16[192,128]{1,0:T(8,128)(2,1)S(1)}, u32[]{:S(2)}, u32[]{:S(2)}) collective-permute-start(bf16[192,128]{1,0:T(8,128)(2,1)S(1)} %convert_element_type.250), channel_id=1, source_target_pairs={{12,0},{13,1},{14,2},{15,3},{0,4},{1,5},{2,6},{3,7},{4,8},{5,9},{6... | collective-permute-start | bytes 147464 | tf_op jit(solution)/shard_map/ppermute | solution.py:69
  89.0 4.3 %collective-permute-start.21 = (bf16[192,128]{1,0:T(8,128)(2,1)S(1)}, bf16[192,128]{1,0:T(8,128)(2,1)S(1)}, u32[]{:S(2)}, u32[]{:S(2)}) collective-permute-start(bf16[192,128]{1,0:T(8,128)(2,1)S(1)} %convert_element_type.250), channel_id=1, source_target_pairs={{4,0},{5,1},{6,2},{7,3},{8,4},{9,5},{10,6},{11,7},{12,8},{13,9},{1... | collective-permute-start | bytes 147464 | tf_op jit(solution)/shard_map/ppermute | solution.py:69
  93.3 5.7 %collective-permute-start.26 = (bf16[192,128]{1,0:T(8,128)(2,1)S(1)}, bf16[192,128]{1,0:T(8,128)(2,1)S(1)}, u32[]{:S(2)}, u32[]{:S(2)}) collective-permute-start(bf16[192,128]{1,0:T(8,128)(2,1)S(1)} %fusion.32), channel_id=1, source_target_pairs={{2,0},{3,1},{0,2},{1,3},{6,4},{7,5},{4,6},{5,7},{10,8},{11,9},{8,1... | collective-permute-start | bytes 147464 | tf_op jit(solution)/shard_map/ppermute | solution.py:69
  94.5 5.3 %collective-permute-start.25 = (bf16[192,128]{1,0:T(8,128)(2,1)S(1)}, bf16[192,128]{1,0:T(8,128)(2,1)S(1)}, u32[]{:S(2)}, u32[]{:S(2)}) collective-permute-start(bf16[192,128]{1,0:T(8,128)(2,1)S(1)} %fusion.32), channel_id=1, source_target_pairs={{3,0},{0,1},{1,2},{2,3},{7,4},{4,5},{5,6},{6,7},{11,8},{8,9},{9,10... | collective-permute-start | bytes 147464 | tf_op jit(solution)/shard_map/ppermute | solution.py:69
  95.3 4.5 %collective-permute-start.24 = (bf16[192,128]{1,0:T(8,128)(2,1)S(1)}, bf16[192,128]{1,0:T(8,128)(2,1)S(1)}, u32[]{:S(2)}, u32[]{:S(2)}) collective-permute-start(bf16[192,128]{1,0:T(8,128)(2,1)S(1)} %fusion.32), channel_id=1, source_target_pairs={{1,0},{2,1},{3,2},{0,3},{5,4},{6,5},{7,6},{4,7},{9,8},{10,9},{11,1... | collective-permute-start | bytes 147464 | tf_op jit(solution)/shard_map/ppermute | solution.py:69
  99.9 1.3 collective-permute-start.27
  101.2 6.6 %collective-permute-start.28 = (bf16[128,128]{1,0:T(8,128)(2,1)S(1)}, bf16[128,128]{1,0:T(8,128)(2,1)S(1)}, u32[]{:S(2)}, u32[]{:S(2)}) collective-permute-start(bf16[128,128]{1,0:T(8,128)(2,1)S(1)} %get-tuple-element.52), channel_id=1, source_target_pairs={{32,0},{33,1},{34,2},{35,3},{36,4},{37,5},{38,6},{39,7},{40,8},{41... | collective-permute-start | bytes 98312 | tf_op jit(solution)/shard_map/ppermute | solution.py:69
  102.2 8.2 %collective-permute-start.20 = (bf16[512,128]{1,0:T(8,128)(2,1)S(1)}, bf16[512,128]{1,0:T(8,128)(2,1)S(1)}, u32[]{:S(2)}, u32[]{:S(2)}) collective-permute-start(bf16[512,128]{1,0:T(8,128)(2,1)S(1)} %convert_element_type.249), channel_id=1, source_target_pairs={{8,0},{9,1},{10,2},{11,3},{12,4},{13,5},{14,6},{15,7},{0,8},{1,9},... | collective-permute-start | bytes 393224 | tf_op jit(solution)/shard_map/ppermute | solution.py:69
  104.5 6.2 %collective-permute-start.19 = (bf16[512,128]{1,0:T(8,128)(2,1)S(1)}, bf16[512,128]{1,0:T(8,128)(2,1)S(1)}, u32[]{:S(2)}, u32[]{:S(2)}) collective-permute-start(bf16[512,128]{1,0:T(8,128)(2,1)S(1)} %convert_element_type.249), channel_id=1, source_target_pairs={{12,0},{13,1},{14,2},{15,3},{0,4},{1,5},{2,6},{3,7},{4,8},{5,9},{6... | collective-permute-start | bytes 393224 | tf_op jit(solution)/shard_map/ppermute | solution.py:69
  106.4 5.0 %collective-permute-start.18 = (bf16[512,128]{1,0:T(8,128)(2,1)S(1)}, bf16[512,128]{1,0:T(8,128)(2,1)S(1)}, u32[]{:S(2)}, u32[]{:S(2)}) collective-permute-start(bf16[512,128]{1,0:T(8,128)(2,1)S(1)} %convert_element_type.249), channel_id=1, source_target_pairs={{4,0},{5,1},{6,2},{7,3},{8,4},{9,5},{10,6},{11,7},{12,8},{13,9},{1... | collective-permute-start | bytes 393224 | tf_op jit(solution)/shard_map/ppermute | solution.py:69
  107.8 5.0 %collective-permute-start.29 = (bf16[64,128]{1,0:T(8,128)(2,1)S(1)}, bf16[64,128]{1,0:T(8,128)(2,1)S(1)}, u32[]{:S(2)}, u32[]{:S(2)}) collective-permute-start(bf16[64,128]{1,0:T(8,128)(2,1)S(1)} %fusion.15), channel_id=1, source_target_pairs={{96,0},{97,1},{98,2},{99,3},{100,4},{101,5},{102,6},{103,7},{104,8... | collective-permute-start | bytes 49160 | tf_op jit(solution)/shard_map/ppermute | solution.py:69
  149.0 1.3 collective-permute-start.30
  150.4 6.1 %collective-permute-start.31 = (bf16[4,2048,128]{2,1,0:T(8,128)(2,1)S(1)}, bf16[4,2048,128]{2,1,0:T(8,128)(2,1)S(1)}, u32[]{:S(2)}, u32[]{:S(2)}) collective-permute-start(bf16[4,2048,128]{2,1,0:T(8,128)(2,1)S(1)} %constant_dynamic-slice_fusion), channel_id=1, source_target_pairs={{16,0},{17,1},{18,2},{19,3},{20,4},{21,5},{22,6},{23,7},{24,8},{25... | collective-permute-start | bytes 6291464 | tf_op jit(solution)/shard_map/ppermute | solution.py:69
  150.7 7.7 %collective-permute-start.34 = (bf16[64,128]{1,0:T(8,128)(2,1)S(1)}, bf16[64,128]{1,0:T(8,128)(2,1)S(1)}, u32[]{:S(2)}, u32[]{:S(2)}) collective-permute-start(bf16[64,128]{1,0:T(8,128)(2,1)S(1)} %get-tuple-element.69), channel_id=1, source_target_pairs={{96,0},{97,1},{98,2},{99,3},{100,4},{101,5},{102,6},{103,7},{104,8... | collective-permute-start | bytes 49160 | tf_op jit(solution)/shard_map/ppermute | solution.py:69
  153.1 5.3 %collective-permute-start.33 = (bf16[64,128]{1,0:T(8,128)(2,1)S(1)}, bf16[64,128]{1,0:T(8,128)(2,1)S(1)}, u32[]{:S(2)}, u32[]{:S(2)}) collective-permute-start(bf16[64,128]{1,0:T(8,128)(2,1)S(1)} %get-tuple-element.69), channel_id=1, source_target_pairs={{64,0},{65,1},{66,2},{67,3},{68,4},{69,5},{70,6},{71,7},{72,8},{73... | collective-permute-start | bytes 49160 | tf_op jit(solution)/shard_map/ppermute | solution.py:69
  153.5 4.9 %collective-permute-start.32 = (bf16[64,128]{1,0:T(8,128)(2,1)S(1)}, bf16[64,128]{1,0:T(8,128)(2,1)S(1)}, u32[]{:S(2)}, u32[]{:S(2)}) collective-permute-start(bf16[64,128]{1,0:T(8,128)(2,1)S(1)} %get-tuple-element.70), channel_id=1, source_target_pairs={{32,0},{33,1},{34,2},{35,3},{36,4},{37,5},{38,6},{39,7},{40,8},{41... | collective-permute-start | bytes 49160 | tf_op jit(solution)/shard_map/ppermute | solution.py:69
  159.5 5.6 %collective-permute-start.40 = (bf16[192,128]{1,0:T(8,128)(2,1)S(1)}, bf16[192,128]{1,0:T(8,128)(2,1)S(1)}, u32[]{:S(2)}, u32[]{:S(2)}) collective-permute-start(bf16[192,128]{1,0:T(8,128)(2,1)S(1)} %convert_element_type.268), channel_id=1, source_target_pairs={{8,0},{9,1},{10,2},{11,3},{12,4},{13,5},{14,6},{15,7},{0,8},{1,9},... | collective-permute-start | bytes 147464 | tf_op jit(solution)/shard_map/ppermute | solution.py:69
  160.9 5.3 %collective-permute-start.39 = (bf16[192,128]{1,0:T(8,128)(2,1)S(1)}, bf16[192,128]{1,0:T(8,128)(2,1)S(1)}, u32[]{:S(2)}, u32[]{:S(2)}) collective-permute-start(bf16[192,128]{1,0:T(8,128)(2,1)S(1)} %convert_element_type.268), channel_id=1, source_target_pairs={{12,0},{13,1},{14,2},{15,3},{0,4},{1,5},{2,6},{3,7},{4,8},{5,9},{6... | collective-permute-start | bytes 147464 | tf_op jit(solution)/shard_map/ppermute | solution.py:69
  161.7 4.5 %collective-permute-start.38 = (bf16[192,128]{1,0:T(8,128)(2,1)S(1)}, bf16[192,128]{1,0:T(8,128)(2,1)S(1)}, u32[]{:S(2)}, u32[]{:S(2)}) collective-permute-start(bf16[192,128]{1,0:T(8,128)(2,1)S(1)} %convert_element_type.268), channel_id=1, source_target_pairs={{4,0},{5,1},{6,2},{7,3},{8,4},{9,5},{10,6},{11,7},{12,8},{13,9},{1... | collective-permute-start | bytes 147464 | tf_op jit(solution)/shard_map/ppermute | solution.py:69
  166.2 5.7 %collective-permute-start.43 = (bf16[192,128]{1,0:T(8,128)(2,1)S(1)}, bf16[192,128]{1,0:T(8,128)(2,1)S(1)}, u32[]{:S(2)}, u32[]{:S(2)}) collective-permute-start(bf16[192,128]{1,0:T(8,128)(2,1)S(1)} %fusion.33), channel_id=1, source_target_pairs={{2,0},{3,1},{0,2},{1,3},{6,4},{7,5},{4,6},{5,7},{10,8},{11,9},{8,1... | collective-permute-start | bytes 147464 | tf_op jit(solution)/shard_map/ppermute | solution.py:69
  167.4 5.3 %collective-permute-start.42 = (bf16[192,128]{1,0:T(8,128)(2,1)S(1)}, bf16[192,128]{1,0:T(8,128)(2,1)S(1)}, u32[]{:S(2)}, u32[]{:S(2)}) collective-permute-start(bf16[192,128]{1,0:T(8,128)(2,1)S(1)} %fusion.33), channel_id=1, source_target_pairs={{3,0},{0,1},{1,2},{2,3},{7,4},{4,5},{5,6},{6,7},{11,8},{8,9},{9,10... | collective-permute-start | bytes 147464 | tf_op jit(solution)/shard_map/ppermute | solution.py:69
  168.3 4.4 %collective-permute-start.41 = (bf16[192,128]{1,0:T(8,128)(2,1)S(1)}, bf16[192,128]{1,0:T(8,128)(2,1)S(1)}, u32[]{:S(2)}, u32[]{:S(2)}) collective-permute-start(bf16[192,128]{1,0:T(8,128)(2,1)S(1)} %fusion.33), channel_id=1, source_target_pairs={{1,0},{2,1},{3,2},{0,3},{5,4},{6,5},{7,6},{4,7},{9,8},{10,9},{11,1... | collective-permute-start | bytes 147464 | tf_op jit(solution)/shard_map/ppermute | solution.py:69
  172.7 1.3 collective-permute-start.44
  174.1 7.2 %collective-permute-start.45 = (bf16[128,128]{1,0:T(8,128)(2,1)S(1)}, bf16[128,128]{1,0:T(8,128)(2,1)S(1)}, u32[]{:S(2)}, u32[]{:S(2)}) collective-permute-start(bf16[128,128]{1,0:T(8,128)(2,1)S(1)} %get-tuple-element.48), channel_id=1, source_target_pairs={{32,0},{33,1},{34,2},{35,3},{36,4},{37,5},{38,6},{39,7},{40,8},{41... | collective-permute-start | bytes 98312 | tf_op jit(solution)/shard_map/ppermute | solution.py:69
  175.5 7.8 %collective-permute-start.37 = (bf16[512,128]{1,0:T(8,128)(2,1)S(1)}, bf16[512,128]{1,0:T(8,128)(2,1)S(1)}, u32[]{:S(2)}, u32[]{:S(2)}) collective-permute-start(bf16[512,128]{1,0:T(8,128)(2,1)S(1)} %convert_element_type.267), channel_id=1, source_target_pairs={{8,0},{9,1},{10,2},{11,3},{12,4},{13,5},{14,6},{15,7},{0,8},{1,9},... | collective-permute-start | bytes 393224 | tf_op jit(solution)/shard_map/ppermute | solution.py:69
  178.1 6.2 %collective-permute-start.36 = (bf16[512,128]{1,0:T(8,128)(2,1)S(1)}, bf16[512,128]{1,0:T(8,128)(2,1)S(1)}, u32[]{:S(2)}, u32[]{:S(2)}) collective-permute-start(bf16[512,128]{1,0:T(8,128)(2,1)S(1)} %convert_element_type.267), channel_id=1, source_target_pairs={{12,0},{13,1},{14,2},{15,3},{0,4},{1,5},{2,6},{3,7},{4,8},{5,9},{6... | collective-permute-start | bytes 393224 | tf_op jit(solution)/shard_map/ppermute | solution.py:69
  179.0 5.2 %collective-permute-start.35 = (bf16[512,128]{1,0:T(8,128)(2,1)S(1)}, bf16[512,128]{1,0:T(8,128)(2,1)S(1)}, u32[]{:S(2)}, u32[]{:S(2)}) collective-permute-start(bf16[512,128]{1,0:T(8,128)(2,1)S(1)} %convert_element_type.267), channel_id=1, source_target_pairs={{4,0},{5,1},{6,2},{7,3},{8,4},{9,5},{10,6},{11,7},{12,8},{13,9},{1... | collective-permute-start | bytes 393224 | tf_op jit(solution)/shard_map/ppermute | solution.py:69
  181.3 5.0 %collective-permute-start.46 = (bf16[64,128]{1,0:T(8,128)(2,1)S(1)}, bf16[64,128]{1,0:T(8,128)(2,1)S(1)}, u32[]{:S(2)}, u32[]{:S(2)}) collective-permute-start(bf16[64,128]{1,0:T(8,128)(2,1)S(1)} %fusion.14), channel_id=1, source_target_pairs={{96,0},{97,1},{98,2},{99,3},{100,4},{101,5},{102,6},{103,7},{104,8... | collective-permute-start | bytes 49160 | tf_op jit(solution)/shard_map/ppermute | solution.py:69
  222.7 1.3 collective-permute-start.47
  224.1 6.3 %collective-permute-start.48 = (bf16[4,2048,128]{2,1,0:T(8,128)(2,1)S(1)}, bf16[4,2048,128]{2,1,0:T(8,128)(2,1)S(1)}, u32[]{:S(2)}, u32[]{:S(2)}) collective-permute-start(bf16[4,2048,128]{2,1,0:T(8,128)(2,1)S(1)} %constant_dynamic-slice_fusion.2), channel_id=1, source_target_pairs={{16,0},{17,1},{18,2},{19,3},{20,4},{21,5},{22,6},{23,7},{24,8},{25... | collective-permute-start | bytes 6291464 | tf_op jit(solution)/shard_map/ppermute | solution.py:69
  224.4 7.9 %collective-permute-start.51 = (bf16[64,128]{1,0:T(8,128)(2,1)S(1)}, bf16[64,128]{1,0:T(8,128)(2,1)S(1)}, u32[]{:S(2)}, u32[]{:S(2)}) collective-permute-start(bf16[64,128]{1,0:T(8,128)(2,1)S(1)} %get-tuple-element.67), channel_id=1, source_target_pairs={{96,0},{97,1},{98,2},{99,3},{100,4},{101,5},{102,6},{103,7},{104,8... | collective-permute-start | bytes 49160 | tf_op jit(solution)/shard_map/ppermute | solution.py:69
  227.0 5.3 %collective-permute-start.50 = (bf16[64,128]{1,0:T(8,128)(2,1)S(1)}, bf16[64,128]{1,0:T(8,128)(2,1)S(1)}, u32[]{:S(2)}, u32[]{:S(2)}) collective-permute-start(bf16[64,128]{1,0:T(8,128)(2,1)S(1)} %get-tuple-element.67), channel_id=1, source_target_pairs={{64,0},{65,1},{66,2},{67,3},{68,4},{69,5},{70,6},{71,7},{72,8},{73... | collective-permute-start | bytes 49160 | tf_op jit(solution)/shard_map/ppermute | solution.py:69
  227.9 4.4 %collective-permute-start.49 = (bf16[64,128]{1,0:T(8,128)(2,1)S(1)}, bf16[64,128]{1,0:T(8,128)(2,1)S(1)}, u32[]{:S(2)}, u32[]{:S(2)}) collective-permute-start(bf16[64,128]{1,0:T(8,128)(2,1)S(1)} %get-tuple-element.68), channel_id=1, source_target_pairs={{32,0},{33,1},{34,2},{35,3},{36,4},{37,5},{38,6},{39,7},{40,8},{41... | collective-permute-start | bytes 49160 | tf_op jit(solution)/shard_map/ppermute | solution.py:69
  230.4 27.0 %copy-start.4 = (bf16[3,64,512]{2,1,0:T(8,128)(2,1)S(1)}, bf16[3,64,512]{2,1,0:T(8,128)(2,1)}, u32[]{:S(2)}) copy-start(bf16[3,64,512]{2,1,0:T(8,128)(2,1)} %param.16) | copy-start | bytes 589828
  233.4 5.7 %collective-permute-start.54 = (bf16[192,128]{1,0:T(8,128)(2,1)S(1)}, bf16[192,128]{1,0:T(8,128)(2,1)S(1)}, u32[]{:S(2)}, u32[]{:S(2)}) collective-permute-start(bf16[192,128]{1,0:T(8,128)(2,1)S(1)} %convert_element_type.285), channel_id=1, source_target_pairs={{8,0},{9,1},{10,2},{11,3},{12,4},{13,5},{14,6},{15,7},{0,8},{1,9},... | collective-permute-start | bytes 147464 | tf_op jit(solution)/shard_map/ppermute | solution.py:69
  233.8 5.8 %collective-permute-start.53 = (bf16[192,128]{1,0:T(8,128)(2,1)S(1)}, bf16[192,128]{1,0:T(8,128)(2,1)S(1)}, u32[]{:S(2)}, u32[]{:S(2)}) collective-permute-start(bf16[192,128]{1,0:T(8,128)(2,1)S(1)} %convert_element_type.285), channel_id=1, source_target_pairs={{12,0},{13,1},{14,2},{15,3},{0,4},{1,5},{2,6},{3,7},{4,8},{5,9},{6... | collective-permute-start | bytes 147464 | tf_op jit(solution)/shard_map/ppermute | solution.py:69
  236.0 4.1 %collective-permute-start.52 = (bf16[192,128]{1,0:T(8,128)(2,1)S(1)}, bf16[192,128]{1,0:T(8,128)(2,1)S(1)}, u32[]{:S(2)}, u32[]{:S(2)}) collective-permute-start(bf16[192,128]{1,0:T(8,128)(2,1)S(1)} %convert_element_type.285), channel_id=1, source_target_pairs={{4,0},{5,1},{6,2},{7,3},{8,4},{9,5},{10,6},{11,7},{12,8},{13,9},{1... | collective-permute-start | bytes 147464 | tf_op jit(solution)/shard_map/ppermute | solution.py:69
  240.1 5.7 %collective-permute-start.57 = (bf16[192,128]{1,0:T(8,128)(2,1)S(1)}, bf16[192,128]{1,0:T(8,128)(2,1)S(1)}, u32[]{:S(2)}, u32[]{:S(2)}) collective-permute-start(bf16[192,128]{1,0:T(8,128)(2,1)S(1)} %fusion.34), channel_id=1, source_target_pairs={{2,0},{3,1},{0,2},{1,3},{6,4},{7,5},{4,6},{5,7},{10,8},{11,9},{8,1... | collective-permute-start | bytes 147464 | tf_op jit(solution)/shard_map/ppermute | solution.py:69
  241.1 5.3 %collective-permute-start.56 = (bf16[192,128]{1,0:T(8,128)(2,1)S(1)}, bf16[192,128]{1,0:T(8,128)(2,1)S(1)}, u32[]{:S(2)}, u32[]{:S(2)}) collective-permute-start(bf16[192,128]{1,0:T(8,128)(2,1)S(1)} %fusion.34), channel_id=1, source_target_pairs={{3,0},{0,1},{1,2},{2,3},{7,4},{4,5},{5,6},{6,7},{11,8},{8,9},{9,10... | collective-permute-start | bytes 147464 | tf_op jit(solution)/shard_map/ppermute | solution.py:69
  242.1 4.3 %collective-permute-start.55 = (bf16[192,128]{1,0:T(8,128)(2,1)S(1)}, bf16[192,128]{1,0:T(8,128)(2,1)S(1)}, u32[]{:S(2)}, u32[]{:S(2)}) collective-permute-start(bf16[192,128]{1,0:T(8,128)(2,1)S(1)} %fusion.34), channel_id=1, source_target_pairs={{1,0},{2,1},{3,2},{0,3},{5,4},{6,5},{7,6},{4,7},{9,8},{10,9},{11,1... | collective-permute-start | bytes 147464 | tf_op jit(solution)/shard_map/ppermute | solution.py:69
  246.5 1.3 collective-permute-start.58
  247.8 4.6 %collective-permute-start.59 = (bf16[128,128]{1,0:T(8,128)(2,1)S(1)}, bf16[128,128]{1,0:T(8,128)(2,1)S(1)}, u32[]{:S(2)}, u32[]{:S(2)}) collective-permute-start(bf16[128,128]{1,0:T(8,128)(2,1)S(1)} %get-tuple-element.44), channel_id=1, source_target_pairs={{32,0},{33,1},{34,2},{35,3},{36,4},{37,5},{38,6},{39,7},{40,8},{41... | collective-permute-start | bytes 98312 | tf_op jit(solution)/shard_map/ppermute | solution.py:69
  252.3 5.0 %collective-permute-start.60 = (bf16[64,128]{1,0:T(8,128)(2,1)S(1)}, bf16[64,128]{1,0:T(8,128)(2,1)S(1)}, u32[]{:S(2)}, u32[]{:S(2)}) collective-permute-start(bf16[64,128]{1,0:T(8,128)(2,1)S(1)} %fusion.13), channel_id=1, source_target_pairs={{96,0},{97,1},{98,2},{99,3},{100,4},{101,5},{102,6},{103,7},{104,8... | collective-permute-start | bytes 49160 | tf_op jit(solution)/shard_map/ppermute | solution.py:69
  (5 other events, 31.8 us)

commit v5 on v4

--- a/solution.py
+++ b/solution.py
@@ -84,8 +84,8 @@
     return term + sum(move(sent, pairs).astype(F32) for pairs in steps)
 
 
-def siblings(term):
-    other = move(term.astype(BF), CORE)
+def siblings(term, sent=None):
+    other = move(term.astype(BF) if sent is None else sent, CORE)
     chip = term[R:] + other[R:].astype(F32)
     near = move(chip.astype(BF), CHIP[0])
     half = chip[R:] + near[R:].astype(F32)
@@ -228,6 +228,14 @@
         pieces[m, RING:, :] = c_terms
 
 
+def sum_kernel(count, term, *refs):
+    total = term[...]
+    for part in refs[:count]:
+        total = total + part[...].astype(F32)
+    refs[-2][...] = total
+    refs[-1][...] = total.astype(BF)
+
+
 def finish_kernel(image, right_side, other, near, far_a, far_b, c_left, leaf_inverse, right, k10, k20, k21, resid, z, terms):
     sums = sibling_sums(other, near, far_a, far_b)
     left_over = right_side[...] - (image[...] + dot_t(c_left[...], sums))
@@ -316,7 +324,7 @@
         c_sums = siblings_beside(c_other, c_terms)
         x = field[:ROWS]
         image = near(8, order, start, none, n_pair, near_blocks, pieces.reshape(8 * PIECE, BS), x)
-        image = near(4, order, start, n_pair, n_live, near_blocks, other.reshape(4 * RING, BS), image)
+        image = near(8, order, start, n_pair, n_live, near_blocks, other.reshape(4 * RING, BS), image)
         resid, z, terms = kernel_call(
             finish_kernel,
             (((ROWS, BS), F32), ((ROWS, BS), F32), ((TERMS, BS), F32)),
@@ -325,8 +333,14 @@
         )
         if step < ITERS - 1:
             terms = add_over(terms, FIRST)
-            z_ring = [z] + ring(z.astype(BF))
-            sums = siblings(add_over(terms, SECOND))
+            beside = ring(z.astype(BF))
+            z_ring = [z] + beside
+            term_b = terms.astype(BF)
+            parts = [move(term_b, pairs) for pairs in SECOND]
+            terms, term_b = kernel_call(
+                functools.partial(sum_kernel, 3), (((TERMS, BS), F32), ((TERMS, BS), BF)), 1, terms, *parts, *beside[:2]
+            )
+            sums = siblings(terms, term_b)
         else:
             sums = sibling_sums(*siblings(add_over(add_over(terms, FIRST), SECOND)))
             x = x + z - dot_t(left, sums)

time: 258 us -> 255 us (0.988)
    pallas_call x6 -> x8, Pallas kernels: 6.62 us -> 6.67 us  [kernel_call(): pl.pallas_call(body, in_specs=[whole] * len(given), out_specs=[whole] * l...]
  transfers between devices with their start and end apart: 61 -> 61, of which waited for: 31 -> 33; matrix products, arithmetic and copies ran while one was open for 2% -> 2% of each run, Pallas kernels for 4% -> 4%
where the time goes in v5:
time: 255 us
  blocking collectives  106 us (42%)
  starting transfers between devices  85.9 us (34%)
  waiting for transfers between devices  35.5 us (14%)
  Pallas kernels  16.2 us (6%)
  matrix products  5.32 us (2%)
  other arithmetic  4.11 us (2%)
    all_to_all x3, blocking collectives, on_device(): lax.all_to_all(pieces, AXES, 0, 0, tiled=True, axis_index_groups=EIGHTS)  106 us
    ppermute x61, starting transfers between devices, move(): return lax.ppermute(array, AXES, pairs)  85.9 us
    ppermute x61, waiting for transfers between devices, move(): return lax.ppermute(array, AXES, pairs)  35.5 us
    pallas_call x6, Pallas kernels, near(): pl.pallas_call(functools.partial(near_kernel, width), in_specs=[small] *...  9.5 us
    pallas_call x8, Pallas kernels, kernel_call(): pl.pallas_call(body, in_specs=[whole] * len(given), out_specs=[whole] * l...  6.67 us
  transfers between devices with their start and end apart: 61, of which 33 were waited for; matrix products, arithmetic and copies ran while one was open for 2% of the time, Pallas kernels for 4%

profile of v5, /device:TPU:0, one launch (start us, length us, event | category | flops | bytes accessed | tf_op | source)
XLA Modules:
  0.0 254.8 jit_solution(1041197413632020855)
XLA Ops:
  1.6 1.2 fusion.74
  4.1 1.1 fusion.71
  5.3 4.0 %collective-permute-start.2 = (bf16[832,128]{1,0:T(8,128)(2,1)S(1)}, bf16[832,128]{1,0:T(8,128)(2,1)S(1)}, u32[]{:S(2)}, u32[]{:S(2)}) collective-permute-start(bf16[832,128]{1,0:T(8,128)(2,1)S(1)} %pad_maximum_fusion.1), channel_id=1, source_target_pairs={{8,0},{9,1},{10,2},{11,3},{12,4},{13,5},{14,6},{15,7},{0,8},{1,9},... | collective-permute-start | bytes 638984 | tf_op jit(solution)/shard_map/ppermute | solution.py:69
  10.4 2.2 collective-permute-start
  13.7 3.2 %collective-permute-start.9 = (bf16[384,512]{1,0:T(8,128)(2,1)S(1)}, bf16[384,512]{1,0:T(8,128)(2,1)S(1)}, u32[]{:S(2)}, u32[]{:S(2)}) collective-permute-start(bf16[384,512]{1,0:T(8,128)(2,1)S(1)} %pad_maximum_fusion.refs_7_.refs_8_), channel_id=1, source_target_pairs={{4,0},{5,1},{6,2},{7,3},{8,4},{9,5},{10,6},{11,7},{12,8},{13,9},{1... | collective-permute-start | bytes 1179656 | tf_op jit(solution)/shard_map/ppermute | solution.py:69
  18.0 3.3 %collective-permute-start.5 = (bf16[320,128]{1,0:T(8,128)(2,1)S(1)}, bf16[320,128]{1,0:T(8,128)(2,1)S(1)}, u32[]{:S(2)}, u32[]{:S(2)}) collective-permute-start(bf16[320,128]{1,0:T(8,128)(2,1)S(1)} %fusion.57), channel_id=1, source_target_pairs={{2,0},{3,1},{0,2},{1,3},{6,4},{7,5},{4,6},{5,7},{10,8},{11,9},{8,1... | collective-permute-start | bytes 245768 | tf_op jit(solution)/shard_map/ppermute | solution.py:69
  21.9 2.6 %collective-permute-start.3 = (bf16[320,128]{1,0:T(8,128)(2,1)S(1)}, bf16[320,128]{1,0:T(8,128)(2,1)S(1)}, u32[]{:S(2)}, u32[]{:S(2)}) collective-permute-start(bf16[320,128]{1,0:T(8,128)(2,1)S(1)} %fusion.57), channel_id=1, source_target_pairs={{1,0},{2,1},{3,2},{0,3},{5,4},{6,5},{7,6},{4,7},{9,8},{10,9},{11,1... | collective-permute-start | bytes 245768 | tf_op jit(solution)/shard_map/ppermute | solution.py:69
  24.5 2.4 collective-permute-done.4
  29.1 1.5 collective-permute-start.7
  31.2 3.3 %collective-permute-start.11 = (bf16[192,512]{1,0:T(8,128)(2,1)S(1)}, bf16[192,512]{1,0:T(8,128)(2,1)S(1)}, u32[]{:S(2)}, u32[]{:S(2)}) collective-permute-start(bf16[192,512]{1,0:T(8,128)(2,1)S(1)} %slice.259), channel_id=1, source_target_pairs={{4,0},{5,1},{6,2},{7,3},{8,4},{9,5},{10,6},{11,7},{12,8},{13,9},{1... | collective-permute-start | bytes 589832 | tf_op jit(solution)/shard_map/ppermute | solution.py:69
  34.7 2.1 collective-permute-start.8
  38.0 1.7 collective-permute-done.8.refs_6_
  39.7 1.2 shard_map.104
  40.9 34.7 %all_to_all.15 = bf16[8,2240,128]{2,1,0:T(8,128)(2,1)S(1)} all-to-all(bf16[8,2240,128]{2,1,0:T(8,128)(2,1)S(1)} %get-tuple-element.26), channel_id=1, replica_groups={{16,20,24,28,32,36,40,44},{17,21,25,29,33,37,41,45},{18,22,26,30,34,38,..., dimensions={0} | all-to-all | bytes 9175040 | tf_op jit(solution)/shard_map/all_to_all | solution.py:317
  75.7 1.2 collective-permute-done.13.other
  77.5 2.4 collective-permute-start.17
  79.9 1.8 collective-permute-start.15
  81.7 1.6 shard_map.105.before
  83.3 1.6 shard_map.106.image
  86.2 1.8 collective-permute-start.23
  88.8 2.3 collective-permute-start.21
  91.3 3.2 %collective-permute-start.18 = (bf16[512,128]{1,0:T(8,128)(2,1)S(1)}, bf16[512,128]{1,0:T(8,128)(2,1)S(1)}, u32[]{:S(2)}, u32[]{:S(2)}) collective-permute-start(bf16[512,128]{1,0:T(8,128)(2,1)S(1)} %convert_element_type.225), channel_id=1, source_target_pairs={{4,0},{5,1},{6,2},{7,3},{8,4},{9,5},{10,6},{11,7},{12,8},{13,9},{1... | collective-permute-start | bytes 393224 | tf_op jit(solution)/shard_map/ppermute | solution.py:69
  94.5 1.2 collective-permute-start.26
  96.8 2.2 collective-permute-start.24
  99.0 1.4 collective-permute-done.26.refs_2_
  101.2 1.2 collective-permute-done.27.refs_5_
  102.4 1.1 collective-permute-start.28
  103.5 1.2 collective-permute-start.20
  104.7 1.7 collective-permute-done.28.refs_6_
  106.4 2.7 %collective-permute-start.29 = (bf16[64,128]{1,0:T(8,128)(2,1)S(1)}, bf16[64,128]{1,0:T(8,128)(2,1)S(1)}, u32[]{:S(2)}, u32[]{:S(2)}) collective-permute-start(bf16[64,128]{1,0:T(8,128)(2,1)S(1)} %fusion.15), channel_id=1, source_target_pairs={{96,0},{97,1},{98,2},{99,3},{100,4},{101,5},{102,6},{103,7},{104,8... | collective-permute-start | bytes 49160 | tf_op jit(solution)/shard_map/ppermute | solution.py:69
  110.0 1.5 collective-permute-done.29.refs_7_
  111.5 1.2 shard_map.109
  112.6 35.7 %all_to_all.16 = bf16[8,2240,128]{2,1,0:T(8,128)(2,1)S(1)} all-to-all(bf16[8,2240,128]{2,1,0:T(8,128)(2,1)S(1)} %get-tuple-element.34), channel_id=1, replica_groups={{16,20,24,28,32,36,40,44},{17,21,25,29,33,37,41,45},{18,22,26,30,34,38,..., dimensions={0} | all-to-all | bytes 9175040 | tf_op jit(solution)/shard_map/all_to_all | solution.py:317
  148.5 1.2 collective-permute-done.30.other
  150.1 2.4 collective-permute-start.34
  152.5 1.8 collective-permute-start.32
  154.3 1.6 shard_map.110.before
  155.9 1.6 shard_map.111.image
  159.0 2.6 %collective-permute-start.39 = (bf16[192,128]{1,0:T(8,128)(2,1)S(1)}, bf16[192,128]{1,0:T(8,128)(2,1)S(1)}, u32[]{:S(2)}, u32[]{:S(2)}) collective-permute-start(bf16[192,128]{1,0:T(8,128)(2,1)S(1)} %convert_element_type.240), channel_id=1, source_target_pairs={{12,0},{13,1},{14,2},{15,3},{0,4},{1,5},{2,6},{3,7},{4,8},{5,9},{6... | collective-permute-start | bytes 147464 | tf_op jit(solution)/shard_map/ppermute | solution.py:69
  162.3 1.5 collective-permute-start.36
  163.8 1.8 collective-permute-start.35
  166.8 1.5 collective-permute-start.42
  168.3 1.7 collective-permute-start.41
  170.0 1.4 collective-permute-done.43.refs_2_
  172.5 1.2 collective-permute-done.44.refs_5_
  173.7 2.0 collective-permute-start.45
  175.8 1.2 collective-permute-start.37
  177.8 3.6 %collective-permute-start.46 = (bf16[64,128]{1,0:T(8,128)(2,1)S(1)}, bf16[64,128]{1,0:T(8,128)(2,1)S(1)}, u32[]{:S(2)}, u32[]{:S(2)}) collective-permute-start(bf16[64,128]{1,0:T(8,128)(2,1)S(1)} %fusion.14), channel_id=1, source_target_pairs={{96,0},{97,1},{98,2},{99,3},{100,4},{101,5},{102,6},{103,7},{104,8... | collective-permute-start | bytes 49160 | tf_op jit(solution)/shard_map/ppermute | solution.py:69
  183.1 1.2 shard_map.114
  184.3 35.1 %all_to_all.17 = bf16[8,2240,128]{2,1,0:T(8,128)(2,1)S(1)} all-to-all(bf16[8,2240,128]{2,1,0:T(8,128)(2,1)S(1)} %get-tuple-element.42), channel_id=1, replica_groups={{16,20,24,28,32,36,40,44},{17,21,25,29,33,37,41,45},{18,22,26,30,34,38,..., dimensions={0} | all-to-all | bytes 9175040 | tf_op jit(solution)/shard_map/all_to_all | solution.py:317
  219.5 1.2 collective-permute-done.47.other
  221.4 2.4 collective-permute-start.51
  223.8 1.8 collective-permute-start.49
  225.6 1.6 shard_map.115.before
  227.2 1.6 shard_map.116.image
  231.1 1.8 collective-permute-start.53
  233.0 1.4 collective-permute-start.52
  234.4 1.3 collective-permute-done.54
  239.2 2.2 collective-permute-start.55
  241.4 1.4 collective-permute-done.57
  243.6 1.2 collective-permute-done.58
  245.9 2.9 %collective-permute-done.59 = bf16[128,128]{1,0:T(8,128)(2,1)S(1)} collective-permute-done((bf16[128,128]{1,0:T(8,128)(2,1)S(1)}, bf16[128,128]{1,0:T(8,128)(2,1)S(1)}, u32[]{:S(2)}, u32[]{:S(2)}) %collective-permute-start.59) | collective-permute-done | bytes 32800 | tf_op jit(solution)/shard_map/ppermute | solution.py:69
  248.8 2.6 %collective-permute-start.60 = (bf16[64,128]{1,0:T(8,128)(2,1)S(1)}, bf16[64,128]{1,0:T(8,128)(2,1)S(1)}, u32[]{:S(2)}, u32[]{:S(2)}) collective-permute-start(bf16[64,128]{1,0:T(8,128)(2,1)S(1)} %fusion.13), channel_id=1, source_target_pairs={{96,0},{97,1},{98,2},{99,3},{100,4},{101,5},{102,6},{103,7},{104,8... | collective-permute-start | bytes 49160 | tf_op jit(solution)/shard_map/ppermute | solution.py:69
  251.5 2.4 collective-permute-done.60
  (166 shorter events, 32.7 us)
Async XLA Ops:
  5.3 12.5 %collective-permute-start.2 = (bf16[832,128]{1,0:T(8,128)(2,1)S(1)}, bf16[832,128]{1,0:T(8,128)(2,1)S(1)}, u32[]{:S(2)}, u32[]{:S(2)}) collective-permute-start(bf16[832,128]{1,0:T(8,128)(2,1)S(1)} %pad_maximum_fusion.1), channel_id=1, source_target_pairs={{8,0},{9,1},{10,2},{11,3},{12,4},{13,5},{14,6},{15,7},{0,8},{1,9},... | collective-permute-start | bytes 638984 | tf_op jit(solution)/shard_map/ppermute | solution.py:69
  9.4 8.5 %collective-permute-start.1 = (bf16[832,128]{1,0:T(8,128)(2,1)S(1)}, bf16[832,128]{1,0:T(8,128)(2,1)S(1)}, u32[]{:S(2)}, u32[]{:S(2)}) collective-permute-start(bf16[832,128]{1,0:T(8,128)(2,1)S(1)} %pad_maximum_fusion.1), channel_id=1, source_target_pairs={{12,0},{13,1},{14,2},{15,3},{0,4},{1,5},{2,6},{3,7},{4,8},{5,9},{6... | collective-permute-start | bytes 638984 | tf_op jit(solution)/shard_map/ppermute | solution.py:69
  10.4 7.5 %collective-permute-start = (bf16[832,128]{1,0:T(8,128)(2,1)S(1)}, bf16[832,128]{1,0:T(8,128)(2,1)S(1)}, u32[]{:S(2)}, u32[]{:S(2)}) collective-permute-start(bf16[832,128]{1,0:T(8,128)(2,1)S(1)} %pad_maximum_fusion.1), channel_id=1, source_target_pairs={{4,0},{5,1},{6,2},{7,3},{8,4},{9,5},{10,6},{11,7},{12,8},{13,9},{1... | collective-permute-start | bytes 638984 | tf_op jit(solution)/shard_map/ppermute | solution.py:69
  13.7 17.3 %collective-permute-start.10 = (bf16[384,512]{1,0:T(8,128)(2,1)S(1)}, bf16[384,512]{1,0:T(8,128)(2,1)S(1)}, u32[]{:S(2)}, u32[]{:S(2)}) collective-permute-start(bf16[384,512]{1,0:T(8,128)(2,1)S(1)} %pad_maximum_fusion.refs_7_.refs_8_), channel_id=1, source_target_pairs={{12,0},{13,1},{14,2},{15,3},{0,4},{1,5},{2,6},{3,7},{4,8},{5,9},{6... | collective-permute-start | bytes 1179656 | tf_op jit(solution)/shard_map/ppermute | solution.py:69
  13.7 17.4 %collective-permute-start.9 = (bf16[384,512]{1,0:T(8,128)(2,1)S(1)}, bf16[384,512]{1,0:T(8,128)(2,1)S(1)}, u32[]{:S(2)}, u32[]{:S(2)}) collective-permute-start(bf16[384,512]{1,0:T(8,128)(2,1)S(1)} %pad_maximum_fusion.refs_7_.refs_8_), channel_id=1, source_target_pairs={{4,0},{5,1},{6,2},{7,3},{8,4},{9,5},{10,6},{11,7},{12,8},{13,9},{1... | collective-permute-start | bytes 1179656 | tf_op jit(solution)/shard_map/ppermute | solution.py:69
  18.0 6.6 %collective-permute-start.5 = (bf16[320,128]{1,0:T(8,128)(2,1)S(1)}, bf16[320,128]{1,0:T(8,128)(2,1)S(1)}, u32[]{:S(2)}, u32[]{:S(2)}) collective-permute-start(bf16[320,128]{1,0:T(8,128)(2,1)S(1)} %fusion.57), channel_id=1, source_target_pairs={{2,0},{3,1},{0,2},{1,3},{6,4},{7,5},{4,6},{5,7},{10,8},{11,9},{8,1... | collective-permute-start | bytes 245768 | tf_op jit(solution)/shard_map/ppermute | solution.py:69
  21.3 5.7 %collective-permute-start.4 = (bf16[320,128]{1,0:T(8,128)(2,1)S(1)}, bf16[320,128]{1,0:T(8,128)(2,1)S(1)}, u32[]{:S(2)}, u32[]{:S(2)}) collective-permute-start(bf16[320,128]{1,0:T(8,128)(2,1)S(1)} %fusion.57), channel_id=1, source_target_pairs={{3,0},{0,1},{1,2},{2,3},{7,4},{4,5},{5,6},{6,7},{11,8},{8,9},{9,10... | collective-permute-start | bytes 245768 | tf_op jit(solution)/shard_map/ppermute | solution.py:69
  21.9 5.0 %collective-permute-start.3 = (bf16[320,128]{1,0:T(8,128)(2,1)S(1)}, bf16[320,128]{1,0:T(8,128)(2,1)S(1)}, u32[]{:S(2)}, u32[]{:S(2)}) collective-permute-start(bf16[320,128]{1,0:T(8,128)(2,1)S(1)} %fusion.57), channel_id=1, source_target_pairs={{1,0},{2,1},{3,2},{0,3},{5,4},{6,5},{7,6},{4,7},{9,8},{10,9},{11,1... | collective-permute-start | bytes 245768 | tf_op jit(solution)/shard_map/ppermute | solution.py:69
  27.0 1.4 collective-permute-start.6
  29.1 5.3 %collective-permute-start.7 = (bf16[192,128]{1,0:T(8,128)(2,1)S(1)}, bf16[192,128]{1,0:T(8,128)(2,1)S(1)}, u32[]{:S(2)}, u32[]{:S(2)}) collective-permute-start(bf16[192,128]{1,0:T(8,128)(2,1)S(1)} %maximum_maximum_fusion), channel_id=1, source_target_pairs={{32,0},{33,1},{34,2},{35,3},{36,4},{37,5},{38,6},{39,7},{40,8},{41... | collective-permute-start | bytes 147464 | tf_op jit(solution)/shard_map/ppermute | solution.py:69
  31.0 7.0 %collective-permute-start.12 = (bf16[192,512]{1,0:T(8,128)(2,1)S(1)}, bf16[192,512]{1,0:T(8,128)(2,1)S(1)}, u32[]{:S(2)}, u32[]{:S(2)}) collective-permute-start(bf16[192,512]{1,0:T(8,128)(2,1)S(1)} %slice.260), channel_id=1, source_target_pairs={{12,0},{13,1},{14,2},{15,3},{0,4},{1,5},{2,6},{3,7},{4,8},{5,9},{6... | collective-permute-start | bytes 589832 | tf_op jit(solution)/shard_map/ppermute | solution.py:69
  31.2 6.5 %collective-permute-start.11 = (bf16[192,512]{1,0:T(8,128)(2,1)S(1)}, bf16[192,512]{1,0:T(8,128)(2,1)S(1)}, u32[]{:S(2)}, u32[]{:S(2)}) collective-permute-start(bf16[192,512]{1,0:T(8,128)(2,1)S(1)} %slice.259), channel_id=1, source_target_pairs={{4,0},{5,1},{6,2},{7,3},{8,4},{9,5},{10,6},{11,7},{12,8},{13,9},{1... | collective-permute-start | bytes 589832 | tf_op jit(solution)/shard_map/ppermute | solution.py:69
  34.7 5.0 %collective-permute-start.8 = (bf16[64,128]{1,0:T(8,128)(2,1)S(1)}, bf16[64,128]{1,0:T(8,128)(2,1)S(1)}, u32[]{:S(2)}, u32[]{:S(2)}) collective-permute-start(bf16[64,128]{1,0:T(8,128)(2,1)S(1)} %fusion.2), channel_id=1, source_target_pairs={{96,0},{97,1},{98,2},{99,3},{100,4},{101,5},{102,6},{103,7},{104,8... | collective-permute-start | bytes 49160 | tf_op jit(solution)/shard_map/ppermute | solution.py:69
  40.8 40.8 %slice-start = ((s8[5242880]{0:T(1024)(128)(4,1)}), s8[4194304]{0:T(1024)(128)(4,1)S(1)}, s32[]{:S(2)}) async-start(s8[5242880]{0:T(1024)(128)(4,1)} %bitcast.29), calls=%async_computation.3 | async-start | bytes 8388608
  40.9 40.8 %slice-start.1 = ((s8[5242880]{0:T(1024)(128)(4,1)}), s8[1048576]{0:T(1024)(128)(4,1)S(1)}, s32[]{:S(2)}) async-start(s8[5242880]{0:T(1024)(128)(4,1)} %bitcast.29), calls=%async_computation.4 | async-start | bytes 2097152
  75.6 1.3 collective-permute-start.13
  77.1 6.2 %collective-permute-start.14 = (bf16[4,2048,128]{2,1,0:T(8,128)(2,1)S(1)}, bf16[4,2048,128]{2,1,0:T(8,128)(2,1)S(1)}, u32[]{:S(2)}, u32[]{:S(2)}) collective-permute-start(bf16[4,2048,128]{2,1,0:T(8,128)(2,1)S(1)} %constant_dynamic-slice_fusion.1), channel_id=1, source_target_pairs={{16,0},{17,1},{18,2},{19,3},{20,4},{21,5},{22,6},{23,7},{24,8},{25... | collective-permute-start | bytes 6291464 | tf_op jit(solution)/shard_map/ppermute | solution.py:69
  77.5 7.4 %collective-permute-start.17 = (bf16[64,128]{1,0:T(8,128)(2,1)S(1)}, bf16[64,128]{1,0:T(8,128)(2,1)S(1)}, u32[]{:S(2)}, u32[]{:S(2)}) collective-permute-start(bf16[64,128]{1,0:T(8,128)(2,1)S(1)} %get-tuple-element.79), channel_id=1, source_target_pairs={{96,0},{97,1},{98,2},{99,3},{100,4},{101,5},{102,6},{103,7},{104,8... | collective-permute-start | bytes 49160 | tf_op jit(solution)/shard_map/ppermute | solution.py:69
  79.9 5.2 %collective-permute-start.16 = (bf16[64,128]{1,0:T(8,128)(2,1)S(1)}, bf16[64,128]{1,0:T(8,128)(2,1)S(1)}, u32[]{:S(2)}, u32[]{:S(2)}) collective-permute-start(bf16[64,128]{1,0:T(8,128)(2,1)S(1)} %get-tuple-element.79), channel_id=1, source_target_pairs={{64,0},{65,1},{66,2},{67,3},{68,4},{69,5},{70,6},{71,7},{72,8},{73... | collective-permute-start | bytes 49160 | tf_op jit(solution)/shard_map/ppermute | solution.py:69
  79.9 5.0 %collective-permute-start.15 = (bf16[64,128]{1,0:T(8,128)(2,1)S(1)}, bf16[64,128]{1,0:T(8,128)(2,1)S(1)}, u32[]{:S(2)}, u32[]{:S(2)}) collective-permute-start(bf16[64,128]{1,0:T(8,128)(2,1)S(1)} %get-tuple-element.80), channel_id=1, source_target_pairs={{32,0},{33,1},{34,2},{35,3},{36,4},{37,5},{38,6},{39,7},{40,8},{41... | collective-permute-start | bytes 49160 | tf_op jit(solution)/shard_map/ppermute | solution.py:69
  86.2 8.3 %collective-permute-start.23 = (bf16[192,128]{1,0:T(8,128)(2,1)S(1)}, bf16[192,128]{1,0:T(8,128)(2,1)S(1)}, u32[]{:S(2)}, u32[]{:S(2)}) collective-permute-start(bf16[192,128]{1,0:T(8,128)(2,1)S(1)} %convert_element_type.226), channel_id=1, source_target_pairs={{8,0},{9,1},{10,2},{11,3},{12,4},{13,5},{14,6},{15,7},{0,8},{1,9},... | collective-permute-start | bytes 147464 | tf_op jit(solution)/shard_map/ppermute | solution.py:69
  87.9 6.6 %collective-permute-start.22 = (bf16[192,128]{1,0:T(8,128)(2,1)S(1)}, bf16[192,128]{1,0:T(8,128)(2,1)S(1)}, u32[]{:S(2)}, u32[]{:S(2)}) collective-permute-start(bf16[192,128]{1,0:T(8,128)(2,1)S(1)} %convert_element_type.226), channel_id=1, source_target_pairs={{12,0},{13,1},{14,2},{15,3},{0,4},{1,5},{2,6},{3,7},{4,8},{5,9},{6... | collective-permute-start | bytes 147464 | tf_op jit(solution)/shard_map/ppermute | solution.py:69
  88.8 5.7 %collective-permute-start.21 = (bf16[192,128]{1,0:T(8,128)(2,1)S(1)}, bf16[192,128]{1,0:T(8,128)(2,1)S(1)}, u32[]{:S(2)}, u32[]{:S(2)}) collective-permute-start(bf16[192,128]{1,0:T(8,128)(2,1)S(1)} %convert_element_type.226), channel_id=1, source_target_pairs={{4,0},{5,1},{6,2},{7,3},{8,4},{9,5},{10,6},{11,7},{12,8},{13,9},{1... | collective-permute-start | bytes 147464 | tf_op jit(solution)/shard_map/ppermute | solution.py:69
  91.2 9.9 %collective-permute-start.19 = (bf16[512,128]{1,0:T(8,128)(2,1)S(1)}, bf16[512,128]{1,0:T(8,128)(2,1)S(1)}, u32[]{:S(2)}, u32[]{:S(2)}) collective-permute-start(bf16[512,128]{1,0:T(8,128)(2,1)S(1)} %convert_element_type.225), channel_id=1, source_target_pairs={{12,0},{13,1},{14,2},{15,3},{0,4},{1,5},{2,6},{3,7},{4,8},{5,9},{6... | collective-permute-start | bytes 393224 | tf_op jit(solution)/shard_map/ppermute | solution.py:69
  91.3 9.8 %collective-permute-start.18 = (bf16[512,128]{1,0:T(8,128)(2,1)S(1)}, bf16[512,128]{1,0:T(8,128)(2,1)S(1)}, u32[]{:S(2)}, u32[]{:S(2)}) collective-permute-start(bf16[512,128]{1,0:T(8,128)(2,1)S(1)} %convert_element_type.225), channel_id=1, source_target_pairs={{4,0},{5,1},{6,2},{7,3},{8,4},{9,5},{10,6},{11,7},{12,8},{13,9},{1... | collective-permute-start | bytes 393224 | tf_op jit(solution)/shard_map/ppermute | solution.py:69
  94.5 5.9 %collective-permute-start.26 = (bf16[192,128]{1,0:T(8,128)(2,1)S(1)}, bf16[192,128]{1,0:T(8,128)(2,1)S(1)}, u32[]{:S(2)}, u32[]{:S(2)}) collective-permute-start(bf16[192,128]{1,0:T(8,128)(2,1)S(1)} %get-tuple-element.62), channel_id=1, source_target_pairs={{2,0},{3,1},{0,2},{1,3},{6,4},{7,5},{4,6},{5,7},{10,8},{11,9},{8,1... | collective-permute-start | bytes 147464 | tf_op jit(solution)/shard_map/ppermute | solution.py:69
  95.7 5.3 %collective-permute-start.25 = (bf16[192,128]{1,0:T(8,128)(2,1)S(1)}, bf16[192,128]{1,0:T(8,128)(2,1)S(1)}, u32[]{:S(2)}, u32[]{:S(2)}) collective-permute-start(bf16[192,128]{1,0:T(8,128)(2,1)S(1)} %get-tuple-element.62), channel_id=1, source_target_pairs={{3,0},{0,1},{1,2},{2,3},{7,4},{4,5},{5,6},{6,7},{11,8},{8,9},{9,10... | collective-permute-start | bytes 147464 | tf_op jit(solution)/shard_map/ppermute | solution.py:69
  96.8 4.3 %collective-permute-start.24 = (bf16[192,128]{1,0:T(8,128)(2,1)S(1)}, bf16[192,128]{1,0:T(8,128)(2,1)S(1)}, u32[]{:S(2)}, u32[]{:S(2)}) collective-permute-start(bf16[192,128]{1,0:T(8,128)(2,1)S(1)} %get-tuple-element.62), channel_id=1, source_target_pairs={{1,0},{2,1},{3,2},{0,3},{5,4},{6,5},{7,6},{4,7},{9,8},{10,9},{11,1... | collective-permute-start | bytes 147464 | tf_op jit(solution)/shard_map/ppermute | solution.py:69
  101.1 1.3 collective-permute-start.27
  102.4 4.0 %collective-permute-start.28 = (bf16[128,128]{1,0:T(8,128)(2,1)S(1)}, bf16[128,128]{1,0:T(8,128)(2,1)S(1)}, u32[]{:S(2)}, u32[]{:S(2)}) collective-permute-start(bf16[128,128]{1,0:T(8,128)(2,1)S(1)} %get-tuple-element.60), channel_id=1, source_target_pairs={{32,0},{33,1},{34,2},{35,3},{36,4},{37,5},{38,6},{39,7},{40,8},{41... | collective-permute-start | bytes 98312 | tf_op jit(solution)/shard_map/ppermute | solution.py:69
  103.5 6.5 %collective-permute-start.20 = (bf16[512,128]{1,0:T(8,128)(2,1)S(1)}, bf16[512,128]{1,0:T(8,128)(2,1)S(1)}, u32[]{:S(2)}, u32[]{:S(2)}) collective-permute-start(bf16[512,128]{1,0:T(8,128)(2,1)S(1)} %convert_element_type.225), channel_id=1, source_target_pairs={{8,0},{9,1},{10,2},{11,3},{12,4},{13,5},{14,6},{15,7},{0,8},{1,9},... | collective-permute-start | bytes 393224 | tf_op jit(solution)/shard_map/ppermute | solution.py:69
  106.4 5.0 %collective-permute-start.29 = (bf16[64,128]{1,0:T(8,128)(2,1)S(1)}, bf16[64,128]{1,0:T(8,128)(2,1)S(1)}, u32[]{:S(2)}, u32[]{:S(2)}) collective-permute-start(bf16[64,128]{1,0:T(8,128)(2,1)S(1)} %fusion.15), channel_id=1, source_target_pairs={{96,0},{97,1},{98,2},{99,3},{100,4},{101,5},{102,6},{103,7},{104,8... | collective-permute-start | bytes 49160 | tf_op jit(solution)/shard_map/ppermute | solution.py:69
  148.4 1.3 collective-permute-start.30
  149.8 6.1 %collective-permute-start.31 = (bf16[4,2048,128]{2,1,0:T(8,128)(2,1)S(1)}, bf16[4,2048,128]{2,1,0:T(8,128)(2,1)S(1)}, u32[]{:S(2)}, u32[]{:S(2)}) collective-permute-start(bf16[4,2048,128]{2,1,0:T(8,128)(2,1)S(1)} %constant_dynamic-slice_fusion), channel_id=1, source_target_pairs={{16,0},{17,1},{18,2},{19,3},{20,4},{21,5},{22,6},{23,7},{24,8},{25... | collective-permute-start | bytes 6291464 | tf_op jit(solution)/shard_map/ppermute | solution.py:69
  150.1 7.4 %collective-permute-start.34 = (bf16[64,128]{1,0:T(8,128)(2,1)S(1)}, bf16[64,128]{1,0:T(8,128)(2,1)S(1)}, u32[]{:S(2)}, u32[]{:S(2)}) collective-permute-start(bf16[64,128]{1,0:T(8,128)(2,1)S(1)} %get-tuple-element.77), channel_id=1, source_target_pairs={{96,0},{97,1},{98,2},{99,3},{100,4},{101,5},{102,6},{103,7},{104,8... | collective-permute-start | bytes 49160 | tf_op jit(solution)/shard_map/ppermute | solution.py:69
  152.5 5.2 %collective-permute-start.33 = (bf16[64,128]{1,0:T(8,128)(2,1)S(1)}, bf16[64,128]{1,0:T(8,128)(2,1)S(1)}, u32[]{:S(2)}, u32[]{:S(2)}) collective-permute-start(bf16[64,128]{1,0:T(8,128)(2,1)S(1)} %get-tuple-element.77), channel_id=1, source_target_pairs={{64,0},{65,1},{66,2},{67,3},{68,4},{69,5},{70,6},{71,7},{72,8},{73... | collective-permute-start | bytes 49160 | tf_op jit(solution)/shard_map/ppermute | solution.py:69
  152.5 5.0 %collective-permute-start.32 = (bf16[64,128]{1,0:T(8,128)(2,1)S(1)}, bf16[64,128]{1,0:T(8,128)(2,1)S(1)}, u32[]{:S(2)}, u32[]{:S(2)}) collective-permute-start(bf16[64,128]{1,0:T(8,128)(2,1)S(1)} %get-tuple-element.78), channel_id=1, source_target_pairs={{32,0},{33,1},{34,2},{35,3},{36,4},{37,5},{38,6},{39,7},{40,8},{41... | collective-permute-start | bytes 49160 | tf_op jit(solution)/shard_map/ppermute | solution.py:69
  158.8 6.8 %collective-permute-start.40 = (bf16[192,128]{1,0:T(8,128)(2,1)S(1)}, bf16[192,128]{1,0:T(8,128)(2,1)S(1)}, u32[]{:S(2)}, u32[]{:S(2)}) collective-permute-start(bf16[192,128]{1,0:T(8,128)(2,1)S(1)} %convert_element_type.240), channel_id=1, source_target_pairs={{8,0},{9,1},{10,2},{11,3},{12,4},{13,5},{14,6},{15,7},{0,8},{1,9},... | collective-permute-start | bytes 147464 | tf_op jit(solution)/shard_map/ppermute | solution.py:69
  159.0 6.6 %collective-permute-start.39 = (bf16[192,128]{1,0:T(8,128)(2,1)S(1)}, bf16[192,128]{1,0:T(8,128)(2,1)S(1)}, u32[]{:S(2)}, u32[]{:S(2)}) collective-permute-start(bf16[192,128]{1,0:T(8,128)(2,1)S(1)} %convert_element_type.240), channel_id=1, source_target_pairs={{12,0},{13,1},{14,2},{15,3},{0,4},{1,5},{2,6},{3,7},{4,8},{5,9},{6... | collective-permute-start | bytes 147464 | tf_op jit(solution)/shard_map/ppermute | solution.py:69
  161.7 4.1 %collective-permute-start.38 = (bf16[192,128]{1,0:T(8,128)(2,1)S(1)}, bf16[192,128]{1,0:T(8,128)(2,1)S(1)}, u32[]{:S(2)}, u32[]{:S(2)}) collective-permute-start(bf16[192,128]{1,0:T(8,128)(2,1)S(1)} %convert_element_type.240), channel_id=1, source_target_pairs={{4,0},{5,1},{6,2},{7,3},{8,4},{9,5},{10,6},{11,7},{12,8},{13,9},{1... | collective-permute-start | bytes 147464 | tf_op jit(solution)/shard_map/ppermute | solution.py:69
  162.3 10.1 %collective-permute-start.36 = (bf16[512,128]{1,0:T(8,128)(2,1)S(1)}, bf16[512,128]{1,0:T(8,128)(2,1)S(1)}, u32[]{:S(2)}, u32[]{:S(2)}) collective-permute-start(bf16[512,128]{1,0:T(8,128)(2,1)S(1)} %convert_element_type.239), channel_id=1, source_target_pairs={{12,0},{13,1},{14,2},{15,3},{0,4},{1,5},{2,6},{3,7},{4,8},{5,9},{6... | collective-permute-start | bytes 393224 | tf_op jit(solution)/shard_map/ppermute | solution.py:69
  163.8 8.6 %collective-permute-start.35 = (bf16[512,128]{1,0:T(8,128)(2,1)S(1)}, bf16[512,128]{1,0:T(8,128)(2,1)S(1)}, u32[]{:S(2)}, u32[]{:S(2)}) collective-permute-start(bf16[512,128]{1,0:T(8,128)(2,1)S(1)} %convert_element_type.239), channel_id=1, source_target_pairs={{4,0},{5,1},{6,2},{7,3},{8,4},{9,5},{10,6},{11,7},{12,8},{13,9},{1... | collective-permute-start | bytes 393224 | tf_op jit(solution)/shard_map/ppermute | solution.py:69
  165.8 5.7 %collective-permute-start.43 = (bf16[192,128]{1,0:T(8,128)(2,1)S(1)}, bf16[192,128]{1,0:T(8,128)(2,1)S(1)}, u32[]{:S(2)}, u32[]{:S(2)}) collective-permute-start(bf16[192,128]{1,0:T(8,128)(2,1)S(1)} %get-tuple-element.58), channel_id=1, source_target_pairs={{2,0},{3,1},{0,2},{1,3},{6,4},{7,5},{4,6},{5,7},{10,8},{11,9},{8,1... | collective-permute-start | bytes 147464 | tf_op jit(solution)/shard_map/ppermute | solution.py:69
  166.8 5.3 %collective-permute-start.42 = (bf16[192,128]{1,0:T(8,128)(2,1)S(1)}, bf16[192,128]{1,0:T(8,128)(2,1)S(1)}, u32[]{:S(2)}, u32[]{:S(2)}) collective-permute-start(bf16[192,128]{1,0:T(8,128)(2,1)S(1)} %get-tuple-element.58), channel_id=1, source_target_pairs={{3,0},{0,1},{1,2},{2,3},{7,4},{4,5},{5,6},{6,7},{11,8},{8,9},{9,10... | collective-permute-start | bytes 147464 | tf_op jit(solution)/shard_map/ppermute | solution.py:69
  168.3 4.1 %collective-permute-start.41 = (bf16[192,128]{1,0:T(8,128)(2,1)S(1)}, bf16[192,128]{1,0:T(8,128)(2,1)S(1)}, u32[]{:S(2)}, u32[]{:S(2)}) collective-permute-start(bf16[192,128]{1,0:T(8,128)(2,1)S(1)} %get-tuple-element.58), channel_id=1, source_target_pairs={{1,0},{2,1},{3,2},{0,3},{5,4},{6,5},{7,6},{4,7},{9,8},{10,9},{11,1... | collective-permute-start | bytes 147464 | tf_op jit(solution)/shard_map/ppermute | solution.py:69
  172.4 1.3 collective-permute-start.44
  173.7 4.0 %collective-permute-start.45 = (bf16[128,128]{1,0:T(8,128)(2,1)S(1)}, bf16[128,128]{1,0:T(8,128)(2,1)S(1)}, u32[]{:S(2)}, u32[]{:S(2)}) collective-permute-start(bf16[128,128]{1,0:T(8,128)(2,1)S(1)} %get-tuple-element.56), channel_id=1, source_target_pairs={{32,0},{33,1},{34,2},{35,3},{36,4},{37,5},{38,6},{39,7},{40,8},{41... | collective-permute-start | bytes 98312 | tf_op jit(solution)/shard_map/ppermute | solution.py:69
  175.8 6.5 %collective-permute-start.37 = (bf16[512,128]{1,0:T(8,128)(2,1)S(1)}, bf16[512,128]{1,0:T(8,128)(2,1)S(1)}, u32[]{:S(2)}, u32[]{:S(2)}) collective-permute-start(bf16[512,128]{1,0:T(8,128)(2,1)S(1)} %convert_element_type.239), channel_id=1, source_target_pairs={{8,0},{9,1},{10,2},{11,3},{12,4},{13,5},{14,6},{15,7},{0,8},{1,9},... | collective-permute-start | bytes 393224 | tf_op jit(solution)/shard_map/ppermute | solution.py:69
  177.8 5.3 %collective-permute-start.46 = (bf16[64,128]{1,0:T(8,128)(2,1)S(1)}, bf16[64,128]{1,0:T(8,128)(2,1)S(1)}, u32[]{:S(2)}, u32[]{:S(2)}) collective-permute-start(bf16[64,128]{1,0:T(8,128)(2,1)S(1)} %fusion.14), channel_id=1, source_target_pairs={{96,0},{97,1},{98,2},{99,3},{100,4},{101,5},{102,6},{103,7},{104,8... | collective-permute-start | bytes 49160 | tf_op jit(solution)/shard_map/ppermute | solution.py:69
  219.4 1.3 collective-permute-start.47
  220.9 6.3 %collective-permute-start.48 = (bf16[4,2048,128]{2,1,0:T(8,128)(2,1)S(1)}, bf16[4,2048,128]{2,1,0:T(8,128)(2,1)S(1)}, u32[]{:S(2)}, u32[]{:S(2)}) collective-permute-start(bf16[4,2048,128]{2,1,0:T(8,128)(2,1)S(1)} %constant_dynamic-slice_fusion.2), channel_id=1, source_target_pairs={{16,0},{17,1},{18,2},{19,3},{20,4},{21,5},{22,6},{23,7},{24,8},{25... | collective-permute-start | bytes 6291464 | tf_op jit(solution)/shard_map/ppermute | solution.py:69
  221.4 7.4 %collective-permute-start.51 = (bf16[64,128]{1,0:T(8,128)(2,1)S(1)}, bf16[64,128]{1,0:T(8,128)(2,1)S(1)}, u32[]{:S(2)}, u32[]{:S(2)}) collective-permute-start(bf16[64,128]{1,0:T(8,128)(2,1)S(1)} %get-tuple-element.75), channel_id=1, source_target_pairs={{96,0},{97,1},{98,2},{99,3},{100,4},{101,5},{102,6},{103,7},{104,8... | collective-permute-start | bytes 49160 | tf_op jit(solution)/shard_map/ppermute | solution.py:69
  223.8 5.2 %collective-permute-start.50 = (bf16[64,128]{1,0:T(8,128)(2,1)S(1)}, bf16[64,128]{1,0:T(8,128)(2,1)S(1)}, u32[]{:S(2)}, u32[]{:S(2)}) collective-permute-start(bf16[64,128]{1,0:T(8,128)(2,1)S(1)} %get-tuple-element.75), channel_id=1, source_target_pairs={{64,0},{65,1},{66,2},{67,3},{68,4},{69,5},{70,6},{71,7},{72,8},{73... | collective-permute-start | bytes 49160 | tf_op jit(solution)/shard_map/ppermute | solution.py:69
  223.8 5.0 %collective-permute-start.49 = (bf16[64,128]{1,0:T(8,128)(2,1)S(1)}, bf16[64,128]{1,0:T(8,128)(2,1)S(1)}, u32[]{:S(2)}, u32[]{:S(2)}) collective-permute-start(bf16[64,128]{1,0:T(8,128)(2,1)S(1)} %get-tuple-element.76), channel_id=1, source_target_pairs={{32,0},{33,1},{34,2},{35,3},{36,4},{37,5},{38,6},{39,7},{40,8},{41... | collective-permute-start | bytes 49160 | tf_op jit(solution)/shard_map/ppermute | solution.py:69
  227.2 26.7 %copy-start.4 = (bf16[3,64,512]{2,1,0:T(8,128)(2,1)S(1)}, bf16[3,64,512]{2,1,0:T(8,128)(2,1)}, u32[]{:S(2)}) copy-start(bf16[3,64,512]{2,1,0:T(8,128)(2,1)} %param.16) | copy-start | bytes 589828
  230.1 5.6 %collective-permute-start.54 = (bf16[192,128]{1,0:T(8,128)(2,1)S(1)}, bf16[192,128]{1,0:T(8,128)(2,1)S(1)}, u32[]{:S(2)}, u32[]{:S(2)}) collective-permute-start(bf16[192,128]{1,0:T(8,128)(2,1)S(1)} %convert_element_type.253), channel_id=1, source_target_pairs={{8,0},{9,1},{10,2},{11,3},{12,4},{13,5},{14,6},{15,7},{0,8},{1,9},... | collective-permute-start | bytes 147464 | tf_op jit(solution)/shard_map/ppermute | solution.py:69
  231.1 5.3 %collective-permute-start.53 = (bf16[192,128]{1,0:T(8,128)(2,1)S(1)}, bf16[192,128]{1,0:T(8,128)(2,1)S(1)}, u32[]{:S(2)}, u32[]{:S(2)}) collective-permute-start(bf16[192,128]{1,0:T(8,128)(2,1)S(1)} %convert_element_type.253), channel_id=1, source_target_pairs={{12,0},{13,1},{14,2},{15,3},{0,4},{1,5},{2,6},{3,7},{4,8},{5,9},{6... | collective-permute-start | bytes 147464 | tf_op jit(solution)/shard_map/ppermute | solution.py:69
  233.0 4.1 %collective-permute-start.52 = (bf16[192,128]{1,0:T(8,128)(2,1)S(1)}, bf16[192,128]{1,0:T(8,128)(2,1)S(1)}, u32[]{:S(2)}, u32[]{:S(2)}) collective-permute-start(bf16[192,128]{1,0:T(8,128)(2,1)S(1)} %convert_element_type.253), channel_id=1, source_target_pairs={{4,0},{5,1},{6,2},{7,3},{8,4},{9,5},{10,6},{11,7},{12,8},{13,9},{1... | collective-permute-start | bytes 147464 | tf_op jit(solution)/shard_map/ppermute | solution.py:69
  237.1 5.7 %collective-permute-start.57 = (bf16[192,128]{1,0:T(8,128)(2,1)S(1)}, bf16[192,128]{1,0:T(8,128)(2,1)S(1)}, u32[]{:S(2)}, u32[]{:S(2)}) collective-permute-start(bf16[192,128]{1,0:T(8,128)(2,1)S(1)} %fusion.32), channel_id=1, source_target_pairs={{2,0},{3,1},{0,2},{1,3},{6,4},{7,5},{4,6},{5,7},{10,8},{11,9},{8,1... | collective-permute-start | bytes 147464 | tf_op jit(solution)/shard_map/ppermute | solution.py:69
  238.1 5.3 %collective-permute-start.56 = (bf16[192,128]{1,0:T(8,128)(2,1)S(1)}, bf16[192,128]{1,0:T(8,128)(2,1)S(1)}, u32[]{:S(2)}, u32[]{:S(2)}) collective-permute-start(bf16[192,128]{1,0:T(8,128)(2,1)S(1)} %fusion.32), channel_id=1, source_target_pairs={{3,0},{0,1},{1,2},{2,3},{7,4},{4,5},{5,6},{6,7},{11,8},{8,9},{9,10... | collective-permute-start | bytes 147464 | tf_op jit(solution)/shard_map/ppermute | solution.py:69
  239.2 4.3 %collective-permute-start.55 = (bf16[192,128]{1,0:T(8,128)(2,1)S(1)}, bf16[192,128]{1,0:T(8,128)(2,1)S(1)}, u32[]{:S(2)}, u32[]{:S(2)}) collective-permute-start(bf16[192,128]{1,0:T(8,128)(2,1)S(1)} %fusion.32), channel_id=1, source_target_pairs={{1,0},{2,1},{3,2},{0,3},{5,4},{6,5},{7,6},{4,7},{9,8},{10,9},{11,1... | collective-permute-start | bytes 147464 | tf_op jit(solution)/shard_map/ppermute | solution.py:69
  243.5 1.3 collective-permute-start.58
  244.8 4.0 %collective-permute-start.59 = (bf16[128,128]{1,0:T(8,128)(2,1)S(1)}, bf16[128,128]{1,0:T(8,128)(2,1)S(1)}, u32[]{:S(2)}, u32[]{:S(2)}) collective-permute-start(bf16[128,128]{1,0:T(8,128)(2,1)S(1)} %get-tuple-element.52), channel_id=1, source_target_pairs={{32,0},{33,1},{34,2},{35,3},{36,4},{37,5},{38,6},{39,7},{40,8},{41... | collective-permute-start | bytes 98312 | tf_op jit(solution)/shard_map/ppermute | solution.py:69
  248.8 5.0 %collective-permute-start.60 = (bf16[64,128]{1,0:T(8,128)(2,1)S(1)}, bf16[64,128]{1,0:T(8,128)(2,1)S(1)}, u32[]{:S(2)}, u32[]{:S(2)}) collective-permute-start(bf16[64,128]{1,0:T(8,128)(2,1)S(1)} %fusion.13), channel_id=1, source_target_pairs={{96,0},{97,1},{98,2},{99,3},{100,4},{101,5},{102,6},{103,7},{104,8... | collective-permute-start | bytes 49160 | tf_op jit(solution)/shard_map/ppermute | solution.py:69
  (5 other events, 31.3 us)

commit v6 on v5

--- a/solution.py
+++ b/solution.py
@@ -248,8 +248,9 @@
 
 
 def leaf(resid, leaf_inverse):
-    tiles = resid.astype(BF).reshape(NBD, BS, BS)
-    return jnp.einsum("bij,bjn->bin", leaf_inverse, tiles, preferred_element_type=F32).reshape(ROWS, BS)
+    tiles = resid.reshape(NBD, BS, BS)
+    image = jnp.einsum("bij,bjn->bin", leaf_inverse.astype(F32), tiles, precision=lax.Precision.DEFAULT)
+    return image.reshape(ROWS, BS)
 
 
 def first_terms(z, right, left):

time: 255 us -> 255 us (level)
  transfers between devices with their start and end apart: 61 -> 61, of which waited for: 33 -> 33; matrix products, arithmetic and copies ran while one was open for 2% -> 2% of each run, Pallas kernels for 4% -> 3%
where the time goes in v6:
time: 255 us; the launch traced here: 254 us
  blocking collectives  105 us (41%)
  starting transfers between devices  86.7 us (34%)
  waiting for transfers between devices  36.1 us (14%)
  Pallas kernels  14.7 us (6%)
  matrix products  5.44 us (2%)
  other arithmetic  3.82 us (1%)
    all_to_all x3, blocking collectives, on_device(): lax.all_to_all(pieces, AXES, 0, 0, tiled=True, axis_index_groups=EIGHTS)  105 us
    ppermute x61, starting transfers between devices, move(): return lax.ppermute(array, AXES, pairs)  86.7 us
    ppermute x61, waiting for transfers between devices, move(): return lax.ppermute(array, AXES, pairs)  36.1 us
    pallas_call x6, Pallas kernels, near(): pl.pallas_call(functools.partial(near_kernel, width), in_specs=[small] *...  8.08 us
    pallas_call x8, Pallas kernels, kernel_call(): pl.pallas_call(body, in_specs=[whole] * len(given), out_specs=[whole] * l...  6.66 us
  transfers between devices with their start and end apart: 61, of which 33 were waited for; matrix products, arithmetic and copies ran while one was open for 2% of the time, Pallas kernels for 3%

profile of v6, /device:TPU:0, one launch (start us, length us, event | category | flops | bytes accessed | tf_op | source)
XLA Modules:
  0.0 254.3 jit_solution(1157307357320887430)
XLA Ops:
  0.6 1.3 fusion.74
  2.0 1.2 fusion.73
  3.2 1.1 fusion.71
  4.5 4.0 %collective-permute-start.2 = (bf16[832,128]{1,0:T(8,128)(2,1)S(1)}, bf16[832,128]{1,0:T(8,128)(2,1)S(1)}, u32[]{:S(2)}, u32[]{:S(2)}) collective-permute-start(bf16[832,128]{1,0:T(8,128)(2,1)S(1)} %pad_maximum_fusion.1), channel_id=1, source_target_pairs={{8,0},{9,1},{10,2},{11,3},{12,4},{13,5},{14,6},{15,7},{0,8},{1,9},... | collective-permute-start | bytes 638984 | tf_op jit(solution)/shard_map/ppermute | solution.py:69
  9.5 2.2 collective-permute-start
  12.9 3.2 %collective-permute-start.9 = (bf16[384,512]{1,0:T(8,128)(2,1)S(1)}, bf16[384,512]{1,0:T(8,128)(2,1)S(1)}, u32[]{:S(2)}, u32[]{:S(2)}) collective-permute-start(bf16[384,512]{1,0:T(8,128)(2,1)S(1)} %pad_maximum_fusion.refs_7_.refs_8_), channel_id=1, source_target_pairs={{4,0},{5,1},{6,2},{7,3},{8,4},{9,5},{10,6},{11,7},{12,8},{13,9},{1... | collective-permute-start | bytes 1179656 | tf_op jit(solution)/shard_map/ppermute | solution.py:69
  17.1 3.3 %collective-permute-start.5 = (bf16[320,128]{1,0:T(8,128)(2,1)S(1)}, bf16[320,128]{1,0:T(8,128)(2,1)S(1)}, u32[]{:S(2)}, u32[]{:S(2)}) collective-permute-start(bf16[320,128]{1,0:T(8,128)(2,1)S(1)} %fusion.57), channel_id=1, source_target_pairs={{2,0},{3,1},{0,2},{1,3},{6,4},{7,5},{4,6},{5,7},{10,8},{11,9},{8,1... | collective-permute-start | bytes 245768 | tf_op jit(solution)/shard_map/ppermute | solution.py:69
  21.1 2.6 %collective-permute-start.3 = (bf16[320,128]{1,0:T(8,128)(2,1)S(1)}, bf16[320,128]{1,0:T(8,128)(2,1)S(1)}, u32[]{:S(2)}, u32[]{:S(2)}) collective-permute-start(bf16[320,128]{1,0:T(8,128)(2,1)S(1)} %fusion.57), channel_id=1, source_target_pairs={{1,0},{2,1},{3,2},{0,3},{5,4},{6,5},{7,6},{4,7},{9,8},{10,9},{11,1... | collective-permute-start | bytes 245768 | tf_op jit(solution)/shard_map/ppermute | solution.py:69
  24.3 1.7 collective-permute-done.4
  28.2 1.5 collective-permute-start.7
  30.3 3.3 %collective-permute-start.11 = (bf16[192,512]{1,0:T(8,128)(2,1)S(1)}, bf16[192,512]{1,0:T(8,128)(2,1)S(1)}, u32[]{:S(2)}, u32[]{:S(2)}) collective-permute-start(bf16[192,512]{1,0:T(8,128)(2,1)S(1)} %slice.259), channel_id=1, source_target_pairs={{4,0},{5,1},{6,2},{7,3},{8,4},{9,5},{10,6},{11,7},{12,8},{13,9},{1... | collective-permute-start | bytes 589832 | tf_op jit(solution)/shard_map/ppermute | solution.py:69
  33.8 2.1 collective-permute-start.8
  37.1 1.7 collective-permute-done.8.refs_6_
  38.8 1.2 shard_map.104
  40.0 34.7 %all_to_all.15 = bf16[8,2240,128]{2,1,0:T(8,128)(2,1)S(1)} all-to-all(bf16[8,2240,128]{2,1,0:T(8,128)(2,1)S(1)} %get-tuple-element.26), channel_id=1, replica_groups={{16,20,24,28,32,36,40,44},{17,21,25,29,33,37,41,45},{18,22,26,30,34,38,..., dimensions={0} | all-to-all | bytes 9175040 | tf_op jit(solution)/shard_map/all_to_all | solution.py:318
  74.9 1.2 collective-permute-done.13.other
  76.6 2.4 collective-permute-start.17
  79.0 1.8 collective-permute-start.15
  80.8 1.6 shard_map.105.before
  82.4 1.1 shard_map.106.image
  85.3 1.8 collective-permute-start.23
  88.0 2.3 collective-permute-start.21
  90.4 3.2 %collective-permute-start.18 = (bf16[512,128]{1,0:T(8,128)(2,1)S(1)}, bf16[512,128]{1,0:T(8,128)(2,1)S(1)}, u32[]{:S(2)}, u32[]{:S(2)}) collective-permute-start(bf16[512,128]{1,0:T(8,128)(2,1)S(1)} %convert_element_type.222), channel_id=1, source_target_pairs={{4,0},{5,1},{6,2},{7,3},{8,4},{9,5},{10,6},{11,7},{12,8},{13,9},{1... | collective-permute-start | bytes 393224 | tf_op jit(solution)/shard_map/ppermute | solution.py:69
  93.7 1.2 collective-permute-start.26
  95.9 2.2 collective-permute-start.24
  98.1 1.4 collective-permute-done.26.refs_2_
  100.3 1.2 collective-permute-done.27.refs_5_
  102.5 1.9 collective-permute-start.20
  104.3 1.2 collective-permute-done.28.refs_6_
  105.6 3.2 %collective-permute-start.29 = (bf16[64,128]{1,0:T(8,128)(2,1)S(1)}, bf16[64,128]{1,0:T(8,128)(2,1)S(1)}, u32[]{:S(2)}, u32[]{:S(2)}) collective-permute-start(bf16[64,128]{1,0:T(8,128)(2,1)S(1)} %fusion.15), channel_id=1, source_target_pairs={{96,0},{97,1},{98,2},{99,3},{100,4},{101,5},{102,6},{103,7},{104,8... | collective-permute-start | bytes 49160 | tf_op jit(solution)/shard_map/ppermute | solution.py:69
  109.0 1.6 collective-permute-done.29.refs_7_
  110.6 1.2 shard_map.109
  111.8 35.7 %all_to_all.16 = bf16[8,2240,128]{2,1,0:T(8,128)(2,1)S(1)} all-to-all(bf16[8,2240,128]{2,1,0:T(8,128)(2,1)S(1)} %get-tuple-element.34), channel_id=1, replica_groups={{16,20,24,28,32,36,40,44},{17,21,25,29,33,37,41,45},{18,22,26,30,34,38,..., dimensions={0} | all-to-all | bytes 9175040 | tf_op jit(solution)/shard_map/all_to_all | solution.py:318
  147.6 1.2 collective-permute-done.30.other
  149.2 2.4 collective-permute-start.34
  151.9 1.5 collective-permute-start.32
  153.4 1.6 shard_map.110.before
  158.6 2.6 %collective-permute-start.39 = (bf16[192,128]{1,0:T(8,128)(2,1)S(1)}, bf16[192,128]{1,0:T(8,128)(2,1)S(1)}, u32[]{:S(2)}, u32[]{:S(2)}) collective-permute-start(bf16[192,128]{1,0:T(8,128)(2,1)S(1)} %convert_element_type.237), channel_id=1, source_target_pairs={{12,0},{13,1},{14,2},{15,3},{0,4},{1,5},{2,6},{3,7},{4,8},{5,9},{6... | collective-permute-start | bytes 147464 | tf_op jit(solution)/shard_map/ppermute | solution.py:69
  161.8 1.5 collective-permute-start.36
  163.3 1.8 collective-permute-start.35
  166.3 2.1 collective-permute-start.42
  168.4 1.1 collective-permute-start.41
  169.6 1.4 collective-permute-done.43.refs_2_
  172.6 1.2 collective-permute-done.44.refs_5_
  174.8 2.4 collective-permute-start.37
  177.9 2.5 collective-permute-start.46
  181.3 1.6 collective-permute-done.46.refs_7_
  182.9 1.2 shard_map.114
  184.1 34.8 %all_to_all.17 = bf16[8,2240,128]{2,1,0:T(8,128)(2,1)S(1)} all-to-all(bf16[8,2240,128]{2,1,0:T(8,128)(2,1)S(1)} %get-tuple-element.42), channel_id=1, replica_groups={{16,20,24,28,32,36,40,44},{17,21,25,29,33,37,41,45},{18,22,26,30,34,38,..., dimensions={0} | all-to-all | bytes 9175040 | tf_op jit(solution)/shard_map/all_to_all | solution.py:318
  219.0 1.2 collective-permute-done.47.other
  220.9 2.4 collective-permute-start.51
  223.3 1.8 collective-permute-start.49
  225.1 1.6 shard_map.115.before
  226.7 1.1 shard_map.116.image
  229.6 1.2 collective-permute-start.54
  230.8 1.6 collective-permute-start.53
  232.4 1.6 collective-permute-start.52
  234.1 1.2 collective-permute-done.54
  238.6 2.2 collective-permute-start.55
  240.8 1.4 collective-permute-done.57
  243.0 1.2 collective-permute-done.58
  245.2 3.1 %collective-permute-done.59 = bf16[128,128]{1,0:T(8,128)(2,1)S(1)} collective-permute-done((bf16[128,128]{1,0:T(8,128)(2,1)S(1)}, bf16[128,128]{1,0:T(8,128)(2,1)S(1)}, u32[]{:S(2)}, u32[]{:S(2)}) %collective-permute-start.59) | collective-permute-done | bytes 32800 | tf_op jit(solution)/shard_map/ppermute | solution.py:69
  248.2 2.9 %collective-permute-start.60 = (bf16[64,128]{1,0:T(8,128)(2,1)S(1)}, bf16[64,128]{1,0:T(8,128)(2,1)S(1)}, u32[]{:S(2)}, u32[]{:S(2)}) collective-permute-start(bf16[64,128]{1,0:T(8,128)(2,1)S(1)} %fusion.13), channel_id=1, source_target_pairs={{96,0},{97,1},{98,2},{99,3},{100,4},{101,5},{102,6},{103,7},{104,8... | collective-permute-start | bytes 49160 | tf_op jit(solution)/shard_map/ppermute | solution.py:69
  251.2 2.1 collective-permute-done.60
  (163 shorter events, 34.0 us)
Async XLA Ops:
  4.5 12.5 %collective-permute-start.2 = (bf16[832,128]{1,0:T(8,128)(2,1)S(1)}, bf16[832,128]{1,0:T(8,128)(2,1)S(1)}, u32[]{:S(2)}, u32[]{:S(2)}) collective-permute-start(bf16[832,128]{1,0:T(8,128)(2,1)S(1)} %pad_maximum_fusion.1), channel_id=1, source_target_pairs={{8,0},{9,1},{10,2},{11,3},{12,4},{13,5},{14,6},{15,7},{0,8},{1,9},... | collective-permute-start | bytes 638984 | tf_op jit(solution)/shard_map/ppermute | solution.py:69
  8.5 8.5 %collective-permute-start.1 = (bf16[832,128]{1,0:T(8,128)(2,1)S(1)}, bf16[832,128]{1,0:T(8,128)(2,1)S(1)}, u32[]{:S(2)}, u32[]{:S(2)}) collective-permute-start(bf16[832,128]{1,0:T(8,128)(2,1)S(1)} %pad_maximum_fusion.1), channel_id=1, source_target_pairs={{12,0},{13,1},{14,2},{15,3},{0,4},{1,5},{2,6},{3,7},{4,8},{5,9},{6... | collective-permute-start | bytes 638984 | tf_op jit(solution)/shard_map/ppermute | solution.py:69
  9.5 7.5 %collective-permute-start = (bf16[832,128]{1,0:T(8,128)(2,1)S(1)}, bf16[832,128]{1,0:T(8,128)(2,1)S(1)}, u32[]{:S(2)}, u32[]{:S(2)}) collective-permute-start(bf16[832,128]{1,0:T(8,128)(2,1)S(1)} %pad_maximum_fusion.1), channel_id=1, source_target_pairs={{4,0},{5,1},{6,2},{7,3},{8,4},{9,5},{10,6},{11,7},{12,8},{13,9},{1... | collective-permute-start | bytes 638984 | tf_op jit(solution)/shard_map/ppermute | solution.py:69
  12.8 17.3 %collective-permute-start.10 = (bf16[384,512]{1,0:T(8,128)(2,1)S(1)}, bf16[384,512]{1,0:T(8,128)(2,1)S(1)}, u32[]{:S(2)}, u32[]{:S(2)}) collective-permute-start(bf16[384,512]{1,0:T(8,128)(2,1)S(1)} %pad_maximum_fusion.refs_7_.refs_8_), channel_id=1, source_target_pairs={{12,0},{13,1},{14,2},{15,3},{0,4},{1,5},{2,6},{3,7},{4,8},{5,9},{6... | collective-permute-start | bytes 1179656 | tf_op jit(solution)/shard_map/ppermute | solution.py:69
  12.9 17.4 %collective-permute-start.9 = (bf16[384,512]{1,0:T(8,128)(2,1)S(1)}, bf16[384,512]{1,0:T(8,128)(2,1)S(1)}, u32[]{:S(2)}, u32[]{:S(2)}) collective-permute-start(bf16[384,512]{1,0:T(8,128)(2,1)S(1)} %pad_maximum_fusion.refs_7_.refs_8_), channel_id=1, source_target_pairs={{4,0},{5,1},{6,2},{7,3},{8,4},{9,5},{10,6},{11,7},{12,8},{13,9},{1... | collective-permute-start | bytes 1179656 | tf_op jit(solution)/shard_map/ppermute | solution.py:69
  17.1 7.2 %collective-permute-start.5 = (bf16[320,128]{1,0:T(8,128)(2,1)S(1)}, bf16[320,128]{1,0:T(8,128)(2,1)S(1)}, u32[]{:S(2)}, u32[]{:S(2)}) collective-permute-start(bf16[320,128]{1,0:T(8,128)(2,1)S(1)} %fusion.57), channel_id=1, source_target_pairs={{2,0},{3,1},{0,2},{1,3},{6,4},{7,5},{4,6},{5,7},{10,8},{11,9},{8,1... | collective-permute-start | bytes 245768 | tf_op jit(solution)/shard_map/ppermute | solution.py:69
  20.4 5.7 %collective-permute-start.4 = (bf16[320,128]{1,0:T(8,128)(2,1)S(1)}, bf16[320,128]{1,0:T(8,128)(2,1)S(1)}, u32[]{:S(2)}, u32[]{:S(2)}) collective-permute-start(bf16[320,128]{1,0:T(8,128)(2,1)S(1)} %fusion.57), channel_id=1, source_target_pairs={{3,0},{0,1},{1,2},{2,3},{7,4},{4,5},{5,6},{6,7},{11,8},{8,9},{9,10... | collective-permute-start | bytes 245768 | tf_op jit(solution)/shard_map/ppermute | solution.py:69
  21.1 5.0 %collective-permute-start.3 = (bf16[320,128]{1,0:T(8,128)(2,1)S(1)}, bf16[320,128]{1,0:T(8,128)(2,1)S(1)}, u32[]{:S(2)}, u32[]{:S(2)}) collective-permute-start(bf16[320,128]{1,0:T(8,128)(2,1)S(1)} %fusion.57), channel_id=1, source_target_pairs={{1,0},{2,1},{3,2},{0,3},{5,4},{6,5},{7,6},{4,7},{9,8},{10,9},{11,1... | collective-permute-start | bytes 245768 | tf_op jit(solution)/shard_map/ppermute | solution.py:69
  26.1 1.4 collective-permute-start.6
  28.2 5.3 %collective-permute-start.7 = (bf16[192,128]{1,0:T(8,128)(2,1)S(1)}, bf16[192,128]{1,0:T(8,128)(2,1)S(1)}, u32[]{:S(2)}, u32[]{:S(2)}) collective-permute-start(bf16[192,128]{1,0:T(8,128)(2,1)S(1)} %maximum_maximum_fusion), channel_id=1, source_target_pairs={{32,0},{33,1},{34,2},{35,3},{36,4},{37,5},{38,6},{39,7},{40,8},{41... | collective-permute-start | bytes 147464 | tf_op jit(solution)/shard_map/ppermute | solution.py:69
  30.2 7.0 %collective-permute-start.12 = (bf16[192,512]{1,0:T(8,128)(2,1)S(1)}, bf16[192,512]{1,0:T(8,128)(2,1)S(1)}, u32[]{:S(2)}, u32[]{:S(2)}) collective-permute-start(bf16[192,512]{1,0:T(8,128)(2,1)S(1)} %slice.260), channel_id=1, source_target_pairs={{12,0},{13,1},{14,2},{15,3},{0,4},{1,5},{2,6},{3,7},{4,8},{5,9},{6... | collective-permute-start | bytes 589832 | tf_op jit(solution)/shard_map/ppermute | solution.py:69
  30.3 6.5 %collective-permute-start.11 = (bf16[192,512]{1,0:T(8,128)(2,1)S(1)}, bf16[192,512]{1,0:T(8,128)(2,1)S(1)}, u32[]{:S(2)}, u32[]{:S(2)}) collective-permute-start(bf16[192,512]{1,0:T(8,128)(2,1)S(1)} %slice.259), channel_id=1, source_target_pairs={{4,0},{5,1},{6,2},{7,3},{8,4},{9,5},{10,6},{11,7},{12,8},{13,9},{1... | collective-permute-start | bytes 589832 | tf_op jit(solution)/shard_map/ppermute | solution.py:69
  33.8 5.0 %collective-permute-start.8 = (bf16[64,128]{1,0:T(8,128)(2,1)S(1)}, bf16[64,128]{1,0:T(8,128)(2,1)S(1)}, u32[]{:S(2)}, u32[]{:S(2)}) collective-permute-start(bf16[64,128]{1,0:T(8,128)(2,1)S(1)} %fusion.2), channel_id=1, source_target_pairs={{96,0},{97,1},{98,2},{99,3},{100,4},{101,5},{102,6},{103,7},{104,8... | collective-permute-start | bytes 49160 | tf_op jit(solution)/shard_map/ppermute | solution.py:69
  40.0 40.8 %slice-start = ((s8[5242880]{0:T(1024)(128)(4,1)}), s8[4194304]{0:T(1024)(128)(4,1)S(1)}, s32[]{:S(2)}) async-start(s8[5242880]{0:T(1024)(128)(4,1)} %bitcast.29), calls=%async_computation.3 | async-start | bytes 8388608
  40.0 40.8 %slice-start.1 = ((s8[5242880]{0:T(1024)(128)(4,1)}), s8[1048576]{0:T(1024)(128)(4,1)S(1)}, s32[]{:S(2)}) async-start(s8[5242880]{0:T(1024)(128)(4,1)} %bitcast.29), calls=%async_computation.4 | async-start | bytes 2097152
  74.8 1.3 collective-permute-start.13
  76.2 6.2 %collective-permute-start.14 = (bf16[4,2048,128]{2,1,0:T(8,128)(2,1)S(1)}, bf16[4,2048,128]{2,1,0:T(8,128)(2,1)S(1)}, u32[]{:S(2)}, u32[]{:S(2)}) collective-permute-start(bf16[4,2048,128]{2,1,0:T(8,128)(2,1)S(1)} %constant_dynamic-slice_fusion.1), channel_id=1, source_target_pairs={{16,0},{17,1},{18,2},{19,3},{20,4},{21,5},{22,6},{23,7},{24,8},{25... | collective-permute-start | bytes 6291464 | tf_op jit(solution)/shard_map/ppermute | solution.py:69
  76.6 7.0 %collective-permute-start.17 = (bf16[64,128]{1,0:T(8,128)(2,1)S(1)}, bf16[64,128]{1,0:T(8,128)(2,1)S(1)}, u32[]{:S(2)}, u32[]{:S(2)}) collective-permute-start(bf16[64,128]{1,0:T(8,128)(2,1)S(1)} %get-tuple-element.79), channel_id=1, source_target_pairs={{96,0},{97,1},{98,2},{99,3},{100,4},{101,5},{102,6},{103,7},{104,8... | collective-permute-start | bytes 49160 | tf_op jit(solution)/shard_map/ppermute | solution.py:69
  79.0 5.2 %collective-permute-start.16 = (bf16[64,128]{1,0:T(8,128)(2,1)S(1)}, bf16[64,128]{1,0:T(8,128)(2,1)S(1)}, u32[]{:S(2)}, u32[]{:S(2)}) collective-permute-start(bf16[64,128]{1,0:T(8,128)(2,1)S(1)} %get-tuple-element.79), channel_id=1, source_target_pairs={{64,0},{65,1},{66,2},{67,3},{68,4},{69,5},{70,6},{71,7},{72,8},{73... | collective-permute-start | bytes 49160 | tf_op jit(solution)/shard_map/ppermute | solution.py:69
  79.0 4.5 %collective-permute-start.15 = (bf16[64,128]{1,0:T(8,128)(2,1)S(1)}, bf16[64,128]{1,0:T(8,128)(2,1)S(1)}, u32[]{:S(2)}, u32[]{:S(2)}) collective-permute-start(bf16[64,128]{1,0:T(8,128)(2,1)S(1)} %get-tuple-element.80), channel_id=1, source_target_pairs={{32,0},{33,1},{34,2},{35,3},{36,4},{37,5},{38,6},{39,7},{40,8},{41... | collective-permute-start | bytes 49160 | tf_op jit(solution)/shard_map/ppermute | solution.py:69
  85.3 8.3 %collective-permute-start.23 = (bf16[192,128]{1,0:T(8,128)(2,1)S(1)}, bf16[192,128]{1,0:T(8,128)(2,1)S(1)}, u32[]{:S(2)}, u32[]{:S(2)}) collective-permute-start(bf16[192,128]{1,0:T(8,128)(2,1)S(1)} %convert_element_type.223), channel_id=1, source_target_pairs={{8,0},{9,1},{10,2},{11,3},{12,4},{13,5},{14,6},{15,7},{0,8},{1,9},... | collective-permute-start | bytes 147464 | tf_op jit(solution)/shard_map/ppermute | solution.py:69
  87.1 6.6 %collective-permute-start.22 = (bf16[192,128]{1,0:T(8,128)(2,1)S(1)}, bf16[192,128]{1,0:T(8,128)(2,1)S(1)}, u32[]{:S(2)}, u32[]{:S(2)}) collective-permute-start(bf16[192,128]{1,0:T(8,128)(2,1)S(1)} %convert_element_type.223), channel_id=1, source_target_pairs={{12,0},{13,1},{14,2},{15,3},{0,4},{1,5},{2,6},{3,7},{4,8},{5,9},{6... | collective-permute-start | bytes 147464 | tf_op jit(solution)/shard_map/ppermute | solution.py:69
  88.0 5.7 %collective-permute-start.21 = (bf16[192,128]{1,0:T(8,128)(2,1)S(1)}, bf16[192,128]{1,0:T(8,128)(2,1)S(1)}, u32[]{:S(2)}, u32[]{:S(2)}) collective-permute-start(bf16[192,128]{1,0:T(8,128)(2,1)S(1)} %convert_element_type.223), channel_id=1, source_target_pairs={{4,0},{5,1},{6,2},{7,3},{8,4},{9,5},{10,6},{11,7},{12,8},{13,9},{1... | collective-permute-start | bytes 147464 | tf_op jit(solution)/shard_map/ppermute | solution.py:69
  90.3 9.9 %collective-permute-start.19 = (bf16[512,128]{1,0:T(8,128)(2,1)S(1)}, bf16[512,128]{1,0:T(8,128)(2,1)S(1)}, u32[]{:S(2)}, u32[]{:S(2)}) collective-permute-start(bf16[512,128]{1,0:T(8,128)(2,1)S(1)} %convert_element_type.222), channel_id=1, source_target_pairs={{12,0},{13,1},{14,2},{15,3},{0,4},{1,5},{2,6},{3,7},{4,8},{5,9},{6... | collective-permute-start | bytes 393224 | tf_op jit(solution)/shard_map/ppermute | solution.py:69
  90.4 9.8 %collective-permute-start.18 = (bf16[512,128]{1,0:T(8,128)(2,1)S(1)}, bf16[512,128]{1,0:T(8,128)(2,1)S(1)}, u32[]{:S(2)}, u32[]{:S(2)}) collective-permute-start(bf16[512,128]{1,0:T(8,128)(2,1)S(1)} %convert_element_type.222), channel_id=1, source_target_pairs={{4,0},{5,1},{6,2},{7,3},{8,4},{9,5},{10,6},{11,7},{12,8},{13,9},{1... | collective-permute-start | bytes 393224 | tf_op jit(solution)/shard_map/ppermute | solution.py:69
  93.7 5.9 %collective-permute-start.26 = (bf16[192,128]{1,0:T(8,128)(2,1)S(1)}, bf16[192,128]{1,0:T(8,128)(2,1)S(1)}, u32[]{:S(2)}, u32[]{:S(2)}) collective-permute-start(bf16[192,128]{1,0:T(8,128)(2,1)S(1)} %get-tuple-element.62), channel_id=1, source_target_pairs={{2,0},{3,1},{0,2},{1,3},{6,4},{7,5},{4,6},{5,7},{10,8},{11,9},{8,1... | collective-permute-start | bytes 147464 | tf_op jit(solution)/shard_map/ppermute | solution.py:69
  94.9 5.3 %collective-permute-start.25 = (bf16[192,128]{1,0:T(8,128)(2,1)S(1)}, bf16[192,128]{1,0:T(8,128)(2,1)S(1)}, u32[]{:S(2)}, u32[]{:S(2)}) collective-permute-start(bf16[192,128]{1,0:T(8,128)(2,1)S(1)} %get-tuple-element.62), channel_id=1, source_target_pairs={{3,0},{0,1},{1,2},{2,3},{7,4},{4,5},{5,6},{6,7},{11,8},{8,9},{9,10... | collective-permute-start | bytes 147464 | tf_op jit(solution)/shard_map/ppermute | solution.py:69
  95.9 4.3 %collective-permute-start.24 = (bf16[192,128]{1,0:T(8,128)(2,1)S(1)}, bf16[192,128]{1,0:T(8,128)(2,1)S(1)}, u32[]{:S(2)}, u32[]{:S(2)}) collective-permute-start(bf16[192,128]{1,0:T(8,128)(2,1)S(1)} %get-tuple-element.62), channel_id=1, source_target_pairs={{1,0},{2,1},{3,2},{0,3},{5,4},{6,5},{7,6},{4,7},{9,8},{10,9},{11,1... | collective-permute-start | bytes 147464 | tf_op jit(solution)/shard_map/ppermute | solution.py:69
  100.2 1.3 collective-permute-start.27
  101.5 4.0 %collective-permute-start.28 = (bf16[128,128]{1,0:T(8,128)(2,1)S(1)}, bf16[128,128]{1,0:T(8,128)(2,1)S(1)}, u32[]{:S(2)}, u32[]{:S(2)}) collective-permute-start(bf16[128,128]{1,0:T(8,128)(2,1)S(1)} %get-tuple-element.60), channel_id=1, source_target_pairs={{32,0},{33,1},{34,2},{35,3},{36,4},{37,5},{38,6},{39,7},{40,8},{41... | collective-permute-start | bytes 98312 | tf_op jit(solution)/shard_map/ppermute | solution.py:69
  102.5 6.5 %collective-permute-start.20 = (bf16[512,128]{1,0:T(8,128)(2,1)S(1)}, bf16[512,128]{1,0:T(8,128)(2,1)S(1)}, u32[]{:S(2)}, u32[]{:S(2)}) collective-permute-start(bf16[512,128]{1,0:T(8,128)(2,1)S(1)} %convert_element_type.222), channel_id=1, source_target_pairs={{8,0},{9,1},{10,2},{11,3},{12,4},{13,5},{14,6},{15,7},{0,8},{1,9},... | collective-permute-start | bytes 393224 | tf_op jit(solution)/shard_map/ppermute | solution.py:69
  105.6 5.0 %collective-permute-start.29 = (bf16[64,128]{1,0:T(8,128)(2,1)S(1)}, bf16[64,128]{1,0:T(8,128)(2,1)S(1)}, u32[]{:S(2)}, u32[]{:S(2)}) collective-permute-start(bf16[64,128]{1,0:T(8,128)(2,1)S(1)} %fusion.15), channel_id=1, source_target_pairs={{96,0},{97,1},{98,2},{99,3},{100,4},{101,5},{102,6},{103,7},{104,8... | collective-permute-start | bytes 49160 | tf_op jit(solution)/shard_map/ppermute | solution.py:69
  147.5 1.3 collective-permute-start.30
  149.0 6.1 %collective-permute-start.31 = (bf16[4,2048,128]{2,1,0:T(8,128)(2,1)S(1)}, bf16[4,2048,128]{2,1,0:T(8,128)(2,1)S(1)}, u32[]{:S(2)}, u32[]{:S(2)}) collective-permute-start(bf16[4,2048,128]{2,1,0:T(8,128)(2,1)S(1)} %constant_dynamic-slice_fusion), channel_id=1, source_target_pairs={{16,0},{17,1},{18,2},{19,3},{20,4},{21,5},{22,6},{23,7},{24,8},{25... | collective-permute-start | bytes 6291464 | tf_op jit(solution)/shard_map/ppermute | solution.py:69
  149.2 6.9 %collective-permute-start.34 = (bf16[64,128]{1,0:T(8,128)(2,1)S(1)}, bf16[64,128]{1,0:T(8,128)(2,1)S(1)}, u32[]{:S(2)}, u32[]{:S(2)}) collective-permute-start(bf16[64,128]{1,0:T(8,128)(2,1)S(1)} %get-tuple-element.77), channel_id=1, source_target_pairs={{96,0},{97,1},{98,2},{99,3},{100,4},{101,5},{102,6},{103,7},{104,8... | collective-permute-start | bytes 49160 | tf_op jit(solution)/shard_map/ppermute | solution.py:69
  151.7 5.2 %collective-permute-start.33 = (bf16[64,128]{1,0:T(8,128)(2,1)S(1)}, bf16[64,128]{1,0:T(8,128)(2,1)S(1)}, u32[]{:S(2)}, u32[]{:S(2)}) collective-permute-start(bf16[64,128]{1,0:T(8,128)(2,1)S(1)} %get-tuple-element.77), channel_id=1, source_target_pairs={{64,0},{65,1},{66,2},{67,3},{68,4},{69,5},{70,6},{71,7},{72,8},{73... | collective-permute-start | bytes 49160 | tf_op jit(solution)/shard_map/ppermute | solution.py:69
  151.9 4.2 %collective-permute-start.32 = (bf16[64,128]{1,0:T(8,128)(2,1)S(1)}, bf16[64,128]{1,0:T(8,128)(2,1)S(1)}, u32[]{:S(2)}, u32[]{:S(2)}) collective-permute-start(bf16[64,128]{1,0:T(8,128)(2,1)S(1)} %get-tuple-element.78), channel_id=1, source_target_pairs={{32,0},{33,1},{34,2},{35,3},{36,4},{37,5},{38,6},{39,7},{40,8},{41... | collective-permute-start | bytes 49160 | tf_op jit(solution)/shard_map/ppermute | solution.py:69
  157.9 7.2 %collective-permute-start.40 = (bf16[192,128]{1,0:T(8,128)(2,1)S(1)}, bf16[192,128]{1,0:T(8,128)(2,1)S(1)}, u32[]{:S(2)}, u32[]{:S(2)}) collective-permute-start(bf16[192,128]{1,0:T(8,128)(2,1)S(1)} %convert_element_type.237), channel_id=1, source_target_pairs={{8,0},{9,1},{10,2},{11,3},{12,4},{13,5},{14,6},{15,7},{0,8},{1,9},... | collective-permute-start | bytes 147464 | tf_op jit(solution)/shard_map/ppermute | solution.py:69
  158.6 6.6 %collective-permute-start.39 = (bf16[192,128]{1,0:T(8,128)(2,1)S(1)}, bf16[192,128]{1,0:T(8,128)(2,1)S(1)}, u32[]{:S(2)}, u32[]{:S(2)}) collective-permute-start(bf16[192,128]{1,0:T(8,128)(2,1)S(1)} %convert_element_type.237), channel_id=1, source_target_pairs={{12,0},{13,1},{14,2},{15,3},{0,4},{1,5},{2,6},{3,7},{4,8},{5,9},{6... | collective-permute-start | bytes 147464 | tf_op jit(solution)/shard_map/ppermute | solution.py:69
  161.2 4.1 %collective-permute-start.38 = (bf16[192,128]{1,0:T(8,128)(2,1)S(1)}, bf16[192,128]{1,0:T(8,128)(2,1)S(1)}, u32[]{:S(2)}, u32[]{:S(2)}) collective-permute-start(bf16[192,128]{1,0:T(8,128)(2,1)S(1)} %convert_element_type.237), channel_id=1, source_target_pairs={{4,0},{5,1},{6,2},{7,3},{8,4},{9,5},{10,6},{11,7},{12,8},{13,9},{1... | collective-permute-start | bytes 147464 | tf_op jit(solution)/shard_map/ppermute | solution.py:69
  161.8 10.7 %collective-permute-start.36 = (bf16[512,128]{1,0:T(8,128)(2,1)S(1)}, bf16[512,128]{1,0:T(8,128)(2,1)S(1)}, u32[]{:S(2)}, u32[]{:S(2)}) collective-permute-start(bf16[512,128]{1,0:T(8,128)(2,1)S(1)} %convert_element_type.236), channel_id=1, source_target_pairs={{12,0},{13,1},{14,2},{15,3},{0,4},{1,5},{2,6},{3,7},{4,8},{5,9},{6... | collective-permute-start | bytes 393224 | tf_op jit(solution)/shard_map/ppermute | solution.py:69
  163.3 9.2 %collective-permute-start.35 = (bf16[512,128]{1,0:T(8,128)(2,1)S(1)}, bf16[512,128]{1,0:T(8,128)(2,1)S(1)}, u32[]{:S(2)}, u32[]{:S(2)}) collective-permute-start(bf16[512,128]{1,0:T(8,128)(2,1)S(1)} %convert_element_type.236), channel_id=1, source_target_pairs={{4,0},{5,1},{6,2},{7,3},{8,4},{9,5},{10,6},{11,7},{12,8},{13,9},{1... | collective-permute-start | bytes 393224 | tf_op jit(solution)/shard_map/ppermute | solution.py:69
  165.3 5.7 %collective-permute-start.43 = (bf16[192,128]{1,0:T(8,128)(2,1)S(1)}, bf16[192,128]{1,0:T(8,128)(2,1)S(1)}, u32[]{:S(2)}, u32[]{:S(2)}) collective-permute-start(bf16[192,128]{1,0:T(8,128)(2,1)S(1)} %get-tuple-element.58), channel_id=1, source_target_pairs={{2,0},{3,1},{0,2},{1,3},{6,4},{7,5},{4,6},{5,7},{10,8},{11,9},{8,1... | collective-permute-start | bytes 147464 | tf_op jit(solution)/shard_map/ppermute | solution.py:69
  166.3 5.3 %collective-permute-start.42 = (bf16[192,128]{1,0:T(8,128)(2,1)S(1)}, bf16[192,128]{1,0:T(8,128)(2,1)S(1)}, u32[]{:S(2)}, u32[]{:S(2)}) collective-permute-start(bf16[192,128]{1,0:T(8,128)(2,1)S(1)} %get-tuple-element.58), channel_id=1, source_target_pairs={{3,0},{0,1},{1,2},{2,3},{7,4},{4,5},{5,6},{6,7},{11,8},{8,9},{9,10... | collective-permute-start | bytes 147464 | tf_op jit(solution)/shard_map/ppermute | solution.py:69
  168.4 4.1 %collective-permute-start.41 = (bf16[192,128]{1,0:T(8,128)(2,1)S(1)}, bf16[192,128]{1,0:T(8,128)(2,1)S(1)}, u32[]{:S(2)}, u32[]{:S(2)}) collective-permute-start(bf16[192,128]{1,0:T(8,128)(2,1)S(1)} %get-tuple-element.58), channel_id=1, source_target_pairs={{1,0},{2,1},{3,2},{0,3},{5,4},{6,5},{7,6},{4,7},{9,8},{10,9},{11,1... | collective-permute-start | bytes 147464 | tf_op jit(solution)/shard_map/ppermute | solution.py:69
  172.5 1.3 collective-permute-start.44
  173.9 4.0 %collective-permute-start.45 = (bf16[128,128]{1,0:T(8,128)(2,1)S(1)}, bf16[128,128]{1,0:T(8,128)(2,1)S(1)}, u32[]{:S(2)}, u32[]{:S(2)}) collective-permute-start(bf16[128,128]{1,0:T(8,128)(2,1)S(1)} %get-tuple-element.56), channel_id=1, source_target_pairs={{32,0},{33,1},{34,2},{35,3},{36,4},{37,5},{38,6},{39,7},{40,8},{41... | collective-permute-start | bytes 98312 | tf_op jit(solution)/shard_map/ppermute | solution.py:69
  174.8 6.5 %collective-permute-start.37 = (bf16[512,128]{1,0:T(8,128)(2,1)S(1)}, bf16[512,128]{1,0:T(8,128)(2,1)S(1)}, u32[]{:S(2)}, u32[]{:S(2)}) collective-permute-start(bf16[512,128]{1,0:T(8,128)(2,1)S(1)} %convert_element_type.236), channel_id=1, source_target_pairs={{8,0},{9,1},{10,2},{11,3},{12,4},{13,5},{14,6},{15,7},{0,8},{1,9},... | collective-permute-start | bytes 393224 | tf_op jit(solution)/shard_map/ppermute | solution.py:69
  177.9 5.0 %collective-permute-start.46 = (bf16[64,128]{1,0:T(8,128)(2,1)S(1)}, bf16[64,128]{1,0:T(8,128)(2,1)S(1)}, u32[]{:S(2)}, u32[]{:S(2)}) collective-permute-start(bf16[64,128]{1,0:T(8,128)(2,1)S(1)} %fusion.14), channel_id=1, source_target_pairs={{96,0},{97,1},{98,2},{99,3},{100,4},{101,5},{102,6},{103,7},{104,8... | collective-permute-start | bytes 49160 | tf_op jit(solution)/shard_map/ppermute | solution.py:69
  218.9 1.3 collective-permute-start.47
  220.4 6.3 %collective-permute-start.48 = (bf16[4,2048,128]{2,1,0:T(8,128)(2,1)S(1)}, bf16[4,2048,128]{2,1,0:T(8,128)(2,1)S(1)}, u32[]{:S(2)}, u32[]{:S(2)}) collective-permute-start(bf16[4,2048,128]{2,1,0:T(8,128)(2,1)S(1)} %constant_dynamic-slice_fusion.2), channel_id=1, source_target_pairs={{16,0},{17,1},{18,2},{19,3},{20,4},{21,5},{22,6},{23,7},{24,8},{25... | collective-permute-start | bytes 6291464 | tf_op jit(solution)/shard_map/ppermute | solution.py:69
  220.9 6.9 %collective-permute-start.51 = (bf16[64,128]{1,0:T(8,128)(2,1)S(1)}, bf16[64,128]{1,0:T(8,128)(2,1)S(1)}, u32[]{:S(2)}, u32[]{:S(2)}) collective-permute-start(bf16[64,128]{1,0:T(8,128)(2,1)S(1)} %get-tuple-element.75), channel_id=1, source_target_pairs={{96,0},{97,1},{98,2},{99,3},{100,4},{101,5},{102,6},{103,7},{104,8... | collective-permute-start | bytes 49160 | tf_op jit(solution)/shard_map/ppermute | solution.py:69
  223.3 5.2 %collective-permute-start.50 = (bf16[64,128]{1,0:T(8,128)(2,1)S(1)}, bf16[64,128]{1,0:T(8,128)(2,1)S(1)}, u32[]{:S(2)}, u32[]{:S(2)}) collective-permute-start(bf16[64,128]{1,0:T(8,128)(2,1)S(1)} %get-tuple-element.75), channel_id=1, source_target_pairs={{64,0},{65,1},{66,2},{67,3},{68,4},{69,5},{70,6},{71,7},{72,8},{73... | collective-permute-start | bytes 49160 | tf_op jit(solution)/shard_map/ppermute | solution.py:69
  223.3 4.5 %collective-permute-start.49 = (bf16[64,128]{1,0:T(8,128)(2,1)S(1)}, bf16[64,128]{1,0:T(8,128)(2,1)S(1)}, u32[]{:S(2)}, u32[]{:S(2)}) collective-permute-start(bf16[64,128]{1,0:T(8,128)(2,1)S(1)} %get-tuple-element.76), channel_id=1, source_target_pairs={{32,0},{33,1},{34,2},{35,3},{36,4},{37,5},{38,6},{39,7},{40,8},{41... | collective-permute-start | bytes 49160 | tf_op jit(solution)/shard_map/ppermute | solution.py:69
  226.7 26.6 %copy-start.4 = (bf16[3,64,512]{2,1,0:T(8,128)(2,1)S(1)}, bf16[3,64,512]{2,1,0:T(8,128)(2,1)}, u32[]{:S(2)}) copy-start(bf16[3,64,512]{2,1,0:T(8,128)(2,1)} %param.16) | copy-start | bytes 589828
  229.6 5.6 %collective-permute-start.54 = (bf16[192,128]{1,0:T(8,128)(2,1)S(1)}, bf16[192,128]{1,0:T(8,128)(2,1)S(1)}, u32[]{:S(2)}, u32[]{:S(2)}) collective-permute-start(bf16[192,128]{1,0:T(8,128)(2,1)S(1)} %convert_element_type.250), channel_id=1, source_target_pairs={{8,0},{9,1},{10,2},{11,3},{12,4},{13,5},{14,6},{15,7},{0,8},{1,9},... | collective-permute-start | bytes 147464 | tf_op jit(solution)/shard_map/ppermute | solution.py:69
  230.8 5.3 %collective-permute-start.53 = (bf16[192,128]{1,0:T(8,128)(2,1)S(1)}, bf16[192,128]{1,0:T(8,128)(2,1)S(1)}, u32[]{:S(2)}, u32[]{:S(2)}) collective-permute-start(bf16[192,128]{1,0:T(8,128)(2,1)S(1)} %convert_element_type.250), channel_id=1, source_target_pairs={{12,0},{13,1},{14,2},{15,3},{0,4},{1,5},{2,6},{3,7},{4,8},{5,9},{6... | collective-permute-start | bytes 147464 | tf_op jit(solution)/shard_map/ppermute | solution.py:69
  232.4 4.1 %collective-permute-start.52 = (bf16[192,128]{1,0:T(8,128)(2,1)S(1)}, bf16[192,128]{1,0:T(8,128)(2,1)S(1)}, u32[]{:S(2)}, u32[]{:S(2)}) collective-permute-start(bf16[192,128]{1,0:T(8,128)(2,1)S(1)} %convert_element_type.250), channel_id=1, source_target_pairs={{4,0},{5,1},{6,2},{7,3},{8,4},{9,5},{10,6},{11,7},{12,8},{13,9},{1... | collective-permute-start | bytes 147464 | tf_op jit(solution)/shard_map/ppermute | solution.py:69
  236.5 5.7 %collective-permute-start.57 = (bf16[192,128]{1,0:T(8,128)(2,1)S(1)}, bf16[192,128]{1,0:T(8,128)(2,1)S(1)}, u32[]{:S(2)}, u32[]{:S(2)}) collective-permute-start(bf16[192,128]{1,0:T(8,128)(2,1)S(1)} %fusion.32), channel_id=1, source_target_pairs={{2,0},{3,1},{0,2},{1,3},{6,4},{7,5},{4,6},{5,7},{10,8},{11,9},{8,1... | collective-permute-start | bytes 147464 | tf_op jit(solution)/shard_map/ppermute | solution.py:69
  237.6 5.3 %collective-permute-start.56 = (bf16[192,128]{1,0:T(8,128)(2,1)S(1)}, bf16[192,128]{1,0:T(8,128)(2,1)S(1)}, u32[]{:S(2)}, u32[]{:S(2)}) collective-permute-start(bf16[192,128]{1,0:T(8,128)(2,1)S(1)} %fusion.32), channel_id=1, source_target_pairs={{3,0},{0,1},{1,2},{2,3},{7,4},{4,5},{5,6},{6,7},{11,8},{8,9},{9,10... | collective-permute-start | bytes 147464 | tf_op jit(solution)/shard_map/ppermute | solution.py:69
  238.6 4.3 %collective-permute-start.55 = (bf16[192,128]{1,0:T(8,128)(2,1)S(1)}, bf16[192,128]{1,0:T(8,128)(2,1)S(1)}, u32[]{:S(2)}, u32[]{:S(2)}) collective-permute-start(bf16[192,128]{1,0:T(8,128)(2,1)S(1)} %fusion.32), channel_id=1, source_target_pairs={{1,0},{2,1},{3,2},{0,3},{5,4},{6,5},{7,6},{4,7},{9,8},{10,9},{11,1... | collective-permute-start | bytes 147464 | tf_op jit(solution)/shard_map/ppermute | solution.py:69
  242.9 1.3 collective-permute-start.58
  244.2 4.0 %collective-permute-start.59 = (bf16[128,128]{1,0:T(8,128)(2,1)S(1)}, bf16[128,128]{1,0:T(8,128)(2,1)S(1)}, u32[]{:S(2)}, u32[]{:S(2)}) collective-permute-start(bf16[128,128]{1,0:T(8,128)(2,1)S(1)} %get-tuple-element.52), channel_id=1, source_target_pairs={{32,0},{33,1},{34,2},{35,3},{36,4},{37,5},{38,6},{39,7},{40,8},{41... | collective-permute-start | bytes 98312 | tf_op jit(solution)/shard_map/ppermute | solution.py:69
  248.2 5.0 %collective-permute-start.60 = (bf16[64,128]{1,0:T(8,128)(2,1)S(1)}, bf16[64,128]{1,0:T(8,128)(2,1)S(1)}, u32[]{:S(2)}, u32[]{:S(2)}) collective-permute-start(bf16[64,128]{1,0:T(8,128)(2,1)S(1)} %fusion.13), channel_id=1, source_target_pairs={{96,0},{97,1},{98,2},{99,3},{100,4},{101,5},{102,6},{103,7},{104,8... | collective-permute-start | bytes 49160 | tf_op jit(solution)/shard_map/ppermute | solution.py:69
  (4 other events, 7.5 us)

commit v7 on v6

--- a/solution.py
+++ b/solution.py
@@ -148,11 +148,14 @@
     start = jnp.sum(jnp.where(put, jnp.where(live, row, 0)[:, :, None], 0), axis=1)
     n_pair = jnp.sum((key == 0).astype(jnp.int32), axis=1)
     n_live = jnp.sum((key < 2).astype(jnp.int32), axis=1)
-    return order.reshape(-1), start.reshape(-1), n_pair, n_live
-
-
-def near_kernel(width, order, start, lo, hi, blocks, field, before, out):
+    slots = order + start // 64 * 256
+    return jnp.concatenate([slots.reshape(-1), jnp.zeros_like(n_pair), n_pair, n_live])
+
+
+def near_kernel(part, width, table, blocks, field, before, out):
     rows = range(NBD)
+    lo = [table[NBD * SLOTS + part * NBD + q] for q in rows]
+    hi = [table[NBD * SLOTS + (part + 1) * NBD + q] for q in rows]
     longest = hi[0] - lo[0]
     for q in rows[1:]:
         longest = jnp.maximum(longest, hi[q] - lo[q])
@@ -164,9 +167,10 @@
             for u in range(width):
                 j = lo[q] + width * i + u
                 at = q * SLOTS + jnp.minimum(j, SLOTS - 1)
-                block = blocks[q, order[at]]
+                slot = table[at]
+                block = blocks[q, slot & 255]
                 left.append(jnp.where(j < hi[q], block, jnp.zeros_like(block)))
-                row = jnp.minimum(start[at], field.shape[0] - BS)
+                row = jnp.minimum((slot >> 8) * 64, field.shape[0] - BS)
                 right.append(field[pl.ds(pl.multiple_of(row, 64), BS), :])
             new.append(
                 sums[q]
@@ -182,16 +186,16 @@
         out[q * BS : (q + 1) * BS, :] = sums[q]
 
 
-def near(width, order, start, lo, hi, near_blocks, field, before):
+def near(part, width, table, near_blocks, field, before):
     small, whole = pl.BlockSpec(memory_space=pltpu.SMEM), pl.BlockSpec(memory_space=pltpu.VMEM)
     return pl.pallas_call(
-        functools.partial(near_kernel, width),
-        in_specs=[small] * 4 + [whole] * 3,
+        functools.partial(near_kernel, part, width),
+        in_specs=[small] + [whole] * 3,
         out_specs=whole,
         out_shape=jax.ShapeDtypeStruct((ROWS, BS), F32),
         compiler_params=pltpu.CompilerParams(vmem_limit_bytes=12 * 2**20),
         cost_estimate=pl.CostEstimate(flops=2 * 80 * BS**3, bytes_accessed=10 * 2**20, transcendentals=0),
-    )(order, start, lo, hi, near_blocks, field, before)
+    )(table, near_blocks, field, before)
 
 
 def kernel_call(body, shapes, cost, *given):
@@ -236,10 +240,11 @@
     refs[-1][...] = total.astype(BF)
 
 
-def finish_kernel(image, right_side, other, near, far_a, far_b, c_left, leaf_inverse, right, k10, k20, k21, resid, z, terms):
+def finish_kernel(image, right_side, other, near, far_a, far_b, c_left, leaf_inverse, right, k10, k20, k21, z, terms, *resid):
     sums = sibling_sums(other, near, far_a, far_b)
     left_over = right_side[...] - (image[...] + dot_t(c_left[...], sums))
-    resid[...] = left_over
+    for ref in resid:
+        ref[...] = left_over
     left_over = left_over.astype(BF)
     for q in range(NBD):
         rows = slice(q * BS, (q + 1) * BS)
@@ -261,23 +266,33 @@
     return jnp.concatenate([terms, low, high], axis=0)
 
 
+def parts(a):
+    return a[:R], a[R : 2 * R], a[2 * R : 3 * R], a[3 * R : 4 * R, :R], a[3 * R : 4 * R, R:], a[4 * R :, :R]
+
+
+def first_chip_kernel(mine, other, chip, sent):
+    a0, a1, a2, m10, m20, m21 = parts(mine[...])
+    b0, b1, b2, k10, k20, k21 = parts(other[...].astype(F32))
+    m21 = m21 + k21
+    chip[:R, :] = a1 - dot(m10, b0) + b1 - dot(k10, a0)
+    chip[R : 2 * R, :] = a2 - dot(m20, b0) + b2 - dot(k20, a0)
+    chip[2 * R :, :] = jnp.concatenate([m21, m21], axis=1)
+    sent[...] = chip[...].astype(BF)
+
+
+def first_half_kernel(chip, near, sent):
+    s1, u2, k21 = near[:R, :], near[R : 2 * R, :].astype(F32), near[2 * R :, :R]
+    half = chip[R : 2 * R, :] - dot(chip[2 * R :, :R], s1) + u2 - dot(k21, chip[:R, :])
+    sent[...] = half.astype(BF)
+
+
 def first_siblings(mine):
-    other = move(mine.astype(BF), CORE).astype(F32)
-
-    def parts(a):
-        return a[:R], a[R : 2 * R], a[2 * R : 3 * R], a[3 * R : 4 * R, :R], a[3 * R : 4 * R, R:], a[4 * R :, :R]
-
-    a0, a1, a2, m10, m20, m21 = parts(mine)
-    b0, b1, b2, k10, k20, k21 = parts(other)
-    t1 = a1 - dot(m10, b0) + b1 - dot(k10, a0)
-    t2 = a2 - dot(m20, b0) + b2 - dot(k20, a0)
-    m21 = m21 + k21
-    chip = jnp.concatenate([t1, t2, jnp.concatenate([m21, m21], axis=1)], axis=0)
-    near_chip = move(chip.astype(BF), CHIP[0]).astype(F32)
-    s1, u2, k21 = near_chip[:R], near_chip[R : 2 * R], near_chip[2 * R :, :R]
-    half = t2 - dot(m21, s1) + u2 - dot(k21, t1)
-    s2 = move(half.astype(BF), CHIP[2])
-    return (b0.astype(BF), s1.astype(BF), s2), (k10.astype(BF), k20.astype(BF), k21.astype(BF))
+    other = move(mine.astype(BF), CORE)
+    chip, sent = kernel_call(first_chip_kernel, (((3 * R, BS), F32), ((3 * R, BS), BF)), 10, mine, other)
+    near = move(sent, CHIP[0])
+    (half,) = kernel_call(first_half_kernel, (((R, BS), BF),), 10, chip, near)
+    b0, _, _, k10, k20, _ = parts(other)
+    return (b0, near[:R], move(half, CHIP[2])), (k10, k20, near[2 * R :, :R])
 
 
 def fold(terms, mixes):
@@ -292,8 +307,7 @@
     right_side, near_blocks, neighbours, counts, leaf_inverse, couple_left, couple_right, prec_left, prec_right
 ):
     half = 4 - 4 * (lax.axis_index("drop") % 2)
-    order, start, n_pair, n_live = slot_tables(neighbours, counts, half)
-    none = jnp.zeros_like(n_pair)
+    table = slot_tables(neighbours, counts, half)
     c_left, c_right, left, right = (
         f.reshape(TERMS, ROWS) for f in (couple_left, couple_right, prec_left, prec_right)
     )
@@ -311,7 +325,7 @@
 
     for step in range(ITERS):
         given = [*z_ring, *sums, *facts]
-        given = given + [order, start, n_pair, n_live] if step == 0 else [field] + given
+        given = given + [table] if step == 0 else [field] + given
         field, pieces = kernel_call(
             functools.partial(start_kernel, step > 0), (field_shape, piece_shape), 500, *given
         )
@@ -324,11 +338,12 @@
         other = move(own, CORE)
         c_sums = siblings_beside(c_other, c_terms)
         x = field[:ROWS]
-        image = near(8, order, start, none, n_pair, near_blocks, pieces.reshape(8 * PIECE, BS), x)
-        image = near(8, order, start, n_pair, n_live, near_blocks, other.reshape(4 * RING, BS), image)
-        resid, z, terms = kernel_call(
+        image = near(0, 8, table, near_blocks, pieces.reshape(8 * PIECE, BS), x)
+        image = near(1, 8, table, near_blocks, other.reshape(4 * RING, BS), image)
+        shapes = (((ROWS, BS), F32), ((TERMS, BS), F32), ((ROWS, BS), F32))
+        z, terms, *resid = kernel_call(
             finish_kernel,
-            (((ROWS, BS), F32), ((ROWS, BS), F32), ((TERMS, BS), F32)),
+            shapes if step == ITERS - 1 else shapes[:2],
             500,
             image, right_side, *c_sums, c_left, leaf_inverse, right, *mixes,
         )
@@ -345,7 +360,7 @@
         else:
             sums = sibling_sums(*siblings(add_over(add_over(terms, FIRST), SECOND)))
             x = x + z - dot_t(left, sums)
-    return x, resid
+    return x, resid[0]
 
 
 def solution(mesh):

time: 255 us -> 256 us (level)
  Pallas kernels: 14.7 us -> 17.6 us
  starting transfers between devices: 86.7 us -> 83.9 us
    pallas_call x6, Pallas kernels: 8.08 us -> 10.9 us  [near(): pl.pallas_call(functools.partial(near_kernel, part, width), in_specs=[sma...]
    ppermute x61, starting transfers between devices: 86.7 us -> 83.9 us  [move(): return lax.ppermute(array, AXES, pairs)]
    pallas_call x8 -> x10, Pallas kernels: 6.66 us -> 6.62 us  [kernel_call(): pl.pallas_call(body, in_specs=[whole] * len(given), out_specs=[whole] * l...]
  transfers between devices with their start and end apart: 61 -> 61, of which waited for: 33 -> 28; matrix products, arithmetic and copies ran while one was open for 2% -> 2% of each run, Pallas kernels for 3% -> 4%
where the time goes in v7:
time: 256 us; the launch traced here: 255 us
  blocking collectives  107 us (42%)
  starting transfers between devices  83.9 us (33%)
  waiting for transfers between devices  35.8 us (14%)
  Pallas kernels  17.6 us (7%)
  matrix products  4.55 us (2%)
  other arithmetic  3.81 us (1%)
    all_to_all x3, blocking collectives, on_device(): lax.all_to_all(pieces, AXES, 0, 0, tiled=True, axis_index_groups=EIGHTS)  107 us
    ppermute x61, starting transfers between devices, move(): return lax.ppermute(array, AXES, pairs)  83.9 us
    ppermute x61, waiting for transfers between devices, move(): return lax.ppermute(array, AXES, pairs)  35.8 us
    pallas_call x6, Pallas kernels, near(): pl.pallas_call(functools.partial(near_kernel, part, width), in_specs=[sma...  10.9 us
    pallas_call x10, Pallas kernels, kernel_call(): pl.pallas_call(body, in_specs=[whole] * len(given), out_specs=[whole] * l...  6.62 us
  transfers between devices with their start and end apart: 61, of which 28 were waited for; matrix products, arithmetic and copies ran while one was open for 2% of the time, Pallas kernels for 4%

profile of v7, /device:TPU:0, one launch (start us, length us, event | category | flops | bytes accessed | tf_op | source)
XLA Modules:
  0.0 255.0 jit_solution(1807503539988393048)
XLA Ops:
  0.6 1.3 fusion.47
  2.0 1.2 fusion.46
  3.2 1.1 fusion.45
  4.5 4.0 %collective-permute-start.2 = (bf16[832,128]{1,0:T(8,128)(2,1)S(1)}, bf16[832,128]{1,0:T(8,128)(2,1)S(1)}, u32[]{:S(2)}, u32[]{:S(2)}) collective-permute-start(bf16[832,128]{1,0:T(8,128)(2,1)S(1)} %pad_maximum_fusion.1), channel_id=1, source_target_pairs={{8,0},{9,1},{10,2},{11,3},{12,4},{13,5},{14,6},{15,7},{0,8},{1,9},... | collective-permute-start | bytes 638984 | tf_op jit(solution)/shard_map/ppermute | solution.py:69
  9.5 2.2 collective-permute-start
  11.7 1.0 pad_maximum_fusion.refs_7_.refs_8_
  12.9 3.2 %collective-permute-start.9 = (bf16[384,512]{1,0:T(8,128)(2,1)S(1)}, bf16[384,512]{1,0:T(8,128)(2,1)S(1)}, u32[]{:S(2)}, u32[]{:S(2)}) collective-permute-start(bf16[384,512]{1,0:T(8,128)(2,1)S(1)} %pad_maximum_fusion.refs_7_.refs_8_), channel_id=1, source_target_pairs={{4,0},{5,1},{6,2},{7,3},{8,4},{9,5},{10,6},{11,7},{12,8},{13,9},{1... | collective-permute-start | bytes 1179656 | tf_op jit(solution)/shard_map/ppermute | solution.py:69
  18.1 3.3 %collective-permute-start.5 = (bf16[320,128]{1,0:T(8,128)(2,1)S(1)}, bf16[320,128]{1,0:T(8,128)(2,1)S(1)}, u32[]{:S(2)}, u32[]{:S(2)}) collective-permute-start(bf16[320,128]{1,0:T(8,128)(2,1)S(1)} %fusion.31), channel_id=1, source_target_pairs={{2,0},{3,1},{0,2},{1,3},{6,4},{7,5},{4,6},{5,7},{10,8},{11,9},{8,1... | collective-permute-start | bytes 245768 | tf_op jit(solution)/shard_map/ppermute | solution.py:69
  22.0 2.6 %collective-permute-start.3 = (bf16[320,128]{1,0:T(8,128)(2,1)S(1)}, bf16[320,128]{1,0:T(8,128)(2,1)S(1)}, u32[]{:S(2)}, u32[]{:S(2)}) collective-permute-start(bf16[320,128]{1,0:T(8,128)(2,1)S(1)} %fusion.31), channel_id=1, source_target_pairs={{1,0},{2,1},{3,2},{0,3},{5,4},{6,5},{7,6},{4,7},{9,8},{10,9},{11,1... | collective-permute-start | bytes 245768 | tf_op jit(solution)/shard_map/ppermute | solution.py:69
  24.9 2.1 collective-permute-done.4
  28.6 1.6 collective-permute-start.7
  30.5 2.3 collective-permute-done.7.near
  33.0 2.8 %collective-permute-start.8 = (bf16[64,128]{1,0:T(8,128)(2,1)S(1)}, bf16[64,128]{1,0:T(8,128)(2,1)S(1)}, u32[]{:S(2)}, u32[]{:S(2)}) collective-permute-start(bf16[64,128]{1,0:T(8,128)(2,1)S(1)} %shard_map.105), channel_id=1, source_target_pairs={{96,0},{97,1},{98,2},{99,3},{100,4},{101,5},{102,6},{103,7},{104,8... | collective-permute-start | bytes 49160 | tf_op jit(solution)/shard_map/ppermute | solution.py:69
  35.8 1.4 collective-permute-done.12
  38.0 1.2 shard_map.106
  39.2 36.0 %all_to_all.15 = bf16[8,2240,128]{2,1,0:T(8,128)(2,1)S(1)} all-to-all(bf16[8,2240,128]{2,1,0:T(8,128)(2,1)S(1)} %get-tuple-element.30), channel_id=1, replica_groups={{16,20,24,28,32,36,40,44},{17,21,25,29,33,37,41,45},{18,22,26,30,34,38,..., dimensions={0} | all-to-all | bytes 9175040 | tf_op jit(solution)/shard_map/all_to_all | solution.py:332
  75.3 1.2 collective-permute-done.13.other
  77.0 2.4 collective-permute-start.17
  79.4 1.8 collective-permute-start.15
  81.2 2.0 shard_map.107.before
  83.3 1.6 shard_map.108.image
  85.9 1.4 collective-permute-start.22
  87.3 2.2 collective-permute-start.21
  89.6 3.2 %collective-permute-start.18 = (bf16[512,128]{1,0:T(8,128)(2,1)S(1)}, bf16[512,128]{1,0:T(8,128)(2,1)S(1)}, u32[]{:S(2)}, u32[]{:S(2)}) collective-permute-start(bf16[512,128]{1,0:T(8,128)(2,1)S(1)} %convert_element_type.195), channel_id=1, source_target_pairs={{4,0},{5,1},{6,2},{7,3},{8,4},{9,5},{10,6},{11,7},{12,8},{13,9},{1... | collective-permute-start | bytes 393224 | tf_op jit(solution)/shard_map/ppermute | solution.py:69
  94.8 2.2 collective-permute-start.24
  97.0 1.8 collective-permute-done.26.refs_2_
  99.4 1.2 collective-permute-done.27.refs_5_
  100.7 1.5 collective-permute-start.28
  102.2 2.4 collective-permute-start.20
  104.7 3.1 %collective-permute-start.29 = (bf16[64,128]{1,0:T(8,128)(2,1)S(1)}, bf16[64,128]{1,0:T(8,128)(2,1)S(1)}, u32[]{:S(2)}, u32[]{:S(2)}) collective-permute-start(bf16[64,128]{1,0:T(8,128)(2,1)S(1)} %fusion.12), channel_id=1, source_target_pairs={{96,0},{97,1},{98,2},{99,3},{100,4},{101,5},{102,6},{103,7},{104,8... | collective-permute-start | bytes 49160 | tf_op jit(solution)/shard_map/ppermute | solution.py:69
  109.7 1.2 shard_map.111
  110.9 35.5 %all_to_all.16 = bf16[8,2240,128]{2,1,0:T(8,128)(2,1)S(1)} all-to-all(bf16[8,2240,128]{2,1,0:T(8,128)(2,1)S(1)} %get-tuple-element.38), channel_id=1, replica_groups={{16,20,24,28,32,36,40,44},{17,21,25,29,33,37,41,45},{18,22,26,30,34,38,..., dimensions={0} | all-to-all | bytes 9175040 | tf_op jit(solution)/shard_map/all_to_all | solution.py:332
  146.5 1.2 collective-permute-done.30.other
  148.1 2.4 collective-permute-start.34
  150.5 1.8 collective-permute-start.32
  152.3 2.0 shard_map.112.before
  154.3 1.6 shard_map.113.image
  156.9 2.1 collective-permute-start.40
  159.5 2.6 %collective-permute-start.38 = (bf16[192,128]{1,0:T(8,128)(2,1)S(1)}, bf16[192,128]{1,0:T(8,128)(2,1)S(1)}, u32[]{:S(2)}, u32[]{:S(2)}) collective-permute-start(bf16[192,128]{1,0:T(8,128)(2,1)S(1)} %convert_element_type.210), channel_id=1, source_target_pairs={{4,0},{5,1},{6,2},{7,3},{8,4},{9,5},{10,6},{11,7},{12,8},{13,9},{1... | collective-permute-start | bytes 147464 | tf_op jit(solution)/shard_map/ppermute | solution.py:69
  162.3 3.2 %collective-permute-start.35 = (bf16[512,128]{1,0:T(8,128)(2,1)S(1)}, bf16[512,128]{1,0:T(8,128)(2,1)S(1)}, u32[]{:S(2)}, u32[]{:S(2)}) collective-permute-start(bf16[512,128]{1,0:T(8,128)(2,1)S(1)} %convert_element_type.209), channel_id=1, source_target_pairs={{4,0},{5,1},{6,2},{7,3},{8,4},{9,5},{10,6},{11,7},{12,8},{13,9},{1... | collective-permute-start | bytes 393224 | tf_op jit(solution)/shard_map/ppermute | solution.py:69
  167.6 2.2 collective-permute-start.41
  169.8 1.4 collective-permute-done.43.refs_2_
  172.0 1.2 collective-permute-done.44.refs_5_
  174.2 1.3 collective-permute-start.37
  175.5 1.7 collective-permute-done.45.refs_6_
  177.2 2.5 collective-permute-start.46
  180.6 1.6 collective-permute-done.46.refs_7_
  182.3 1.2 shard_map.116
  183.5 35.7 %all_to_all.17 = bf16[8,2240,128]{2,1,0:T(8,128)(2,1)S(1)} all-to-all(bf16[8,2240,128]{2,1,0:T(8,128)(2,1)S(1)} %get-tuple-element.46), channel_id=1, replica_groups={{16,20,24,28,32,36,40,44},{17,21,25,29,33,37,41,45},{18,22,26,30,34,38,..., dimensions={0} | all-to-all | bytes 9175040 | tf_op jit(solution)/shard_map/all_to_all | solution.py:332
  219.3 1.2 collective-permute-done.47.other
  221.1 2.4 collective-permute-start.51
  223.6 1.8 collective-permute-start.49
  225.3 2.0 shard_map.117.before
  227.4 1.6 shard_map.118.image
  230.1 2.6 %collective-permute-start.53 = (bf16[192,128]{1,0:T(8,128)(2,1)S(1)}, bf16[192,128]{1,0:T(8,128)(2,1)S(1)}, u32[]{:S(2)}, u32[]{:S(2)}) collective-permute-start(bf16[192,128]{1,0:T(8,128)(2,1)S(1)} %convert_element_type.223), channel_id=1, source_target_pairs={{12,0},{13,1},{14,2},{15,3},{0,4},{1,5},{2,6},{3,7},{4,8},{5,9},{6... | collective-permute-start | bytes 147464 | tf_op jit(solution)/shard_map/ppermute | solution.py:69
  233.4 2.4 collective-permute-done.54
  236.8 1.5 collective-permute-start.57
  238.9 2.7 %collective-permute-start.55 = (bf16[192,128]{1,0:T(8,128)(2,1)S(1)}, bf16[192,128]{1,0:T(8,128)(2,1)S(1)}, u32[]{:S(2)}, u32[]{:S(2)}) collective-permute-start(bf16[192,128]{1,0:T(8,128)(2,1)S(1)} %fusion.13), channel_id=1, source_target_pairs={{1,0},{2,1},{3,2},{0,3},{5,4},{6,5},{7,6},{4,7},{9,8},{10,9},{11,1... | collective-permute-start | bytes 147464 | tf_op jit(solution)/shard_map/ppermute | solution.py:69
  242.5 1.2 collective-permute-done.56
  243.8 1.2 collective-permute-done.58
  245.0 1.0 collective-permute-start.59
  246.1 2.9 %collective-permute-done.59 = bf16[128,128]{1,0:T(8,128)(2,1)S(1)} collective-permute-done((bf16[128,128]{1,0:T(8,128)(2,1)S(1)}, bf16[128,128]{1,0:T(8,128)(2,1)S(1)}, u32[]{:S(2)}, u32[]{:S(2)}) %collective-permute-start.59) | collective-permute-done | bytes 32800 | tf_op jit(solution)/shard_map/ppermute | solution.py:69
  249.0 2.6 %collective-permute-start.60 = (bf16[64,128]{1,0:T(8,128)(2,1)S(1)}, bf16[64,128]{1,0:T(8,128)(2,1)S(1)}, u32[]{:S(2)}, u32[]{:S(2)}) collective-permute-start(bf16[64,128]{1,0:T(8,128)(2,1)S(1)} %fusion.10), channel_id=1, source_target_pairs={{96,0},{97,1},{98,2},{99,3},{100,4},{101,5},{102,6},{103,7},{104,8... | collective-permute-start | bytes 49160 | tf_op jit(solution)/shard_map/ppermute | solution.py:69
  251.6 2.4 collective-permute-done.60
  (158 shorter events, 26.2 us)
Async XLA Ops:
  4.5 13.5 %collective-permute-start.2 = (bf16[832,128]{1,0:T(8,128)(2,1)S(1)}, bf16[832,128]{1,0:T(8,128)(2,1)S(1)}, u32[]{:S(2)}, u32[]{:S(2)}) collective-permute-start(bf16[832,128]{1,0:T(8,128)(2,1)S(1)} %pad_maximum_fusion.1), channel_id=1, source_target_pairs={{8,0},{9,1},{10,2},{11,3},{12,4},{13,5},{14,6},{15,7},{0,8},{1,9},... | collective-permute-start | bytes 638984 | tf_op jit(solution)/shard_map/ppermute | solution.py:69
  8.5 9.5 %collective-permute-start.1 = (bf16[832,128]{1,0:T(8,128)(2,1)S(1)}, bf16[832,128]{1,0:T(8,128)(2,1)S(1)}, u32[]{:S(2)}, u32[]{:S(2)}) collective-permute-start(bf16[832,128]{1,0:T(8,128)(2,1)S(1)} %pad_maximum_fusion.1), channel_id=1, source_target_pairs={{12,0},{13,1},{14,2},{15,3},{0,4},{1,5},{2,6},{3,7},{4,8},{5,9},{6... | collective-permute-start | bytes 638984 | tf_op jit(solution)/shard_map/ppermute | solution.py:69
  9.5 8.5 %collective-permute-start = (bf16[832,128]{1,0:T(8,128)(2,1)S(1)}, bf16[832,128]{1,0:T(8,128)(2,1)S(1)}, u32[]{:S(2)}, u32[]{:S(2)}) collective-permute-start(bf16[832,128]{1,0:T(8,128)(2,1)S(1)} %pad_maximum_fusion.1), channel_id=1, source_target_pairs={{4,0},{5,1},{6,2},{7,3},{8,4},{9,5},{10,6},{11,7},{12,8},{13,9},{1... | collective-permute-start | bytes 638984 | tf_op jit(solution)/shard_map/ppermute | solution.py:69
  12.8 17.4 %collective-permute-start.10 = (bf16[384,512]{1,0:T(8,128)(2,1)S(1)}, bf16[384,512]{1,0:T(8,128)(2,1)S(1)}, u32[]{:S(2)}, u32[]{:S(2)}) collective-permute-start(bf16[384,512]{1,0:T(8,128)(2,1)S(1)} %pad_maximum_fusion.refs_7_.refs_8_), channel_id=1, source_target_pairs={{12,0},{13,1},{14,2},{15,3},{0,4},{1,5},{2,6},{3,7},{4,8},{5,9},{6... | collective-permute-start | bytes 1179656 | tf_op jit(solution)/shard_map/ppermute | solution.py:69
  12.9 14.3 %collective-permute-start.9 = (bf16[384,512]{1,0:T(8,128)(2,1)S(1)}, bf16[384,512]{1,0:T(8,128)(2,1)S(1)}, u32[]{:S(2)}, u32[]{:S(2)}) collective-permute-start(bf16[384,512]{1,0:T(8,128)(2,1)S(1)} %pad_maximum_fusion.refs_7_.refs_8_), channel_id=1, source_target_pairs={{4,0},{5,1},{6,2},{7,3},{8,4},{9,5},{10,6},{11,7},{12,8},{13,9},{1... | collective-permute-start | bytes 1179656 | tf_op jit(solution)/shard_map/ppermute | solution.py:69
  18.1 6.8 %collective-permute-start.5 = (bf16[320,128]{1,0:T(8,128)(2,1)S(1)}, bf16[320,128]{1,0:T(8,128)(2,1)S(1)}, u32[]{:S(2)}, u32[]{:S(2)}) collective-permute-start(bf16[320,128]{1,0:T(8,128)(2,1)S(1)} %fusion.31), channel_id=1, source_target_pairs={{2,0},{3,1},{0,2},{1,3},{6,4},{7,5},{4,6},{5,7},{10,8},{11,9},{8,1... | collective-permute-start | bytes 245768 | tf_op jit(solution)/shard_map/ppermute | solution.py:69
  21.3 5.7 %collective-permute-start.4 = (bf16[320,128]{1,0:T(8,128)(2,1)S(1)}, bf16[320,128]{1,0:T(8,128)(2,1)S(1)}, u32[]{:S(2)}, u32[]{:S(2)}) collective-permute-start(bf16[320,128]{1,0:T(8,128)(2,1)S(1)} %fusion.31), channel_id=1, source_target_pairs={{3,0},{0,1},{1,2},{2,3},{7,4},{4,5},{5,6},{6,7},{11,8},{8,9},{9,10... | collective-permute-start | bytes 245768 | tf_op jit(solution)/shard_map/ppermute | solution.py:69
  22.0 5.0 %collective-permute-start.3 = (bf16[320,128]{1,0:T(8,128)(2,1)S(1)}, bf16[320,128]{1,0:T(8,128)(2,1)S(1)}, u32[]{:S(2)}, u32[]{:S(2)}) collective-permute-start(bf16[320,128]{1,0:T(8,128)(2,1)S(1)} %fusion.31), channel_id=1, source_target_pairs={{1,0},{2,1},{3,2},{0,3},{5,4},{6,5},{7,6},{4,7},{9,8},{10,9},{11,1... | collective-permute-start | bytes 245768 | tf_op jit(solution)/shard_map/ppermute | solution.py:69
  27.1 1.4 collective-permute-start.6
  27.2 8.6 %collective-permute-start.11 = (bf16[192,512]{1,0:T(8,128)(2,1)S(1)}, bf16[192,512]{1,0:T(8,128)(2,1)S(1)}, u32[]{:S(2)}, u32[]{:S(2)}) collective-permute-start(bf16[192,512]{1,0:T(8,128)(2,1)S(1)} %slice.194), channel_id=1, source_target_pairs={{4,0},{5,1},{6,2},{7,3},{8,4},{9,5},{10,6},{11,7},{12,8},{13,9},{1... | collective-permute-start | bytes 589832 | tf_op jit(solution)/shard_map/ppermute | solution.py:69
  28.6 4.2 %collective-permute-start.7 = (bf16[192,128]{1,0:T(8,128)(2,1)S(1)}, bf16[192,128]{1,0:T(8,128)(2,1)S(1)}, u32[]{:S(2)}, u32[]{:S(2)}) collective-permute-start(bf16[192,128]{1,0:T(8,128)(2,1)S(1)} %get-tuple-element.27), channel_id=1, source_target_pairs={{32,0},{33,1},{34,2},{35,3},{36,4},{37,5},{38,6},{39,7},{40,8},{41... | collective-permute-start | bytes 147464 | tf_op jit(solution)/shard_map/ppermute | solution.py:69
  30.2 7.0 %collective-permute-start.12 = (bf16[192,512]{1,0:T(8,128)(2,1)S(1)}, bf16[192,512]{1,0:T(8,128)(2,1)S(1)}, u32[]{:S(2)}, u32[]{:S(2)}) collective-permute-start(bf16[192,512]{1,0:T(8,128)(2,1)S(1)} %slice.195), channel_id=1, source_target_pairs={{12,0},{13,1},{14,2},{15,3},{0,4},{1,5},{2,6},{3,7},{4,8},{5,9},{6... | collective-permute-start | bytes 589832 | tf_op jit(solution)/shard_map/ppermute | solution.py:69
  33.0 5.0 %collective-permute-start.8 = (bf16[64,128]{1,0:T(8,128)(2,1)S(1)}, bf16[64,128]{1,0:T(8,128)(2,1)S(1)}, u32[]{:S(2)}, u32[]{:S(2)}) collective-permute-start(bf16[64,128]{1,0:T(8,128)(2,1)S(1)} %shard_map.105), channel_id=1, source_target_pairs={{96,0},{97,1},{98,2},{99,3},{100,4},{101,5},{102,6},{103,7},{104,8... | collective-permute-start | bytes 49160 | tf_op jit(solution)/shard_map/ppermute | solution.py:69
  39.2 42.0 %slice-start = ((s8[5242880]{0:T(1024)(128)(4,1)}), s8[4194304]{0:T(1024)(128)(4,1)S(1)}, s32[]{:S(2)}) async-start(s8[5242880]{0:T(1024)(128)(4,1)} %bitcast.27), calls=%async_computation.3 | async-start | bytes 8388608
  39.2 42.0 %slice-start.1 = ((s8[5242880]{0:T(1024)(128)(4,1)}), s8[1048576]{0:T(1024)(128)(4,1)S(1)}, s32[]{:S(2)}) async-start(s8[5242880]{0:T(1024)(128)(4,1)} %bitcast.27), calls=%async_computation.4 | async-start | bytes 2097152
  75.2 1.3 collective-permute-start.13
  76.6 6.6 %collective-permute-start.14 = (bf16[4,2048,128]{2,1,0:T(8,128)(2,1)S(1)}, bf16[4,2048,128]{2,1,0:T(8,128)(2,1)S(1)}, u32[]{:S(2)}, u32[]{:S(2)}) collective-permute-start(bf16[4,2048,128]{2,1,0:T(8,128)(2,1)S(1)} %constant_dynamic-slice_fusion.2), channel_id=1, source_target_pairs={{16,0},{17,1},{18,2},{19,3},{20,4},{21,5},{22,6},{23,7},{24,8},{25... | collective-permute-start | bytes 6291464 | tf_op jit(solution)/shard_map/ppermute | solution.py:69
  77.0 7.9 %collective-permute-start.17 = (bf16[64,128]{1,0:T(8,128)(2,1)S(1)}, bf16[64,128]{1,0:T(8,128)(2,1)S(1)}, u32[]{:S(2)}, u32[]{:S(2)}) collective-permute-start(bf16[64,128]{1,0:T(8,128)(2,1)S(1)} %get-tuple-element.84), channel_id=1, source_target_pairs={{96,0},{97,1},{98,2},{99,3},{100,4},{101,5},{102,6},{103,7},{104,8... | collective-permute-start | bytes 49160 | tf_op jit(solution)/shard_map/ppermute | solution.py:69
  79.4 5.5 %collective-permute-start.16 = (bf16[64,128]{1,0:T(8,128)(2,1)S(1)}, bf16[64,128]{1,0:T(8,128)(2,1)S(1)}, u32[]{:S(2)}, u32[]{:S(2)}) collective-permute-start(bf16[64,128]{1,0:T(8,128)(2,1)S(1)} %get-tuple-element.84), channel_id=1, source_target_pairs={{64,0},{65,1},{66,2},{67,3},{68,4},{69,5},{70,6},{71,7},{72,8},{73... | collective-permute-start | bytes 49160 | tf_op jit(solution)/shard_map/ppermute | solution.py:69
  79.4 5.5 %collective-permute-start.15 = (bf16[64,128]{1,0:T(8,128)(2,1)S(1)}, bf16[64,128]{1,0:T(8,128)(2,1)S(1)}, u32[]{:S(2)}, u32[]{:S(2)}) collective-permute-start(bf16[64,128]{1,0:T(8,128)(2,1)S(1)} %get-tuple-element.85), channel_id=1, source_target_pairs={{32,0},{33,1},{34,2},{35,3},{36,4},{37,5},{38,6},{39,7},{40,8},{41... | collective-permute-start | bytes 49160 | tf_op jit(solution)/shard_map/ppermute | solution.py:69
  85.8 7.0 %collective-permute-start.23 = (bf16[192,128]{1,0:T(8,128)(2,1)S(1)}, bf16[192,128]{1,0:T(8,128)(2,1)S(1)}, u32[]{:S(2)}, u32[]{:S(2)}) collective-permute-start(bf16[192,128]{1,0:T(8,128)(2,1)S(1)} %convert_element_type.196), channel_id=1, source_target_pairs={{8,0},{9,1},{10,2},{11,3},{12,4},{13,5},{14,6},{15,7},{0,8},{1,9},... | collective-permute-start | bytes 147464 | tf_op jit(solution)/shard_map/ppermute | solution.py:69
  85.9 6.9 %collective-permute-start.22 = (bf16[192,128]{1,0:T(8,128)(2,1)S(1)}, bf16[192,128]{1,0:T(8,128)(2,1)S(1)}, u32[]{:S(2)}, u32[]{:S(2)}) collective-permute-start(bf16[192,128]{1,0:T(8,128)(2,1)S(1)} %convert_element_type.196), channel_id=1, source_target_pairs={{12,0},{13,1},{14,2},{15,3},{0,4},{1,5},{2,6},{3,7},{4,8},{5,9},{6... | collective-permute-start | bytes 147464 | tf_op jit(solution)/shard_map/ppermute | solution.py:69
  87.3 5.6 %collective-permute-start.21 = (bf16[192,128]{1,0:T(8,128)(2,1)S(1)}, bf16[192,128]{1,0:T(8,128)(2,1)S(1)}, u32[]{:S(2)}, u32[]{:S(2)}) collective-permute-start(bf16[192,128]{1,0:T(8,128)(2,1)S(1)} %convert_element_type.196), channel_id=1, source_target_pairs={{4,0},{5,1},{6,2},{7,3},{8,4},{9,5},{10,6},{11,7},{12,8},{13,9},{1... | collective-permute-start | bytes 147464 | tf_op jit(solution)/shard_map/ppermute | solution.py:69
  89.6 9.7 %collective-permute-start.19 = (bf16[512,128]{1,0:T(8,128)(2,1)S(1)}, bf16[512,128]{1,0:T(8,128)(2,1)S(1)}, u32[]{:S(2)}, u32[]{:S(2)}) collective-permute-start(bf16[512,128]{1,0:T(8,128)(2,1)S(1)} %convert_element_type.195), channel_id=1, source_target_pairs={{12,0},{13,1},{14,2},{15,3},{0,4},{1,5},{2,6},{3,7},{4,8},{5,9},{6... | collective-permute-start | bytes 393224 | tf_op jit(solution)/shard_map/ppermute | solution.py:69
  89.6 9.7 %collective-permute-start.18 = (bf16[512,128]{1,0:T(8,128)(2,1)S(1)}, bf16[512,128]{1,0:T(8,128)(2,1)S(1)}, u32[]{:S(2)}, u32[]{:S(2)}) collective-permute-start(bf16[512,128]{1,0:T(8,128)(2,1)S(1)} %convert_element_type.195), channel_id=1, source_target_pairs={{4,0},{5,1},{6,2},{7,3},{8,4},{9,5},{10,6},{11,7},{12,8},{13,9},{1... | collective-permute-start | bytes 393224 | tf_op jit(solution)/shard_map/ppermute | solution.py:69
  92.9 5.9 %collective-permute-start.26 = (bf16[192,128]{1,0:T(8,128)(2,1)S(1)}, bf16[192,128]{1,0:T(8,128)(2,1)S(1)}, u32[]{:S(2)}, u32[]{:S(2)}) collective-permute-start(bf16[192,128]{1,0:T(8,128)(2,1)S(1)} %get-tuple-element.66), channel_id=1, source_target_pairs={{2,0},{3,1},{0,2},{1,3},{6,4},{7,5},{4,6},{5,7},{10,8},{11,9},{8,1... | collective-permute-start | bytes 147464 | tf_op jit(solution)/shard_map/ppermute | solution.py:69
  93.8 5.5 %collective-permute-start.25 = (bf16[192,128]{1,0:T(8,128)(2,1)S(1)}, bf16[192,128]{1,0:T(8,128)(2,1)S(1)}, u32[]{:S(2)}, u32[]{:S(2)}) collective-permute-start(bf16[192,128]{1,0:T(8,128)(2,1)S(1)} %get-tuple-element.66), channel_id=1, source_target_pairs={{3,0},{0,1},{1,2},{2,3},{7,4},{4,5},{5,6},{6,7},{11,8},{8,9},{9,10... | collective-permute-start | bytes 147464 | tf_op jit(solution)/shard_map/ppermute | solution.py:69
  94.8 4.5 %collective-permute-start.24 = (bf16[192,128]{1,0:T(8,128)(2,1)S(1)}, bf16[192,128]{1,0:T(8,128)(2,1)S(1)}, u32[]{:S(2)}, u32[]{:S(2)}) collective-permute-start(bf16[192,128]{1,0:T(8,128)(2,1)S(1)} %get-tuple-element.66), channel_id=1, source_target_pairs={{1,0},{2,1},{3,2},{0,3},{5,4},{6,5},{7,6},{4,7},{9,8},{10,9},{11,1... | collective-permute-start | bytes 147464 | tf_op jit(solution)/shard_map/ppermute | solution.py:69
  99.3 1.3 collective-permute-start.27
  100.7 4.0 %collective-permute-start.28 = (bf16[128,128]{1,0:T(8,128)(2,1)S(1)}, bf16[128,128]{1,0:T(8,128)(2,1)S(1)}, u32[]{:S(2)}, u32[]{:S(2)}) collective-permute-start(bf16[128,128]{1,0:T(8,128)(2,1)S(1)} %get-tuple-element.64), channel_id=1, source_target_pairs={{32,0},{33,1},{34,2},{35,3},{36,4},{37,5},{38,6},{39,7},{40,8},{41... | collective-permute-start | bytes 98312 | tf_op jit(solution)/shard_map/ppermute | solution.py:69
  102.2 6.5 %collective-permute-start.20 = (bf16[512,128]{1,0:T(8,128)(2,1)S(1)}, bf16[512,128]{1,0:T(8,128)(2,1)S(1)}, u32[]{:S(2)}, u32[]{:S(2)}) collective-permute-start(bf16[512,128]{1,0:T(8,128)(2,1)S(1)} %convert_element_type.195), channel_id=1, source_target_pairs={{8,0},{9,1},{10,2},{11,3},{12,4},{13,5},{14,6},{15,7},{0,8},{1,9},... | collective-permute-start | bytes 393224 | tf_op jit(solution)/shard_map/ppermute | solution.py:69
  104.7 5.0 %collective-permute-start.29 = (bf16[64,128]{1,0:T(8,128)(2,1)S(1)}, bf16[64,128]{1,0:T(8,128)(2,1)S(1)}, u32[]{:S(2)}, u32[]{:S(2)}) collective-permute-start(bf16[64,128]{1,0:T(8,128)(2,1)S(1)} %fusion.12), channel_id=1, source_target_pairs={{96,0},{97,1},{98,2},{99,3},{100,4},{101,5},{102,6},{103,7},{104,8... | collective-permute-start | bytes 49160 | tf_op jit(solution)/shard_map/ppermute | solution.py:69
  146.4 1.3 collective-permute-start.30
  147.8 6.5 %collective-permute-start.31 = (bf16[4,2048,128]{2,1,0:T(8,128)(2,1)S(1)}, bf16[4,2048,128]{2,1,0:T(8,128)(2,1)S(1)}, u32[]{:S(2)}, u32[]{:S(2)}) collective-permute-start(bf16[4,2048,128]{2,1,0:T(8,128)(2,1)S(1)} %constant_dynamic-slice_fusion.1), channel_id=1, source_target_pairs={{16,0},{17,1},{18,2},{19,3},{20,4},{21,5},{22,6},{23,7},{24,8},{25... | collective-permute-start | bytes 6291464 | tf_op jit(solution)/shard_map/ppermute | solution.py:69
  148.1 7.9 %collective-permute-start.34 = (bf16[64,128]{1,0:T(8,128)(2,1)S(1)}, bf16[64,128]{1,0:T(8,128)(2,1)S(1)}, u32[]{:S(2)}, u32[]{:S(2)}) collective-permute-start(bf16[64,128]{1,0:T(8,128)(2,1)S(1)} %get-tuple-element.82), channel_id=1, source_target_pairs={{96,0},{97,1},{98,2},{99,3},{100,4},{101,5},{102,6},{103,7},{104,8... | collective-permute-start | bytes 49160 | tf_op jit(solution)/shard_map/ppermute | solution.py:69
  150.5 5.5 %collective-permute-start.33 = (bf16[64,128]{1,0:T(8,128)(2,1)S(1)}, bf16[64,128]{1,0:T(8,128)(2,1)S(1)}, u32[]{:S(2)}, u32[]{:S(2)}) collective-permute-start(bf16[64,128]{1,0:T(8,128)(2,1)S(1)} %get-tuple-element.82), channel_id=1, source_target_pairs={{64,0},{65,1},{66,2},{67,3},{68,4},{69,5},{70,6},{71,7},{72,8},{73... | collective-permute-start | bytes 49160 | tf_op jit(solution)/shard_map/ppermute | solution.py:69
  150.5 5.4 %collective-permute-start.32 = (bf16[64,128]{1,0:T(8,128)(2,1)S(1)}, bf16[64,128]{1,0:T(8,128)(2,1)S(1)}, u32[]{:S(2)}, u32[]{:S(2)}) collective-permute-start(bf16[64,128]{1,0:T(8,128)(2,1)S(1)} %get-tuple-element.83), channel_id=1, source_target_pairs={{32,0},{33,1},{34,2},{35,3},{36,4},{37,5},{38,6},{39,7},{40,8},{41... | collective-permute-start | bytes 49160 | tf_op jit(solution)/shard_map/ppermute | solution.py:69
  156.9 8.6 %collective-permute-start.40 = (bf16[192,128]{1,0:T(8,128)(2,1)S(1)}, bf16[192,128]{1,0:T(8,128)(2,1)S(1)}, u32[]{:S(2)}, u32[]{:S(2)}) collective-permute-start(bf16[192,128]{1,0:T(8,128)(2,1)S(1)} %convert_element_type.210), channel_id=1, source_target_pairs={{8,0},{9,1},{10,2},{11,3},{12,4},{13,5},{14,6},{15,7},{0,8},{1,9},... | collective-permute-start | bytes 147464 | tf_op jit(solution)/shard_map/ppermute | solution.py:69
  158.9 6.6 %collective-permute-start.39 = (bf16[192,128]{1,0:T(8,128)(2,1)S(1)}, bf16[192,128]{1,0:T(8,128)(2,1)S(1)}, u32[]{:S(2)}, u32[]{:S(2)}) collective-permute-start(bf16[192,128]{1,0:T(8,128)(2,1)S(1)} %convert_element_type.210), channel_id=1, source_target_pairs={{12,0},{13,1},{14,2},{15,3},{0,4},{1,5},{2,6},{3,7},{4,8},{5,9},{6... | collective-permute-start | bytes 147464 | tf_op jit(solution)/shard_map/ppermute | solution.py:69
  159.5 6.0 %collective-permute-start.38 = (bf16[192,128]{1,0:T(8,128)(2,1)S(1)}, bf16[192,128]{1,0:T(8,128)(2,1)S(1)}, u32[]{:S(2)}, u32[]{:S(2)}) collective-permute-start(bf16[192,128]{1,0:T(8,128)(2,1)S(1)} %convert_element_type.210), channel_id=1, source_target_pairs={{4,0},{5,1},{6,2},{7,3},{8,4},{9,5},{10,6},{11,7},{12,8},{13,9},{1... | collective-permute-start | bytes 147464 | tf_op jit(solution)/shard_map/ppermute | solution.py:69
  162.2 9.7 %collective-permute-start.36 = (bf16[512,128]{1,0:T(8,128)(2,1)S(1)}, bf16[512,128]{1,0:T(8,128)(2,1)S(1)}, u32[]{:S(2)}, u32[]{:S(2)}) collective-permute-start(bf16[512,128]{1,0:T(8,128)(2,1)S(1)} %convert_element_type.209), channel_id=1, source_target_pairs={{12,0},{13,1},{14,2},{15,3},{0,4},{1,5},{2,6},{3,7},{4,8},{5,9},{6... | collective-permute-start | bytes 393224 | tf_op jit(solution)/shard_map/ppermute | solution.py:69
  162.3 9.6 %collective-permute-start.35 = (bf16[512,128]{1,0:T(8,128)(2,1)S(1)}, bf16[512,128]{1,0:T(8,128)(2,1)S(1)}, u32[]{:S(2)}, u32[]{:S(2)}) collective-permute-start(bf16[512,128]{1,0:T(8,128)(2,1)S(1)} %convert_element_type.209), channel_id=1, source_target_pairs={{4,0},{5,1},{6,2},{7,3},{8,4},{9,5},{10,6},{11,7},{12,8},{13,9},{1... | collective-permute-start | bytes 393224 | tf_op jit(solution)/shard_map/ppermute | solution.py:69
  165.5 5.7 %collective-permute-start.43 = (bf16[192,128]{1,0:T(8,128)(2,1)S(1)}, bf16[192,128]{1,0:T(8,128)(2,1)S(1)}, u32[]{:S(2)}, u32[]{:S(2)}) collective-permute-start(bf16[192,128]{1,0:T(8,128)(2,1)S(1)} %get-tuple-element.62), channel_id=1, source_target_pairs={{2,0},{3,1},{0,2},{1,3},{6,4},{7,5},{4,6},{5,7},{10,8},{11,9},{8,1... | collective-permute-start | bytes 147464 | tf_op jit(solution)/shard_map/ppermute | solution.py:69
  166.6 5.3 %collective-permute-start.42 = (bf16[192,128]{1,0:T(8,128)(2,1)S(1)}, bf16[192,128]{1,0:T(8,128)(2,1)S(1)}, u32[]{:S(2)}, u32[]{:S(2)}) collective-permute-start(bf16[192,128]{1,0:T(8,128)(2,1)S(1)} %get-tuple-element.62), channel_id=1, source_target_pairs={{3,0},{0,1},{1,2},{2,3},{7,4},{4,5},{5,6},{6,7},{11,8},{8,9},{9,10... | collective-permute-start | bytes 147464 | tf_op jit(solution)/shard_map/ppermute | solution.py:69
  167.6 4.3 %collective-permute-start.41 = (bf16[192,128]{1,0:T(8,128)(2,1)S(1)}, bf16[192,128]{1,0:T(8,128)(2,1)S(1)}, u32[]{:S(2)}, u32[]{:S(2)}) collective-permute-start(bf16[192,128]{1,0:T(8,128)(2,1)S(1)} %get-tuple-element.62), channel_id=1, source_target_pairs={{1,0},{2,1},{3,2},{0,3},{5,4},{6,5},{7,6},{4,7},{9,8},{10,9},{11,1... | collective-permute-start | bytes 147464 | tf_op jit(solution)/shard_map/ppermute | solution.py:69
  171.9 1.3 collective-permute-start.44
  173.2 4.0 %collective-permute-start.45 = (bf16[128,128]{1,0:T(8,128)(2,1)S(1)}, bf16[128,128]{1,0:T(8,128)(2,1)S(1)}, u32[]{:S(2)}, u32[]{:S(2)}) collective-permute-start(bf16[128,128]{1,0:T(8,128)(2,1)S(1)} %get-tuple-element.60), channel_id=1, source_target_pairs={{32,0},{33,1},{34,2},{35,3},{36,4},{37,5},{38,6},{39,7},{40,8},{41... | collective-permute-start | bytes 98312 | tf_op jit(solution)/shard_map/ppermute | solution.py:69
  174.2 6.5 %collective-permute-start.37 = (bf16[512,128]{1,0:T(8,128)(2,1)S(1)}, bf16[512,128]{1,0:T(8,128)(2,1)S(1)}, u32[]{:S(2)}, u32[]{:S(2)}) collective-permute-start(bf16[512,128]{1,0:T(8,128)(2,1)S(1)} %convert_element_type.209), channel_id=1, source_target_pairs={{8,0},{9,1},{10,2},{11,3},{12,4},{13,5},{14,6},{15,7},{0,8},{1,9},... | collective-permute-start | bytes 393224 | tf_op jit(solution)/shard_map/ppermute | solution.py:69
  177.2 5.0 %collective-permute-start.46 = (bf16[64,128]{1,0:T(8,128)(2,1)S(1)}, bf16[64,128]{1,0:T(8,128)(2,1)S(1)}, u32[]{:S(2)}, u32[]{:S(2)}) collective-permute-start(bf16[64,128]{1,0:T(8,128)(2,1)S(1)} %fusion.11), channel_id=1, source_target_pairs={{96,0},{97,1},{98,2},{99,3},{100,4},{101,5},{102,6},{103,7},{104,8... | collective-permute-start | bytes 49160 | tf_op jit(solution)/shard_map/ppermute | solution.py:69
  219.2 1.3 collective-permute-start.47
  220.6 6.7 %collective-permute-start.48 = (bf16[4,2048,128]{2,1,0:T(8,128)(2,1)S(1)}, bf16[4,2048,128]{2,1,0:T(8,128)(2,1)S(1)}, u32[]{:S(2)}, u32[]{:S(2)}) collective-permute-start(bf16[4,2048,128]{2,1,0:T(8,128)(2,1)S(1)} %constant_dynamic-slice_fusion), channel_id=1, source_target_pairs={{16,0},{17,1},{18,2},{19,3},{20,4},{21,5},{22,6},{23,7},{24,8},{25... | collective-permute-start | bytes 6291464 | tf_op jit(solution)/shard_map/ppermute | solution.py:69
  221.1 7.9 %collective-permute-start.51 = (bf16[64,128]{1,0:T(8,128)(2,1)S(1)}, bf16[64,128]{1,0:T(8,128)(2,1)S(1)}, u32[]{:S(2)}, u32[]{:S(2)}) collective-permute-start(bf16[64,128]{1,0:T(8,128)(2,1)S(1)} %get-tuple-element.80), channel_id=1, source_target_pairs={{96,0},{97,1},{98,2},{99,3},{100,4},{101,5},{102,6},{103,7},{104,8... | collective-permute-start | bytes 49160 | tf_op jit(solution)/shard_map/ppermute | solution.py:69
  223.6 5.5 %collective-permute-start.50 = (bf16[64,128]{1,0:T(8,128)(2,1)S(1)}, bf16[64,128]{1,0:T(8,128)(2,1)S(1)}, u32[]{:S(2)}, u32[]{:S(2)}) collective-permute-start(bf16[64,128]{1,0:T(8,128)(2,1)S(1)} %get-tuple-element.80), channel_id=1, source_target_pairs={{64,0},{65,1},{66,2},{67,3},{68,4},{69,5},{70,6},{71,7},{72,8},{73... | collective-permute-start | bytes 49160 | tf_op jit(solution)/shard_map/ppermute | solution.py:69
  223.6 5.5 %collective-permute-start.49 = (bf16[64,128]{1,0:T(8,128)(2,1)S(1)}, bf16[64,128]{1,0:T(8,128)(2,1)S(1)}, u32[]{:S(2)}, u32[]{:S(2)}) collective-permute-start(bf16[64,128]{1,0:T(8,128)(2,1)S(1)} %get-tuple-element.81), channel_id=1, source_target_pairs={{32,0},{33,1},{34,2},{35,3},{36,4},{37,5},{38,6},{39,7},{40,8},{41... | collective-permute-start | bytes 49160 | tf_op jit(solution)/shard_map/ppermute | solution.py:69
  227.4 26.7 %copy-start.4 = (bf16[3,64,512]{2,1,0:T(8,128)(2,1)S(1)}, bf16[3,64,512]{2,1,0:T(8,128)(2,1)}, u32[]{:S(2)}) copy-start(bf16[3,64,512]{2,1,0:T(8,128)(2,1)} %param.16) | copy-start | bytes 589828
  230.1 5.7 %collective-permute-start.54 = (bf16[192,128]{1,0:T(8,128)(2,1)S(1)}, bf16[192,128]{1,0:T(8,128)(2,1)S(1)}, u32[]{:S(2)}, u32[]{:S(2)}) collective-permute-start(bf16[192,128]{1,0:T(8,128)(2,1)S(1)} %convert_element_type.223), channel_id=1, source_target_pairs={{8,0},{9,1},{10,2},{11,3},{12,4},{13,5},{14,6},{15,7},{0,8},{1,9},... | collective-permute-start | bytes 147464 | tf_op jit(solution)/shard_map/ppermute | solution.py:69
  230.1 5.9 %collective-permute-start.53 = (bf16[192,128]{1,0:T(8,128)(2,1)S(1)}, bf16[192,128]{1,0:T(8,128)(2,1)S(1)}, u32[]{:S(2)}, u32[]{:S(2)}) collective-permute-start(bf16[192,128]{1,0:T(8,128)(2,1)S(1)} %convert_element_type.223), channel_id=1, source_target_pairs={{12,0},{13,1},{14,2},{15,3},{0,4},{1,5},{2,6},{3,7},{4,8},{5,9},{6... | collective-permute-start | bytes 147464 | tf_op jit(solution)/shard_map/ppermute | solution.py:69
  232.7 4.1 %collective-permute-start.52 = (bf16[192,128]{1,0:T(8,128)(2,1)S(1)}, bf16[192,128]{1,0:T(8,128)(2,1)S(1)}, u32[]{:S(2)}, u32[]{:S(2)}) collective-permute-start(bf16[192,128]{1,0:T(8,128)(2,1)S(1)} %convert_element_type.223), channel_id=1, source_target_pairs={{4,0},{5,1},{6,2},{7,3},{8,4},{9,5},{10,6},{11,7},{12,8},{13,9},{1... | collective-permute-start | bytes 147464 | tf_op jit(solution)/shard_map/ppermute | solution.py:69
  236.8 5.7 %collective-permute-start.57 = (bf16[192,128]{1,0:T(8,128)(2,1)S(1)}, bf16[192,128]{1,0:T(8,128)(2,1)S(1)}, u32[]{:S(2)}, u32[]{:S(2)}) collective-permute-start(bf16[192,128]{1,0:T(8,128)(2,1)S(1)} %fusion.13), channel_id=1, source_target_pairs={{2,0},{3,1},{0,2},{1,3},{6,4},{7,5},{4,6},{5,7},{10,8},{11,9},{8,1... | collective-permute-start | bytes 147464 | tf_op jit(solution)/shard_map/ppermute | solution.py:69
  238.3 5.3 %collective-permute-start.56 = (bf16[192,128]{1,0:T(8,128)(2,1)S(1)}, bf16[192,128]{1,0:T(8,128)(2,1)S(1)}, u32[]{:S(2)}, u32[]{:S(2)}) collective-permute-start(bf16[192,128]{1,0:T(8,128)(2,1)S(1)} %fusion.13), channel_id=1, source_target_pairs={{3,0},{0,1},{1,2},{2,3},{7,4},{4,5},{5,6},{6,7},{11,8},{8,9},{9,10... | collective-permute-start | bytes 147464 | tf_op jit(solution)/shard_map/ppermute | solution.py:69
  238.9 4.8 %collective-permute-start.55 = (bf16[192,128]{1,0:T(8,128)(2,1)S(1)}, bf16[192,128]{1,0:T(8,128)(2,1)S(1)}, u32[]{:S(2)}, u32[]{:S(2)}) collective-permute-start(bf16[192,128]{1,0:T(8,128)(2,1)S(1)} %fusion.13), channel_id=1, source_target_pairs={{1,0},{2,1},{3,2},{0,3},{5,4},{6,5},{7,6},{4,7},{9,8},{10,9},{11,1... | collective-permute-start | bytes 147464 | tf_op jit(solution)/shard_map/ppermute | solution.py:69
  243.7 1.3 collective-permute-start.58
  245.0 4.0 %collective-permute-start.59 = (bf16[128,128]{1,0:T(8,128)(2,1)S(1)}, bf16[128,128]{1,0:T(8,128)(2,1)S(1)}, u32[]{:S(2)}, u32[]{:S(2)}) collective-permute-start(bf16[128,128]{1,0:T(8,128)(2,1)S(1)} %get-tuple-element.56), channel_id=1, source_target_pairs={{32,0},{33,1},{34,2},{35,3},{36,4},{37,5},{38,6},{39,7},{40,8},{41... | collective-permute-start | bytes 98312 | tf_op jit(solution)/shard_map/ppermute | solution.py:69
  249.0 5.0 %collective-permute-start.60 = (bf16[64,128]{1,0:T(8,128)(2,1)S(1)}, bf16[64,128]{1,0:T(8,128)(2,1)S(1)}, u32[]{:S(2)}, u32[]{:S(2)}) collective-permute-start(bf16[64,128]{1,0:T(8,128)(2,1)S(1)} %fusion.10), channel_id=1, source_target_pairs={{96,0},{97,1},{98,2},{99,3},{100,4},{101,5},{102,6},{103,7},{104,8... | collective-permute-start | bytes 49160 | tf_op jit(solution)/shard_map/ppermute | solution.py:69
  (4 other events, 6.9 us)

commit v8 on v6

--- a/solution.py
+++ b/solution.py
@@ -148,11 +148,14 @@
     start = jnp.sum(jnp.where(put, jnp.where(live, row, 0)[:, :, None], 0), axis=1)
     n_pair = jnp.sum((key == 0).astype(jnp.int32), axis=1)
     n_live = jnp.sum((key < 2).astype(jnp.int32), axis=1)
-    return order.reshape(-1), start.reshape(-1), n_pair, n_live
-
-
-def near_kernel(width, order, start, lo, hi, blocks, field, before, out):
+    slots = order + start // 64 * 256
+    return jnp.concatenate([slots.reshape(-1), jnp.zeros_like(n_pair), n_pair, n_live])
+
+
+def near_kernel(part, width, table, blocks, field, before, out):
     rows = range(NBD)
+    lo = [table[NBD * SLOTS + part * NBD + q] for q in rows]
+    hi = [table[NBD * SLOTS + (part + 1) * NBD + q] for q in rows]
     longest = hi[0] - lo[0]
     for q in rows[1:]:
         longest = jnp.maximum(longest, hi[q] - lo[q])
@@ -164,9 +167,10 @@
             for u in range(width):
                 j = lo[q] + width * i + u
                 at = q * SLOTS + jnp.minimum(j, SLOTS - 1)
-                block = blocks[q, order[at]]
+                slot = table[at]
+                block = blocks[q, slot & 255]
                 left.append(jnp.where(j < hi[q], block, jnp.zeros_like(block)))
-                row = jnp.minimum(start[at], field.shape[0] - BS)
+                row = jnp.minimum((slot >> 8) * 64, field.shape[0] - BS)
                 right.append(field[pl.ds(pl.multiple_of(row, 64), BS), :])
             new.append(
                 sums[q]
@@ -182,16 +186,16 @@
         out[q * BS : (q + 1) * BS, :] = sums[q]
 
 
-def near(width, order, start, lo, hi, near_blocks, field, before):
+def near(part, width, table, near_blocks, field, before):
     small, whole = pl.BlockSpec(memory_space=pltpu.SMEM), pl.BlockSpec(memory_space=pltpu.VMEM)
     return pl.pallas_call(
-        functools.partial(near_kernel, width),
-        in_specs=[small] * 4 + [whole] * 3,
+        functools.partial(near_kernel, part, width),
+        in_specs=[small] + [whole] * 3,
         out_specs=whole,
         out_shape=jax.ShapeDtypeStruct((ROWS, BS), F32),
         compiler_params=pltpu.CompilerParams(vmem_limit_bytes=12 * 2**20),
         cost_estimate=pl.CostEstimate(flops=2 * 80 * BS**3, bytes_accessed=10 * 2**20, transcendentals=0),
-    )(order, start, lo, hi, near_blocks, field, before)
+    )(table, near_blocks, field, before)
 
 
 def kernel_call(body, shapes, cost, *given):
@@ -292,8 +296,7 @@
     right_side, near_blocks, neighbours, counts, leaf_inverse, couple_left, couple_right, prec_left, prec_right
 ):
     half = 4 - 4 * (lax.axis_index("drop") % 2)
-    order, start, n_pair, n_live = slot_tables(neighbours, counts, half)
-    none = jnp.zeros_like(n_pair)
+    table = slot_tables(neighbours, counts, half)
     c_left, c_right, left, right = (
         f.reshape(TERMS, ROWS) for f in (couple_left, couple_right, prec_left, prec_right)
     )
@@ -311,7 +314,7 @@
 
     for step in range(ITERS):
         given = [*z_ring, *sums, *facts]
-        given = given + [order, start, n_pair, n_live] if step == 0 else [field] + given
+        given = given + [table] if step == 0 else [field] + given
         field, pieces = kernel_call(
             functools.partial(start_kernel, step > 0), (field_shape, piece_shape), 500, *given
         )
@@ -324,8 +327,8 @@
         other = move(own, CORE)
         c_sums = siblings_beside(c_other, c_terms)
         x = field[:ROWS]
-        image = near(8, order, start, none, n_pair, near_blocks, pieces.reshape(8 * PIECE, BS), x)
-        image = near(8, order, start, n_pair, n_live, near_blocks, other.reshape(4 * RING, BS), image)
+        image = near(0, 8, table, near_blocks, pieces.reshape(8 * PIECE, BS), x)
+        image = near(1, 8, table, near_blocks, other.reshape(4 * RING, BS), image)
         resid, z, terms = kernel_call(
             finish_kernel,
             (((ROWS, BS), F32), ((ROWS, BS), F32), ((TERMS, BS), F32)),

time: 255 us -> 255 us (level)
  transfers between devices with their start and end apart: 61 -> 61, of which waited for: 33 -> 31; matrix products, arithmetic and copies ran while one was open for 2% -> 2% of each run, Pallas kernels for 3% -> 3%
where the time goes in v8:
time: 255 us; the launch traced here: 254 us
  blocking collectives  106 us (42%)
  starting transfers between devices  86.1 us (34%)
  waiting for transfers between devices  35.6 us (14%)
  Pallas kernels  14.8 us (6%)
  matrix products  5.43 us (2%)
  other arithmetic  3.91 us (2%)
    all_to_all x3, blocking collectives, on_device(): lax.all_to_all(pieces, AXES, 0, 0, tiled=True, axis_index_groups=EIGHTS)  106 us
    ppermute x61, starting transfers between devices, move(): return lax.ppermute(array, AXES, pairs)  86.1 us
    ppermute x61, waiting for transfers between devices, move(): return lax.ppermute(array, AXES, pairs)  35.6 us
    pallas_call x6, Pallas kernels, near(): pl.pallas_call(functools.partial(near_kernel, part, width), in_specs=[sma...  8.12 us
    pallas_call x8, Pallas kernels, kernel_call(): pl.pallas_call(body, in_specs=[whole] * len(given), out_specs=[whole] * l...  6.67 us
  transfers between devices with their start and end apart: 61, of which 31 were waited for; matrix products, arithmetic and copies ran while one was open for 2% of the time, Pallas kernels for 3%

profile of v8, /device:TPU:0, one launch (start us, length us, event | category | flops | bytes accessed | tf_op | source)
XLA Modules:
  0.0 254.1 jit_solution(5003342810665542780)
XLA Ops:
  0.6 1.3 fusion.74
  2.0 1.2 fusion.73
  3.2 1.1 fusion.71
  4.5 4.0 %collective-permute-start.2 = (bf16[832,128]{1,0:T(8,128)(2,1)S(1)}, bf16[832,128]{1,0:T(8,128)(2,1)S(1)}, u32[]{:S(2)}, u32[]{:S(2)}) collective-permute-start(bf16[832,128]{1,0:T(8,128)(2,1)S(1)} %pad_maximum_fusion.1), channel_id=1, source_target_pairs={{8,0},{9,1},{10,2},{11,3},{12,4},{13,5},{14,6},{15,7},{0,8},{1,9},... | collective-permute-start | bytes 638984 | tf_op jit(solution)/shard_map/ppermute | solution.py:69
  9.5 2.2 collective-permute-start
  12.9 3.2 %collective-permute-start.9 = (bf16[384,512]{1,0:T(8,128)(2,1)S(1)}, bf16[384,512]{1,0:T(8,128)(2,1)S(1)}, u32[]{:S(2)}, u32[]{:S(2)}) collective-permute-start(bf16[384,512]{1,0:T(8,128)(2,1)S(1)} %pad_maximum_fusion.refs_7_.refs_8_), channel_id=1, source_target_pairs={{4,0},{5,1},{6,2},{7,3},{8,4},{9,5},{10,6},{11,7},{12,8},{13,9},{1... | collective-permute-start | bytes 1179656 | tf_op jit(solution)/shard_map/ppermute | solution.py:69
  18.1 3.3 %collective-permute-start.5 = (bf16[320,128]{1,0:T(8,128)(2,1)S(1)}, bf16[320,128]{1,0:T(8,128)(2,1)S(1)}, u32[]{:S(2)}, u32[]{:S(2)}) collective-permute-start(bf16[320,128]{1,0:T(8,128)(2,1)S(1)} %fusion.57), channel_id=1, source_target_pairs={{2,0},{3,1},{0,2},{1,3},{6,4},{7,5},{4,6},{5,7},{10,8},{11,9},{8,1... | collective-permute-start | bytes 245768 | tf_op jit(solution)/shard_map/ppermute | solution.py:69
  22.0 2.6 %collective-permute-start.3 = (bf16[320,128]{1,0:T(8,128)(2,1)S(1)}, bf16[320,128]{1,0:T(8,128)(2,1)S(1)}, u32[]{:S(2)}, u32[]{:S(2)}) collective-permute-start(bf16[320,128]{1,0:T(8,128)(2,1)S(1)} %fusion.57), channel_id=1, source_target_pairs={{1,0},{2,1},{3,2},{0,3},{5,4},{6,5},{7,6},{4,7},{9,8},{10,9},{11,1... | collective-permute-start | bytes 245768 | tf_op jit(solution)/shard_map/ppermute | solution.py:69
  24.9 2.1 collective-permute-done.4
  27.2 1.2 collective-permute-done.6
  29.2 1.5 collective-permute-start.7
  31.0 3.3 %collective-permute-start.11 = (bf16[192,512]{1,0:T(8,128)(2,1)S(1)}, bf16[192,512]{1,0:T(8,128)(2,1)S(1)}, u32[]{:S(2)}, u32[]{:S(2)}) collective-permute-start(bf16[192,512]{1,0:T(8,128)(2,1)S(1)} %slice.259), channel_id=1, source_target_pairs={{4,0},{5,1},{6,2},{7,3},{8,4},{9,5},{10,6},{11,7},{12,8},{13,9},{1... | collective-permute-start | bytes 589832 | tf_op jit(solution)/shard_map/ppermute | solution.py:69
  34.6 2.1 collective-permute-start.8
  37.9 1.7 collective-permute-done.8.refs_6_
  39.5 1.2 shard_map.104
  40.7 35.0 %all_to_all.15 = bf16[8,2240,128]{2,1,0:T(8,128)(2,1)S(1)} all-to-all(bf16[8,2240,128]{2,1,0:T(8,128)(2,1)S(1)} %get-tuple-element.26), channel_id=1, replica_groups={{16,20,24,28,32,36,40,44},{17,21,25,29,33,37,41,45},{18,22,26,30,34,38,..., dimensions={0} | all-to-all | bytes 9175040 | tf_op jit(solution)/shard_map/all_to_all | solution.py:321
  75.8 1.2 collective-permute-done.13.other
  77.5 2.4 collective-permute-start.17
  80.0 1.8 collective-permute-start.15
  82.9 1.6 shard_map.106.image
  86.8 1.5 collective-permute-start.22
  88.4 1.7 collective-permute-start.21
  90.5 2.9 %collective-permute-start.18 = (bf16[512,128]{1,0:T(8,128)(2,1)S(1)}, bf16[512,128]{1,0:T(8,128)(2,1)S(1)}, u32[]{:S(2)}, u32[]{:S(2)}) collective-permute-start(bf16[512,128]{1,0:T(8,128)(2,1)S(1)} %convert_element_type.222), channel_id=1, source_target_pairs={{4,0},{5,1},{6,2},{7,3},{8,4},{9,5},{10,6},{11,7},{12,8},{13,9},{1... | collective-permute-start | bytes 393224 | tf_op jit(solution)/shard_map/ppermute | solution.py:69
  93.4 1.3 collective-permute-start.26
  95.7 2.3 collective-permute-start.24
  98.0 1.3 collective-permute-done.26.refs_2_
  100.2 1.2 collective-permute-done.27.refs_5_
  102.4 1.5 collective-permute-start.20
  103.9 1.6 collective-permute-done.28.refs_6_
  105.4 3.1 %collective-permute-start.29 = (bf16[64,128]{1,0:T(8,128)(2,1)S(1)}, bf16[64,128]{1,0:T(8,128)(2,1)S(1)}, u32[]{:S(2)}, u32[]{:S(2)}) collective-permute-start(bf16[64,128]{1,0:T(8,128)(2,1)S(1)} %fusion.15), channel_id=1, source_target_pairs={{96,0},{97,1},{98,2},{99,3},{100,4},{101,5},{102,6},{103,7},{104,8... | collective-permute-start | bytes 49160 | tf_op jit(solution)/shard_map/ppermute | solution.py:69
  108.9 1.6 collective-permute-done.29.refs_7_
  110.5 1.2 shard_map.109
  111.7 35.7 %all_to_all.16 = bf16[8,2240,128]{2,1,0:T(8,128)(2,1)S(1)} all-to-all(bf16[8,2240,128]{2,1,0:T(8,128)(2,1)S(1)} %get-tuple-element.34), channel_id=1, replica_groups={{16,20,24,28,32,36,40,44},{17,21,25,29,33,37,41,45},{18,22,26,30,34,38,..., dimensions={0} | all-to-all | bytes 9175040 | tf_op jit(solution)/shard_map/all_to_all | solution.py:321
  147.5 1.2 collective-permute-done.30.other
  149.1 2.4 collective-permute-start.34
  151.6 1.7 collective-permute-start.32
  154.4 1.6 shard_map.111.image
  158.4 2.3 collective-permute-start.39
  161.7 1.1 collective-permute-start.36
  162.8 2.2 collective-permute-start.35
  166.1 1.6 collective-permute-start.42
  167.7 1.6 collective-permute-start.41
  169.3 1.4 collective-permute-done.43.refs_2_
  171.9 1.2 collective-permute-done.44.refs_5_
  173.9 2.2 collective-permute-start.37
  177.1 3.3 %collective-permute-start.46 = (bf16[64,128]{1,0:T(8,128)(2,1)S(1)}, bf16[64,128]{1,0:T(8,128)(2,1)S(1)}, u32[]{:S(2)}, u32[]{:S(2)}) collective-permute-start(bf16[64,128]{1,0:T(8,128)(2,1)S(1)} %fusion.14), channel_id=1, source_target_pairs={{96,0},{97,1},{98,2},{99,3},{100,4},{101,5},{102,6},{103,7},{104,8... | collective-permute-start | bytes 49160 | tf_op jit(solution)/shard_map/ppermute | solution.py:69
  180.4 1.8 collective-permute-done.46.refs_7_
  182.2 1.2 shard_map.114
  183.3 35.3 %all_to_all.17 = bf16[8,2240,128]{2,1,0:T(8,128)(2,1)S(1)} all-to-all(bf16[8,2240,128]{2,1,0:T(8,128)(2,1)S(1)} %get-tuple-element.42), channel_id=1, replica_groups={{16,20,24,28,32,36,40,44},{17,21,25,29,33,37,41,45},{18,22,26,30,34,38,..., dimensions={0} | all-to-all | bytes 9175040 | tf_op jit(solution)/shard_map/all_to_all | solution.py:321
  218.8 1.2 collective-permute-done.47.other
  220.7 2.4 collective-permute-start.51
  223.2 1.7 collective-permute-start.49
  226.0 1.6 shard_map.116.image
  229.4 1.5 collective-permute-start.54
  230.9 1.3 collective-permute-start.53
  232.2 1.9 collective-permute-start.52
  235.0 1.2 collective-permute-done.53
  238.4 2.2 collective-permute-start.55
  240.6 1.4 collective-permute-done.57
  242.8 1.2 collective-permute-done.58
  244.0 1.2 collective-permute-start.59
  245.2 2.8 %collective-permute-done.59 = bf16[128,128]{1,0:T(8,128)(2,1)S(1)} collective-permute-done((bf16[128,128]{1,0:T(8,128)(2,1)S(1)}, bf16[128,128]{1,0:T(8,128)(2,1)S(1)}, u32[]{:S(2)}, u32[]{:S(2)}) %collective-permute-start.59) | collective-permute-done | bytes 32800 | tf_op jit(solution)/shard_map/ppermute | solution.py:69
  248.0 3.0 %collective-permute-start.60 = (bf16[64,128]{1,0:T(8,128)(2,1)S(1)}, bf16[64,128]{1,0:T(8,128)(2,1)S(1)}, u32[]{:S(2)}, u32[]{:S(2)}) collective-permute-start(bf16[64,128]{1,0:T(8,128)(2,1)S(1)} %fusion.13), channel_id=1, source_target_pairs={{96,0},{97,1},{98,2},{99,3},{100,4},{101,5},{102,6},{103,7},{104,8... | collective-permute-start | bytes 49160 | tf_op jit(solution)/shard_map/ppermute | solution.py:69
  251.1 2.0 collective-permute-done.60
  (165 shorter events, 33.1 us)
Async XLA Ops:
  4.5 13.5 %collective-permute-start.2 = (bf16[832,128]{1,0:T(8,128)(2,1)S(1)}, bf16[832,128]{1,0:T(8,128)(2,1)S(1)}, u32[]{:S(2)}, u32[]{:S(2)}) collective-permute-start(bf16[832,128]{1,0:T(8,128)(2,1)S(1)} %pad_maximum_fusion.1), channel_id=1, source_target_pairs={{8,0},{9,1},{10,2},{11,3},{12,4},{13,5},{14,6},{15,7},{0,8},{1,9},... | collective-permute-start | bytes 638984 | tf_op jit(solution)/shard_map/ppermute | solution.py:69
  8.5 9.5 %collective-permute-start.1 = (bf16[832,128]{1,0:T(8,128)(2,1)S(1)}, bf16[832,128]{1,0:T(8,128)(2,1)S(1)}, u32[]{:S(2)}, u32[]{:S(2)}) collective-permute-start(bf16[832,128]{1,0:T(8,128)(2,1)S(1)} %pad_maximum_fusion.1), channel_id=1, source_target_pairs={{12,0},{13,1},{14,2},{15,3},{0,4},{1,5},{2,6},{3,7},{4,8},{5,9},{6... | collective-permute-start | bytes 638984 | tf_op jit(solution)/shard_map/ppermute | solution.py:69
  9.5 8.5 %collective-permute-start = (bf16[832,128]{1,0:T(8,128)(2,1)S(1)}, bf16[832,128]{1,0:T(8,128)(2,1)S(1)}, u32[]{:S(2)}, u32[]{:S(2)}) collective-permute-start(bf16[832,128]{1,0:T(8,128)(2,1)S(1)} %pad_maximum_fusion.1), channel_id=1, source_target_pairs={{4,0},{5,1},{6,2},{7,3},{8,4},{9,5},{10,6},{11,7},{12,8},{13,9},{1... | collective-permute-start | bytes 638984 | tf_op jit(solution)/shard_map/ppermute | solution.py:69
  12.8 18.1 %collective-permute-start.10 = (bf16[384,512]{1,0:T(8,128)(2,1)S(1)}, bf16[384,512]{1,0:T(8,128)(2,1)S(1)}, u32[]{:S(2)}, u32[]{:S(2)}) collective-permute-start(bf16[384,512]{1,0:T(8,128)(2,1)S(1)} %pad_maximum_fusion.refs_7_.refs_8_), channel_id=1, source_target_pairs={{12,0},{13,1},{14,2},{15,3},{0,4},{1,5},{2,6},{3,7},{4,8},{5,9},{6... | collective-permute-start | bytes 1179656 | tf_op jit(solution)/shard_map/ppermute | solution.py:69
  12.9 18.1 %collective-permute-start.9 = (bf16[384,512]{1,0:T(8,128)(2,1)S(1)}, bf16[384,512]{1,0:T(8,128)(2,1)S(1)}, u32[]{:S(2)}, u32[]{:S(2)}) collective-permute-start(bf16[384,512]{1,0:T(8,128)(2,1)S(1)} %pad_maximum_fusion.refs_7_.refs_8_), channel_id=1, source_target_pairs={{4,0},{5,1},{6,2},{7,3},{8,4},{9,5},{10,6},{11,7},{12,8},{13,9},{1... | collective-permute-start | bytes 1179656 | tf_op jit(solution)/shard_map/ppermute | solution.py:69
  18.1 6.8 %collective-permute-start.5 = (bf16[320,128]{1,0:T(8,128)(2,1)S(1)}, bf16[320,128]{1,0:T(8,128)(2,1)S(1)}, u32[]{:S(2)}, u32[]{:S(2)}) collective-permute-start(bf16[320,128]{1,0:T(8,128)(2,1)S(1)} %fusion.57), channel_id=1, source_target_pairs={{2,0},{3,1},{0,2},{1,3},{6,4},{7,5},{4,6},{5,7},{10,8},{11,9},{8,1... | collective-permute-start | bytes 245768 | tf_op jit(solution)/shard_map/ppermute | solution.py:69
  21.3 5.7 %collective-permute-start.4 = (bf16[320,128]{1,0:T(8,128)(2,1)S(1)}, bf16[320,128]{1,0:T(8,128)(2,1)S(1)}, u32[]{:S(2)}, u32[]{:S(2)}) collective-permute-start(bf16[320,128]{1,0:T(8,128)(2,1)S(1)} %fusion.57), channel_id=1, source_target_pairs={{3,0},{0,1},{1,2},{2,3},{7,4},{4,5},{5,6},{6,7},{11,8},{8,9},{9,10... | collective-permute-start | bytes 245768 | tf_op jit(solution)/shard_map/ppermute | solution.py:69
  22.0 5.0 %collective-permute-start.3 = (bf16[320,128]{1,0:T(8,128)(2,1)S(1)}, bf16[320,128]{1,0:T(8,128)(2,1)S(1)}, u32[]{:S(2)}, u32[]{:S(2)}) collective-permute-start(bf16[320,128]{1,0:T(8,128)(2,1)S(1)} %fusion.57), channel_id=1, source_target_pairs={{1,0},{2,1},{3,2},{0,3},{5,4},{6,5},{7,6},{4,7},{9,8},{10,9},{11,1... | collective-permute-start | bytes 245768 | tf_op jit(solution)/shard_map/ppermute | solution.py:69
  27.1 1.4 collective-permute-start.6
  29.2 5.1 %collective-permute-start.7 = (bf16[192,128]{1,0:T(8,128)(2,1)S(1)}, bf16[192,128]{1,0:T(8,128)(2,1)S(1)}, u32[]{:S(2)}, u32[]{:S(2)}) collective-permute-start(bf16[192,128]{1,0:T(8,128)(2,1)S(1)} %maximum_maximum_fusion), channel_id=1, source_target_pairs={{32,0},{33,1},{34,2},{35,3},{36,4},{37,5},{38,6},{39,7},{40,8},{41... | collective-permute-start | bytes 147464 | tf_op jit(solution)/shard_map/ppermute | solution.py:69
  30.9 7.0 %collective-permute-start.12 = (bf16[192,512]{1,0:T(8,128)(2,1)S(1)}, bf16[192,512]{1,0:T(8,128)(2,1)S(1)}, u32[]{:S(2)}, u32[]{:S(2)}) collective-permute-start(bf16[192,512]{1,0:T(8,128)(2,1)S(1)} %slice.260), channel_id=1, source_target_pairs={{12,0},{13,1},{14,2},{15,3},{0,4},{1,5},{2,6},{3,7},{4,8},{5,9},{6... | collective-permute-start | bytes 589832 | tf_op jit(solution)/shard_map/ppermute | solution.py:69
  31.0 6.5 %collective-permute-start.11 = (bf16[192,512]{1,0:T(8,128)(2,1)S(1)}, bf16[192,512]{1,0:T(8,128)(2,1)S(1)}, u32[]{:S(2)}, u32[]{:S(2)}) collective-permute-start(bf16[192,512]{1,0:T(8,128)(2,1)S(1)} %slice.259), channel_id=1, source_target_pairs={{4,0},{5,1},{6,2},{7,3},{8,4},{9,5},{10,6},{11,7},{12,8},{13,9},{1... | collective-permute-start | bytes 589832 | tf_op jit(solution)/shard_map/ppermute | solution.py:69
  34.6 5.0 %collective-permute-start.8 = (bf16[64,128]{1,0:T(8,128)(2,1)S(1)}, bf16[64,128]{1,0:T(8,128)(2,1)S(1)}, u32[]{:S(2)}, u32[]{:S(2)}) collective-permute-start(bf16[64,128]{1,0:T(8,128)(2,1)S(1)} %fusion.2), channel_id=1, source_target_pairs={{96,0},{97,1},{98,2},{99,3},{100,4},{101,5},{102,6},{103,7},{104,8... | collective-permute-start | bytes 49160 | tf_op jit(solution)/shard_map/ppermute | solution.py:69
  40.7 41.0 %slice-start = ((s8[5242880]{0:T(1024)(128)(4,1)}), s8[4194304]{0:T(1024)(128)(4,1)S(1)}, s32[]{:S(2)}) async-start(s8[5242880]{0:T(1024)(128)(4,1)} %bitcast.29), calls=%async_computation.3 | async-start | bytes 8388608
  40.7 41.0 %slice-start.1 = ((s8[5242880]{0:T(1024)(128)(4,1)}), s8[1048576]{0:T(1024)(128)(4,1)S(1)}, s32[]{:S(2)}) async-start(s8[5242880]{0:T(1024)(128)(4,1)} %bitcast.29), calls=%async_computation.4 | async-start | bytes 2097152
  75.7 1.3 collective-permute-start.13
  77.2 5.7 %collective-permute-start.14 = (bf16[4,2048,128]{2,1,0:T(8,128)(2,1)S(1)}, bf16[4,2048,128]{2,1,0:T(8,128)(2,1)S(1)}, u32[]{:S(2)}, u32[]{:S(2)}) collective-permute-start(bf16[4,2048,128]{2,1,0:T(8,128)(2,1)S(1)} %constant_dynamic-slice_fusion.2), channel_id=1, source_target_pairs={{16,0},{17,1},{18,2},{19,3},{20,4},{21,5},{22,6},{23,7},{24,8},{25... | collective-permute-start | bytes 6291464 | tf_op jit(solution)/shard_map/ppermute | solution.py:69
  77.5 7.0 %collective-permute-start.17 = (bf16[64,128]{1,0:T(8,128)(2,1)S(1)}, bf16[64,128]{1,0:T(8,128)(2,1)S(1)}, u32[]{:S(2)}, u32[]{:S(2)}) collective-permute-start(bf16[64,128]{1,0:T(8,128)(2,1)S(1)} %get-tuple-element.80), channel_id=1, source_target_pairs={{96,0},{97,1},{98,2},{99,3},{100,4},{101,5},{102,6},{103,7},{104,8... | collective-permute-start | bytes 49160 | tf_op jit(solution)/shard_map/ppermute | solution.py:69
  80.0 5.2 %collective-permute-start.16 = (bf16[64,128]{1,0:T(8,128)(2,1)S(1)}, bf16[64,128]{1,0:T(8,128)(2,1)S(1)}, u32[]{:S(2)}, u32[]{:S(2)}) collective-permute-start(bf16[64,128]{1,0:T(8,128)(2,1)S(1)} %get-tuple-element.80), channel_id=1, source_target_pairs={{64,0},{65,1},{66,2},{67,3},{68,4},{69,5},{70,6},{71,7},{72,8},{73... | collective-permute-start | bytes 49160 | tf_op jit(solution)/shard_map/ppermute | solution.py:69
  80.0 4.5 %collective-permute-start.15 = (bf16[64,128]{1,0:T(8,128)(2,1)S(1)}, bf16[64,128]{1,0:T(8,128)(2,1)S(1)}, u32[]{:S(2)}, u32[]{:S(2)}) collective-permute-start(bf16[64,128]{1,0:T(8,128)(2,1)S(1)} %get-tuple-element.81), channel_id=1, source_target_pairs={{32,0},{33,1},{34,2},{35,3},{36,4},{37,5},{38,6},{39,7},{40,8},{41... | collective-permute-start | bytes 49160 | tf_op jit(solution)/shard_map/ppermute | solution.py:69
  86.3 7.1 %collective-permute-start.23 = (bf16[192,128]{1,0:T(8,128)(2,1)S(1)}, bf16[192,128]{1,0:T(8,128)(2,1)S(1)}, u32[]{:S(2)}, u32[]{:S(2)}) collective-permute-start(bf16[192,128]{1,0:T(8,128)(2,1)S(1)} %convert_element_type.223), channel_id=1, source_target_pairs={{8,0},{9,1},{10,2},{11,3},{12,4},{13,5},{14,6},{15,7},{0,8},{1,9},... | collective-permute-start | bytes 147464 | tf_op jit(solution)/shard_map/ppermute | solution.py:69
  86.8 6.6 %collective-permute-start.22 = (bf16[192,128]{1,0:T(8,128)(2,1)S(1)}, bf16[192,128]{1,0:T(8,128)(2,1)S(1)}, u32[]{:S(2)}, u32[]{:S(2)}) collective-permute-start(bf16[192,128]{1,0:T(8,128)(2,1)S(1)} %convert_element_type.223), channel_id=1, source_target_pairs={{12,0},{13,1},{14,2},{15,3},{0,4},{1,5},{2,6},{3,7},{4,8},{5,9},{6... | collective-permute-start | bytes 147464 | tf_op jit(solution)/shard_map/ppermute | solution.py:69
  88.4 5.0 %collective-permute-start.21 = (bf16[192,128]{1,0:T(8,128)(2,1)S(1)}, bf16[192,128]{1,0:T(8,128)(2,1)S(1)}, u32[]{:S(2)}, u32[]{:S(2)}) collective-permute-start(bf16[192,128]{1,0:T(8,128)(2,1)S(1)} %convert_element_type.223), channel_id=1, source_target_pairs={{4,0},{5,1},{6,2},{7,3},{8,4},{9,5},{10,6},{11,7},{12,8},{13,9},{1... | collective-permute-start | bytes 147464 | tf_op jit(solution)/shard_map/ppermute | solution.py:69
  90.1 10.0 %collective-permute-start.19 = (bf16[512,128]{1,0:T(8,128)(2,1)S(1)}, bf16[512,128]{1,0:T(8,128)(2,1)S(1)}, u32[]{:S(2)}, u32[]{:S(2)}) collective-permute-start(bf16[512,128]{1,0:T(8,128)(2,1)S(1)} %convert_element_type.222), channel_id=1, source_target_pairs={{12,0},{13,1},{14,2},{15,3},{0,4},{1,5},{2,6},{3,7},{4,8},{5,9},{6... | collective-permute-start | bytes 393224 | tf_op jit(solution)/shard_map/ppermute | solution.py:69
  90.5 9.6 %collective-permute-start.18 = (bf16[512,128]{1,0:T(8,128)(2,1)S(1)}, bf16[512,128]{1,0:T(8,128)(2,1)S(1)}, u32[]{:S(2)}, u32[]{:S(2)}) collective-permute-start(bf16[512,128]{1,0:T(8,128)(2,1)S(1)} %convert_element_type.222), channel_id=1, source_target_pairs={{4,0},{5,1},{6,2},{7,3},{8,4},{9,5},{10,6},{11,7},{12,8},{13,9},{1... | collective-permute-start | bytes 393224 | tf_op jit(solution)/shard_map/ppermute | solution.py:69
  93.4 5.9 %collective-permute-start.26 = (bf16[192,128]{1,0:T(8,128)(2,1)S(1)}, bf16[192,128]{1,0:T(8,128)(2,1)S(1)}, u32[]{:S(2)}, u32[]{:S(2)}) collective-permute-start(bf16[192,128]{1,0:T(8,128)(2,1)S(1)} %get-tuple-element.62), channel_id=1, source_target_pairs={{2,0},{3,1},{0,2},{1,3},{6,4},{7,5},{4,6},{5,7},{10,8},{11,9},{8,1... | collective-permute-start | bytes 147464 | tf_op jit(solution)/shard_map/ppermute | solution.py:69
  94.8 5.3 %collective-permute-start.25 = (bf16[192,128]{1,0:T(8,128)(2,1)S(1)}, bf16[192,128]{1,0:T(8,128)(2,1)S(1)}, u32[]{:S(2)}, u32[]{:S(2)}) collective-permute-start(bf16[192,128]{1,0:T(8,128)(2,1)S(1)} %get-tuple-element.62), channel_id=1, source_target_pairs={{3,0},{0,1},{1,2},{2,3},{7,4},{4,5},{5,6},{6,7},{11,8},{8,9},{9,10... | collective-permute-start | bytes 147464 | tf_op jit(solution)/shard_map/ppermute | solution.py:69
  95.7 4.4 %collective-permute-start.24 = (bf16[192,128]{1,0:T(8,128)(2,1)S(1)}, bf16[192,128]{1,0:T(8,128)(2,1)S(1)}, u32[]{:S(2)}, u32[]{:S(2)}) collective-permute-start(bf16[192,128]{1,0:T(8,128)(2,1)S(1)} %get-tuple-element.62), channel_id=1, source_target_pairs={{1,0},{2,1},{3,2},{0,3},{5,4},{6,5},{7,6},{4,7},{9,8},{10,9},{11,1... | collective-permute-start | bytes 147464 | tf_op jit(solution)/shard_map/ppermute | solution.py:69
  100.1 1.3 collective-permute-start.27
  101.4 4.0 %collective-permute-start.28 = (bf16[128,128]{1,0:T(8,128)(2,1)S(1)}, bf16[128,128]{1,0:T(8,128)(2,1)S(1)}, u32[]{:S(2)}, u32[]{:S(2)}) collective-permute-start(bf16[128,128]{1,0:T(8,128)(2,1)S(1)} %get-tuple-element.60), channel_id=1, source_target_pairs={{32,0},{33,1},{34,2},{35,3},{36,4},{37,5},{38,6},{39,7},{40,8},{41... | collective-permute-start | bytes 98312 | tf_op jit(solution)/shard_map/ppermute | solution.py:69
  102.4 6.5 %collective-permute-start.20 = (bf16[512,128]{1,0:T(8,128)(2,1)S(1)}, bf16[512,128]{1,0:T(8,128)(2,1)S(1)}, u32[]{:S(2)}, u32[]{:S(2)}) collective-permute-start(bf16[512,128]{1,0:T(8,128)(2,1)S(1)} %convert_element_type.222), channel_id=1, source_target_pairs={{8,0},{9,1},{10,2},{11,3},{12,4},{13,5},{14,6},{15,7},{0,8},{1,9},... | collective-permute-start | bytes 393224 | tf_op jit(solution)/shard_map/ppermute | solution.py:69
  105.4 5.0 %collective-permute-start.29 = (bf16[64,128]{1,0:T(8,128)(2,1)S(1)}, bf16[64,128]{1,0:T(8,128)(2,1)S(1)}, u32[]{:S(2)}, u32[]{:S(2)}) collective-permute-start(bf16[64,128]{1,0:T(8,128)(2,1)S(1)} %fusion.15), channel_id=1, source_target_pairs={{96,0},{97,1},{98,2},{99,3},{100,4},{101,5},{102,6},{103,7},{104,8... | collective-permute-start | bytes 49160 | tf_op jit(solution)/shard_map/ppermute | solution.py:69
  147.4 1.3 collective-permute-start.30
  148.8 5.6 %collective-permute-start.31 = (bf16[4,2048,128]{2,1,0:T(8,128)(2,1)S(1)}, bf16[4,2048,128]{2,1,0:T(8,128)(2,1)S(1)}, u32[]{:S(2)}, u32[]{:S(2)}) collective-permute-start(bf16[4,2048,128]{2,1,0:T(8,128)(2,1)S(1)} %constant_dynamic-slice_fusion.1), channel_id=1, source_target_pairs={{16,0},{17,1},{18,2},{19,3},{20,4},{21,5},{22,6},{23,7},{24,8},{25... | collective-permute-start | bytes 6291464 | tf_op jit(solution)/shard_map/ppermute | solution.py:69
  149.1 6.9 %collective-permute-start.34 = (bf16[64,128]{1,0:T(8,128)(2,1)S(1)}, bf16[64,128]{1,0:T(8,128)(2,1)S(1)}, u32[]{:S(2)}, u32[]{:S(2)}) collective-permute-start(bf16[64,128]{1,0:T(8,128)(2,1)S(1)} %get-tuple-element.78), channel_id=1, source_target_pairs={{96,0},{97,1},{98,2},{99,3},{100,4},{101,5},{102,6},{103,7},{104,8... | collective-permute-start | bytes 49160 | tf_op jit(solution)/shard_map/ppermute | solution.py:69
  151.5 5.2 %collective-permute-start.33 = (bf16[64,128]{1,0:T(8,128)(2,1)S(1)}, bf16[64,128]{1,0:T(8,128)(2,1)S(1)}, u32[]{:S(2)}, u32[]{:S(2)}) collective-permute-start(bf16[64,128]{1,0:T(8,128)(2,1)S(1)} %get-tuple-element.78), channel_id=1, source_target_pairs={{64,0},{65,1},{66,2},{67,3},{68,4},{69,5},{70,6},{71,7},{72,8},{73... | collective-permute-start | bytes 49160 | tf_op jit(solution)/shard_map/ppermute | solution.py:69
  151.6 4.4 %collective-permute-start.32 = (bf16[64,128]{1,0:T(8,128)(2,1)S(1)}, bf16[64,128]{1,0:T(8,128)(2,1)S(1)}, u32[]{:S(2)}, u32[]{:S(2)}) collective-permute-start(bf16[64,128]{1,0:T(8,128)(2,1)S(1)} %get-tuple-element.79), channel_id=1, source_target_pairs={{32,0},{33,1},{34,2},{35,3},{36,4},{37,5},{38,6},{39,7},{40,8},{41... | collective-permute-start | bytes 49160 | tf_op jit(solution)/shard_map/ppermute | solution.py:69
  157.8 7.2 %collective-permute-start.40 = (bf16[192,128]{1,0:T(8,128)(2,1)S(1)}, bf16[192,128]{1,0:T(8,128)(2,1)S(1)}, u32[]{:S(2)}, u32[]{:S(2)}) collective-permute-start(bf16[192,128]{1,0:T(8,128)(2,1)S(1)} %convert_element_type.237), channel_id=1, source_target_pairs={{8,0},{9,1},{10,2},{11,3},{12,4},{13,5},{14,6},{15,7},{0,8},{1,9},... | collective-permute-start | bytes 147464 | tf_op jit(solution)/shard_map/ppermute | solution.py:69
  158.4 6.6 %collective-permute-start.39 = (bf16[192,128]{1,0:T(8,128)(2,1)S(1)}, bf16[192,128]{1,0:T(8,128)(2,1)S(1)}, u32[]{:S(2)}, u32[]{:S(2)}) collective-permute-start(bf16[192,128]{1,0:T(8,128)(2,1)S(1)} %convert_element_type.237), channel_id=1, source_target_pairs={{12,0},{13,1},{14,2},{15,3},{0,4},{1,5},{2,6},{3,7},{4,8},{5,9},{6... | collective-permute-start | bytes 147464 | tf_op jit(solution)/shard_map/ppermute | solution.py:69
  160.7 4.3 %collective-permute-start.38 = (bf16[192,128]{1,0:T(8,128)(2,1)S(1)}, bf16[192,128]{1,0:T(8,128)(2,1)S(1)}, u32[]{:S(2)}, u32[]{:S(2)}) collective-permute-start(bf16[192,128]{1,0:T(8,128)(2,1)S(1)} %convert_element_type.237), channel_id=1, source_target_pairs={{4,0},{5,1},{6,2},{7,3},{8,4},{9,5},{10,6},{11,7},{12,8},{13,9},{1... | collective-permute-start | bytes 147464 | tf_op jit(solution)/shard_map/ppermute | solution.py:69
  161.7 10.1 %collective-permute-start.36 = (bf16[512,128]{1,0:T(8,128)(2,1)S(1)}, bf16[512,128]{1,0:T(8,128)(2,1)S(1)}, u32[]{:S(2)}, u32[]{:S(2)}) collective-permute-start(bf16[512,128]{1,0:T(8,128)(2,1)S(1)} %convert_element_type.236), channel_id=1, source_target_pairs={{12,0},{13,1},{14,2},{15,3},{0,4},{1,5},{2,6},{3,7},{4,8},{5,9},{6... | collective-permute-start | bytes 393224 | tf_op jit(solution)/shard_map/ppermute | solution.py:69
  162.8 9.0 %collective-permute-start.35 = (bf16[512,128]{1,0:T(8,128)(2,1)S(1)}, bf16[512,128]{1,0:T(8,128)(2,1)S(1)}, u32[]{:S(2)}, u32[]{:S(2)}) collective-permute-start(bf16[512,128]{1,0:T(8,128)(2,1)S(1)} %convert_element_type.236), channel_id=1, source_target_pairs={{4,0},{5,1},{6,2},{7,3},{8,4},{9,5},{10,6},{11,7},{12,8},{13,9},{1... | collective-permute-start | bytes 393224 | tf_op jit(solution)/shard_map/ppermute | solution.py:69
  165.0 5.7 %collective-permute-start.43 = (bf16[192,128]{1,0:T(8,128)(2,1)S(1)}, bf16[192,128]{1,0:T(8,128)(2,1)S(1)}, u32[]{:S(2)}, u32[]{:S(2)}) collective-permute-start(bf16[192,128]{1,0:T(8,128)(2,1)S(1)} %get-tuple-element.58), channel_id=1, source_target_pairs={{2,0},{3,1},{0,2},{1,3},{6,4},{7,5},{4,6},{5,7},{10,8},{11,9},{8,1... | collective-permute-start | bytes 147464 | tf_op jit(solution)/shard_map/ppermute | solution.py:69
  166.1 5.3 %collective-permute-start.42 = (bf16[192,128]{1,0:T(8,128)(2,1)S(1)}, bf16[192,128]{1,0:T(8,128)(2,1)S(1)}, u32[]{:S(2)}, u32[]{:S(2)}) collective-permute-start(bf16[192,128]{1,0:T(8,128)(2,1)S(1)} %get-tuple-element.58), channel_id=1, source_target_pairs={{3,0},{0,1},{1,2},{2,3},{7,4},{4,5},{5,6},{6,7},{11,8},{8,9},{9,10... | collective-permute-start | bytes 147464 | tf_op jit(solution)/shard_map/ppermute | solution.py:69
  167.7 4.1 %collective-permute-start.41 = (bf16[192,128]{1,0:T(8,128)(2,1)S(1)}, bf16[192,128]{1,0:T(8,128)(2,1)S(1)}, u32[]{:S(2)}, u32[]{:S(2)}) collective-permute-start(bf16[192,128]{1,0:T(8,128)(2,1)S(1)} %get-tuple-element.58), channel_id=1, source_target_pairs={{1,0},{2,1},{3,2},{0,3},{5,4},{6,5},{7,6},{4,7},{9,8},{10,9},{11,1... | collective-permute-start | bytes 147464 | tf_op jit(solution)/shard_map/ppermute | solution.py:69
  171.8 1.3 collective-permute-start.44
  173.1 4.0 %collective-permute-start.45 = (bf16[128,128]{1,0:T(8,128)(2,1)S(1)}, bf16[128,128]{1,0:T(8,128)(2,1)S(1)}, u32[]{:S(2)}, u32[]{:S(2)}) collective-permute-start(bf16[128,128]{1,0:T(8,128)(2,1)S(1)} %get-tuple-element.56), channel_id=1, source_target_pairs={{32,0},{33,1},{34,2},{35,3},{36,4},{37,5},{38,6},{39,7},{40,8},{41... | collective-permute-start | bytes 98312 | tf_op jit(solution)/shard_map/ppermute | solution.py:69
  173.9 6.5 %collective-permute-start.37 = (bf16[512,128]{1,0:T(8,128)(2,1)S(1)}, bf16[512,128]{1,0:T(8,128)(2,1)S(1)}, u32[]{:S(2)}, u32[]{:S(2)}) collective-permute-start(bf16[512,128]{1,0:T(8,128)(2,1)S(1)} %convert_element_type.236), channel_id=1, source_target_pairs={{8,0},{9,1},{10,2},{11,3},{12,4},{13,5},{14,6},{15,7},{0,8},{1,9},... | collective-permute-start | bytes 393224 | tf_op jit(solution)/shard_map/ppermute | solution.py:69
  177.1 5.0 %collective-permute-start.46 = (bf16[64,128]{1,0:T(8,128)(2,1)S(1)}, bf16[64,128]{1,0:T(8,128)(2,1)S(1)}, u32[]{:S(2)}, u32[]{:S(2)}) collective-permute-start(bf16[64,128]{1,0:T(8,128)(2,1)S(1)} %fusion.14), channel_id=1, source_target_pairs={{96,0},{97,1},{98,2},{99,3},{100,4},{101,5},{102,6},{103,7},{104,8... | collective-permute-start | bytes 49160 | tf_op jit(solution)/shard_map/ppermute | solution.py:69
  218.7 1.3 collective-permute-start.47
  220.2 5.8 %collective-permute-start.48 = (bf16[4,2048,128]{2,1,0:T(8,128)(2,1)S(1)}, bf16[4,2048,128]{2,1,0:T(8,128)(2,1)S(1)}, u32[]{:S(2)}, u32[]{:S(2)}) collective-permute-start(bf16[4,2048,128]{2,1,0:T(8,128)(2,1)S(1)} %constant_dynamic-slice_fusion), channel_id=1, source_target_pairs={{16,0},{17,1},{18,2},{19,3},{20,4},{21,5},{22,6},{23,7},{24,8},{25... | collective-permute-start | bytes 6291464 | tf_op jit(solution)/shard_map/ppermute | solution.py:69
  220.7 6.9 %collective-permute-start.51 = (bf16[64,128]{1,0:T(8,128)(2,1)S(1)}, bf16[64,128]{1,0:T(8,128)(2,1)S(1)}, u32[]{:S(2)}, u32[]{:S(2)}) collective-permute-start(bf16[64,128]{1,0:T(8,128)(2,1)S(1)} %get-tuple-element.76), channel_id=1, source_target_pairs={{96,0},{97,1},{98,2},{99,3},{100,4},{101,5},{102,6},{103,7},{104,8... | collective-permute-start | bytes 49160 | tf_op jit(solution)/shard_map/ppermute | solution.py:69
  223.1 5.2 %collective-permute-start.50 = (bf16[64,128]{1,0:T(8,128)(2,1)S(1)}, bf16[64,128]{1,0:T(8,128)(2,1)S(1)}, u32[]{:S(2)}, u32[]{:S(2)}) collective-permute-start(bf16[64,128]{1,0:T(8,128)(2,1)S(1)} %get-tuple-element.76), channel_id=1, source_target_pairs={{64,0},{65,1},{66,2},{67,3},{68,4},{69,5},{70,6},{71,7},{72,8},{73... | collective-permute-start | bytes 49160 | tf_op jit(solution)/shard_map/ppermute | solution.py:69
  223.2 4.4 %collective-permute-start.49 = (bf16[64,128]{1,0:T(8,128)(2,1)S(1)}, bf16[64,128]{1,0:T(8,128)(2,1)S(1)}, u32[]{:S(2)}, u32[]{:S(2)}) collective-permute-start(bf16[64,128]{1,0:T(8,128)(2,1)S(1)} %get-tuple-element.77), channel_id=1, source_target_pairs={{32,0},{33,1},{34,2},{35,3},{36,4},{37,5},{38,6},{39,7},{40,8},{41... | collective-permute-start | bytes 49160 | tf_op jit(solution)/shard_map/ppermute | solution.py:69
  225.9 27.1 %copy-start.4 = (bf16[3,64,512]{2,1,0:T(8,128)(2,1)S(1)}, bf16[3,64,512]{2,1,0:T(8,128)(2,1)}, u32[]{:S(2)}) copy-start(bf16[3,64,512]{2,1,0:T(8,128)(2,1)} %param.16) | copy-start | bytes 589828
  229.4 5.6 %collective-permute-start.54 = (bf16[192,128]{1,0:T(8,128)(2,1)S(1)}, bf16[192,128]{1,0:T(8,128)(2,1)S(1)}, u32[]{:S(2)}, u32[]{:S(2)}) collective-permute-start(bf16[192,128]{1,0:T(8,128)(2,1)S(1)} %convert_element_type.250), channel_id=1, source_target_pairs={{8,0},{9,1},{10,2},{11,3},{12,4},{13,5},{14,6},{15,7},{0,8},{1,9},... | collective-permute-start | bytes 147464 | tf_op jit(solution)/shard_map/ppermute | solution.py:69
  230.9 5.3 %collective-permute-start.53 = (bf16[192,128]{1,0:T(8,128)(2,1)S(1)}, bf16[192,128]{1,0:T(8,128)(2,1)S(1)}, u32[]{:S(2)}, u32[]{:S(2)}) collective-permute-start(bf16[192,128]{1,0:T(8,128)(2,1)S(1)} %convert_element_type.250), channel_id=1, source_target_pairs={{12,0},{13,1},{14,2},{15,3},{0,4},{1,5},{2,6},{3,7},{4,8},{5,9},{6... | collective-permute-start | bytes 147464 | tf_op jit(solution)/shard_map/ppermute | solution.py:69
  232.2 4.1 %collective-permute-start.52 = (bf16[192,128]{1,0:T(8,128)(2,1)S(1)}, bf16[192,128]{1,0:T(8,128)(2,1)S(1)}, u32[]{:S(2)}, u32[]{:S(2)}) collective-permute-start(bf16[192,128]{1,0:T(8,128)(2,1)S(1)} %convert_element_type.250), channel_id=1, source_target_pairs={{4,0},{5,1},{6,2},{7,3},{8,4},{9,5},{10,6},{11,7},{12,8},{13,9},{1... | collective-permute-start | bytes 147464 | tf_op jit(solution)/shard_map/ppermute | solution.py:69
  236.3 5.7 %collective-permute-start.57 = (bf16[192,128]{1,0:T(8,128)(2,1)S(1)}, bf16[192,128]{1,0:T(8,128)(2,1)S(1)}, u32[]{:S(2)}, u32[]{:S(2)}) collective-permute-start(bf16[192,128]{1,0:T(8,128)(2,1)S(1)} %fusion.32), channel_id=1, source_target_pairs={{2,0},{3,1},{0,2},{1,3},{6,4},{7,5},{4,6},{5,7},{10,8},{11,9},{8,1... | collective-permute-start | bytes 147464 | tf_op jit(solution)/shard_map/ppermute | solution.py:69
  237.4 5.3 %collective-permute-start.56 = (bf16[192,128]{1,0:T(8,128)(2,1)S(1)}, bf16[192,128]{1,0:T(8,128)(2,1)S(1)}, u32[]{:S(2)}, u32[]{:S(2)}) collective-permute-start(bf16[192,128]{1,0:T(8,128)(2,1)S(1)} %fusion.32), channel_id=1, source_target_pairs={{3,0},{0,1},{1,2},{2,3},{7,4},{4,5},{5,6},{6,7},{11,8},{8,9},{9,10... | collective-permute-start | bytes 147464 | tf_op jit(solution)/shard_map/ppermute | solution.py:69
  238.4 4.3 %collective-permute-start.55 = (bf16[192,128]{1,0:T(8,128)(2,1)S(1)}, bf16[192,128]{1,0:T(8,128)(2,1)S(1)}, u32[]{:S(2)}, u32[]{:S(2)}) collective-permute-start(bf16[192,128]{1,0:T(8,128)(2,1)S(1)} %fusion.32), channel_id=1, source_target_pairs={{1,0},{2,1},{3,2},{0,3},{5,4},{6,5},{7,6},{4,7},{9,8},{10,9},{11,1... | collective-permute-start | bytes 147464 | tf_op jit(solution)/shard_map/ppermute | solution.py:69
  242.7 1.3 collective-permute-start.58
  244.0 4.0 %collective-permute-start.59 = (bf16[128,128]{1,0:T(8,128)(2,1)S(1)}, bf16[128,128]{1,0:T(8,128)(2,1)S(1)}, u32[]{:S(2)}, u32[]{:S(2)}) collective-permute-start(bf16[128,128]{1,0:T(8,128)(2,1)S(1)} %get-tuple-element.52), channel_id=1, source_target_pairs={{32,0},{33,1},{34,2},{35,3},{36,4},{37,5},{38,6},{39,7},{40,8},{41... | collective-permute-start | bytes 98312 | tf_op jit(solution)/shard_map/ppermute | solution.py:69
  248.0 5.0 %collective-permute-start.60 = (bf16[64,128]{1,0:T(8,128)(2,1)S(1)}, bf16[64,128]{1,0:T(8,128)(2,1)S(1)}, u32[]{:S(2)}, u32[]{:S(2)}) collective-permute-start(bf16[64,128]{1,0:T(8,128)(2,1)S(1)} %fusion.13), channel_id=1, source_target_pairs={{96,0},{97,1},{98,2},{99,3},{100,4},{101,5},{102,6},{103,7},{104,8... | collective-permute-start | bytes 49160 | tf_op jit(solution)/shard_map/ppermute | solution.py:69
  (4 other events, 9.5 us)
